TPU v7x, 32 devices: a whole 2x2x4 slice. The times are simulated.
32 devices in a mesh: seq: 8 (over z, x), dp: 4 (over y, core).
Axes of the slice: x: 2, y: 2, z: 4, core: 2. Of those that a mesh axis runs over, the one named last changes fastest.
Arguments:
- tokens: bfloat16 [4, 1024, 4096], P('dp', 'seq'), may hold values from -6 to 6
- frozen_projections: bfloat16 [3, 4, 1024, 2048], P(None, 'dp', 'seq'), may hold values from -8 to 8
- output_gradient: bfloat16 [4, 1024, 2048], P('dp', 'seq'), may hold values from -2 to 2
- down_weight: bfloat16 [3, 8, 4096], replicated, may hold values from -0.09375 to 0.09375
- up_weight: bfloat16 [3, 8, 2048], replicated, may hold values from -1 to 1
Outputs:
- down_gradient: float32 [3, 8, 4096], replicated
- up_gradient: float32 [3, 8, 2048], replicated
All inputs are finite; a program needn't handle non-finite values.
Results may differ from a plain program's by a relative error of at most 0.004.
The roundings to bfloat16 on the way count: a program that leaves them out, or rounds other values in their place, can miss the bound.
Values may be sent and summed in bfloat16 or wider, within the bound.
No kernel may reach another device: no remote copies, remote signals or barrier semaphores. Data moves between devices by JAX's collectives and lax.ppermute only.
A program may use at most 64 MiB of HBM per device.

v0:
```python
import jax
import jax.numpy as jnp
from jax import lax
from jax.sharding import PartitionSpec as P

HEAD_DIM = 128


adapter_scale = 2.0


def shifted(x, axis, by):
    peers = lax.axis_size(axis)
    return lax.ppermute(x, axis, [(i, (i + by) % peers) for i in range(peers)])


def attend(query_in, key_in, value_in, grad_in):
    score_scale = HEAD_DIM ** (-0.5)
    count, full_width = query_in.shape
    key_count = key_in.shape[0]
    heads_here = full_width // HEAD_DIM
    query_rows = query_in.reshape(count, heads_here, HEAD_DIM)
    key_rows = key_in.reshape(key_count, heads_here, HEAD_DIM)
    value_rows = value_in.reshape(key_count, heads_here, HEAD_DIM)
    grad_rows = grad_in.reshape(count, heads_here, HEAD_DIM)
    scores = (
        jnp.einsum("qhd,khd->hqk", query_rows, key_rows, preferred_element_type=jnp.float32)
        * score_scale
    )
    causal = jnp.arange(key_count)[None, :] <= jnp.arange(count)[:, None]
    scores = jnp.where(causal[None], scores, -jnp.inf)
    row_max = jnp.max(scores, axis=-1, keepdims=True)
    weights_exp = jnp.exp(scores - row_max)
    attn_prob = weights_exp / jnp.sum(weights_exp, axis=-1, keepdims=True)
    prob_b = attn_prob.astype(jnp.bfloat16)
    output = jnp.einsum("hqk,khd->qhd", prob_b, value_rows, preferred_element_type=jnp.float32)
    row_dot = jnp.sum(grad_rows.astype(jnp.float32) * output, axis=-1)
    dprob = jnp.einsum("qhd,khd->hqk", grad_rows, value_rows, preferred_element_type=jnp.float32)
    dscore = (attn_prob * (dprob - jnp.transpose(row_dot)[:, :, None]) * score_scale).astype(
        jnp.bfloat16
    )
    grad_query = jnp.einsum("hqk,khd->qhd", dscore, key_rows, preferred_element_type=jnp.float32)
    grad_key = jnp.einsum("hqk,qhd->khd", dscore, query_rows, preferred_element_type=jnp.float32)
    grad_value = jnp.einsum("hqk,qhd->khd", prob_b, grad_rows, preferred_element_type=jnp.float32)
    return (
        grad_query.reshape(count, full_width),
        grad_key.reshape(key_count, full_width),
        grad_value.reshape(key_count, full_width),
    )


def attend_block(stacked, grad_in):
    grad_query, grad_key, grad_value = attend(stacked[0], stacked[1], stacked[2], grad_in)
    return jnp.stack([grad_query, grad_key, grad_value])


def on_device(tokens, frozen_projections, output_gradient, down_weight, up_weight):
    highest_precision = lax.Precision.HIGHEST
    layer_inputs = tokens[0]
    base_projection = frozen_projections[:, 0]
    out_grad = output_gradient[0]
    group_rows = layer_inputs.shape[0]
    half_rows = group_rows // 2
    half_width = base_projection.shape[-1] // 2
    rank_product = jnp.einsum(
        "gw,psw->pgs", layer_inputs, down_weight, preferred_element_type=jnp.float32
    ).astype(jnp.bfloat16)
    adapter_output = jnp.einsum(
        "osg,ogd->osd", rank_product, up_weight, preferred_element_type=jnp.float32
    )
    projected_rows = (base_projection.astype(jnp.float32) + adapter_scale * adapter_output).astype(
        jnp.bfloat16
    )
    up_weight_float = up_weight.astype(jnp.float32)
    low_rank_float = rank_product.astype(jnp.float32)
    plain_grads = attend_block(projected_rows[..., :half_width], out_grad[:, :half_width])
    front_proj = projected_rows[:, :half_rows, half_width:]
    front_grad = out_grad[:half_rows, half_width:]
    far_proj, far_grad = shifted((front_proj, front_grad), "seq", -1)
    moved_proj = jnp.concatenate([projected_rows[:, half_rows:, half_width:], far_proj], axis=1)
    moved_grad = jnp.concatenate([out_grad[half_rows:, half_width:], far_grad], axis=0)
    moved_grads = attend_block(moved_proj, moved_grad)
    returned = shifted(moved_grads[:, half_rows:], "seq", 1)
    shifted_part = jnp.concatenate([returned, moved_grads[:, :half_rows]], axis=1)
    projection_grad = jnp.concatenate([plain_grads, shifted_part], axis=-1)
    rank_gradient = jnp.einsum(
        "jth,jrh->jtr", projection_grad, up_weight_float, precision=highest_precision
    )
    up_gradient = adapter_scale * jnp.einsum(
        "gdz,gdl->gzl", low_rank_float, projection_grad, precision=highest_precision
    )
    down_gradient = adapter_scale * jnp.einsum(
        "jtr,td->jrd",
        rank_gradient,
        layer_inputs,
        precision=highest_precision,
        preferred_element_type=jnp.float32,
    )
    down_gradient, up_gradient = lax.psum((down_gradient, up_gradient), ("seq", "dp"))
    return (down_gradient, up_gradient)


def solution(mesh):
    return jax.shard_map(
        on_device,
        mesh=mesh,
        in_specs=(P("dp", "seq", None), P(None, "dp", "seq", None), P("dp", "seq", None), P(), P()),
        out_specs=(P(), P()),
        check_vma=False,
    )
```

profile of v0, /device:TPU:0, one launch (start us, length us, event | category | flops | bytes accessed | tf_op | source)
XLA Modules:
  0.0 211.0 jit_solution(1990312747967835118)
XLA Ops:
  7.2 1.4 copy.42
  8.7 0.8 fusion.38
  9.4 6.0 %collective-permute-start.1 = (bf16[64,1024]{0,1:T(8,128)(2,1)}, bf16[64,1024]{0,1:T(8,128)(2,1)}, u32[]{:S(2)}, u32[]{:S(2)}) collective-permute-start(bf16[64,1024]{0,1:T(8,128)(2,1)} %get-tuple-element.15), channel_id=1, source_target_pairs={{0,28},{4,0},{8,4},{12,8},{16,12},{20,16},{24,20},{28,24},{1,29},{... | collective-permute-start | bytes 393224 | tf_op jit(solution)/shard_map/ppermute | solution.py:14
  17.0 0.8 fusion.37
  19.1 1.5 fusion.40
  21.4 0.8 copy.83
  22.2 2.1 fusion.32
  24.3 1.1 pad_maximum_fusion.2
  25.4 4.3 %collective-permute-done = bf16[3,64,1024]{2,1,0:T(8,128)(2,1)} collective-permute-done((bf16[3,64,1024]{2,1,0:T(8,128)(2,1)}, bf16[3,64,1024]{2,1,0:T(8,128)(2,1)}, u32[]{:S(2)}, u32[]{:S(2)}) %collective-permute-start) | collective-permute-done | bytes 393248 | tf_op jit(solution)/shard_map/ppermute | solution.py:14
  29.7 1.1 pad_maximum_fusion.1
  30.8 0.8 copy.86
  32.3 0.9 fusion.39
  33.2 1.2 multiply_reduce_fusion
  34.5 1.1 fusion.27
  35.6 1.4 fusion.17
  37.3 1.0 fusion.43
  38.4 1.2 copy.69
  39.6 2.0 copy.67
  41.7 1.0 copy.68
  42.7 1.3 pad_maximum_fusion
  44.0 1.0 fusion.36
  45.4 1.4 fusion.18
  46.8 2.1 copy.54
  48.8 1.3 fusion.16
  50.4 1.0 copy.52
  51.9 15.3 %collective-permute-done.2 = f32[3,64,1024]{2,1,0:T(8,128)} collective-permute-done((f32[3,64,1024]{2,1,0:T(8,128)}, f32[3,64,1024]{2,1,0:T(8,128)}, u32[]{:S(2)}, u32[]{:S(2)}) %collective-permute-start.2) | collective-permute-done | bytes 786464 | tf_op jit(solution)/shard_map/ppermute | solution.py:14
  67.2 3.0 %fusion.3 = f32[3,128,8]{1,2,0:T(8,128)S(1)} fusion(bf16[3,8,2048]{2,1,0:T(8,128)(2,1)S(1)} %copy-done.7, f32[3,64,1024]{2,1,0:T(8,128)S(1)} %get-tuple-element.8, f32[3,64,1024]{2,1,0:T(8,128)} %collective-permute-done.2, f32[1,128,1024]{2,1,0:T(8,128)} %copy.54, f32[1,128,1024]{2,1,0:T(8,128)S(1)} %copy.53, f32[1,128,1024]{2,1,0:T(8,128)} %copy.52), kind=kOutput, calls=%fused_computation.8 | convolution fusion | flops 78643200 | bytes 3256320 | tf_op jit(solution)/shard_map/jth,jrh->jtr/dot_general | solution.py:86
  70.3 1.3 convolution_multiply_fusion
  71.6 2.9 %convolution_multiply_fusion.1 = f32[3,8,2048]{2,1,0:T(8,128)} fusion(bf16[3,8,128]{2,1,0:T(8,128)(2,1)S(1)} %copy-done.9, f32[3,64,1024]{2,1,0:T(8,128)S(1)} %get-tuple-element.8, f32[3,64,1024]{2,1,0:T(8,128)} %collective-permute-done.2, f32[1,128,1024]{2,1,0:T(8,128)S(1)} %copy-done.3, f32[1,128,1024]{2,1,0:T(8,128)S(1)} %copy.53, ...), kind=kOutput, calls=%fused_computation.6 | convolution fusion | flops 78692352 | bytes 3348480 | tf_op jit(solution)/shard_map/gdz,gdl->gzl/dot_general | solution.py:89
  74.5 126.2 %all-reduce.3.cloned.1.call-done = (f32[3,8,4096]{2,1,0:T(8,128)}, f32[3,8,2048]{2,1,0:T(8,128)}) async-done(((f32[3,8,4096]{2,1,0:T(8,128)}, f32[3,8,2048]{2,1,0:T(8,128)}), (f32[3,8,4096]{2,1,0:T(8,128)}, f32[3,8,2048]{2,1,0:T(8,128)})) %all-reduce.3.cloned.1.call-update) | async-done | bytes 589840 | tf_op jit(solution)/shard_map/psum | solution.py:99
  200.7 1.8 copy.89
  202.5 1.6 copy.90
  (42 shorter events, 5.6 us)
Async XLA Ops:
  7.2 8.3 %copy-start = (bf16[1,128,4096]{2,1,0:T(8,128)(2,1)S(1)}, bf16[1,128,4096]{2,1,0:T(8,128)(2,1)}, u32[]{:S(2)}) copy-start(bf16[1,128,4096]{2,1,0:T(8,128)(2,1)} %param.5) | copy-start | bytes 3145732
  7.2 8.3 %copy-start.5 = (bf16[3,8,4096]{2,1,0:T(8,128)(2,1)S(1)}, bf16[3,8,4096]{2,1,0:T(8,128)(2,1)}, u32[]{:S(2)}) copy-start(bf16[3,8,4096]{2,1,0:T(8,128)(2,1)} %param.8) | copy-start | bytes 589828
  7.2 9.2 %copy-start.6 = (bf16[3,8,2048]{2,1,0:T(8,128)(2,1)S(1)}, bf16[3,8,2048]{2,1,0:T(8,128)(2,1)}, u32[]{:S(2)}) copy-start(bf16[3,8,2048]{2,1,0:T(8,128)(2,1)} %param.9) | copy-start | bytes 294916
  7.2 193.5 %all-reduce.3.cloned.1.call-start = ((), (), s32[]{:S(2)}) async-start(), calls=%async_computation | async-start | bytes 1179648 | tf_op jit(solution)/shard_map/psum | solution.py:99
  8.7 7.8 %copy-start.1 = (bf16[3,1,128,2048]{3,2,1,0:T(8,128)(2,1)S(1)}, bf16[3,1,128,2048]{3,2,1,0:T(8,128)(2,1)}, u32[]{:S(2)}) copy-start(bf16[3,1,128,2048]{3,2,1,0:T(8,128)(2,1)} %param.6) | copy-start | bytes 4718596
  9.4 14.9 %collective-permute-start.1 = (bf16[64,1024]{0,1:T(8,128)(2,1)}, bf16[64,1024]{0,1:T(8,128)(2,1)}, u32[]{:S(2)}, u32[]{:S(2)}) collective-permute-start(bf16[64,1024]{0,1:T(8,128)(2,1)} %get-tuple-element.15), channel_id=1, source_target_pairs={{0,28},{4,0},{8,4},{12,8},{16,12},{20,16},{24,20},{28,24},{1,29},{... | collective-permute-start | bytes 393224 | tf_op jit(solution)/shard_map/ppermute | solution.py:14
  15.8 0.6 copy-start.8
  17.9 11.9 %collective-permute-start = (bf16[3,64,1024]{2,1,0:T(8,128)(2,1)}, bf16[3,64,1024]{2,1,0:T(8,128)(2,1)}, u32[]{:S(2)}, u32[]{:S(2)}) collective-permute-start(bf16[3,64,1024]{2,1,0:T(8,128)(2,1)} %get-tuple-element.9), channel_id=1, source_target_pairs={{0,28},{4,0},{8,4},{12,8},{16,12},{20,16},{24,20},{28,24},{1,29},{... | collective-permute-start | bytes 1179656 | tf_op jit(solution)/shard_map/ppermute | solution.py:14
  44.0 1.4 copy-start.10
  45.1 22.2 %collective-permute-start.2 = (f32[3,64,1024]{2,1,0:T(8,128)}, f32[3,64,1024]{2,1,0:T(8,128)}, u32[]{:S(2)}, u32[]{:S(2)}) collective-permute-start(f32[3,64,1024]{2,1,0:T(8,128)} %get-tuple-element.7), channel_id=1, source_target_pairs={{0,4},{4,8},{8,12},{12,16},{16,20},{20,24},{24,28},{28,0},{1,5},{5... | collective-permute-start | bytes 2359304 | tf_op jit(solution)/shard_map/ppermute | solution.py:14
  45.4 3.5 %copy-start.2 = (f32[8,128,128]{1,2,0:T(8,128)S(1)}, f32[8,128,128]{1,2,0:T(8,128)}, u32[]{:S(2)}) copy-start(f32[8,128,128]{1,2,0:T(8,128)} %get-tuple-element.19) | copy-start | bytes 1572868
  50.4 16.8 %copy-start.7 = (bf16[3,8,2048]{2,1,0:T(8,128)(2,1)S(1)}, bf16[3,8,2048]{2,1,0:T(8,128)(2,1)}, u32[]{:S(2)}) copy-start(bf16[3,8,2048]{2,1,0:T(8,128)(2,1)} %param.9) | copy-start | bytes 294916
  67.2 4.3 %copy-start.3 = (f32[1,128,1024]{2,1,0:T(8,128)S(1)}, f32[1,128,1024]{2,1,0:T(8,128)}, u32[]{:S(2)}) copy-start(f32[1,128,1024]{2,1,0:T(8,128)} %copy.54) | copy-start | bytes 1572868
  67.2 4.3 %copy-start.4 = (f32[1,128,1024]{2,1,0:T(8,128)S(1)}, f32[1,128,1024]{2,1,0:T(8,128)}, u32[]{:S(2)}) copy-start(f32[1,128,1024]{2,1,0:T(8,128)} %copy.52) | copy-start | bytes 1572868
  67.2 4.3 %copy-start.9 = (bf16[3,8,128]{2,1,0:T(8,128)(2,1)S(1)}, bf16[3,8,128]{2,1,0:T(8,128)(2,1)}, u32[]{:S(2)}) copy-start(bf16[3,8,128]{2,1,0:T(8,128)(2,1)} %copy-done.8) | copy-start | bytes 18436
Sparse Core Ops, SparseCore 0:
  74.6 126.0 all-reduce.2
where the time goes:
time: 212 us; the launch traced here: 211 us
  waiting for transfers between devices  146 us (69%)
  matrix products  19.3 us (9%)
  local copies, waits for them, and re-layouts  18.8 us (9%)
  between operations  14.2 us (7%)
  starting transfers between devices  6.89 us (3%)
  other arithmetic  5.95 us (3%)
    psum x1, waiting for transfers between devices, on_device(): lax.psum((down_gradient, up_gradient), ('seq', 'dp'))  126 us
    ppermute x3, waiting for transfers between devices, shifted(): return lax.ppermute(x, axis, [(i, (i + by) % peers) for i in range(peers)])  19.6 us
    another operation x6, local copies, waits for them, and re-layouts, attend_block(): return jnp.stack([grad_query, grad_key, grad_value])  7.55 us
    ppermute x3, starting transfers between devices, shifted(): return lax.ppermute(x, axis, [(i, (i + by) % peers) for i in range(peers)])  6.85 us
    unnamed x25, local copies, waits for them, and re-layouts  5.43 us
  transfers between devices with their start and end apart: 4, of which 3 were waited for; matrix products, arithmetic and copies ran while one was open for 7% of the time, Pallas kernels for 0%

commit v1 on v0

v1 whole, which is shorter than its diff:
```python
import jax
import jax.numpy as jnp
from jax import lax
from jax.experimental import pallas as pl
from jax.experimental.pallas import tpu as pltpu
from jax.sharding import PartitionSpec as P

HEAD_DIM = 128
RANK = 8
SCALE = HEAD_DIM ** -0.5
ADAPTER_SCALE = 2.0
BF = jnp.bfloat16
F32 = jnp.float32
AXES = ("seq", "dp")
VMEM = pl.BlockSpec(memory_space=pltpu.VMEM)
LIMIT = 48 * 1024 * 1024


def nt(a, b):
    return lax.dot_general(a, b, (((1,), (1,)), ((), ())), preferred_element_type=F32)


def nn(a, b):
    return lax.dot_general(a, b, (((1,), (0,)), ((), ())), preferred_element_type=F32)


def tn(a, b):
    return lax.dot_general(a, b, (((0,), (0,)), ((), ())), preferred_element_type=F32)


def hi_lo(x):
    high = x.astype(BF).astype(F32)
    return [high, x - high]


def rows(parts):
    return jnp.concatenate(parts, axis=0).astype(BF)


def project(frozen, low_t, up):
    return (frozen.astype(F32) + ADAPTER_SCALE * tn(low_t, up)).astype(BF)


def head(q, k, v, g, ups, low_q, low_k, low_v, mask):
    st = jnp.where(mask, nt(k, q) * SCALE, -jnp.inf)
    e = jnp.exp(st - jnp.max(st, axis=0, keepdims=True))
    p = e * (1.0 / jnp.sum(e, axis=0, keepdims=True))
    pb = p.astype(BF)
    dp = nt(v, g)
    row_dot = jnp.sum(pb.astype(F32) * dp, axis=0, keepdims=True)
    ds = (p * (dp - row_dot) * SCALE).astype(BF)
    bq, bk, bv = nt(ups[0], k), nt(ups[1], q), nt(ups[2], g)
    by_q = nn(rows([low_k] + hi_lo(bq)), ds)
    by_k = nt(rows([low_q] + hi_lo(bk)), ds)
    av = nn(low_v.astype(BF), pb)
    rv = nt(rows(hi_lo(bv)), pb)
    uq = nn(rows(hi_lo(by_k[:8])), k)
    uk = nn(rows(hi_lo(by_q[:8])), q)
    uv = nn(rows(hi_lo(av)), g)
    grads = [u[:8] + u[8:] for u in (uq, uk, uv)]
    ranks = [by_q[8:16] + by_q[16:24], by_k[8:16] + by_k[16:24], rv[:8] + rv[8:]]
    return grads, ranks


def causal(keys, queries, offset):
    return lax.broadcasted_iota(jnp.int32, (keys, queries), 0) <= offset + lax.broadcasted_iota(
        jnp.int32, (keys, queries), 1
    )


def local_kernel(frozen, grad, low_t, up, far_out, up_out, rank_out):
    count, width = grad.shape[1:]
    half, half_width = count // 2, width // 2
    low = [low_t[j] for j in range(3)]
    low_f = [x.astype(F32) for x in low]
    near_f = [x[:, half:] for x in low_f]
    ranks = [jnp.zeros((RANK, count), F32)] * 3
    full_mask = causal(count, count, 0)
    half_mask = causal(half, half, 0)
    for h in range(half_width // HEAD_DIM):
        cols = slice(h * HEAD_DIM, (h + 1) * HEAD_DIM)
        ups = [up[j, :, cols] for j in range(3)]
        q, k, v = [project(frozen[j, 0, :, cols], low[j], ups[j]) for j in range(3)]
        grads, parts = head(q, k, v, grad[0, :, cols], ups, *low_f, full_mask)
        for j in range(3):
            up_out[8 * j : 8 * j + 8, cols] = grads[j]
        ranks = [a + b for a, b in zip(ranks, parts)]
    near_ranks = [jnp.zeros((RANK, half), F32)] * 3
    for h in range(half_width // HEAD_DIM):
        cols = slice(half_width + h * HEAD_DIM, half_width + (h + 1) * HEAD_DIM)
        ups = [up[j, :, cols] for j in range(3)]
        whole = [project(frozen[j, 0, :, cols], low[j], ups[j]) for j in range(3)]
        for j in range(3):
            far_out[j, :, h * HEAD_DIM : (h + 1) * HEAD_DIM] = whole[j][:half]
        q, k, v = [x[half:] for x in whole]
        grads, parts = head(q, k, v, grad[0, half:, cols], ups, *near_f, half_mask)
        for j in range(3):
            up_out[8 * j : 8 * j + 8, cols] = grads[j]
        near_ranks = [a + b for a, b in zip(near_ranks, parts)]
    for j in range(3):
        rank_out[8 * j : 8 * j + 8, :] = ranks[j] + jnp.concatenate(
            [jnp.zeros((RANK, half), F32), near_ranks[j]], axis=1
        )


def far_kernel(own, frozen_kv, low_kv, grad, low_t, up, up_in, rank_in, up_out, rank_out, cross_out):
    half = own.shape[1]
    width = up.shape[2]
    half_width = width // 2
    far_f = [low_t[j].astype(F32)[:, :half] for j in range(3)]
    near = [low_kv[0], low_kv[1]]
    low_k = jnp.concatenate([near[0].astype(F32), far_f[1]], axis=1)
    low_v = jnp.concatenate([near[1].astype(F32), far_f[2]], axis=1)
    mask = causal(2 * half, half, half)
    rank_q = jnp.zeros((RANK, half), F32)
    rank_k = jnp.zeros((RANK, 2 * half), F32)
    rank_v = jnp.zeros((RANK, 2 * half), F32)
    up_out[:, :half_width] = up_in[:, :half_width]
    for h in range(half_width // HEAD_DIM):
        here = slice(h * HEAD_DIM, (h + 1) * HEAD_DIM)
        cols = slice(half_width + h * HEAD_DIM, half_width + (h + 1) * HEAD_DIM)
        ups = [up[j, :, cols] for j in range(3)]
        near_k, near_v = [project(frozen_kv[j, :, here], near[j], ups[j + 1]) for j in range(2)]
        k = jnp.concatenate([near_k, own[1, :, here]], axis=0)
        v = jnp.concatenate([near_v, own[2, :, here]], axis=0)
        grads, parts = head(
            own[0, :, here], k, v, grad[0, :half, cols], ups, far_f[0], low_k, low_v, mask
        )
        for j in range(3):
            up_out[8 * j : 8 * j + 8, cols] = up_in[8 * j : 8 * j + 8, cols] + grads[j]
        rank_q, rank_k, rank_v = rank_q + parts[0], rank_k + parts[1], rank_v + parts[2]
    none = jnp.zeros((RANK, half), F32)
    for j, part in enumerate([rank_q, rank_k[:, half:], rank_v[:, half:]]):
        rank_out[8 * j : 8 * j + 8, :] = rank_in[8 * j : 8 * j + 8, :] + jnp.concatenate(
            [part, none], axis=1
        )
    for j, part in enumerate([rank_k[:, :half], rank_v[:, :half]]):
        cross_out[8 * j : 8 * j + 8, :] = jnp.concatenate([none, part], axis=1)


def position():
    dp = lax.axis_index("dp")
    return dp & 1, (dp & 2) | (lax.axis_index("seq") & 1)


def down_kernel(tokens, rank_in, cross, up_in, keep, send):
    core, place = position()
    ranks = rank_in[...] + jnp.concatenate([jnp.zeros((RANK, rank_in.shape[1]), F32), cross[...]], axis=0)
    both = rows(hi_lo(ranks))
    n = ranks.shape[0]
    up_step, down_step = up_in.shape[1] // 8, tokens.shape[2] // 8
    for c in range(8):
        d = nn(both, tokens[0, :, c * down_step : (c + 1) * down_step])
        d = ADAPTER_SCALE * (d[:n] + d[n:])
        u = ADAPTER_SCALE * up_in[:, c * up_step : (c + 1) * up_step]
        slot = place ^ (c >> 1)

        def put(ref):
            ref[slot, :, :up_step] = u
            ref[slot, :, up_step:] = d

        pl.when(core == (c & 1))(lambda: put(keep))
        pl.when(core != (c & 1))(lambda: put(send))


def spread_kernel(mine, other, down_out, up_out):
    core, place = position()
    up_step, down_step = up_out.shape[2] // 8, down_out.shape[2] // 8
    for c in range(8):
        slot = place ^ (c >> 1)

        def put(ref):
            x = ref[slot].astype(F32)
            for j in range(3):
                up_out[j, :, c * up_step : (c + 1) * up_step] = x[8 * j : 8 * j + 8, :up_step]
                down_out[j, :, c * down_step : (c + 1) * down_step] = x[8 * j : 8 * j + 8, up_step:]

        pl.when(core == (c & 1))(lambda: put(mine))
        pl.when(core != (c & 1))(lambda: put(other))


def call(kernel, outs, *args):
    return pl.pallas_call(
        kernel,
        out_shape=outs,
        in_specs=[VMEM] * len(args),
        out_specs=jax.tree.map(lambda _: VMEM, outs),
        compiler_params=pltpu.CompilerParams(vmem_limit_bytes=LIMIT),
        cost_estimate=pl.CostEstimate(flops=10**9, bytes_accessed=10**6, transcendentals=0),
    )(*args)


def swap(x, bits, total):
    return lax.ppermute(x, AXES, [(i, i ^ bits) for i in range(total)])


def total_sum(keep, send, seqs, dps):
    total = seqs * dps
    keep = keep + swap(send, 1, total)
    own = keep[0]
    got = [swap(keep[s].astype(BF), (s & 2) | (dps if s & 1 else 0), total) for s in (1, 2, 3)]
    own = own + got[0].astype(F32) + got[1].astype(F32) + got[2].astype(F32)
    bit = 2
    while bit < seqs:
        piece = own.astype(BF)
        own = piece.astype(F32) + swap(piece, bit * dps, total).astype(F32)
        bit *= 2
    piece = own.astype(BF)
    mine = jnp.stack([piece] + [swap(piece, (s & 2) | (dps if s & 1 else 0), total) for s in (1, 2, 3)])
    return mine, swap(mine, 1, total)


def on_device(tokens, frozen, grad, down_weight, up_weight):
    seqs, dps = lax.axis_size("seq"), lax.axis_size("dp")
    count, width = grad.shape[1:]
    half, half_width = count // 2, width // 2
    forward = [(i, (i + 1) % seqs) for i in range(seqs)]
    backward = [(i, (i - 1) % seqs) for i in range(seqs)]
    frozen_kv = lax.ppermute(frozen[1:, 0, half:, half_width:], "seq", forward)
    low_t = jnp.einsum("psw,gw->psg", down_weight, tokens[0], preferred_element_type=F32).astype(BF)
    low_kv = lax.ppermute(low_t[1:, :, half:], "seq", forward)
    sds = jax.ShapeDtypeStruct
    own, up_part, rank_part = call(
        local_kernel,
        [sds((3, half, half_width), BF), sds((24, width), F32), sds((24, count), F32)],
        frozen, grad, low_t, up_weight,
    )
    up_part, rank_part, cross = call(
        far_kernel,
        [sds((24, width), F32), sds((24, count), F32), sds((16, count), F32)],
        own, frozen_kv, low_kv, grad, low_t, up_weight, up_part, rank_part,
    )
    cross = lax.ppermute(cross, "seq", backward)
    columns = (width + tokens.shape[2]) // 8
    piece = sds((4, 24, columns), F32)
    keep, send = call(down_kernel, [piece, piece], tokens, rank_part, cross, up_part)
    mine, other = total_sum(keep, send, seqs, dps)
    return tuple(
        call(spread_kernel, [sds((3, RANK, tokens.shape[2]), F32), sds((3, RANK, width), F32)], mine, other)
    )


def solution(mesh):
    return jax.shard_map(
        on_device,
        mesh=mesh,
        in_specs=(P("dp", "seq", None), P(None, "dp", "seq", None), P("dp", "seq", None), P(), P()),
        out_specs=(P(), P()),
        check_vma=False,
    )
```

time: 212 us -> 55 us (0.26)
  waiting for transfers between devices: 146 us -> 16.2 us
  matrix products: 19.3 us -> 1.6 us
  local copies, waits for them, and re-layouts: 18.8 us -> 2.27 us
  Pallas kernels: 0 us -> 14.9 us
  between operations: 14.2 us -> 0.76 us
  starting transfers between devices: 6.89 us -> 18.9 us
  other arithmetic: 5.95 us -> 0.11 us
    psum x1 -> x0, waiting for transfers between devices: 126 us -> none  [on_device(): lax.psum((down_gradient, up_gradient), ('seq', 'dp'))]
    dot_general x17 -> x1, matrix products: 19.3 us -> 1.6 us  [on_device(): jnp.einsum('psw,gw->psg', down_weight, tokens[0], preferred_element_type=...]
    pallas_call x0 -> x4, Pallas kernels: none -> 14.9 us  [call(): pl.pallas_call(kernel, out_shape=outs, in_specs=[VMEM] * len(args), out_s...]
    ppermute x3 -> x13, starting transfers between devices: 6.85 us -> 18.9 us  [the longest x10 11.2 us: swap(): return lax.ppermute(x, AXES, [(i, i ^ bits) for i in range(total)])]
    another operation x12 -> x0, local copies, waits for them, and re-layouts: 9.92 us -> none  [the longest x6 7.55 us: attend_block(): return jnp.stack([grad_query, grad_key, grad_value])]
    unnamed x25 -> x12, local copies, waits for them, and re-layouts: 5.43 us -> 1.07 us
    ppermute x3 -> x13, waiting for transfers between devices: 19.6 us -> 16.2 us  [the longest x10 14.8 us: swap(): return lax.ppermute(x, AXES, [(i, i ^ bits) for i in range(total)])]
    slice x5 -> x1, local copies, waits for them, and re-layouts: 3.45 us -> 0.08 us  [on_device(): low_kv = lax.ppermute(low_t[1:, :, half:], 'seq', forward)]
  transfers between devices with their start and end apart: 4 -> 13, of which waited for: 3 -> 11; matrix products, arithmetic and copies ran while one was open for 7% -> 3% of each run, Pallas kernels for 0% -> 17%
where the time goes in v1:
time: 55 us; the launch traced here: 54.8 us
  starting transfers between devices  18.9 us (34%)
  waiting for transfers between devices  16.2 us (29%)
  Pallas kernels  14.9 us (27%)
  local copies, waits for them, and re-layouts  2.27 us (4%)
  matrix products  1.6 us (3%)
  between operations  0.76 us (1%)
    pallas_call x4, Pallas kernels, call(): pl.pallas_call(kernel, out_shape=outs, in_specs=[VMEM] * len(args), out_s...  14.9 us
    ppermute x10, waiting for transfers between devices, swap(): return lax.ppermute(x, AXES, [(i, i ^ bits) for i in range(total)])  14.8 us
    ppermute x10, starting transfers between devices, swap(): return lax.ppermute(x, AXES, [(i, i ^ bits) for i in range(total)])  11.2 us
    ppermute x1, starting transfers between devices, on_device(): cross = lax.ppermute(cross, 'seq', backward)  3.23 us
    ppermute x1, starting transfers between devices, on_device(): frozen_kv = lax.ppermute(frozen[1:, 0, half:, half_width:], 'seq', forward)  2.99 us
    dot_general x1, matrix products, on_device(): jnp.einsum('psw,gw->psg', down_weight, tokens[0], preferred_element_type=...  1.6 us
    ppermute x1, starting transfers between devices, on_device(): low_kv = lax.ppermute(low_t[1:, :, half:], 'seq', forward)  1.56 us
    ppermute x1, waiting for transfers between devices, on_device(): cross = lax.ppermute(cross, 'seq', backward)  1.37 us
  transfers between devices with their start and end apart: 13, of which 11 were waited for; matrix products, arithmetic and copies ran while one was open for 3% of the time, Pallas kernels for 17%

profile of v1, /device:TPU:0, one launch (start us, length us, event | category | flops | bytes accessed | tf_op | source)
XLA Modules:
  0.0 54.8 jit_solution(7271369289098331975)
XLA Ops:
  0.7 1.1 %slice_bitcast_fusion = bf16[2,64,1024]{2,1,0:T(8,128)(2,1)S(1)} fusion(bf16[3,1,128,2048]{3,2,0,1:T(8,128)(2,1)} %bitcast.28), kind=kLoop, calls=%fused_computation.2 | loop fusion | bytes 524288 | tf_op jit(solution)/shard_map/squeeze | solution.py:219
  1.8 3.0 %collective-permute-start = (bf16[2,64,1024]{2,1,0:T(8,128)(2,1)S(1)}, bf16[2,64,1024]{2,1,0:T(8,128)(2,1)S(1)}, u32[]{:S(2)}, u32[]{:S(2)}) collective-permute-start(bf16[2,64,1024]{2,1,0:T(8,128)(2,1)S(1)} %slice_bitcast_fusion), channel_id=1, source_target_pairs={{0,4},{4,8},{8,12},{12,16},{16,20},{20,24},{24,28},{28,0},{1,5},{5... | collective-permute-start | bytes 786440 | tf_op jit(solution)/shard_map/ppermute | solution.py:219
  4.8 1.6 %convolution_convert_fusion.low_t = bf16[3,8,128]{2,1,0:T(8,128)(2,1)S(1)} fusion(bf16[3,8,4096]{2,1,0:T(8,128)(2,1)S(1)} %copy-done, bf16[1,128,4096]{2,1,0:T(8,128)(2,1)} %tokens.1), kind=kOutput, calls=%fused_computation | convolution fusion | flops 25168896 | bytes 1251328 | tf_op jit(solution)/shard_map/psw,gw->psg/dot_general | solution.py:220
  6.4 0.1 slice.28
  6.5 1.6 %collective-permute-start.1 = (bf16[2,8,64]{2,1,0:T(8,128)(2,1)S(1)}, bf16[2,8,64]{2,1,0:T(8,128)(2,1)S(1)}, u32[]{:S(2)}, u32[]{:S(2)}) collective-permute-start(bf16[2,8,64]{2,1,0:T(8,128)(2,1)S(1)} %slice.28), channel_id=1, source_target_pairs={{0,4},{4,8},{8,12},{12,16},{16,20},{20,24},{24,28},{28,0},{1,5},{5... | collective-permute-start | bytes 6152 | tf_op jit(solution)/shard_map/ppermute | solution.py:221
  8.0 1.0 %copy-done.3 = bf16[1,128,2048]{2,1,0:T(8,128)(2,1)S(1)} copy-done((bf16[1,128,2048]{2,1,0:T(8,128)(2,1)S(1)}, bf16[1,128,2048]{2,1,0:T(8,128)(2,1)}, u32[]{:S(2)}) %copy-start.3) | copy-done | bytes 524312
  9.1 9.1 %shard_map.68 = (bf16[3,64,1024]{2,1,0:T(8,128)(2,1)S(1)}, f32[24,2048]{1,0:T(8,128)S(1)}, f32[24,128]{1,0:T(8,128)S(1)}) custom-call(bf16[3,1,128,2048]{3,2,1,0:T(8,128)(2,1)S(1)} %copy-done.2, bf16[1,128,2048]{2,1,0:T(8,128)(2,1)S(1)} %copy-done.3, bf16[3,8,128]{2,1,0:T(8,128)(2,1)S(1)} %convolution_convert_fusion.low_t, bf16[3,8,2048]{2,1,0:T(8,128)(2,1)S(1)} %copy-done.5), custom_call_target="tpu_custom_call" | custom-call | flops 1000000000 | bytes 1000000 | tf_op jit(solution)/shard_map/pallas_call | solution.py:183
  18.2 3.7 %shard_map.69 = (f32[24,2048]{1,0:T(8,128)S(1)}, f32[24,128]{1,0:T(8,128)S(1)}, f32[16,128]{1,0:T(8,128)S(1)}) custom-call(bf16[3,64,1024]{2,1,0:T(8,128)(2,1)S(1)} %get-tuple-element.10.own, bf16[2,64,1024]{2,1,0:T(8,128)(2,1)S(1)} %collective-permute-done.frozen_kv, bf16[2,8,64]{2,1,0:T(8,128)(2,1)S(1)} %collective-permute-done.1.low_kv, ...), custom_call_target="tpu_custom_call" | custom-call | flops 1000000000 | bytes 1000000 | tf_op jit(solution)/shard_map/pallas_call | solution.py:183
  21.9 3.2 %collective-permute-start.2 = (f32[16,128]{1,0:T(8,128)S(1)}, f32[16,128]{1,0:T(8,128)S(1)}, u32[]{:S(2)}, u32[]{:S(2)}) collective-permute-start(f32[16,128]{1,0:T(8,128)S(1)} %get-tuple-element.14), channel_id=1, source_target_pairs={{0,28},{4,0},{8,4},{12,8},{16,12},{20,16},{24,20},{28,24},{1,29},{... | collective-permute-start | bytes 24584 | tf_op jit(solution)/shard_map/ppermute | solution.py:233
  25.2 1.4 %collective-permute-done.2.cross = f32[16,128]{1,0:T(8,128)S(1)} collective-permute-done((f32[16,128]{1,0:T(8,128)S(1)}, f32[16,128]{1,0:T(8,128)S(1)}, u32[]{:S(2)}, u32[]{:S(2)}) %collective-permute-start.2) | collective-permute-done | bytes 8224 | tf_op jit(solution)/shard_map/ppermute | solution.py:233
  26.6 1.2 %shard_map.70 = (f32[4,24,768]{2,1,0:T(8,128)S(1)}, f32[4,24,768]{2,1,0:T(8,128)S(1)}) custom-call(bf16[1,128,4096]{2,1,0:T(8,128)(2,1)S(1)} %copy-done.1, f32[24,128]{1,0:T(8,128)S(1)} %get-tuple-element.13.rank_in, f32[16,128]{1,0:T(8,128)S(1)} %collective-permute-done.2.cross, f32[24,2048]{1,0:T(8,128)S(1)} %get-tuple-element.15.up_in), custom_call_target="tpu_custom_call" | custom-call | flops 1000000000 | bytes 1000000 | tf_op jit(solution)/shard_map/pallas_call | solution.py:183
  27.7 0.1 collective-permute-start.3
  27.8 1.6 %collective-permute-done.3 = f32[4,24,768]{2,1,0:T(8,128)S(1)} collective-permute-done((f32[4,24,768]{2,1,0:T(8,128)S(1)}, f32[4,24,768]{2,1,0:T(8,128)S(1)}, u32[]{:S(2)}, u32[]{:S(2)}) %collective-permute-start.3) | collective-permute-done | bytes 294944 | tf_op jit(solution)/shard_map/ppermute | solution.py:194
  29.4 1.6 %collective-permute-start.4 = (bf16[24,768]{1,0:T(8,128)(2,1)S(1)}, bf16[24,768]{1,0:T(8,128)(2,1)S(1)}, u32[]{:S(2)}, u32[]{:S(2)}) collective-permute-start(bf16[24,768]{1,0:T(8,128)(2,1)S(1)} %get-tuple-element.20), channel_id=1, source_target_pairs={{0,4},{1,5},{2,6},{3,7},{4,0},{5,1},{6,2},{7,3},{8,12},{9,13},{10,... | collective-permute-start | bytes 110600 | tf_op jit(solution)/shard_map/ppermute | solution.py:194
  31.0 1.5 %collective-permute-start.6 = (bf16[24,768]{1,0:T(8,128)(2,1)S(1)}, bf16[24,768]{1,0:T(8,128)(2,1)S(1)}, u32[]{:S(2)}, u32[]{:S(2)}) collective-permute-start(bf16[24,768]{1,0:T(8,128)(2,1)S(1)} %get-tuple-element.21), channel_id=1, source_target_pairs={{0,6},{1,7},{2,4},{3,5},{4,2},{5,3},{6,0},{7,1},{8,14},{9,15},{10,... | collective-permute-start | bytes 110600 | tf_op jit(solution)/shard_map/ppermute | solution.py:194
  32.5 0.5 collective-permute-start.5
  33.0 0.5 collective-permute-done.4
  33.5 2.4 %collective-permute-done.6 = bf16[24,768]{1,0:T(8,128)(2,1)S(1)} collective-permute-done((bf16[24,768]{1,0:T(8,128)(2,1)S(1)}, bf16[24,768]{1,0:T(8,128)(2,1)S(1)}, u32[]{:S(2)}, u32[]{:S(2)}) %collective-permute-start.6) | collective-permute-done | bytes 36896 | tf_op jit(solution)/shard_map/ppermute | solution.py:194
  35.9 0.6 %collective-permute-done.5 = bf16[24,768]{1,0:T(8,128)(2,1)S(1)} collective-permute-done((bf16[24,768]{1,0:T(8,128)(2,1)S(1)}, bf16[24,768]{1,0:T(8,128)(2,1)S(1)}, u32[]{:S(2)}, u32[]{:S(2)}) %collective-permute-start.5) | collective-permute-done | bytes 36896 | tf_op jit(solution)/shard_map/ppermute | solution.py:194
  36.5 1.5 %collective-permute-start.7 = (bf16[24,768]{1,0:T(8,128)(2,1)S(1)}, bf16[24,768]{1,0:T(8,128)(2,1)S(1)}, u32[]{:S(2)}, u32[]{:S(2)}) collective-permute-start(bf16[24,768]{1,0:T(8,128)(2,1)S(1)} %fusion.4), channel_id=1, source_target_pairs={{0,8},{1,9},{2,10},{3,11},{4,12},{5,13},{6,14},{7,15},{8,0},{9,1},... | collective-permute-start | bytes 110600 | tf_op jit(solution)/shard_map/ppermute | solution.py:194
  37.9 2.6 %collective-permute-done.7 = bf16[24,768]{1,0:T(8,128)(2,1)S(1)} collective-permute-done((bf16[24,768]{1,0:T(8,128)(2,1)S(1)}, bf16[24,768]{1,0:T(8,128)(2,1)S(1)}, u32[]{:S(2)}, u32[]{:S(2)}) %collective-permute-start.7) | collective-permute-done | bytes 36896 | tf_op jit(solution)/shard_map/ppermute | solution.py:194
  40.5 2.5 %collective-permute-start.8 = (bf16[24,768]{1,0:T(8,128)(2,1)S(1)}, bf16[24,768]{1,0:T(8,128)(2,1)S(1)}, u32[]{:S(2)}, u32[]{:S(2)}) collective-permute-start(bf16[24,768]{1,0:T(8,128)(2,1)S(1)} %add_convert_fusion.1), channel_id=1, source_target_pairs={{0,16},{1,17},{2,18},{3,19},{4,20},{5,21},{6,22},{7,23},{8,24},{9,... | collective-permute-start | bytes 110600 | tf_op jit(solution)/shard_map/ppermute | solution.py:194
  43.0 2.5 %collective-permute-done.8 = bf16[24,768]{1,0:T(8,128)(2,1)S(1)} collective-permute-done((bf16[24,768]{1,0:T(8,128)(2,1)S(1)}, bf16[24,768]{1,0:T(8,128)(2,1)S(1)}, u32[]{:S(2)}, u32[]{:S(2)}) %collective-permute-start.8) | collective-permute-done | bytes 36896 | tf_op jit(solution)/shard_map/ppermute | solution.py:194
  45.5 1.5 %collective-permute-start.11 = (bf16[24,768]{1,0:T(8,128)(2,1)S(1)}, bf16[24,768]{1,0:T(8,128)(2,1)S(1)}, u32[]{:S(2)}, u32[]{:S(2)}) collective-permute-start(bf16[24,768]{1,0:T(8,128)(2,1)S(1)} %add_convert_fusion), channel_id=1, source_target_pairs={{0,6},{1,7},{2,4},{3,5},{4,2},{5,3},{6,0},{7,1},{8,14},{9,15},{10,... | collective-permute-start | bytes 110600 | tf_op jit(solution)/shard_map/ppermute | solution.py:194
  47.0 1.5 %collective-permute-start.10 = (bf16[24,768]{1,0:T(8,128)(2,1)S(1)}, bf16[24,768]{1,0:T(8,128)(2,1)S(1)}, u32[]{:S(2)}, u32[]{:S(2)}) collective-permute-start(bf16[24,768]{1,0:T(8,128)(2,1)S(1)} %add_convert_fusion), channel_id=1, source_target_pairs={{0,2},{1,3},{2,0},{3,1},{4,6},{5,7},{6,4},{7,5},{8,10},{9,11},{10,... | collective-permute-start | bytes 110600 | tf_op jit(solution)/shard_map/ppermute | solution.py:194
  48.5 0.5 collective-permute-start.9
  49.0 1.4 %collective-permute-done.11 = bf16[24,768]{1,0:T(8,128)(2,1)S(1)} collective-permute-done((bf16[24,768]{1,0:T(8,128)(2,1)S(1)}, bf16[24,768]{1,0:T(8,128)(2,1)S(1)}, u32[]{:S(2)}, u32[]{:S(2)}) %collective-permute-start.11) | collective-permute-done | bytes 36896 | tf_op jit(solution)/shard_map/ppermute | solution.py:194
  50.4 0.5 collective-permute-done.10
  50.9 1.5 %collective-permute-done.9 = bf16[24,768]{1,0:T(8,128)(2,1)S(1)} collective-permute-done((bf16[24,768]{1,0:T(8,128)(2,1)S(1)}, bf16[24,768]{1,0:T(8,128)(2,1)S(1)}, u32[]{:S(2)}, u32[]{:S(2)}) %collective-permute-start.9) | collective-permute-done | bytes 36896 | tf_op jit(solution)/shard_map/ppermute | solution.py:194
  52.5 0.1 collective-permute-start.12
  52.5 1.4 %collective-permute-done.12.other = bf16[4,24,768]{2,1,0:T(8,128)(2,1)S(1)} collective-permute-done((bf16[4,24,768]{2,1,0:T(8,128)(2,1)S(1)}, bf16[4,24,768]{2,1,0:T(8,128)(2,1)S(1)}, u32[]{:S(2)}, u32[]{:S(2)}) %collective-permute-start.12) | collective-permute-done | bytes 147488 | tf_op jit(solution)/shard_map/ppermute | solution.py:194
  53.9 0.9 %shard_map.71 = (f32[3,8,4096]{2,1,0:T(8,128)}, f32[3,8,2048]{2,1,0:T(8,128)}) custom-call(bf16[4,24,768]{2,1,0:T(8,128)(2,1)S(1)} %pad_maximum_fusion.mine, bf16[4,24,768]{2,1,0:T(8,128)(2,1)S(1)} %collective-permute-done.12.other), custom_call_target="tpu_custom_call" | custom-call | flops 1000000000 | bytes 1000000 | tf_op jit(solution)/shard_map/pallas_call | solution.py:183
  (19 shorter events, 0.2 us)
Async XLA Ops:
  0.6 4.1 %copy-start = (bf16[3,8,4096]{2,1,0:T(8,128)(2,1)S(1)}, bf16[3,8,4096]{2,1,0:T(8,128)(2,1)}, u32[]{:S(2)}) copy-start(bf16[3,8,4096]{2,1,0:T(8,128)(2,1)} %param.8) | copy-start | bytes 589828
  0.6 7.4 %copy-start.2 = (bf16[3,1,128,2048]{3,2,1,0:T(8,128)(2,1)S(1)}, bf16[3,1,128,2048]{3,2,1,0:T(8,128)(2,1)}, u32[]{:S(2)}) copy-start(bf16[3,1,128,2048]{3,2,1,0:T(8,128)(2,1)} %frozen.1) | copy-start | bytes 4718596
  0.7 7.4 %copy-start.5 = (bf16[3,8,2048]{2,1,0:T(8,128)(2,1)S(1)}, bf16[3,8,2048]{2,1,0:T(8,128)(2,1)}, u32[]{:S(2)}) copy-start(bf16[3,8,2048]{2,1,0:T(8,128)(2,1)} %up.3) | copy-start | bytes 294916
  1.8 16.4 %collective-permute-start = (bf16[2,64,1024]{2,1,0:T(8,128)(2,1)S(1)}, bf16[2,64,1024]{2,1,0:T(8,128)(2,1)S(1)}, u32[]{:S(2)}, u32[]{:S(2)}) collective-permute-start(bf16[2,64,1024]{2,1,0:T(8,128)(2,1)S(1)} %slice_bitcast_fusion), channel_id=1, source_target_pairs={{0,4},{4,8},{8,12},{12,16},{16,20},{20,24},{24,28},{28,0},{1,5},{5... | collective-permute-start | bytes 786440 | tf_op jit(solution)/shard_map/ppermute | solution.py:219
  6.5 11.7 %collective-permute-start.1 = (bf16[2,8,64]{2,1,0:T(8,128)(2,1)S(1)}, bf16[2,8,64]{2,1,0:T(8,128)(2,1)S(1)}, u32[]{:S(2)}, u32[]{:S(2)}) collective-permute-start(bf16[2,8,64]{2,1,0:T(8,128)(2,1)S(1)} %slice.28), channel_id=1, source_target_pairs={{0,4},{4,8},{8,12},{12,16},{16,20},{20,24},{24,28},{28,0},{1,5},{5... | collective-permute-start | bytes 6152 | tf_op jit(solution)/shard_map/ppermute | solution.py:221
  8.0 1.0 %copy-start.3 = (bf16[1,128,2048]{2,1,0:T(8,128)(2,1)S(1)}, bf16[1,128,2048]{2,1,0:T(8,128)(2,1)}, u32[]{:S(2)}) copy-start(bf16[1,128,2048]{2,1,0:T(8,128)(2,1)} %grad.3) | copy-start | bytes 1572868
  9.1 9.1 %copy-start.4 = (bf16[1,128,2048]{2,1,0:T(8,128)(2,1)S(1)}, bf16[1,128,2048]{2,1,0:T(8,128)(2,1)}, u32[]{:S(2)}) copy-start(bf16[1,128,2048]{2,1,0:T(8,128)(2,1)} %grad.3) | copy-start | bytes 1572868
  18.2 8.3 %copy-start.1 = (bf16[1,128,4096]{2,1,0:T(8,128)(2,1)S(1)}, bf16[1,128,4096]{2,1,0:T(8,128)(2,1)}, u32[]{:S(2)}) copy-start(bf16[1,128,4096]{2,1,0:T(8,128)(2,1)} %tokens.1) | copy-start | bytes 3145732
  21.9 4.6 %collective-permute-start.2 = (f32[16,128]{1,0:T(8,128)S(1)}, f32[16,128]{1,0:T(8,128)S(1)}, u32[]{:S(2)}, u32[]{:S(2)}) collective-permute-start(f32[16,128]{1,0:T(8,128)S(1)} %get-tuple-element.14), channel_id=1, source_target_pairs={{0,28},{4,0},{8,4},{12,8},{16,12},{20,16},{24,20},{28,24},{1,29},{... | collective-permute-start | bytes 24584 | tf_op jit(solution)/shard_map/ppermute | solution.py:233
  27.7 1.6 %collective-permute-start.3 = (f32[4,24,768]{2,1,0:T(8,128)S(1)}, f32[4,24,768]{2,1,0:T(8,128)S(1)}, u32[]{:S(2)}, u32[]{:S(2)}) collective-permute-start(f32[4,24,768]{2,1,0:T(8,128)S(1)} %get-tuple-element.17), channel_id=1, source_target_pairs={{0,1},{1,0},{2,3},{3,2},{4,5},{5,4},{6,7},{7,6},{8,9},{9,8},{10,11... | collective-permute-start | bytes 884744 | tf_op jit(solution)/shard_map/ppermute | solution.py:194
  29.4 4.0 %collective-permute-start.4 = (bf16[24,768]{1,0:T(8,128)(2,1)S(1)}, bf16[24,768]{1,0:T(8,128)(2,1)S(1)}, u32[]{:S(2)}, u32[]{:S(2)}) collective-permute-start(bf16[24,768]{1,0:T(8,128)(2,1)S(1)} %get-tuple-element.20), channel_id=1, source_target_pairs={{0,4},{1,5},{2,6},{3,7},{4,0},{5,1},{6,2},{7,3},{8,12},{9,13},{10,... | collective-permute-start | bytes 110600 | tf_op jit(solution)/shard_map/ppermute | solution.py:194
  31.0 4.9 %collective-permute-start.6 = (bf16[24,768]{1,0:T(8,128)(2,1)S(1)}, bf16[24,768]{1,0:T(8,128)(2,1)S(1)}, u32[]{:S(2)}, u32[]{:S(2)}) collective-permute-start(bf16[24,768]{1,0:T(8,128)(2,1)S(1)} %get-tuple-element.21), channel_id=1, source_target_pairs={{0,6},{1,7},{2,4},{3,5},{4,2},{5,3},{6,0},{7,1},{8,14},{9,15},{10,... | collective-permute-start | bytes 110600 | tf_op jit(solution)/shard_map/ppermute | solution.py:194
  32.5 4.0 %collective-permute-start.5 = (bf16[24,768]{1,0:T(8,128)(2,1)S(1)}, bf16[24,768]{1,0:T(8,128)(2,1)S(1)}, u32[]{:S(2)}, u32[]{:S(2)}) collective-permute-start(bf16[24,768]{1,0:T(8,128)(2,1)S(1)} %get-tuple-element.22), channel_id=1, source_target_pairs={{0,2},{1,3},{2,0},{3,1},{4,6},{5,7},{6,4},{7,5},{8,10},{9,11},{10,... | collective-permute-start | bytes 110600 | tf_op jit(solution)/shard_map/ppermute | solution.py:194
  36.5 4.0 %collective-permute-start.7 = (bf16[24,768]{1,0:T(8,128)(2,1)S(1)}, bf16[24,768]{1,0:T(8,128)(2,1)S(1)}, u32[]{:S(2)}, u32[]{:S(2)}) collective-permute-start(bf16[24,768]{1,0:T(8,128)(2,1)S(1)} %fusion.4), channel_id=1, source_target_pairs={{0,8},{1,9},{2,10},{3,11},{4,12},{5,13},{6,14},{7,15},{8,0},{9,1},... | collective-permute-start | bytes 110600 | tf_op jit(solution)/shard_map/ppermute | solution.py:194
  40.5 4.9 %collective-permute-start.8 = (bf16[24,768]{1,0:T(8,128)(2,1)S(1)}, bf16[24,768]{1,0:T(8,128)(2,1)S(1)}, u32[]{:S(2)}, u32[]{:S(2)}) collective-permute-start(bf16[24,768]{1,0:T(8,128)(2,1)S(1)} %add_convert_fusion.1), channel_id=1, source_target_pairs={{0,16},{1,17},{2,18},{3,19},{4,20},{5,21},{6,22},{7,23},{8,24},{9,... | collective-permute-start | bytes 110600 | tf_op jit(solution)/shard_map/ppermute | solution.py:194
  45.5 4.9 %collective-permute-start.11 = (bf16[24,768]{1,0:T(8,128)(2,1)S(1)}, bf16[24,768]{1,0:T(8,128)(2,1)S(1)}, u32[]{:S(2)}, u32[]{:S(2)}) collective-permute-start(bf16[24,768]{1,0:T(8,128)(2,1)S(1)} %add_convert_fusion), channel_id=1, source_target_pairs={{0,6},{1,7},{2,4},{3,5},{4,2},{5,3},{6,0},{7,1},{8,14},{9,15},{10,... | collective-permute-start | bytes 110600 | tf_op jit(solution)/shard_map/ppermute | solution.py:194
  47.0 4.0 %collective-permute-start.10 = (bf16[24,768]{1,0:T(8,128)(2,1)S(1)}, bf16[24,768]{1,0:T(8,128)(2,1)S(1)}, u32[]{:S(2)}, u32[]{:S(2)}) collective-permute-start(bf16[24,768]{1,0:T(8,128)(2,1)S(1)} %add_convert_fusion), channel_id=1, source_target_pairs={{0,2},{1,3},{2,0},{3,1},{4,6},{5,7},{6,4},{7,5},{8,10},{9,11},{10,... | collective-permute-start | bytes 110600 | tf_op jit(solution)/shard_map/ppermute | solution.py:194
  48.5 4.0 %collective-permute-start.9 = (bf16[24,768]{1,0:T(8,128)(2,1)S(1)}, bf16[24,768]{1,0:T(8,128)(2,1)S(1)}, u32[]{:S(2)}, u32[]{:S(2)}) collective-permute-start(bf16[24,768]{1,0:T(8,128)(2,1)S(1)} %add_convert_fusion), channel_id=1, source_target_pairs={{0,4},{1,5},{2,6},{3,7},{4,0},{5,1},{6,2},{7,3},{8,12},{9,13},{10,... | collective-permute-start | bytes 110600 | tf_op jit(solution)/shard_map/ppermute | solution.py:194
  52.5 1.4 %collective-permute-start.12 = (bf16[4,24,768]{2,1,0:T(8,128)(2,1)S(1)}, bf16[4,24,768]{2,1,0:T(8,128)(2,1)S(1)}, u32[]{:S(2)}, u32[]{:S(2)}) collective-permute-start(bf16[4,24,768]{2,1,0:T(8,128)(2,1)S(1)} %pad_maximum_fusion.mine), channel_id=1, source_target_pairs={{0,1},{1,0},{2,3},{3,2},{4,5},{5,4},{6,7},{7,6},{8,9},{9,8},{10,11... | collective-permute-start | bytes 442376 | tf_op jit(solution)/shard_map/ppermute | solution.py:194

commit v2 on v1

--- a/solution.py
+++ b/solution.py
@@ -13,6 +13,7 @@
 F32 = jnp.float32
 AXES = ("seq", "dp")
 VMEM = pl.BlockSpec(memory_space=pltpu.VMEM)
+TOGETHER = 8
 LIMIT = 48 * 1024 * 1024
 
 
@@ -41,25 +42,31 @@
     return (frozen.astype(F32) + ADAPTER_SCALE * tn(low_t, up)).astype(BF)
 
 
-def head(q, k, v, g, ups, low_q, low_k, low_v, mask):
-    st = jnp.where(mask, nt(k, q) * SCALE, -jnp.inf)
-    e = jnp.exp(st - jnp.max(st, axis=0, keepdims=True))
-    p = e * (1.0 / jnp.sum(e, axis=0, keepdims=True))
-    pb = p.astype(BF)
-    dp = nt(v, g)
-    row_dot = jnp.sum(pb.astype(F32) * dp, axis=0, keepdims=True)
-    ds = (p * (dp - row_dot) * SCALE).astype(BF)
-    bq, bk, bv = nt(ups[0], k), nt(ups[1], q), nt(ups[2], g)
-    by_q = nn(rows([low_k] + hi_lo(bq)), ds)
-    by_k = nt(rows([low_q] + hi_lo(bk)), ds)
-    av = nn(low_v.astype(BF), pb)
-    rv = nt(rows(hi_lo(bv)), pb)
-    uq = nn(rows(hi_lo(by_k[:8])), k)
-    uk = nn(rows(hi_lo(by_q[:8])), q)
-    uv = nn(rows(hi_lo(av)), g)
-    grads = [u[:8] + u[8:] for u in (uq, uk, uv)]
-    ranks = [by_q[8:16] + by_q[16:24], by_k[8:16] + by_k[16:24], rv[:8] + rv[8:]]
-    return grads, ranks
+def heads(items, mask):
+    sts = [nt(k, q) for q, k, v, g, ups, lows in items]
+    dps = [nt(v, g) for q, k, v, g, ups, lows in items]
+    bs = [(nt(ups[0], k), nt(ups[1], q), nt(ups[2], g)) for q, k, v, g, ups, lows in items]
+    pbs, dss = [], []
+    for st, dp in zip(sts, dps):
+        st = jnp.where(mask, st * SCALE, -jnp.inf)
+        e = jnp.exp(st - jnp.max(st, axis=0, keepdims=True))
+        p = e * (1.0 / jnp.sum(e, axis=0, keepdims=True))
+        pb = p.astype(BF)
+        row_dot = jnp.sum(pb.astype(F32) * dp, axis=0, keepdims=True)
+        pbs.append(pb)
+        dss.append((p * (dp - row_dot) * SCALE).astype(BF))
+    by_q = [nn(rows([it[5][1]] + hi_lo(b[0])), ds) for it, b, ds in zip(items, bs, dss)]
+    by_k = [nt(rows([it[5][0]] + hi_lo(b[1])), ds) for it, b, ds in zip(items, bs, dss)]
+    av = [nn(it[5][2].astype(BF), pb) for it, pb in zip(items, pbs)]
+    rv = [nt(rows(hi_lo(b[2])), pb) for b, pb in zip(bs, pbs)]
+    out = []
+    for it, bq, bk, a, r in zip(items, by_q, by_k, av, rv):
+        q, k, v, g = it[:4]
+        us = [nn(rows(hi_lo(bk[:8])), k), nn(rows(hi_lo(bq[:8])), q), nn(rows(hi_lo(a)), g)]
+        grads = [u[:8] + u[8:] for u in us]
+        ranks = [bq[8:16] + bq[16:24], bk[8:16] + bk[16:24], r[:8] + r[8:]]
+        out.append((grads, ranks))
+    return out
 
 
 def causal(keys, queries, offset):
@@ -77,26 +84,34 @@
     ranks = [jnp.zeros((RANK, count), F32)] * 3
     full_mask = causal(count, count, 0)
     half_mask = causal(half, half, 0)
-    for h in range(half_width // HEAD_DIM):
-        cols = slice(h * HEAD_DIM, (h + 1) * HEAD_DIM)
-        ups = [up[j, :, cols] for j in range(3)]
-        q, k, v = [project(frozen[j, 0, :, cols], low[j], ups[j]) for j in range(3)]
-        grads, parts = head(q, k, v, grad[0, :, cols], ups, *low_f, full_mask)
-        for j in range(3):
-            up_out[8 * j : 8 * j + 8, cols] = grads[j]
-        ranks = [a + b for a, b in zip(ranks, parts)]
+    for first in range(0, half_width, TOGETHER * HEAD_DIM):
+        items, places = [], []
+        for start in range(first, first + TOGETHER * HEAD_DIM, HEAD_DIM):
+            cols = slice(start, start + HEAD_DIM)
+            ups = [up[j, :, cols] for j in range(3)]
+            q, k, v = [project(frozen[j, 0, :, cols], low[j], ups[j]) for j in range(3)]
+            items.append((q, k, v, grad[0, :, cols], ups, low_f))
+            places.append(cols)
+        for cols, (grads, parts) in zip(places, heads(items, full_mask)):
+            for j in range(3):
+                up_out[8 * j : 8 * j + 8, cols] = grads[j]
+            ranks = [a + b for a, b in zip(ranks, parts)]
     near_ranks = [jnp.zeros((RANK, half), F32)] * 3
-    for h in range(half_width // HEAD_DIM):
-        cols = slice(half_width + h * HEAD_DIM, half_width + (h + 1) * HEAD_DIM)
-        ups = [up[j, :, cols] for j in range(3)]
-        whole = [project(frozen[j, 0, :, cols], low[j], ups[j]) for j in range(3)]
-        for j in range(3):
-            far_out[j, :, h * HEAD_DIM : (h + 1) * HEAD_DIM] = whole[j][:half]
-        q, k, v = [x[half:] for x in whole]
-        grads, parts = head(q, k, v, grad[0, half:, cols], ups, *near_f, half_mask)
-        for j in range(3):
-            up_out[8 * j : 8 * j + 8, cols] = grads[j]
-        near_ranks = [a + b for a, b in zip(near_ranks, parts)]
+    for first in range(half_width, width, TOGETHER * HEAD_DIM):
+        items, places = [], []
+        for start in range(first, first + TOGETHER * HEAD_DIM, HEAD_DIM):
+            cols = slice(start, start + HEAD_DIM)
+            ups = [up[j, :, cols] for j in range(3)]
+            whole = [project(frozen[j, 0, :, cols], low[j], ups[j]) for j in range(3)]
+            for j in range(3):
+                far_out[j, :, start - half_width : start - half_width + HEAD_DIM] = whole[j][:half]
+            q, k, v = [x[half:] for x in whole]
+            items.append((q, k, v, grad[0, half:, cols], ups, near_f))
+            places.append(cols)
+        for cols, (grads, parts) in zip(places, heads(items, half_mask)):
+            for j in range(3):
+                up_out[8 * j : 8 * j + 8, cols] = grads[j]
+            near_ranks = [a + b for a, b in zip(near_ranks, parts)]
     for j in range(3):
         rank_out[8 * j : 8 * j + 8, :] = ranks[j] + jnp.concatenate(
             [jnp.zeros((RANK, half), F32), near_ranks[j]], axis=1
@@ -116,19 +131,21 @@
     rank_k = jnp.zeros((RANK, 2 * half), F32)
     rank_v = jnp.zeros((RANK, 2 * half), F32)
     up_out[:, :half_width] = up_in[:, :half_width]
-    for h in range(half_width // HEAD_DIM):
-        here = slice(h * HEAD_DIM, (h + 1) * HEAD_DIM)
-        cols = slice(half_width + h * HEAD_DIM, half_width + (h + 1) * HEAD_DIM)
-        ups = [up[j, :, cols] for j in range(3)]
-        near_k, near_v = [project(frozen_kv[j, :, here], near[j], ups[j + 1]) for j in range(2)]
-        k = jnp.concatenate([near_k, own[1, :, here]], axis=0)
-        v = jnp.concatenate([near_v, own[2, :, here]], axis=0)
-        grads, parts = head(
-            own[0, :, here], k, v, grad[0, :half, cols], ups, far_f[0], low_k, low_v, mask
-        )
-        for j in range(3):
-            up_out[8 * j : 8 * j + 8, cols] = up_in[8 * j : 8 * j + 8, cols] + grads[j]
-        rank_q, rank_k, rank_v = rank_q + parts[0], rank_k + parts[1], rank_v + parts[2]
+    for first in range(half_width, width, TOGETHER * HEAD_DIM):
+        items, places = [], []
+        for start in range(first, first + TOGETHER * HEAD_DIM, HEAD_DIM):
+            here = slice(start - half_width, start - half_width + HEAD_DIM)
+            cols = slice(start, start + HEAD_DIM)
+            ups = [up[j, :, cols] for j in range(3)]
+            near_k, near_v = [project(frozen_kv[j, :, here], near[j], ups[j + 1]) for j in range(2)]
+            k = jnp.concatenate([near_k, own[1, :, here]], axis=0)
+            v = jnp.concatenate([near_v, own[2, :, here]], axis=0)
+            items.append((own[0, :, here], k, v, grad[0, :half, cols], ups, (far_f[0], low_k, low_v)))
+            places.append(cols)
+        for cols, (grads, parts) in zip(places, heads(items, mask)):
+            for j in range(3):
+                up_out[8 * j : 8 * j + 8, cols] = up_in[8 * j : 8 * j + 8, cols] + grads[j]
+            rank_q, rank_k, rank_v = rank_q + parts[0], rank_k + parts[1], rank_v + parts[2]
     none = jnp.zeros((RANK, half), F32)
     for j, part in enumerate([rank_q, rank_k[:, half:], rank_v[:, half:]]):
         rank_out[8 * j : 8 * j + 8, :] = rank_in[8 * j : 8 * j + 8, :] + jnp.concatenate(
@@ -202,8 +219,7 @@
     own = own + got[0].astype(F32) + got[1].astype(F32) + got[2].astype(F32)
     bit = 2
     while bit < seqs:
-        piece = own.astype(BF)
-        own = piece.astype(F32) + swap(piece, bit * dps, total).astype(F32)
+        own = own + swap(own, bit * dps, total)
         bit *= 2
     piece = own.astype(BF)
     mine = jnp.stack([piece] + [swap(piece, (s & 2) | (dps if s & 1 else 0), total) for s in (1, 2, 3)])

time: 55 us -> 47.9 us (0.87)
  Pallas kernels: 14.9 us -> 6.34 us
  waiting for transfers between devices: 16.2 us -> 21 us
  starting transfers between devices: 18.9 us -> 15.6 us
    pallas_call x4, Pallas kernels: 14.9 us -> 6.34 us  [call(): pl.pallas_call(kernel, out_shape=outs, in_specs=[VMEM] * len(args), out_s...]
    ppermute x1, waiting for transfers between devices: 0.01 us -> 2.26 us  [on_device(): low_kv = lax.ppermute(low_t[1:, :, half:], 'seq', forward)]
    ppermute x10, waiting for transfers between devices: 14.8 us -> 16.8 us  [swap(): return lax.ppermute(x, AXES, [(i, i ^ bits) for i in range(total)])]
    ppermute x10, starting transfers between devices: 11.2 us -> 9.3 us  [swap(): return lax.ppermute(x, AXES, [(i, i ^ bits) for i in range(total)])]
    ppermute x1, starting transfers between devices: 3.23 us -> 1.79 us  [on_device(): cross = lax.ppermute(cross, 'seq', backward)]
  transfers between devices with their start and end apart: 13 -> 13, of which waited for: 11 -> 11; matrix products, arithmetic and copies ran while one was open for 3% -> 4% of each run, Pallas kernels for 17% -> 6%
where the time goes in v2:
time: 47.9 us; the launch traced here: 47.6 us
  waiting for transfers between devices  21 us (44%)
  starting transfers between devices  15.6 us (33%)
  Pallas kernels  6.34 us (13%)
  local copies, waits for them, and re-layouts  2.27 us (5%)
  matrix products  1.6 us (3%)
  between operations  0.74 us (2%)
    ppermute x10, waiting for transfers between devices, swap(): return lax.ppermute(x, AXES, [(i, i ^ bits) for i in range(total)])  16.8 us
    ppermute x10, starting transfers between devices, swap(): return lax.ppermute(x, AXES, [(i, i ^ bits) for i in range(total)])  9.3 us
    pallas_call x4, Pallas kernels, call(): pl.pallas_call(kernel, out_shape=outs, in_specs=[VMEM] * len(args), out_s...  6.34 us
    ppermute x1, starting transfers between devices, on_device(): frozen_kv = lax.ppermute(frozen[1:, 0, half:, half_width:], 'seq', forward)  2.99 us
    ppermute x1, waiting for transfers between devices, on_device(): low_kv = lax.ppermute(low_t[1:, :, half:], 'seq', forward)  2.26 us
    ppermute x1, waiting for transfers between devices, on_device(): cross = lax.ppermute(cross, 'seq', backward)  1.91 us
    ppermute x1, starting transfers between devices, on_device(): cross = lax.ppermute(cross, 'seq', backward)  1.79 us
    dot_general x1, matrix products, on_device(): jnp.einsum('psw,gw->psg', down_weight, tokens[0], preferred_element_type=...  1.6 us
  transfers between devices with their start and end apart: 13, of which 11 were waited for; matrix products, arithmetic and copies ran while one was open for 4% of the time, Pallas kernels for 6%

profile of v2, /device:TPU:0, one launch (start us, length us, event | category | flops | bytes accessed | tf_op | source)
XLA Modules:
  0.0 47.6 jit_solution(6602761801115039869)
XLA Ops:
  0.7 1.1 %slice_bitcast_fusion = bf16[2,64,1024]{2,1,0:T(8,128)(2,1)S(1)} fusion(bf16[3,1,128,2048]{3,2,0,1:T(8,128)(2,1)} %bitcast.26), kind=kLoop, calls=%fused_computation.2 | loop fusion | bytes 524288 | tf_op jit(solution)/shard_map/squeeze | solution.py:235
  1.8 3.0 %collective-permute-start = (bf16[2,64,1024]{2,1,0:T(8,128)(2,1)S(1)}, bf16[2,64,1024]{2,1,0:T(8,128)(2,1)S(1)}, u32[]{:S(2)}, u32[]{:S(2)}) collective-permute-start(bf16[2,64,1024]{2,1,0:T(8,128)(2,1)S(1)} %slice_bitcast_fusion), channel_id=1, source_target_pairs={{0,4},{4,8},{8,12},{12,16},{16,20},{20,24},{24,28},{28,0},{1,5},{5... | collective-permute-start | bytes 786440 | tf_op jit(solution)/shard_map/ppermute | solution.py:235
  4.8 1.6 %convolution_convert_fusion.low_t = bf16[3,8,128]{2,1,0:T(8,128)(2,1)S(1)} fusion(bf16[3,8,4096]{2,1,0:T(8,128)(2,1)S(1)} %copy-done, bf16[1,128,4096]{2,1,0:T(8,128)(2,1)} %tokens.1), kind=kOutput, calls=%fused_computation | convolution fusion | flops 25168896 | bytes 1251328 | tf_op jit(solution)/shard_map/psw,gw->psg/dot_general | solution.py:236
  6.4 0.1 slice.28
  6.5 1.6 %collective-permute-start.1 = (bf16[2,8,64]{2,1,0:T(8,128)(2,1)S(1)}, bf16[2,8,64]{2,1,0:T(8,128)(2,1)S(1)}, u32[]{:S(2)}, u32[]{:S(2)}) collective-permute-start(bf16[2,8,64]{2,1,0:T(8,128)(2,1)S(1)} %slice.28), channel_id=1, source_target_pairs={{0,4},{4,8},{8,12},{12,16},{16,20},{20,24},{24,28},{28,0},{1,5},{5... | collective-permute-start | bytes 6152 | tf_op jit(solution)/shard_map/ppermute | solution.py:237
  8.0 1.0 %copy-done.3 = bf16[1,128,2048]{2,1,0:T(8,128)(2,1)S(1)} copy-done((bf16[1,128,2048]{2,1,0:T(8,128)(2,1)S(1)}, bf16[1,128,2048]{2,1,0:T(8,128)(2,1)}, u32[]{:S(2)}) %copy-start.3) | copy-done | bytes 524312
  9.1 2.9 %shard_map.68 = (bf16[3,64,1024]{2,1,0:T(8,128)(2,1)S(1)}, f32[24,2048]{1,0:T(8,128)S(1)}, f32[24,128]{1,0:T(8,128)S(1)}) custom-call(bf16[3,1,128,2048]{3,2,1,0:T(8,128)(2,1)S(1)} %copy-done.2, bf16[1,128,2048]{2,1,0:T(8,128)(2,1)S(1)} %copy-done.3, bf16[3,8,128]{2,1,0:T(8,128)(2,1)S(1)} %convolution_convert_fusion.low_t, bf16[3,8,2048]{2,1,0:T(8,128)(2,1)S(1)} %copy-done.5), custom_call_target="tpu_custom_call" | custom-call | flops 1000000000 | bytes 1000000 | tf_op jit(solution)/shard_map/pallas_call | solution.py:200
  11.9 2.3 %collective-permute-done.1.low_kv = bf16[2,8,64]{2,1,0:T(8,128)(2,1)S(1)} collective-permute-done((bf16[2,8,64]{2,1,0:T(8,128)(2,1)S(1)}, bf16[2,8,64]{2,1,0:T(8,128)(2,1)S(1)}, u32[]{:S(2)}, u32[]{:S(2)}) %collective-permute-start.1) | collective-permute-done | bytes 2080 | tf_op jit(solution)/shard_map/ppermute | solution.py:237
  14.2 1.4 %shard_map.69 = (f32[24,2048]{1,0:T(8,128)S(1)}, f32[24,128]{1,0:T(8,128)S(1)}, f32[16,128]{1,0:T(8,128)S(1)}) custom-call(bf16[3,64,1024]{2,1,0:T(8,128)(2,1)S(1)} %get-tuple-element.10.own, bf16[2,64,1024]{2,1,0:T(8,128)(2,1)S(1)} %collective-permute-done.frozen_kv, bf16[2,8,64]{2,1,0:T(8,128)(2,1)S(1)} %collective-permute-done.1.low_kv, ...), custom_call_target="tpu_custom_call" | custom-call | flops 1000000000 | bytes 1000000 | tf_op jit(solution)/shard_map/pallas_call | solution.py:200
  15.6 1.8 %collective-permute-start.2 = (f32[16,128]{1,0:T(8,128)S(1)}, f32[16,128]{1,0:T(8,128)S(1)}, u32[]{:S(2)}, u32[]{:S(2)}) collective-permute-start(f32[16,128]{1,0:T(8,128)S(1)} %get-tuple-element.14), channel_id=1, source_target_pairs={{0,28},{4,0},{8,4},{12,8},{16,12},{20,16},{24,20},{28,24},{1,29},{... | collective-permute-start | bytes 24584 | tf_op jit(solution)/shard_map/ppermute | solution.py:249
  17.4 1.9 %collective-permute-done.2.cross = f32[16,128]{1,0:T(8,128)S(1)} collective-permute-done((f32[16,128]{1,0:T(8,128)S(1)}, f32[16,128]{1,0:T(8,128)S(1)}, u32[]{:S(2)}, u32[]{:S(2)}) %collective-permute-start.2) | collective-permute-done | bytes 8224 | tf_op jit(solution)/shard_map/ppermute | solution.py:249
  19.3 1.2 %shard_map.70 = (f32[4,24,768]{2,1,0:T(8,128)S(1)}, f32[4,24,768]{2,1,0:T(8,128)S(1)}) custom-call(bf16[1,128,4096]{2,1,0:T(8,128)(2,1)S(1)} %copy-done.1, f32[24,128]{1,0:T(8,128)S(1)} %get-tuple-element.13.rank_in, f32[16,128]{1,0:T(8,128)S(1)} %collective-permute-done.2.cross, f32[24,2048]{1,0:T(8,128)S(1)} %get-tuple-element.15.up_in), custom_call_target="tpu_custom_call" | custom-call | flops 1000000000 | bytes 1000000 | tf_op jit(solution)/shard_map/pallas_call | solution.py:200
  20.5 0.1 collective-permute-start.3
  20.6 1.6 %collective-permute-done.3 = f32[4,24,768]{2,1,0:T(8,128)S(1)} collective-permute-done((f32[4,24,768]{2,1,0:T(8,128)S(1)}, f32[4,24,768]{2,1,0:T(8,128)S(1)}, u32[]{:S(2)}, u32[]{:S(2)}) %collective-permute-start.3) | collective-permute-done | bytes 294944 | tf_op jit(solution)/shard_map/ppermute | solution.py:211
  22.2 0.2 collective-permute-start.4
  22.4 2.8 %collective-permute-start.6 = (bf16[24,768]{1,0:T(8,128)(2,1)S(1)}, bf16[24,768]{1,0:T(8,128)(2,1)S(1)}, u32[]{:S(2)}, u32[]{:S(2)}) collective-permute-start(bf16[24,768]{1,0:T(8,128)(2,1)S(1)} %get-tuple-element.21), channel_id=1, source_target_pairs={{0,6},{1,7},{2,4},{3,5},{4,2},{5,3},{6,0},{7,1},{8,14},{9,15},{10,... | collective-permute-start | bytes 110600 | tf_op jit(solution)/shard_map/ppermute | solution.py:211
  25.2 0.5 %collective-permute-start.5 = (bf16[24,768]{1,0:T(8,128)(2,1)S(1)}, bf16[24,768]{1,0:T(8,128)(2,1)S(1)}, u32[]{:S(2)}, u32[]{:S(2)}) collective-permute-start(bf16[24,768]{1,0:T(8,128)(2,1)S(1)} %get-tuple-element.22), channel_id=1, source_target_pairs={{0,2},{1,3},{2,0},{3,1},{4,6},{5,7},{6,4},{7,5},{8,10},{9,11},{10,... | collective-permute-start | bytes 110600 | tf_op jit(solution)/shard_map/ppermute | solution.py:211
  25.8 0.7 %collective-permute-done.4 = bf16[24,768]{1,0:T(8,128)(2,1)S(1)} collective-permute-done((bf16[24,768]{1,0:T(8,128)(2,1)S(1)}, bf16[24,768]{1,0:T(8,128)(2,1)S(1)}, u32[]{:S(2)}, u32[]{:S(2)}) %collective-permute-start.4) | collective-permute-done | bytes 36896 | tf_op jit(solution)/shard_map/ppermute | solution.py:211
  26.4 1.2 %collective-permute-done.6 = bf16[24,768]{1,0:T(8,128)(2,1)S(1)} collective-permute-done((bf16[24,768]{1,0:T(8,128)(2,1)S(1)}, bf16[24,768]{1,0:T(8,128)(2,1)S(1)}, u32[]{:S(2)}, u32[]{:S(2)}) %collective-permute-start.6) | collective-permute-done | bytes 36896 | tf_op jit(solution)/shard_map/ppermute | solution.py:211
  27.6 1.6 %collective-permute-done.5 = bf16[24,768]{1,0:T(8,128)(2,1)S(1)} collective-permute-done((bf16[24,768]{1,0:T(8,128)(2,1)S(1)}, bf16[24,768]{1,0:T(8,128)(2,1)S(1)}, u32[]{:S(2)}, u32[]{:S(2)}) %collective-permute-start.5) | collective-permute-done | bytes 36896 | tf_op jit(solution)/shard_map/ppermute | solution.py:211
  29.2 0.1 collective-permute-start.7
  29.4 4.3 %collective-permute-done.7 = f32[24,768]{1,0:T(8,128)S(1)} collective-permute-done((f32[24,768]{1,0:T(8,128)S(1)}, f32[24,768]{1,0:T(8,128)S(1)}, u32[]{:S(2)}, u32[]{:S(2)}) %collective-permute-start.7) | collective-permute-done | bytes 73760 | tf_op jit(solution)/shard_map/ppermute | solution.py:211
  33.7 1.9 %collective-permute-start.8 = (f32[24,768]{1,0:T(8,128)S(1)}, f32[24,768]{1,0:T(8,128)S(1)}, u32[]{:S(2)}, u32[]{:S(2)}) collective-permute-start(f32[24,768]{1,0:T(8,128)S(1)} %add.22), channel_id=1, source_target_pairs={{0,16},{1,17},{2,18},{3,19},{4,20},{5,21},{6,22},{7,23},{8,24},{9,... | collective-permute-start | bytes 221192 | tf_op jit(solution)/shard_map/ppermute | solution.py:211
  35.6 4.2 %collective-permute-done.8 = f32[24,768]{1,0:T(8,128)S(1)} collective-permute-done((f32[24,768]{1,0:T(8,128)S(1)}, f32[24,768]{1,0:T(8,128)S(1)}, u32[]{:S(2)}, u32[]{:S(2)}) %collective-permute-start.8) | collective-permute-done | bytes 73760 | tf_op jit(solution)/shard_map/ppermute | solution.py:211
  39.8 0.2 collective-permute-start.11
  40.0 1.2 %collective-permute-start.10 = (bf16[24,768]{1,0:T(8,128)(2,1)S(1)}, bf16[24,768]{1,0:T(8,128)(2,1)S(1)}, u32[]{:S(2)}, u32[]{:S(2)}) collective-permute-start(bf16[24,768]{1,0:T(8,128)(2,1)S(1)} %add_convert_fusion), channel_id=1, source_target_pairs={{0,2},{1,3},{2,0},{3,1},{4,6},{5,7},{6,4},{7,5},{8,10},{9,11},{10,... | collective-permute-start | bytes 110600 | tf_op jit(solution)/shard_map/ppermute | solution.py:211
  41.2 2.2 %collective-permute-start.9 = (bf16[24,768]{1,0:T(8,128)(2,1)S(1)}, bf16[24,768]{1,0:T(8,128)(2,1)S(1)}, u32[]{:S(2)}, u32[]{:S(2)}) collective-permute-start(bf16[24,768]{1,0:T(8,128)(2,1)S(1)} %add_convert_fusion), channel_id=1, source_target_pairs={{0,4},{1,5},{2,6},{3,7},{4,0},{5,1},{6,2},{7,3},{8,12},{9,13},{10,... | collective-permute-start | bytes 110600 | tf_op jit(solution)/shard_map/ppermute | solution.py:211
  43.3 1.4 %collective-permute-done.11 = bf16[24,768]{1,0:T(8,128)(2,1)S(1)} collective-permute-done((bf16[24,768]{1,0:T(8,128)(2,1)S(1)}, bf16[24,768]{1,0:T(8,128)(2,1)S(1)}, u32[]{:S(2)}, u32[]{:S(2)}) %collective-permute-start.11) | collective-permute-done | bytes 36896 | tf_op jit(solution)/shard_map/ppermute | solution.py:211
  44.7 0.6 %collective-permute-done.9 = bf16[24,768]{1,0:T(8,128)(2,1)S(1)} collective-permute-done((bf16[24,768]{1,0:T(8,128)(2,1)S(1)}, bf16[24,768]{1,0:T(8,128)(2,1)S(1)}, u32[]{:S(2)}, u32[]{:S(2)}) %collective-permute-start.9) | collective-permute-done | bytes 36896 | tf_op jit(solution)/shard_map/ppermute | solution.py:211
  45.3 0.1 collective-permute-start.12
  45.4 1.4 %collective-permute-done.12.other = bf16[4,24,768]{2,1,0:T(8,128)(2,1)S(1)} collective-permute-done((bf16[4,24,768]{2,1,0:T(8,128)(2,1)S(1)}, bf16[4,24,768]{2,1,0:T(8,128)(2,1)S(1)}, u32[]{:S(2)}, u32[]{:S(2)}) %collective-permute-start.12) | collective-permute-done | bytes 147488 | tf_op jit(solution)/shard_map/ppermute | solution.py:211
  46.7 0.9 %shard_map.71 = (f32[3,8,4096]{2,1,0:T(8,128)}, f32[3,8,2048]{2,1,0:T(8,128)}) custom-call(bf16[4,24,768]{2,1,0:T(8,128)(2,1)S(1)} %pad_maximum_fusion.mine, bf16[4,24,768]{2,1,0:T(8,128)(2,1)S(1)} %collective-permute-done.12.other), custom_call_target="tpu_custom_call" | custom-call | flops 1000000000 | bytes 1000000 | tf_op jit(solution)/shard_map/pallas_call | solution.py:200
  (19 shorter events, 0.1 us)
Async XLA Ops:
  0.6 4.1 %copy-start = (bf16[3,8,4096]{2,1,0:T(8,128)(2,1)S(1)}, bf16[3,8,4096]{2,1,0:T(8,128)(2,1)}, u32[]{:S(2)}) copy-start(bf16[3,8,4096]{2,1,0:T(8,128)(2,1)} %param.8) | copy-start | bytes 589828
  0.6 7.4 %copy-start.2 = (bf16[3,1,128,2048]{3,2,1,0:T(8,128)(2,1)S(1)}, bf16[3,1,128,2048]{3,2,1,0:T(8,128)(2,1)}, u32[]{:S(2)}) copy-start(bf16[3,1,128,2048]{3,2,1,0:T(8,128)(2,1)} %frozen.1) | copy-start | bytes 4718596
  0.7 7.4 %copy-start.5 = (bf16[3,8,2048]{2,1,0:T(8,128)(2,1)S(1)}, bf16[3,8,2048]{2,1,0:T(8,128)(2,1)}, u32[]{:S(2)}) copy-start(bf16[3,8,2048]{2,1,0:T(8,128)(2,1)} %up.3) | copy-start | bytes 294916
  1.8 12.4 %collective-permute-start = (bf16[2,64,1024]{2,1,0:T(8,128)(2,1)S(1)}, bf16[2,64,1024]{2,1,0:T(8,128)(2,1)S(1)}, u32[]{:S(2)}, u32[]{:S(2)}) collective-permute-start(bf16[2,64,1024]{2,1,0:T(8,128)(2,1)S(1)} %slice_bitcast_fusion), channel_id=1, source_target_pairs={{0,4},{4,8},{8,12},{12,16},{16,20},{20,24},{24,28},{28,0},{1,5},{5... | collective-permute-start | bytes 786440 | tf_op jit(solution)/shard_map/ppermute | solution.py:235
  6.5 7.7 %collective-permute-start.1 = (bf16[2,8,64]{2,1,0:T(8,128)(2,1)S(1)}, bf16[2,8,64]{2,1,0:T(8,128)(2,1)S(1)}, u32[]{:S(2)}, u32[]{:S(2)}) collective-permute-start(bf16[2,8,64]{2,1,0:T(8,128)(2,1)S(1)} %slice.28), channel_id=1, source_target_pairs={{0,4},{4,8},{8,12},{12,16},{16,20},{20,24},{24,28},{28,0},{1,5},{5... | collective-permute-start | bytes 6152 | tf_op jit(solution)/shard_map/ppermute | solution.py:237
  8.0 1.0 %copy-start.3 = (bf16[1,128,2048]{2,1,0:T(8,128)(2,1)S(1)}, bf16[1,128,2048]{2,1,0:T(8,128)(2,1)}, u32[]{:S(2)}) copy-start(bf16[1,128,2048]{2,1,0:T(8,128)(2,1)} %grad.3) | copy-start | bytes 1572868
  9.1 5.1 %copy-start.4 = (bf16[1,128,2048]{2,1,0:T(8,128)(2,1)S(1)}, bf16[1,128,2048]{2,1,0:T(8,128)(2,1)}, u32[]{:S(2)}) copy-start(bf16[1,128,2048]{2,1,0:T(8,128)(2,1)} %grad.3) | copy-start | bytes 1572868
  14.2 5.1 %copy-start.1 = (bf16[1,128,4096]{2,1,0:T(8,128)(2,1)S(1)}, bf16[1,128,4096]{2,1,0:T(8,128)(2,1)}, u32[]{:S(2)}) copy-start(bf16[1,128,4096]{2,1,0:T(8,128)(2,1)} %tokens.1) | copy-start | bytes 3145732
  15.6 3.7 %collective-permute-start.2 = (f32[16,128]{1,0:T(8,128)S(1)}, f32[16,128]{1,0:T(8,128)S(1)}, u32[]{:S(2)}, u32[]{:S(2)}) collective-permute-start(f32[16,128]{1,0:T(8,128)S(1)} %get-tuple-element.14), channel_id=1, source_target_pairs={{0,28},{4,0},{8,4},{12,8},{16,12},{20,16},{24,20},{28,24},{1,29},{... | collective-permute-start | bytes 24584 | tf_op jit(solution)/shard_map/ppermute | solution.py:249
  20.5 1.6 %collective-permute-start.3 = (f32[4,24,768]{2,1,0:T(8,128)S(1)}, f32[4,24,768]{2,1,0:T(8,128)S(1)}, u32[]{:S(2)}, u32[]{:S(2)}) collective-permute-start(f32[4,24,768]{2,1,0:T(8,128)S(1)} %get-tuple-element.17), channel_id=1, source_target_pairs={{0,1},{1,0},{2,3},{3,2},{4,5},{5,4},{6,7},{7,6},{8,9},{9,8},{10,11... | collective-permute-start | bytes 884744 | tf_op jit(solution)/shard_map/ppermute | solution.py:211
  22.2 4.2 %collective-permute-start.4 = (bf16[24,768]{1,0:T(8,128)(2,1)S(1)}, bf16[24,768]{1,0:T(8,128)(2,1)S(1)}, u32[]{:S(2)}, u32[]{:S(2)}) collective-permute-start(bf16[24,768]{1,0:T(8,128)(2,1)S(1)} %get-tuple-element.20), channel_id=1, source_target_pairs={{0,4},{1,5},{2,6},{3,7},{4,0},{5,1},{6,2},{7,3},{8,12},{9,13},{10,... | collective-permute-start | bytes 110600 | tf_op jit(solution)/shard_map/ppermute | solution.py:211
  22.4 5.1 %collective-permute-start.6 = (bf16[24,768]{1,0:T(8,128)(2,1)S(1)}, bf16[24,768]{1,0:T(8,128)(2,1)S(1)}, u32[]{:S(2)}, u32[]{:S(2)}) collective-permute-start(bf16[24,768]{1,0:T(8,128)(2,1)S(1)} %get-tuple-element.21), channel_id=1, source_target_pairs={{0,6},{1,7},{2,4},{3,5},{4,2},{5,3},{6,0},{7,1},{8,14},{9,15},{10,... | collective-permute-start | bytes 110600 | tf_op jit(solution)/shard_map/ppermute | solution.py:211
  25.2 4.0 %collective-permute-start.5 = (bf16[24,768]{1,0:T(8,128)(2,1)S(1)}, bf16[24,768]{1,0:T(8,128)(2,1)S(1)}, u32[]{:S(2)}, u32[]{:S(2)}) collective-permute-start(bf16[24,768]{1,0:T(8,128)(2,1)S(1)} %get-tuple-element.22), channel_id=1, source_target_pairs={{0,2},{1,3},{2,0},{3,1},{4,6},{5,7},{6,4},{7,5},{8,10},{9,11},{10,... | collective-permute-start | bytes 110600 | tf_op jit(solution)/shard_map/ppermute | solution.py:211
  29.2 4.4 %collective-permute-start.7 = (f32[24,768]{1,0:T(8,128)S(1)}, f32[24,768]{1,0:T(8,128)S(1)}, u32[]{:S(2)}, u32[]{:S(2)}) collective-permute-start(f32[24,768]{1,0:T(8,128)S(1)} %fusion.3), channel_id=1, source_target_pairs={{0,8},{1,9},{2,10},{3,11},{4,12},{5,13},{6,14},{7,15},{8,0},{9,1},... | collective-permute-start | bytes 221192 | tf_op jit(solution)/shard_map/ppermute | solution.py:211
  33.7 6.1 %collective-permute-start.8 = (f32[24,768]{1,0:T(8,128)S(1)}, f32[24,768]{1,0:T(8,128)S(1)}, u32[]{:S(2)}, u32[]{:S(2)}) collective-permute-start(f32[24,768]{1,0:T(8,128)S(1)} %add.22), channel_id=1, source_target_pairs={{0,16},{1,17},{2,18},{3,19},{4,20},{5,21},{6,22},{7,23},{8,24},{9,... | collective-permute-start | bytes 221192 | tf_op jit(solution)/shard_map/ppermute | solution.py:211
  39.8 4.9 %collective-permute-start.11 = (bf16[24,768]{1,0:T(8,128)(2,1)S(1)}, bf16[24,768]{1,0:T(8,128)(2,1)S(1)}, u32[]{:S(2)}, u32[]{:S(2)}) collective-permute-start(bf16[24,768]{1,0:T(8,128)(2,1)S(1)} %add_convert_fusion), channel_id=1, source_target_pairs={{0,6},{1,7},{2,4},{3,5},{4,2},{5,3},{6,0},{7,1},{8,14},{9,15},{10,... | collective-permute-start | bytes 110600 | tf_op jit(solution)/shard_map/ppermute | solution.py:211
  40.0 4.7 %collective-permute-start.10 = (bf16[24,768]{1,0:T(8,128)(2,1)S(1)}, bf16[24,768]{1,0:T(8,128)(2,1)S(1)}, u32[]{:S(2)}, u32[]{:S(2)}) collective-permute-start(bf16[24,768]{1,0:T(8,128)(2,1)S(1)} %add_convert_fusion), channel_id=1, source_target_pairs={{0,2},{1,3},{2,0},{3,1},{4,6},{5,7},{6,4},{7,5},{8,10},{9,11},{10,... | collective-permute-start | bytes 110600 | tf_op jit(solution)/shard_map/ppermute | solution.py:211
  41.2 4.1 %collective-permute-start.9 = (bf16[24,768]{1,0:T(8,128)(2,1)S(1)}, bf16[24,768]{1,0:T(8,128)(2,1)S(1)}, u32[]{:S(2)}, u32[]{:S(2)}) collective-permute-start(bf16[24,768]{1,0:T(8,128)(2,1)S(1)} %add_convert_fusion), channel_id=1, source_target_pairs={{0,4},{1,5},{2,6},{3,7},{4,0},{5,1},{6,2},{7,3},{8,12},{9,13},{10,... | collective-permute-start | bytes 110600 | tf_op jit(solution)/shard_map/ppermute | solution.py:211
  45.3 1.4 %collective-permute-start.12 = (bf16[4,24,768]{2,1,0:T(8,128)(2,1)S(1)}, bf16[4,24,768]{2,1,0:T(8,128)(2,1)S(1)}, u32[]{:S(2)}, u32[]{:S(2)}) collective-permute-start(bf16[4,24,768]{2,1,0:T(8,128)(2,1)S(1)} %pad_maximum_fusion.mine), channel_id=1, source_target_pairs={{0,1},{1,0},{2,3},{3,2},{4,5},{5,4},{6,7},{7,6},{8,9},{9,8},{10,11... | collective-permute-start | bytes 442376 | tf_op jit(solution)/shard_map/ppermute | solution.py:211

commit v3 on v2

--- a/solution.py
+++ b/solution.py
@@ -155,36 +155,29 @@
         cross_out[8 * j : 8 * j + 8, :] = jnp.concatenate([none, part], axis=1)
 
 
-def position():
-    dp = lax.axis_index("dp")
-    return dp & 1, (dp & 2) | (lax.axis_index("seq") & 1)
-
-
-def down_kernel(tokens, rank_in, cross, up_in, keep, send):
-    core, place = position()
+def place():
+    return (lax.axis_index("dp") & 2) | (lax.axis_index("seq") & 1)
+
+
+def down_kernel(tokens, rank_in, cross, up_in, out):
+    here = place()
     ranks = rank_in[...] + jnp.concatenate([jnp.zeros((RANK, rank_in.shape[1]), F32), cross[...]], axis=0)
     both = rows(hi_lo(ranks))
     n = ranks.shape[0]
-    up_step, down_step = up_in.shape[1] // 8, tokens.shape[2] // 8
-    for c in range(8):
+    up_step, down_step = up_in.shape[1] // 4, tokens.shape[2] // 4
+    for c in range(4):
         d = nn(both, tokens[0, :, c * down_step : (c + 1) * down_step])
-        d = ADAPTER_SCALE * (d[:n] + d[n:])
-        u = ADAPTER_SCALE * up_in[:, c * up_step : (c + 1) * up_step]
-        slot = place ^ (c >> 1)
-
-        def put(ref):
-            ref[slot, :, :up_step] = u
-            ref[slot, :, up_step:] = d
-
-        pl.when(core == (c & 1))(lambda: put(keep))
-        pl.when(core != (c & 1))(lambda: put(send))
+        slot = here ^ c
+        out[slot, :, :up_step] = ADAPTER_SCALE * up_in[:, c * up_step : (c + 1) * up_step]
+        out[slot, :, up_step:] = ADAPTER_SCALE * (d[:n] + d[n:])
 
 
 def spread_kernel(mine, other, down_out, up_out):
-    core, place = position()
-    up_step, down_step = up_out.shape[2] // 8, down_out.shape[2] // 8
-    for c in range(8):
-        slot = place ^ (c >> 1)
+    here = place()
+    odd = (lax.axis_index("dp") & 1) == 1
+    up_step, down_step = up_out.shape[2] // 4, down_out.shape[2] // 4
+    for c in range(4):
+        slot = here ^ c
 
         def put(ref):
             x = ref[slot].astype(F32)
@@ -192,8 +185,8 @@
                 up_out[j, :, c * up_step : (c + 1) * up_step] = x[8 * j : 8 * j + 8, :up_step]
                 down_out[j, :, c * down_step : (c + 1) * down_step] = x[8 * j : 8 * j + 8, up_step:]
 
-        pl.when(core == (c & 1))(lambda: put(mine))
-        pl.when(core != (c & 1))(lambda: put(other))
+        pl.when(odd)(lambda: put(mine))
+        pl.when(jnp.logical_not(odd))(lambda: put(other))
 
 
 def call(kernel, outs, *args):
@@ -207,23 +200,37 @@
     )(*args)
 
 
-def swap(x, bits, total):
-    return lax.ppermute(x, AXES, [(i, i ^ bits) for i in range(total)])
-
-
-def total_sum(keep, send, seqs, dps):
+def odd_swap(x, bits, total):
+    return lax.ppermute(x, AXES, [(i, i ^ bits) for i in range(1, total, 2)])
+
+
+def along(x, pairs, seqs, dps):
+    moves = [
+        (i, i + (b - a) * 2 * dps)
+        for i in range(1, seqs * dps, 2)
+        for a, b in pairs
+        if (i // (2 * dps)) % 4 == a
+    ]
+    return lax.ppermute(x, AXES, moves)
+
+
+def total_sum(part, seqs, dps):
     total = seqs * dps
-    keep = keep + swap(send, 1, total)
-    own = keep[0]
-    got = [swap(keep[s].astype(BF), (s & 2) | (dps if s & 1 else 0), total) for s in (1, 2, 3)]
-    own = own + got[0].astype(F32) + got[1].astype(F32) + got[2].astype(F32)
-    bit = 2
+    bits = [(s & 2) | (dps if s & 1 else 0) for s in range(4)]
+    part = part + lax.ppermute(part, AXES, [(i, i + 1) for i in range(0, total, 2)])
+    got = [odd_swap(part[s].astype(BF), bits[s], total).astype(F32) for s in (1, 2, 3)]
+    own = part[0] + got[0] + got[1] + got[2]
+    bit = 8
     while bit < seqs:
-        own = own + swap(own, bit * dps, total)
+        own = own + odd_swap(own, bit * dps, total)
         bit *= 2
+    own = own + along(own, [(0, 1), (3, 2)], seqs, dps)
+    own = own + along(own, [(1, 2), (2, 1)], seqs, dps)
     piece = own.astype(BF)
-    mine = jnp.stack([piece] + [swap(piece, (s & 2) | (dps if s & 1 else 0), total) for s in (1, 2, 3)])
-    return mine, swap(mine, 1, total)
+    line = (lax.axis_index("seq") // 2) % 4
+    piece = jnp.where((line == 0) | (line == 3), along(piece, [(1, 0), (2, 3)], seqs, dps), piece)
+    mine = jnp.stack([piece] + [odd_swap(piece, bits[s], total) for s in (1, 2, 3)])
+    return mine, lax.ppermute(mine, AXES, [(i, i - 1) for i in range(1, total, 2)])
 
 
 def on_device(tokens, frozen, grad, down_weight, up_weight):
@@ -247,10 +254,9 @@
         own, frozen_kv, low_kv, grad, low_t, up_weight, up_part, rank_part,
     )
     cross = lax.ppermute(cross, "seq", backward)
-    columns = (width + tokens.shape[2]) // 8
-    piece = sds((4, 24, columns), F32)
-    keep, send = call(down_kernel, [piece, piece], tokens, rank_part, cross, up_part)
-    mine, other = total_sum(keep, send, seqs, dps)
+    columns = (width + tokens.shape[2]) // 4
+    part = call(down_kernel, sds((4, 24, columns), F32), tokens, rank_part, cross, up_part)
+    mine, other = total_sum(part, seqs, dps)
     return tuple(
         call(spread_kernel, [sds((3, RANK, tokens.shape[2]), F32), sds((3, RANK, width), F32)], mine, other)
     )

time: 47.9 us -> 64.3 us (1.34)
  waiting for transfers between devices: 21 us -> 38.4 us
  Pallas kernels: 6.34 us -> 5.41 us
    ppermute x10 -> x11, waiting for transfers between devices: 16.8 us -> 34.3 us  [the longest x1 32.7 us: total_sum(): lax.ppermute(mine, AXES, [(i, i - 1) for i in range(1, total, 2)])]
    pallas_call x4, Pallas kernels: 6.34 us -> 5.41 us  [call(): pl.pallas_call(kernel, out_shape=outs, in_specs=[VMEM] * len(args), out_s...]
    ppermute x10 -> x11, starting transfers between devices: 9.3 us -> 8.62 us  [the longest x6 3.99 us: odd_swap(): return lax.ppermute(x, AXES, [(i, i ^ bits) for i in range(1, total, 2)])]
  transfers between devices with their start and end apart: 13 -> 14, of which waited for: 11 -> 4; matrix products, arithmetic and copies ran while one was open for 4% -> 3% of each run, Pallas kernels for 6% -> 4%
where the time goes in v3:
time: 64.3 us; the launch traced here: 63.8 us
  waiting for transfers between devices  38.4 us (60%)
  starting transfers between devices  15 us (23%)
  Pallas kernels  5.41 us (8%)
  local copies, waits for them, and re-layouts  2.27 us (4%)
  matrix products  1.6 us (2%)
  between operations  0.93 us (1%)
    ppermute x1, waiting for transfers between devices, total_sum(): lax.ppermute(mine, AXES, [(i, i - 1) for i in range(1, total, 2)])  32.7 us
    pallas_call x4, Pallas kernels, call(): pl.pallas_call(kernel, out_shape=outs, in_specs=[VMEM] * len(args), out_s...  5.41 us
    ppermute x6, starting transfers between devices, odd_swap(): return lax.ppermute(x, AXES, [(i, i ^ bits) for i in range(1, total, 2)])  3.99 us
    ppermute x1, starting transfers between devices, on_device(): frozen_kv = lax.ppermute(frozen[1:, 0, half:, half_width:], 'seq', forward)  2.99 us
    ppermute x1, waiting for transfers between devices, on_device(): low_kv = lax.ppermute(low_t[1:, :, half:], 'seq', forward)  2.26 us
    ppermute x3, starting transfers between devices, along(): return lax.ppermute(x, AXES, moves)  2.01 us
    ppermute x1, waiting for transfers between devices, on_device(): cross = lax.ppermute(cross, 'seq', backward)  1.91 us
    ppermute x1, starting transfers between devices, on_device(): cross = lax.ppermute(cross, 'seq', backward)  1.79 us
  transfers between devices with their start and end apart: 14, of which 4 were waited for; matrix products, arithmetic and copies ran while one was open for 3% of the time, Pallas kernels for 4%

profile of v3, /device:TPU:0, one launch (start us, length us, event | category | flops | bytes accessed | tf_op | source)
XLA Modules:
  0.0 63.8 jit_solution(11015097130424416710)
XLA Ops:
  0.6 0.0 copy-start
  0.7 1.1 %slice_bitcast_fusion = bf16[2,64,1024]{2,1,0:T(8,128)(2,1)S(1)} fusion(bf16[3,1,128,2048]{3,2,0,1:T(8,128)(2,1)} %bitcast.26), kind=kLoop, calls=%fused_computation.3 | loop fusion | bytes 524288 | tf_op jit(solution)/shard_map/squeeze | solution.py:242
  1.8 3.0 %collective-permute-start = (bf16[2,64,1024]{2,1,0:T(8,128)(2,1)S(1)}, bf16[2,64,1024]{2,1,0:T(8,128)(2,1)S(1)}, u32[]{:S(2)}, u32[]{:S(2)}) collective-permute-start(bf16[2,64,1024]{2,1,0:T(8,128)(2,1)S(1)} %slice_bitcast_fusion), channel_id=1, source_target_pairs={{0,4},{4,8},{8,12},{12,16},{16,20},{20,24},{24,28},{28,0},{1,5},{5... | collective-permute-start | bytes 786440 | tf_op jit(solution)/shard_map/ppermute | solution.py:242
  4.8 1.6 %convolution_convert_fusion.low_t = bf16[3,8,128]{2,1,0:T(8,128)(2,1)S(1)} fusion(bf16[3,8,4096]{2,1,0:T(8,128)(2,1)S(1)} %copy-done, bf16[1,128,4096]{2,1,0:T(8,128)(2,1)} %tokens.1), kind=kOutput, calls=%fused_computation | convolution fusion | flops 25168896 | bytes 1251328 | tf_op jit(solution)/shard_map/psw,gw->psg/dot_general | solution.py:243
  6.4 0.1 slice.28
  6.5 1.6 %collective-permute-start.1 = (bf16[2,8,64]{2,1,0:T(8,128)(2,1)S(1)}, bf16[2,8,64]{2,1,0:T(8,128)(2,1)S(1)}, u32[]{:S(2)}, u32[]{:S(2)}) collective-permute-start(bf16[2,8,64]{2,1,0:T(8,128)(2,1)S(1)} %slice.28), channel_id=1, source_target_pairs={{0,4},{4,8},{8,12},{12,16},{16,20},{20,24},{24,28},{28,0},{1,5},{5... | collective-permute-start | bytes 6152 | tf_op jit(solution)/shard_map/ppermute | solution.py:244
  8.0 1.0 %copy-done.3 = bf16[1,128,2048]{2,1,0:T(8,128)(2,1)S(1)} copy-done((bf16[1,128,2048]{2,1,0:T(8,128)(2,1)S(1)}, bf16[1,128,2048]{2,1,0:T(8,128)(2,1)}, u32[]{:S(2)}) %copy-start.3) | copy-done | bytes 524312
  9.1 2.9 %shard_map.68 = (bf16[3,64,1024]{2,1,0:T(8,128)(2,1)S(1)}, f32[24,2048]{1,0:T(8,128)S(1)}, f32[24,128]{1,0:T(8,128)S(1)}) custom-call(bf16[3,1,128,2048]{3,2,1,0:T(8,128)(2,1)S(1)} %copy-done.2, bf16[1,128,2048]{2,1,0:T(8,128)(2,1)S(1)} %copy-done.3, bf16[3,8,128]{2,1,0:T(8,128)(2,1)S(1)} %convolution_convert_fusion.low_t, bf16[3,8,2048]{2,1,0:T(8,128)(2,1)S(1)} %copy-done.5), custom_call_target="tpu_custom_call" | custom-call | flops 1000000000 | bytes 1000000 | tf_op jit(solution)/shard_map/pallas_call | solution.py:193
  11.9 2.3 %collective-permute-done.1.low_kv = bf16[2,8,64]{2,1,0:T(8,128)(2,1)S(1)} collective-permute-done((bf16[2,8,64]{2,1,0:T(8,128)(2,1)S(1)}, bf16[2,8,64]{2,1,0:T(8,128)(2,1)S(1)}, u32[]{:S(2)}, u32[]{:S(2)}) %collective-permute-start.1) | collective-permute-done | bytes 2080 | tf_op jit(solution)/shard_map/ppermute | solution.py:244
  14.2 1.4 %shard_map.69 = (f32[24,2048]{1,0:T(8,128)S(1)}, f32[24,128]{1,0:T(8,128)S(1)}, f32[16,128]{1,0:T(8,128)S(1)}) custom-call(bf16[3,64,1024]{2,1,0:T(8,128)(2,1)S(1)} %get-tuple-element.8.own, bf16[2,64,1024]{2,1,0:T(8,128)(2,1)S(1)} %collective-permute-done.frozen_kv, bf16[2,8,64]{2,1,0:T(8,128)(2,1)S(1)} %collective-permute-done.1.low_kv, ...), custom_call_target="tpu_custom_call" | custom-call | flops 1000000000 | bytes 1000000 | tf_op jit(solution)/shard_map/pallas_call | solution.py:193
  15.6 1.8 %collective-permute-start.2 = (f32[16,128]{1,0:T(8,128)S(1)}, f32[16,128]{1,0:T(8,128)S(1)}, u32[]{:S(2)}, u32[]{:S(2)}) collective-permute-start(f32[16,128]{1,0:T(8,128)S(1)} %get-tuple-element.12), channel_id=1, source_target_pairs={{0,28},{4,0},{8,4},{12,8},{16,12},{20,16},{24,20},{28,24},{1,29},{... | collective-permute-start | bytes 24584 | tf_op jit(solution)/shard_map/ppermute | solution.py:256
  17.4 1.9 %collective-permute-done.2.cross = f32[16,128]{1,0:T(8,128)S(1)} collective-permute-done((f32[16,128]{1,0:T(8,128)S(1)}, f32[16,128]{1,0:T(8,128)S(1)}, u32[]{:S(2)}, u32[]{:S(2)}) %collective-permute-start.2) | collective-permute-done | bytes 8224 | tf_op jit(solution)/shard_map/ppermute | solution.py:256
  19.3 0.3 shard_map.70
  19.6 1.3 %collective-permute-start.3 = (f32[4,24,1536]{2,1,0:T(8,128)S(1)}, f32[4,24,1536]{2,1,0:T(8,128)S(1)}, u32[]{:S(2)}, u32[]{:S(2)}) collective-permute-start(f32[4,24,1536]{2,1,0:T(8,128)S(1)} %shard_map.70), channel_id=1, source_target_pairs={{0,1},{2,3},{4,5},{6,7},{8,9},{10,11},{12,13},{14,15},{16,17},{18,... | collective-permute-start | bytes 1769480 | tf_op jit(solution)/shard_map/ppermute | solution.py:220
  20.9 1.6 %collective-permute-done.3 = f32[4,24,1536]{2,1,0:T(8,128)S(1)} collective-permute-done((f32[4,24,1536]{2,1,0:T(8,128)S(1)}, f32[4,24,1536]{2,1,0:T(8,128)S(1)}, u32[]{:S(2)}, u32[]{:S(2)}) %collective-permute-start.3) | collective-permute-done | bytes 589856 | tf_op jit(solution)/shard_map/ppermute | solution.py:220
  22.5 0.1 fusion.4
  22.6 0.7 %collective-permute-start.4 = (bf16[24,1536]{1,0:T(8,128)(2,1)S(1)}, bf16[24,1536]{1,0:T(8,128)(2,1)S(1)}, u32[]{:S(2)}, u32[]{:S(2)}) collective-permute-start(bf16[24,1536]{1,0:T(8,128)(2,1)S(1)} %get-tuple-element.16), channel_id=1, source_target_pairs={{1,5},{3,7},{5,1},{7,3},{9,13},{11,15},{13,9},{15,11},{17,21},{19,... | collective-permute-start | bytes 221192 | tf_op jit(solution)/shard_map/ppermute | solution.py:204
  23.3 0.7 %collective-permute-start.5 = (bf16[24,1536]{1,0:T(8,128)(2,1)S(1)}, bf16[24,1536]{1,0:T(8,128)(2,1)S(1)}, u32[]{:S(2)}, u32[]{:S(2)}) collective-permute-start(bf16[24,1536]{1,0:T(8,128)(2,1)S(1)} %get-tuple-element.18), channel_id=1, source_target_pairs={{1,3},{3,1},{5,7},{7,5},{9,11},{11,9},{13,15},{15,13},{17,19},{19,... | collective-permute-start | bytes 221192 | tf_op jit(solution)/shard_map/ppermute | solution.py:204
  24.0 0.7 %collective-permute-start.6 = (bf16[24,1536]{1,0:T(8,128)(2,1)S(1)}, bf16[24,1536]{1,0:T(8,128)(2,1)S(1)}, u32[]{:S(2)}, u32[]{:S(2)}) collective-permute-start(bf16[24,1536]{1,0:T(8,128)(2,1)S(1)} %get-tuple-element.17), channel_id=1, source_target_pairs={{1,7},{3,5},{5,3},{7,1},{9,15},{11,13},{13,11},{15,9},{17,23},{19,... | collective-permute-start | bytes 221192 | tf_op jit(solution)/shard_map/ppermute | solution.py:204
  24.6 0.0 collective-permute-done.4
  24.7 0.7 %collective-permute-start.7 = (f32[24,1536]{1,0:T(8,128)S(1)}, f32[24,1536]{1,0:T(8,128)S(1)}, u32[]{:S(2)}, u32[]{:S(2)}) collective-permute-start(f32[24,1536]{1,0:T(8,128)S(1)} %fusion.3), channel_id=1, source_target_pairs={{1,9},{3,11},{5,13},{7,15},{25,17},{27,19},{29,21},{31,23}} | collective-permute-start | bytes 442376 | tf_op jit(solution)/shard_map/ppermute | solution.py:214
  25.4 0.0 collective-permute-done.7
  25.4 0.7 %collective-permute-start.8 = (f32[24,1536]{1,0:T(8,128)S(1)}, f32[24,1536]{1,0:T(8,128)S(1)}, u32[]{:S(2)}, u32[]{:S(2)}) collective-permute-start(f32[24,1536]{1,0:T(8,128)S(1)} %add.28), channel_id=1, source_target_pairs={{9,17},{11,19},{13,21},{15,23},{17,9},{19,11},{21,13},{23,15}} | collective-permute-start | bytes 442376 | tf_op jit(solution)/shard_map/ppermute | solution.py:214
  26.1 0.0 collective-permute-done.8
  26.1 0.7 %collective-permute-start.9 = (bf16[24,1536]{1,0:T(8,128)(2,1)S(1)}, bf16[24,1536]{1,0:T(8,128)(2,1)S(1)}, u32[]{:S(2)}, u32[]{:S(2)}) collective-permute-start(bf16[24,1536]{1,0:T(8,128)(2,1)S(1)} %add_convert_fusion), channel_id=1, source_target_pairs={{9,1},{11,3},{13,5},{15,7},{17,25},{19,27},{21,29},{23,31}} | collective-permute-start | bytes 221192 | tf_op jit(solution)/shard_map/ppermute | solution.py:214
  26.9 0.7 %collective-permute-start.11 = (bf16[24,1536]{1,0:T(8,128)(2,1)S(1)}, bf16[24,1536]{1,0:T(8,128)(2,1)S(1)}, u32[]{:S(2)}, u32[]{:S(2)}) collective-permute-start(bf16[24,1536]{1,0:T(8,128)(2,1)S(1)} %broadcast_select_fusion), channel_id=1, source_target_pairs={{1,3},{3,1},{5,7},{7,5},{9,11},{11,9},{13,15},{15,13},{17,19},{19,... | collective-permute-start | bytes 221192 | tf_op jit(solution)/shard_map/ppermute | solution.py:204
  27.6 0.7 %collective-permute-start.12 = (bf16[24,1536]{1,0:T(8,128)(2,1)S(1)}, bf16[24,1536]{1,0:T(8,128)(2,1)S(1)}, u32[]{:S(2)}, u32[]{:S(2)}) collective-permute-start(bf16[24,1536]{1,0:T(8,128)(2,1)S(1)} %broadcast_select_fusion), channel_id=1, source_target_pairs={{1,7},{3,5},{5,3},{7,1},{9,15},{11,13},{13,11},{15,9},{17,23},{19,... | collective-permute-start | bytes 221192 | tf_op jit(solution)/shard_map/ppermute | solution.py:204
  28.2 0.7 %collective-permute-start.10 = (bf16[24,1536]{1,0:T(8,128)(2,1)S(1)}, bf16[24,1536]{1,0:T(8,128)(2,1)S(1)}, u32[]{:S(2)}, u32[]{:S(2)}) collective-permute-start(bf16[24,1536]{1,0:T(8,128)(2,1)S(1)} %broadcast_select_fusion), channel_id=1, source_target_pairs={{1,5},{3,7},{5,1},{7,3},{9,13},{11,15},{13,9},{15,11},{17,21},{19,... | collective-permute-start | bytes 221192 | tf_op jit(solution)/shard_map/ppermute | solution.py:204
  28.9 0.0 collective-permute-done.11
  29.0 1.3 %collective-permute-start.13 = (bf16[4,24,1536]{2,1,0:T(8,128)(2,1)S(1)}, bf16[4,24,1536]{2,1,0:T(8,128)(2,1)S(1)}, u32[]{:S(2)}, u32[]{:S(2)}) collective-permute-start(bf16[4,24,1536]{2,1,0:T(8,128)(2,1)S(1)} %pad_maximum_fusion.mine), channel_id=1, source_target_pairs={{1,0},{3,2},{5,4},{7,6},{9,8},{11,10},{13,12},{15,14},{17,16},{19,... | collective-permute-start | bytes 884744 | tf_op jit(solution)/shard_map/ppermute | solution.py:233
  30.3 32.7 %collective-permute-done.13.other = bf16[4,24,1536]{2,1,0:T(8,128)(2,1)S(1)} collective-permute-done((bf16[4,24,1536]{2,1,0:T(8,128)(2,1)S(1)}, bf16[4,24,1536]{2,1,0:T(8,128)(2,1)S(1)}, u32[]{:S(2)}, u32[]{:S(2)}) %collective-permute-start.13) | collective-permute-done | bytes 294944 | tf_op jit(solution)/shard_map/ppermute | solution.py:233
  63.0 0.9 %shard_map.71 = (f32[3,8,4096]{2,1,0:T(8,128)}, f32[3,8,2048]{2,1,0:T(8,128)}) custom-call(bf16[4,24,1536]{2,1,0:T(8,128)(2,1)S(1)} %pad_maximum_fusion.mine, bf16[4,24,1536]{2,1,0:T(8,128)(2,1)S(1)} %collective-permute-done.13.other), custom_call_target="tpu_custom_call" | custom-call | flops 1000000000 | bytes 1000000 | tf_op jit(solution)/shard_map/pallas_call | solution.py:193
  (22 shorter events, 0.2 us)
Async XLA Ops:
  0.6 4.1 %copy-start = (bf16[3,8,4096]{2,1,0:T(8,128)(2,1)S(1)}, bf16[3,8,4096]{2,1,0:T(8,128)(2,1)}, u32[]{:S(2)}) copy-start(bf16[3,8,4096]{2,1,0:T(8,128)(2,1)} %param.8) | copy-start | bytes 589828
  0.6 7.4 %copy-start.2 = (bf16[3,1,128,2048]{3,2,1,0:T(8,128)(2,1)S(1)}, bf16[3,1,128,2048]{3,2,1,0:T(8,128)(2,1)}, u32[]{:S(2)}) copy-start(bf16[3,1,128,2048]{3,2,1,0:T(8,128)(2,1)} %frozen.1) | copy-start | bytes 4718596
  0.7 7.4 %copy-start.5 = (bf16[3,8,2048]{2,1,0:T(8,128)(2,1)S(1)}, bf16[3,8,2048]{2,1,0:T(8,128)(2,1)}, u32[]{:S(2)}) copy-start(bf16[3,8,2048]{2,1,0:T(8,128)(2,1)} %up.3) | copy-start | bytes 294916
  1.8 12.4 %collective-permute-start = (bf16[2,64,1024]{2,1,0:T(8,128)(2,1)S(1)}, bf16[2,64,1024]{2,1,0:T(8,128)(2,1)S(1)}, u32[]{:S(2)}, u32[]{:S(2)}) collective-permute-start(bf16[2,64,1024]{2,1,0:T(8,128)(2,1)S(1)} %slice_bitcast_fusion), channel_id=1, source_target_pairs={{0,4},{4,8},{8,12},{12,16},{16,20},{20,24},{24,28},{28,0},{1,5},{5... | collective-permute-start | bytes 786440 | tf_op jit(solution)/shard_map/ppermute | solution.py:242
  6.5 7.7 %collective-permute-start.1 = (bf16[2,8,64]{2,1,0:T(8,128)(2,1)S(1)}, bf16[2,8,64]{2,1,0:T(8,128)(2,1)S(1)}, u32[]{:S(2)}, u32[]{:S(2)}) collective-permute-start(bf16[2,8,64]{2,1,0:T(8,128)(2,1)S(1)} %slice.28), channel_id=1, source_target_pairs={{0,4},{4,8},{8,12},{12,16},{16,20},{20,24},{24,28},{28,0},{1,5},{5... | collective-permute-start | bytes 6152 | tf_op jit(solution)/shard_map/ppermute | solution.py:244
  8.0 1.0 %copy-start.3 = (bf16[1,128,2048]{2,1,0:T(8,128)(2,1)S(1)}, bf16[1,128,2048]{2,1,0:T(8,128)(2,1)}, u32[]{:S(2)}) copy-start(bf16[1,128,2048]{2,1,0:T(8,128)(2,1)} %grad.3) | copy-start | bytes 1572868
  9.1 5.1 %copy-start.4 = (bf16[1,128,2048]{2,1,0:T(8,128)(2,1)S(1)}, bf16[1,128,2048]{2,1,0:T(8,128)(2,1)}, u32[]{:S(2)}) copy-start(bf16[1,128,2048]{2,1,0:T(8,128)(2,1)} %grad.3) | copy-start | bytes 1572868
  14.2 5.1 %copy-start.1 = (bf16[1,128,4096]{2,1,0:T(8,128)(2,1)S(1)}, bf16[1,128,4096]{2,1,0:T(8,128)(2,1)}, u32[]{:S(2)}) copy-start(bf16[1,128,4096]{2,1,0:T(8,128)(2,1)} %tokens.1) | copy-start | bytes 3145732
  15.6 3.7 %collective-permute-start.2 = (f32[16,128]{1,0:T(8,128)S(1)}, f32[16,128]{1,0:T(8,128)S(1)}, u32[]{:S(2)}, u32[]{:S(2)}) collective-permute-start(f32[16,128]{1,0:T(8,128)S(1)} %get-tuple-element.12), channel_id=1, source_target_pairs={{0,28},{4,0},{8,4},{12,8},{16,12},{20,16},{24,20},{28,24},{1,29},{... | collective-permute-start | bytes 24584 | tf_op jit(solution)/shard_map/ppermute | solution.py:256
  19.6 2.9 %collective-permute-start.3 = (f32[4,24,1536]{2,1,0:T(8,128)S(1)}, f32[4,24,1536]{2,1,0:T(8,128)S(1)}, u32[]{:S(2)}, u32[]{:S(2)}) collective-permute-start(f32[4,24,1536]{2,1,0:T(8,128)S(1)} %shard_map.70), channel_id=1, source_target_pairs={{0,1},{2,3},{4,5},{6,7},{8,9},{10,11},{12,13},{14,15},{16,17},{18,... | collective-permute-start | bytes 1769480 | tf_op jit(solution)/shard_map/ppermute | solution.py:220
  22.6 2.0 %collective-permute-start.4 = (bf16[24,1536]{1,0:T(8,128)(2,1)S(1)}, bf16[24,1536]{1,0:T(8,128)(2,1)S(1)}, u32[]{:S(2)}, u32[]{:S(2)}) collective-permute-start(bf16[24,1536]{1,0:T(8,128)(2,1)S(1)} %get-tuple-element.16), channel_id=1, source_target_pairs={{1,5},{3,7},{5,1},{7,3},{9,13},{11,15},{13,9},{15,11},{17,21},{19,... | collective-permute-start | bytes 221192 | tf_op jit(solution)/shard_map/ppermute | solution.py:204
  23.3 1.4 %collective-permute-start.5 = (bf16[24,1536]{1,0:T(8,128)(2,1)S(1)}, bf16[24,1536]{1,0:T(8,128)(2,1)S(1)}, u32[]{:S(2)}, u32[]{:S(2)}) collective-permute-start(bf16[24,1536]{1,0:T(8,128)(2,1)S(1)} %get-tuple-element.18), channel_id=1, source_target_pairs={{1,3},{3,1},{5,7},{7,5},{9,11},{11,9},{13,15},{15,13},{17,19},{19,... | collective-permute-start | bytes 221192 | tf_op jit(solution)/shard_map/ppermute | solution.py:204
  24.0 0.7 %collective-permute-start.6 = (bf16[24,1536]{1,0:T(8,128)(2,1)S(1)}, bf16[24,1536]{1,0:T(8,128)(2,1)S(1)}, u32[]{:S(2)}, u32[]{:S(2)}) collective-permute-start(bf16[24,1536]{1,0:T(8,128)(2,1)S(1)} %get-tuple-element.17), channel_id=1, source_target_pairs={{1,7},{3,5},{5,3},{7,1},{9,15},{11,13},{13,11},{15,9},{17,23},{19,... | collective-permute-start | bytes 221192 | tf_op jit(solution)/shard_map/ppermute | solution.py:204
  24.7 0.7 %collective-permute-start.7 = (f32[24,1536]{1,0:T(8,128)S(1)}, f32[24,1536]{1,0:T(8,128)S(1)}, u32[]{:S(2)}, u32[]{:S(2)}) collective-permute-start(f32[24,1536]{1,0:T(8,128)S(1)} %fusion.3), channel_id=1, source_target_pairs={{1,9},{3,11},{5,13},{7,15},{25,17},{27,19},{29,21},{31,23}} | collective-permute-start | bytes 442376 | tf_op jit(solution)/shard_map/ppermute | solution.py:214
  25.4 0.7 %collective-permute-start.8 = (f32[24,1536]{1,0:T(8,128)S(1)}, f32[24,1536]{1,0:T(8,128)S(1)}, u32[]{:S(2)}, u32[]{:S(2)}) collective-permute-start(f32[24,1536]{1,0:T(8,128)S(1)} %add.28), channel_id=1, source_target_pairs={{9,17},{11,19},{13,21},{15,23},{17,9},{19,11},{21,13},{23,15}} | collective-permute-start | bytes 442376 | tf_op jit(solution)/shard_map/ppermute | solution.py:214
  26.1 0.7 %collective-permute-start.9 = (bf16[24,1536]{1,0:T(8,128)(2,1)S(1)}, bf16[24,1536]{1,0:T(8,128)(2,1)S(1)}, u32[]{:S(2)}, u32[]{:S(2)}) collective-permute-start(bf16[24,1536]{1,0:T(8,128)(2,1)S(1)} %add_convert_fusion), channel_id=1, source_target_pairs={{9,1},{11,3},{13,5},{15,7},{17,25},{19,27},{21,29},{23,31}} | collective-permute-start | bytes 221192 | tf_op jit(solution)/shard_map/ppermute | solution.py:214
  26.9 2.0 %collective-permute-start.11 = (bf16[24,1536]{1,0:T(8,128)(2,1)S(1)}, bf16[24,1536]{1,0:T(8,128)(2,1)S(1)}, u32[]{:S(2)}, u32[]{:S(2)}) collective-permute-start(bf16[24,1536]{1,0:T(8,128)(2,1)S(1)} %broadcast_select_fusion), channel_id=1, source_target_pairs={{1,3},{3,1},{5,7},{7,5},{9,11},{11,9},{13,15},{15,13},{17,19},{19,... | collective-permute-start | bytes 221192 | tf_op jit(solution)/shard_map/ppermute | solution.py:204
  27.6 1.4 %collective-permute-start.12 = (bf16[24,1536]{1,0:T(8,128)(2,1)S(1)}, bf16[24,1536]{1,0:T(8,128)(2,1)S(1)}, u32[]{:S(2)}, u32[]{:S(2)}) collective-permute-start(bf16[24,1536]{1,0:T(8,128)(2,1)S(1)} %broadcast_select_fusion), channel_id=1, source_target_pairs={{1,7},{3,5},{5,3},{7,1},{9,15},{11,13},{13,11},{15,9},{17,23},{19,... | collective-permute-start | bytes 221192 | tf_op jit(solution)/shard_map/ppermute | solution.py:204
  28.2 0.7 %collective-permute-start.10 = (bf16[24,1536]{1,0:T(8,128)(2,1)S(1)}, bf16[24,1536]{1,0:T(8,128)(2,1)S(1)}, u32[]{:S(2)}, u32[]{:S(2)}) collective-permute-start(bf16[24,1536]{1,0:T(8,128)(2,1)S(1)} %broadcast_select_fusion), channel_id=1, source_target_pairs={{1,5},{3,7},{5,1},{7,3},{9,13},{11,15},{13,9},{15,11},{17,21},{19,... | collective-permute-start | bytes 221192 | tf_op jit(solution)/shard_map/ppermute | solution.py:204
  29.0 34.0 %collective-permute-start.13 = (bf16[4,24,1536]{2,1,0:T(8,128)(2,1)S(1)}, bf16[4,24,1536]{2,1,0:T(8,128)(2,1)S(1)}, u32[]{:S(2)}, u32[]{:S(2)}) collective-permute-start(bf16[4,24,1536]{2,1,0:T(8,128)(2,1)S(1)} %pad_maximum_fusion.mine), channel_id=1, source_target_pairs={{1,0},{3,2},{5,4},{7,6},{9,8},{11,10},{13,12},{15,14},{17,16},{19,... | collective-permute-start | bytes 884744 | tf_op jit(solution)/shard_map/ppermute | solution.py:233

commit v4 on v2

--- a/solution.py
+++ b/solution.py
@@ -156,44 +156,67 @@
 
 
 def position():
-    dp = lax.axis_index("dp")
-    return dp & 1, (dp & 2) | (lax.axis_index("seq") & 1)
+    seq, dp = lax.axis_index("seq"), lax.axis_index("dp")
+    bits = seq ^ dp
+    for shift in (4, 2, 1):
+        bits = bits ^ (bits >> shift)
+    return bits & 1, (dp & 2) | (seq & 1)
 
 
 def down_kernel(tokens, rank_in, cross, up_in, keep, send):
-    core, place = position()
+    half, quarter = position()
+    first = half == 0
     ranks = rank_in[...] + jnp.concatenate([jnp.zeros((RANK, rank_in.shape[1]), F32), cross[...]], axis=0)
     both = rows(hi_lo(ranks))
     n = ranks.shape[0]
     up_step, down_step = up_in.shape[1] // 8, tokens.shape[2] // 8
-    for c in range(8):
-        d = nn(both, tokens[0, :, c * down_step : (c + 1) * down_step])
+    for c in range(4):
+        d = nn(both, tokens[0, :, 2 * c * down_step : 2 * (c + 1) * down_step])
         d = ADAPTER_SCALE * (d[:n] + d[n:])
-        u = ADAPTER_SCALE * up_in[:, c * up_step : (c + 1) * up_step]
-        slot = place ^ (c >> 1)
-
-        def put(ref):
-            ref[slot, :, :up_step] = u
-            ref[slot, :, up_step:] = d
-
-        pl.when(core == (c & 1))(lambda: put(keep))
-        pl.when(core != (c & 1))(lambda: put(send))
+        u = ADAPTER_SCALE * up_in[:, 2 * c * up_step : 2 * (c + 1) * up_step]
+        slot = quarter ^ c
+        keep[slot, :, :up_step] = jnp.where(first, u[:, :up_step], u[:, up_step:])
+        send[slot, :, :up_step] = jnp.where(first, u[:, up_step:], u[:, :up_step])
+        keep[slot, :, up_step:] = jnp.where(first, d[:, :down_step], d[:, down_step:])
+        send[slot, :, up_step:] = jnp.where(first, d[:, down_step:], d[:, :down_step])
 
 
 def spread_kernel(mine, other, down_out, up_out):
-    core, place = position()
+    half, quarter = position()
     up_step, down_step = up_out.shape[2] // 8, down_out.shape[2] // 8
-    for c in range(8):
-        slot = place ^ (c >> 1)
-
-        def put(ref):
-            x = ref[slot].astype(F32)
-            for j in range(3):
-                up_out[j, :, c * up_step : (c + 1) * up_step] = x[8 * j : 8 * j + 8, :up_step]
-                down_out[j, :, c * down_step : (c + 1) * down_step] = x[8 * j : 8 * j + 8, up_step:]
-
-        pl.when(core == (c & 1))(lambda: put(mine))
-        pl.when(core != (c & 1))(lambda: put(other))
+    for c in range(4):
+        slot = quarter ^ c
+        a, b = mine[slot].astype(F32), other[slot].astype(F32)
+        for h in range(2):
+            x = jnp.where(half == h, a, b)
+            at = 2 * c + h
+            for j in range(3):
+                part = x[8 * j : 8 * j + 8]
+                up_out[j, :, at * up_step : (at + 1) * up_step] = part[:, :up_step]
+                down_out[j, :, at * down_step : (at + 1) * down_step] = part[:, up_step:]
+
+
+def cut_kernel(frozen, out, sems):
+    half, half_width = out.shape[1:]
+    copies = [
+        pltpu.make_async_copy(frozen.at[j + 1, 0, pl.ds(half, half), pl.ds(half_width, half_width)], out.at[j], sems.at[j])
+        for j in range(2)
+    ]
+    for copy in copies:
+        copy.start()
+    for copy in copies:
+        copy.wait()
+
+
+def cut(frozen):
+    half, half_width = frozen.shape[2] // 2, frozen.shape[3] // 2
+    return pl.pallas_call(
+        cut_kernel,
+        out_shape=jax.ShapeDtypeStruct((2, half, half_width), BF),
+        in_specs=[pl.BlockSpec(memory_space=pl.ANY)],
+        out_specs=VMEM,
+        scratch_shapes=[pltpu.SemaphoreType.DMA((2,))],
+    )(frozen)
 
 
 def call(kernel, outs, *args):
@@ -213,16 +236,16 @@
 
 def total_sum(keep, send, seqs, dps):
     total = seqs * dps
+    partner = {1: dps | 1, 2: 3, 3: dps | 2}
     keep = keep + swap(send, 1, total)
-    own = keep[0]
-    got = [swap(keep[s].astype(BF), (s & 2) | (dps if s & 1 else 0), total) for s in (1, 2, 3)]
-    own = own + got[0].astype(F32) + got[1].astype(F32) + got[2].astype(F32)
+    got = [swap(keep[s].astype(BF), partner[s], total).astype(F32) for s in (1, 2, 3)]
+    own = keep[0] + got[0] + got[1] + got[2]
     bit = 2
     while bit < seqs:
-        own = own + swap(own, bit * dps, total)
+        own = own + swap(own, bit * dps | 1, total)
         bit *= 2
     piece = own.astype(BF)
-    mine = jnp.stack([piece] + [swap(piece, (s & 2) | (dps if s & 1 else 0), total) for s in (1, 2, 3)])
+    mine = jnp.stack([piece] + [swap(piece, partner[s], total) for s in (1, 2, 3)])
     return mine, swap(mine, 1, total)
 
 
@@ -232,7 +255,7 @@
     half, half_width = count // 2, width // 2
     forward = [(i, (i + 1) % seqs) for i in range(seqs)]
     backward = [(i, (i - 1) % seqs) for i in range(seqs)]
-    frozen_kv = lax.ppermute(frozen[1:, 0, half:, half_width:], "seq", forward)
+    frozen_kv = lax.ppermute(cut(frozen), "seq", forward)
     low_t = jnp.einsum("psw,gw->psg", down_weight, tokens[0], preferred_element_type=F32).astype(BF)
     low_kv = lax.ppermute(low_t[1:, :, half:], "seq", forward)
     sds = jax.ShapeDtypeStruct

time: 47.9 us -> 48 us (level)
  local copies, waits for them, and re-layouts: 2.27 us -> 0.12 us
  waiting for transfers between devices: 21 us -> 22.7 us
  Pallas kernels: 6.34 us -> 7.25 us
    pallas_call x0 -> x1, Pallas kernels: none -> 1.84 us  [cut(): pl.pallas_call(cut_kernel, out_shape=jax.ShapeDtypeStruct((2, half, half_...]
    ppermute x1, waiting for transfers between devices: 2.26 us -> 3.51 us  [on_device(): low_kv = lax.ppermute(low_t[1:, :, half:], 'seq', forward)]
    squeeze x1 -> x0, local copies, waits for them, and re-layouts: 1.11 us -> none  [on_device(): frozen_kv = lax.ppermute(frozen[1:, 0, half:, half_width:], 'seq', forward)]
    unnamed x12 -> x10, local copies, waits for them, and re-layouts: 1.07 us -> 0.03 us
    pallas_call x4, Pallas kernels: 6.34 us -> 5.41 us  [call(): pl.pallas_call(kernel, out_shape=outs, in_specs=[VMEM] * len(args), out_s...]
where the time goes in v4:
time: 48 us; the launch traced here: 47.8 us
  waiting for transfers between devices  22.7 us (47%)
  starting transfers between devices  15.3 us (32%)
  Pallas kernels  7.25 us (15%)
  matrix products  1.6 us (3%)
  between operations  0.75 us (2%)
    ppermute x10, waiting for transfers between devices, swap(): return lax.ppermute(x, AXES, [(i, i ^ bits) for i in range(total)])  17.3 us
    ppermute x10, starting transfers between devices, swap(): return lax.ppermute(x, AXES, [(i, i ^ bits) for i in range(total)])  8.99 us
    pallas_call x4, Pallas kernels, call(): pl.pallas_call(kernel, out_shape=outs, in_specs=[VMEM] * len(args), out_s...  5.41 us
    ppermute x1, waiting for transfers between devices, on_device(): low_kv = lax.ppermute(low_t[1:, :, half:], 'seq', forward)  3.51 us
    ppermute x1, starting transfers between devices, on_device(): frozen_kv = lax.ppermute(cut(frozen), 'seq', forward)  2.99 us
    ppermute x1, waiting for transfers between devices, on_device(): cross = lax.ppermute(cross, 'seq', backward)  1.93 us
    pallas_call x1, Pallas kernels, cut(): pl.pallas_call(cut_kernel, out_shape=jax.ShapeDtypeStruct((2, half, half_...  1.84 us
    ppermute x1, starting transfers between devices, on_device(): cross = lax.ppermute(cross, 'seq', backward)  1.77 us
  transfers between devices with their start and end apart: 13, of which 11 were waited for; matrix products, arithmetic and copies ran while one was open for 4% of the time, Pallas kernels for 6%

profile of v4, /device:TPU:0, one launch (start us, length us, event | category | flops | bytes accessed | tf_op | source)
XLA Modules:
  0.0 47.8 jit_solution(5274784792933207138)
XLA Ops:
  0.7 1.8 %shard_map.69 = bf16[2,64,1024]{2,1,0:T(8,128)(2,1)} custom-call(bf16[3,1,128,2048]{3,2,1,0:T(8,128)(2,1)} %frozen.3), custom_call_target="tpu_custom_call" | custom-call | tf_op jit(solution)/shard_map/pallas_call | solution.py:213
  2.5 3.0 %collective-permute-start = (bf16[2,64,1024]{2,1,0:T(8,128)(2,1)}, bf16[2,64,1024]{2,1,0:T(8,128)(2,1)S(1)}, u32[]{:S(2)}, u32[]{:S(2)}) collective-permute-start(bf16[2,64,1024]{2,1,0:T(8,128)(2,1)} %shard_map.69), channel_id=1, source_target_pairs={{0,4},{4,8},{8,12},{12,16},{16,20},{20,24},{24,28},{28,0},{1,5},{5... | collective-permute-start | bytes 786440 | tf_op jit(solution)/shard_map/ppermute | solution.py:258
  5.5 1.6 %convolution_convert_fusion.low_t = bf16[3,8,128]{2,1,0:T(8,128)(2,1)S(1)} fusion(bf16[3,8,4096]{2,1,0:T(8,128)(2,1)S(1)} %copy-done, bf16[1,128,4096]{2,1,0:T(8,128)(2,1)} %tokens.1), kind=kOutput, calls=%fused_computation | convolution fusion | flops 25168896 | bytes 1251328 | tf_op jit(solution)/shard_map/psw,gw->psg/dot_general | solution.py:259
  7.1 0.1 slice.23
  7.2 1.6 %collective-permute-start.1 = (bf16[2,8,64]{2,1,0:T(8,128)(2,1)S(1)}, bf16[2,8,64]{2,1,0:T(8,128)(2,1)S(1)}, u32[]{:S(2)}, u32[]{:S(2)}) collective-permute-start(bf16[2,8,64]{2,1,0:T(8,128)(2,1)S(1)} %slice.23), channel_id=1, source_target_pairs={{0,4},{4,8},{8,12},{12,16},{16,20},{20,24},{24,28},{28,0},{1,5},{5... | collective-permute-start | bytes 6152 | tf_op jit(solution)/shard_map/ppermute | solution.py:260
  8.8 2.9 %shard_map.68 = (bf16[3,64,1024]{2,1,0:T(8,128)(2,1)S(1)}, f32[24,2048]{1,0:T(8,128)S(1)}, f32[24,128]{1,0:T(8,128)S(1)}) custom-call(bf16[3,1,128,2048]{3,2,1,0:T(8,128)(2,1)S(1)} %copy-done.1, bf16[1,128,2048]{2,1,0:T(8,128)(2,1)S(1)} %copy-done.3, bf16[3,8,128]{2,1,0:T(8,128)(2,1)S(1)} %convolution_convert_fusion.low_t, bf16[3,8,2048]{2,1,0:T(8,128)(2,1)S(1)} %copy-done.4), custom_call_target="tpu_custom_call" | custom-call | flops 1000000000 | bytes 1000000 | tf_op jit(solution)/shard_map/pallas_call | solution.py:223
  11.6 3.5 %collective-permute-done.1.low_kv = bf16[2,8,64]{2,1,0:T(8,128)(2,1)S(1)} collective-permute-done((bf16[2,8,64]{2,1,0:T(8,128)(2,1)S(1)}, bf16[2,8,64]{2,1,0:T(8,128)(2,1)S(1)}, u32[]{:S(2)}, u32[]{:S(2)}) %collective-permute-start.1) | collective-permute-done | bytes 2080 | tf_op jit(solution)/shard_map/ppermute | solution.py:260
  15.2 1.4 %shard_map.70 = (f32[24,2048]{1,0:T(8,128)S(1)}, f32[24,128]{1,0:T(8,128)S(1)}, f32[16,128]{1,0:T(8,128)S(1)}) custom-call(bf16[3,64,1024]{2,1,0:T(8,128)(2,1)S(1)} %get-tuple-element.10.own, bf16[2,64,1024]{2,1,0:T(8,128)(2,1)S(1)} %collective-permute-done.frozen_kv, bf16[2,8,64]{2,1,0:T(8,128)(2,1)S(1)} %collective-permute-done.1.low_kv, ...), custom_call_target="tpu_custom_call" | custom-call | flops 1000000000 | bytes 1000000 | tf_op jit(solution)/shard_map/pallas_call | solution.py:223
  16.6 1.8 %collective-permute-start.2 = (f32[16,128]{1,0:T(8,128)S(1)}, f32[16,128]{1,0:T(8,128)S(1)}, u32[]{:S(2)}, u32[]{:S(2)}) collective-permute-start(f32[16,128]{1,0:T(8,128)S(1)} %get-tuple-element.14), channel_id=1, source_target_pairs={{0,28},{4,0},{8,4},{12,8},{16,12},{20,16},{24,20},{28,24},{1,29},{... | collective-permute-start | bytes 24584 | tf_op jit(solution)/shard_map/ppermute | solution.py:272
  18.3 1.9 %collective-permute-done.2.cross = f32[16,128]{1,0:T(8,128)S(1)} collective-permute-done((f32[16,128]{1,0:T(8,128)S(1)}, f32[16,128]{1,0:T(8,128)S(1)}, u32[]{:S(2)}, u32[]{:S(2)}) %collective-permute-start.2) | collective-permute-done | bytes 8224 | tf_op jit(solution)/shard_map/ppermute | solution.py:272
  20.3 0.3 shard_map.71
  20.6 0.1 collective-permute-start.3
  20.7 1.6 %collective-permute-done.3 = f32[4,24,768]{2,1,0:T(8,128)S(1)} collective-permute-done((f32[4,24,768]{2,1,0:T(8,128)S(1)}, f32[4,24,768]{2,1,0:T(8,128)S(1)}, u32[]{:S(2)}, u32[]{:S(2)}) %collective-permute-start.3) | collective-permute-done | bytes 294944 | tf_op jit(solution)/shard_map/ppermute | solution.py:234
  22.2 0.1 fusion.4
  22.3 0.1 collective-permute-start.4
  22.4 2.7 %collective-permute-start.6 = (bf16[24,768]{1,0:T(8,128)(2,1)S(1)}, bf16[24,768]{1,0:T(8,128)(2,1)S(1)}, u32[]{:S(2)}, u32[]{:S(2)}) collective-permute-start(bf16[24,768]{1,0:T(8,128)(2,1)S(1)} %get-tuple-element.21), channel_id=1, source_target_pairs={{0,6},{1,7},{2,4},{3,5},{4,2},{5,3},{6,0},{7,1},{8,14},{9,15},{10,... | collective-permute-start | bytes 110600 | tf_op jit(solution)/shard_map/ppermute | solution.py:234
  25.1 0.2 collective-permute-start.5
  25.3 0.5 %collective-permute-done.4 = bf16[24,768]{1,0:T(8,128)(2,1)S(1)} collective-permute-done((bf16[24,768]{1,0:T(8,128)(2,1)S(1)}, bf16[24,768]{1,0:T(8,128)(2,1)S(1)}, u32[]{:S(2)}, u32[]{:S(2)}) %collective-permute-start.4) | collective-permute-done | bytes 36896 | tf_op jit(solution)/shard_map/ppermute | solution.py:234
  25.8 2.1 %collective-permute-done.6 = bf16[24,768]{1,0:T(8,128)(2,1)S(1)} collective-permute-done((bf16[24,768]{1,0:T(8,128)(2,1)S(1)}, bf16[24,768]{1,0:T(8,128)(2,1)S(1)}, u32[]{:S(2)}, u32[]{:S(2)}) %collective-permute-start.6) | collective-permute-done | bytes 36896 | tf_op jit(solution)/shard_map/ppermute | solution.py:234
  27.9 0.7 %collective-permute-done.5 = bf16[24,768]{1,0:T(8,128)(2,1)S(1)} collective-permute-done((bf16[24,768]{1,0:T(8,128)(2,1)S(1)}, bf16[24,768]{1,0:T(8,128)(2,1)S(1)}, u32[]{:S(2)}, u32[]{:S(2)}) %collective-permute-start.5) | collective-permute-done | bytes 36896 | tf_op jit(solution)/shard_map/ppermute | solution.py:234
  28.6 0.1 collective-permute-start.7
  28.7 4.2 %collective-permute-done.7 = f32[24,768]{1,0:T(8,128)S(1)} collective-permute-done((f32[24,768]{1,0:T(8,128)S(1)}, f32[24,768]{1,0:T(8,128)S(1)}, u32[]{:S(2)}, u32[]{:S(2)}) %collective-permute-start.7) | collective-permute-done | bytes 73760 | tf_op jit(solution)/shard_map/ppermute | solution.py:234
  33.0 2.2 %collective-permute-start.8 = (f32[24,768]{1,0:T(8,128)S(1)}, f32[24,768]{1,0:T(8,128)S(1)}, u32[]{:S(2)}, u32[]{:S(2)}) collective-permute-start(f32[24,768]{1,0:T(8,128)S(1)} %add.22), channel_id=1, source_target_pairs={{0,17},{1,16},{2,19},{3,18},{4,21},{5,20},{6,23},{7,22},{8,25},{9,... | collective-permute-start | bytes 221192 | tf_op jit(solution)/shard_map/ppermute | solution.py:234
  35.2 4.6 %collective-permute-done.8 = f32[24,768]{1,0:T(8,128)S(1)} collective-permute-done((f32[24,768]{1,0:T(8,128)S(1)}, f32[24,768]{1,0:T(8,128)S(1)}, u32[]{:S(2)}, u32[]{:S(2)}) %collective-permute-start.8) | collective-permute-done | bytes 73760 | tf_op jit(solution)/shard_map/ppermute | solution.py:234
  39.8 1.7 %collective-permute-start.11 = (bf16[24,768]{1,0:T(8,128)(2,1)S(1)}, bf16[24,768]{1,0:T(8,128)(2,1)S(1)}, u32[]{:S(2)}, u32[]{:S(2)}) collective-permute-start(bf16[24,768]{1,0:T(8,128)(2,1)S(1)} %add_convert_fusion), channel_id=1, source_target_pairs={{0,6},{1,7},{2,4},{3,5},{4,2},{5,3},{6,0},{7,1},{8,14},{9,15},{10,... | collective-permute-start | bytes 110600 | tf_op jit(solution)/shard_map/ppermute | solution.py:234
  41.5 0.2 collective-permute-start.10
  41.7 1.4 %collective-permute-start.9 = (bf16[24,768]{1,0:T(8,128)(2,1)S(1)}, bf16[24,768]{1,0:T(8,128)(2,1)S(1)}, u32[]{:S(2)}, u32[]{:S(2)}) collective-permute-start(bf16[24,768]{1,0:T(8,128)(2,1)S(1)} %add_convert_fusion), channel_id=1, source_target_pairs={{0,5},{1,4},{2,7},{3,6},{4,1},{5,0},{6,3},{7,2},{8,13},{9,12},{10,... | collective-permute-start | bytes 110600 | tf_op jit(solution)/shard_map/ppermute | solution.py:234
  43.1 1.7 %collective-permute-done.11 = bf16[24,768]{1,0:T(8,128)(2,1)S(1)} collective-permute-done((bf16[24,768]{1,0:T(8,128)(2,1)S(1)}, bf16[24,768]{1,0:T(8,128)(2,1)S(1)}, u32[]{:S(2)}, u32[]{:S(2)}) %collective-permute-start.11) | collective-permute-done | bytes 36896 | tf_op jit(solution)/shard_map/ppermute | solution.py:234
  44.8 0.8 %collective-permute-done.10 = bf16[24,768]{1,0:T(8,128)(2,1)S(1)} collective-permute-done((bf16[24,768]{1,0:T(8,128)(2,1)S(1)}, bf16[24,768]{1,0:T(8,128)(2,1)S(1)}, u32[]{:S(2)}, u32[]{:S(2)}) %collective-permute-start.10) | collective-permute-done | bytes 36896 | tf_op jit(solution)/shard_map/ppermute | solution.py:234
  45.5 0.3 collective-permute-start.12
  45.9 1.1 %collective-permute-done.12.other = bf16[4,24,768]{2,1,0:T(8,128)(2,1)S(1)} collective-permute-done((bf16[4,24,768]{2,1,0:T(8,128)(2,1)S(1)}, bf16[4,24,768]{2,1,0:T(8,128)(2,1)S(1)}, u32[]{:S(2)}, u32[]{:S(2)}) %collective-permute-start.12) | collective-permute-done | bytes 147488 | tf_op jit(solution)/shard_map/ppermute | solution.py:234
  47.0 0.9 %shard_map.72 = (f32[3,8,4096]{2,1,0:T(8,128)}, f32[3,8,2048]{2,1,0:T(8,128)}) custom-call(bf16[4,24,768]{2,1,0:T(8,128)(2,1)S(1)} %pad_maximum_fusion.mine, bf16[4,24,768]{2,1,0:T(8,128)(2,1)S(1)} %collective-permute-done.12.other), custom_call_target="tpu_custom_call" | custom-call | flops 1000000000 | bytes 1000000 | tf_op jit(solution)/shard_map/pallas_call | solution.py:223
  (17 shorter events, 0.1 us)
Async XLA Ops:
  0.6 4.9 %copy-start = (bf16[3,8,4096]{2,1,0:T(8,128)(2,1)S(1)}, bf16[3,8,4096]{2,1,0:T(8,128)(2,1)}, u32[]{:S(2)}) copy-start(bf16[3,8,4096]{2,1,0:T(8,128)(2,1)} %param.8) | copy-start | bytes 589828
  0.6 8.1 %copy-start.1 = (bf16[3,1,128,2048]{3,2,1,0:T(8,128)(2,1)S(1)}, bf16[3,1,128,2048]{3,2,1,0:T(8,128)(2,1)}, u32[]{:S(2)}) copy-start(bf16[3,1,128,2048]{3,2,1,0:T(8,128)(2,1)} %frozen.3) | copy-start | bytes 4718596
  0.7 8.1 %copy-start.4 = (bf16[3,8,2048]{2,1,0:T(8,128)(2,1)S(1)}, bf16[3,8,2048]{2,1,0:T(8,128)(2,1)}, u32[]{:S(2)}) copy-start(bf16[3,8,2048]{2,1,0:T(8,128)(2,1)} %up.3) | copy-start | bytes 294916
  0.7 8.1 %copy-start.3 = (bf16[1,128,2048]{2,1,0:T(8,128)(2,1)S(1)}, bf16[1,128,2048]{2,1,0:T(8,128)(2,1)}, u32[]{:S(2)}) copy-start(bf16[1,128,2048]{2,1,0:T(8,128)(2,1)} %grad.3) | copy-start | bytes 1572868
  2.5 12.6 %collective-permute-start = (bf16[2,64,1024]{2,1,0:T(8,128)(2,1)}, bf16[2,64,1024]{2,1,0:T(8,128)(2,1)S(1)}, u32[]{:S(2)}, u32[]{:S(2)}) collective-permute-start(bf16[2,64,1024]{2,1,0:T(8,128)(2,1)} %shard_map.69), channel_id=1, source_target_pairs={{0,4},{4,8},{8,12},{12,16},{16,20},{20,24},{24,28},{28,0},{1,5},{5... | collective-permute-start | bytes 786440 | tf_op jit(solution)/shard_map/ppermute | solution.py:258
  7.2 8.0 %collective-permute-start.1 = (bf16[2,8,64]{2,1,0:T(8,128)(2,1)S(1)}, bf16[2,8,64]{2,1,0:T(8,128)(2,1)S(1)}, u32[]{:S(2)}, u32[]{:S(2)}) collective-permute-start(bf16[2,8,64]{2,1,0:T(8,128)(2,1)S(1)} %slice.23), channel_id=1, source_target_pairs={{0,4},{4,8},{8,12},{12,16},{16,20},{20,24},{24,28},{28,0},{1,5},{5... | collective-permute-start | bytes 6152 | tf_op jit(solution)/shard_map/ppermute | solution.py:260
  15.2 5.1 %copy-start.2 = (bf16[1,128,4096]{2,1,0:T(8,128)(2,1)S(1)}, bf16[1,128,4096]{2,1,0:T(8,128)(2,1)}, u32[]{:S(2)}) copy-start(bf16[1,128,4096]{2,1,0:T(8,128)(2,1)} %tokens.1) | copy-start | bytes 3145732
  16.6 3.7 %collective-permute-start.2 = (f32[16,128]{1,0:T(8,128)S(1)}, f32[16,128]{1,0:T(8,128)S(1)}, u32[]{:S(2)}, u32[]{:S(2)}) collective-permute-start(f32[16,128]{1,0:T(8,128)S(1)} %get-tuple-element.14), channel_id=1, source_target_pairs={{0,28},{4,0},{8,4},{12,8},{16,12},{20,16},{24,20},{28,24},{1,29},{... | collective-permute-start | bytes 24584 | tf_op jit(solution)/shard_map/ppermute | solution.py:272
  20.6 1.6 %collective-permute-start.3 = (f32[4,24,768]{2,1,0:T(8,128)S(1)}, f32[4,24,768]{2,1,0:T(8,128)S(1)}, u32[]{:S(2)}, u32[]{:S(2)}) collective-permute-start(f32[4,24,768]{2,1,0:T(8,128)S(1)} %get-tuple-element.17), channel_id=1, source_target_pairs={{0,1},{1,0},{2,3},{3,2},{4,5},{5,4},{6,7},{7,6},{8,9},{9,8},{10,11... | collective-permute-start | bytes 884744 | tf_op jit(solution)/shard_map/ppermute | solution.py:234
  22.3 3.5 %collective-permute-start.4 = (bf16[24,768]{1,0:T(8,128)(2,1)S(1)}, bf16[24,768]{1,0:T(8,128)(2,1)S(1)}, u32[]{:S(2)}, u32[]{:S(2)}) collective-permute-start(bf16[24,768]{1,0:T(8,128)(2,1)S(1)} %get-tuple-element.20), channel_id=1, source_target_pairs={{0,5},{1,4},{2,7},{3,6},{4,1},{5,0},{6,3},{7,2},{8,13},{9,12},{10,... | collective-permute-start | bytes 110600 | tf_op jit(solution)/shard_map/ppermute | solution.py:234
  22.4 5.5 %collective-permute-start.6 = (bf16[24,768]{1,0:T(8,128)(2,1)S(1)}, bf16[24,768]{1,0:T(8,128)(2,1)S(1)}, u32[]{:S(2)}, u32[]{:S(2)}) collective-permute-start(bf16[24,768]{1,0:T(8,128)(2,1)S(1)} %get-tuple-element.21), channel_id=1, source_target_pairs={{0,6},{1,7},{2,4},{3,5},{4,2},{5,3},{6,0},{7,1},{8,14},{9,15},{10,... | collective-permute-start | bytes 110600 | tf_op jit(solution)/shard_map/ppermute | solution.py:234
  25.1 3.5 %collective-permute-start.5 = (bf16[24,768]{1,0:T(8,128)(2,1)S(1)}, bf16[24,768]{1,0:T(8,128)(2,1)S(1)}, u32[]{:S(2)}, u32[]{:S(2)}) collective-permute-start(bf16[24,768]{1,0:T(8,128)(2,1)S(1)} %get-tuple-element.22), channel_id=1, source_target_pairs={{0,3},{1,2},{2,1},{3,0},{4,7},{5,6},{6,5},{7,4},{8,11},{9,10},{10,... | collective-permute-start | bytes 110600 | tf_op jit(solution)/shard_map/ppermute | solution.py:234
  28.6 4.3 %collective-permute-start.7 = (f32[24,768]{1,0:T(8,128)S(1)}, f32[24,768]{1,0:T(8,128)S(1)}, u32[]{:S(2)}, u32[]{:S(2)}) collective-permute-start(f32[24,768]{1,0:T(8,128)S(1)} %fusion.3), channel_id=1, source_target_pairs={{0,9},{1,8},{2,11},{3,10},{4,13},{5,12},{6,15},{7,14},{8,1},{9,0},... | collective-permute-start | bytes 221192 | tf_op jit(solution)/shard_map/ppermute | solution.py:234
  33.0 6.8 %collective-permute-start.8 = (f32[24,768]{1,0:T(8,128)S(1)}, f32[24,768]{1,0:T(8,128)S(1)}, u32[]{:S(2)}, u32[]{:S(2)}) collective-permute-start(f32[24,768]{1,0:T(8,128)S(1)} %add.22), channel_id=1, source_target_pairs={{0,17},{1,16},{2,19},{3,18},{4,21},{5,20},{6,23},{7,22},{8,25},{9,... | collective-permute-start | bytes 221192 | tf_op jit(solution)/shard_map/ppermute | solution.py:234
  39.8 4.9 %collective-permute-start.11 = (bf16[24,768]{1,0:T(8,128)(2,1)S(1)}, bf16[24,768]{1,0:T(8,128)(2,1)S(1)}, u32[]{:S(2)}, u32[]{:S(2)}) collective-permute-start(bf16[24,768]{1,0:T(8,128)(2,1)S(1)} %add_convert_fusion), channel_id=1, source_target_pairs={{0,6},{1,7},{2,4},{3,5},{4,2},{5,3},{6,0},{7,1},{8,14},{9,15},{10,... | collective-permute-start | bytes 110600 | tf_op jit(solution)/shard_map/ppermute | solution.py:234
  41.5 4.0 %collective-permute-start.10 = (bf16[24,768]{1,0:T(8,128)(2,1)S(1)}, bf16[24,768]{1,0:T(8,128)(2,1)S(1)}, u32[]{:S(2)}, u32[]{:S(2)}) collective-permute-start(bf16[24,768]{1,0:T(8,128)(2,1)S(1)} %add_convert_fusion), channel_id=1, source_target_pairs={{0,3},{1,2},{2,1},{3,0},{4,7},{5,6},{6,5},{7,4},{8,11},{9,10},{10,... | collective-permute-start | bytes 110600 | tf_op jit(solution)/shard_map/ppermute | solution.py:234
  41.7 3.8 %collective-permute-start.9 = (bf16[24,768]{1,0:T(8,128)(2,1)S(1)}, bf16[24,768]{1,0:T(8,128)(2,1)S(1)}, u32[]{:S(2)}, u32[]{:S(2)}) collective-permute-start(bf16[24,768]{1,0:T(8,128)(2,1)S(1)} %add_convert_fusion), channel_id=1, source_target_pairs={{0,5},{1,4},{2,7},{3,6},{4,1},{5,0},{6,3},{7,2},{8,13},{9,12},{10,... | collective-permute-start | bytes 110600 | tf_op jit(solution)/shard_map/ppermute | solution.py:234
  45.5 1.4 %collective-permute-start.12 = (bf16[4,24,768]{2,1,0:T(8,128)(2,1)S(1)}, bf16[4,24,768]{2,1,0:T(8,128)(2,1)S(1)}, u32[]{:S(2)}, u32[]{:S(2)}) collective-permute-start(bf16[4,24,768]{2,1,0:T(8,128)(2,1)S(1)} %pad_maximum_fusion.mine), channel_id=1, source_target_pairs={{0,1},{1,0},{2,3},{3,2},{4,5},{5,4},{6,7},{7,6},{8,9},{9,8},{10,11... | collective-permute-start | bytes 442376 | tf_op jit(solution)/shard_map/ppermute | solution.py:234

commit v5 on v4

--- a/solution.py
+++ b/solution.py
@@ -42,10 +42,10 @@
     return (frozen.astype(F32) + ADAPTER_SCALE * tn(low_t, up)).astype(BF)
 
 
-def heads(items, mask):
+def scores(items, mask):
     sts = [nt(k, q) for q, k, v, g, ups, lows in items]
     dps = [nt(v, g) for q, k, v, g, ups, lows in items]
-    bs = [(nt(ups[0], k), nt(ups[1], q), nt(ups[2], g)) for q, k, v, g, ups, lows in items]
+    bs = [(nt(ups[1], q), nt(ups[2], g)) for q, k, v, g, ups, lows in items]
     pbs, dss = [], []
     for st, dp in zip(sts, dps):
         st = jnp.where(mask, st * SCALE, -jnp.inf)
@@ -55,18 +55,31 @@
         row_dot = jnp.sum(pb.astype(F32) * dp, axis=0, keepdims=True)
         pbs.append(pb)
         dss.append((p * (dp - row_dot) * SCALE).astype(BF))
-    by_q = [nn(rows([it[5][1]] + hi_lo(b[0])), ds) for it, b, ds in zip(items, bs, dss)]
-    by_k = [nt(rows([it[5][0]] + hi_lo(b[1])), ds) for it, b, ds in zip(items, bs, dss)]
-    av = [nn(it[5][2].astype(BF), pb) for it, pb in zip(items, pbs)]
-    rv = [nt(rows(hi_lo(b[2])), pb) for b, pb in zip(bs, pbs)]
+    by_k = [nt(rows([it[5][0]] + hi_lo(b[0])), ds) for it, b, ds in zip(items, bs, dss)]
+    by_v = [nt(rows(hi_lo(b[1])), pb) for b, pb in zip(bs, pbs)]
+    return [
+        (pb, ds, bk[:8], bk[8:16] + bk[16:24], r[:8] + r[8:])
+        for pb, ds, bk, r in zip(pbs, dss, by_k, by_v)
+    ]
+
+
+def rest(items, found):
+    bqs = [nt(it[4][0], it[1]) for it in items]
+    by_q = [nn(rows([it[5][1]] + hi_lo(b)), f[1]) for it, b, f in zip(items, bqs, found)]
+    av = [nn(it[5][2].astype(BF), f[0]) for it, f in zip(items, found)]
     out = []
-    for it, bq, bk, a, r in zip(items, by_q, by_k, av, rv):
+    for it, f, bq, a in zip(items, found, by_q, av):
         q, k, v, g = it[:4]
-        us = [nn(rows(hi_lo(bk[:8])), k), nn(rows(hi_lo(bq[:8])), q), nn(rows(hi_lo(a)), g)]
-        grads = [u[:8] + u[8:] for u in us]
-        ranks = [bq[8:16] + bq[16:24], bk[8:16] + bk[16:24], r[:8] + r[8:]]
-        out.append((grads, ranks))
+        us = [nn(rows(hi_lo(f[2])), k), nn(rows(hi_lo(bq[:8])), q), nn(rows(hi_lo(a)), g)]
+        out.append(([u[:8] + u[8:] for u in us], bq[8:16] + bq[16:24]))
     return out
+
+
+def heads(items, mask):
+    found = scores(items, mask)
+    return [
+        (grads, [rank_q, f[3], f[4]]) for f, (grads, rank_q) in zip(found, rest(items, found))
+    ]
 
 
 def causal(keys, queries, offset):
@@ -118,41 +131,87 @@
         )
 
 
-def far_kernel(own, frozen_kv, low_kv, grad, low_t, up, up_in, rank_in, up_out, rank_out, cross_out):
+def far_items(own, near_kv, low_kv, grad, low_t, up, first):
     half = own.shape[1]
-    width = up.shape[2]
-    half_width = width // 2
+    half_width = up.shape[2] // 2
     far_f = [low_t[j].astype(F32)[:, :half] for j in range(3)]
-    near = [low_kv[0], low_kv[1]]
-    low_k = jnp.concatenate([near[0].astype(F32), far_f[1]], axis=1)
-    low_v = jnp.concatenate([near[1].astype(F32), far_f[2]], axis=1)
-    mask = causal(2 * half, half, half)
-    rank_q = jnp.zeros((RANK, half), F32)
-    rank_k = jnp.zeros((RANK, 2 * half), F32)
-    rank_v = jnp.zeros((RANK, 2 * half), F32)
-    up_out[:, :half_width] = up_in[:, :half_width]
-    for first in range(half_width, width, TOGETHER * HEAD_DIM):
-        items, places = [], []
-        for start in range(first, first + TOGETHER * HEAD_DIM, HEAD_DIM):
-            here = slice(start - half_width, start - half_width + HEAD_DIM)
-            cols = slice(start, start + HEAD_DIM)
-            ups = [up[j, :, cols] for j in range(3)]
-            near_k, near_v = [project(frozen_kv[j, :, here], near[j], ups[j + 1]) for j in range(2)]
-            k = jnp.concatenate([near_k, own[1, :, here]], axis=0)
-            v = jnp.concatenate([near_v, own[2, :, here]], axis=0)
-            items.append((own[0, :, here], k, v, grad[0, :half, cols], ups, (far_f[0], low_k, low_v)))
-            places.append(cols)
-        for cols, (grads, parts) in zip(places, heads(items, mask)):
-            for j in range(3):
-                up_out[8 * j : 8 * j + 8, cols] = up_in[8 * j : 8 * j + 8, cols] + grads[j]
-            rank_q, rank_k, rank_v = rank_q + parts[0], rank_k + parts[1], rank_v + parts[2]
-    none = jnp.zeros((RANK, half), F32)
-    for j, part in enumerate([rank_q, rank_k[:, half:], rank_v[:, half:]]):
-        rank_out[8 * j : 8 * j + 8, :] = rank_in[8 * j : 8 * j + 8, :] + jnp.concatenate(
-            [part, none], axis=1
+    lows = [far_f[0]] + [
+        jnp.concatenate([low_kv[j].astype(F32), far_f[j + 1]], axis=1) for j in range(2)
+    ]
+    items = []
+    for h, near in enumerate(near_kv):
+        here = slice(first + h * HEAD_DIM, first + (h + 1) * HEAD_DIM)
+        cols = slice(half_width + here.start, half_width + here.stop)
+        ups = [up[j, :, cols] for j in range(3)]
+        k, v = [jnp.concatenate([near[j], own[j + 1, :, here]], axis=0) for j in range(2)]
+        items.append((own[0, :, here], k, v, grad[0, :half, cols], ups, lows))
+    return items
+
+
+def near_rows(frozen_kv, low_kv, up, first):
+    half_width = up.shape[2] // 2
+    near = []
+    for h in range(frozen_kv.shape[2] // HEAD_DIM):
+        here = slice(h * HEAD_DIM, (h + 1) * HEAD_DIM)
+        start = half_width + first + h * HEAD_DIM
+        near.append(
+            [project(frozen_kv[j, :, here], low_kv[j], up[j + 1, :, start : start + HEAD_DIM]) for j in range(2)]
         )
-    for j, part in enumerate([rank_k[:, :half], rank_v[:, :half]]):
-        cross_out[8 * j : 8 * j + 8, :] = jnp.concatenate([none, part], axis=1)
+    return near
+
+
+def left(x):
+    return jnp.concatenate([x, jnp.zeros_like(x)], axis=1)
+
+
+def right(x):
+    return jnp.concatenate([jnp.zeros_like(x), x], axis=1)
+
+
+def far_first(own, frozen_kv, low_kv, grad, low_t, up, rank_in, up_out, rank_out, cross_out):
+    half = own.shape[1]
+    items = far_items(own, near_rows(frozen_kv, low_kv, up, 0), low_kv, grad, low_t, up, 0)
+    parts = heads(items, causal(2 * half, half, half))
+    for h, (grads, _) in enumerate(parts):
+        for j in range(3):
+            up_out[8 * j : 8 * j + 8, h * HEAD_DIM : (h + 1) * HEAD_DIM] = grads[j]
+    for j in range(3):
+        part = sum(ranks[j] for _, ranks in parts)
+        rank_out[8 * j : 8 * j + 8, :] = rank_in[8 * j : 8 * j + 8, :] + left(part[:, -half:])
+        if j > 0:
+            cross_out[8 * j - 8 : 8 * j, :] = right(part[:, :half])
+
+
+def far_second(
+    own, frozen_kv, low_kv, grad, low_t, up, rank_in, cross_in, rank_out, cross_out, near_out, pb_out, ds_out, aq_out
+):
+    half = own.shape[1]
+    first = own.shape[2] - frozen_kv.shape[2]
+    near = near_rows(frozen_kv, low_kv, up, first)
+    items = far_items(own, near, low_kv, grad, low_t, up, first)
+    found = scores(items, causal(2 * half, half, half))
+    rank_out[:8, :] = rank_in[:8, :]
+    for j in (1, 2):
+        part = sum(f[j + 2] for f in found)
+        rank_out[8 * j : 8 * j + 8, :] = rank_in[8 * j : 8 * j + 8, :] + left(part[:, half:])
+        cross_out[8 * j - 8 : 8 * j, :] = cross_in[8 * j - 8 : 8 * j, :] + right(part[:, :half])
+    for h, f in enumerate(found):
+        near_out[h] = near[h][0]
+        pb_out[h] = f[0]
+        ds_out[h] = f[1]
+        aq_out[8 * h : 8 * h + 8, :] = f[2]
+
+
+def far_rest(own, low_kv, grad, low_t, up, rank_in, near, pb, ds, aq, up_out, rank_out):
+    n = near.shape[0]
+    first = own.shape[2] - n * HEAD_DIM
+    items = far_items(own, [[near[h]] * 2 for h in range(n)], low_kv, grad, low_t, up, first)
+    parts = rest(items, [(pb[h], ds[h], aq[8 * h : 8 * h + 8, :]) for h in range(n)])
+    for h, (grads, _) in enumerate(parts):
+        for j in range(3):
+            up_out[8 * j : 8 * j + 8, h * HEAD_DIM : (h + 1) * HEAD_DIM] = grads[j]
+    rank_out[:8, :] = rank_in[:8, :] + left(sum(rank for _, rank in parts))
+    rank_out[8:, :] = rank_in[8:, :]
 
 
 def position():
@@ -163,7 +222,7 @@
     return bits & 1, (dp & 2) | (seq & 1)
 
 
-def down_kernel(tokens, rank_in, cross, up_in, keep, send):
+def down_kernel(tokens, rank_in, cross, up_in, up_a, up_b, keep, send):
     half, quarter = position()
     first = half == 0
     ranks = rank_in[...] + jnp.concatenate([jnp.zeros((RANK, rank_in.shape[1]), F32), cross[...]], axis=0)
@@ -173,7 +232,8 @@
     for c in range(4):
         d = nn(both, tokens[0, :, 2 * c * down_step : 2 * (c + 1) * down_step])
         d = ADAPTER_SCALE * (d[:n] + d[n:])
-        u = ADAPTER_SCALE * up_in[:, 2 * c * up_step : 2 * (c + 1) * up_step]
+        u = up_in[:, 2 * c * up_step : 2 * (c + 1) * up_step]
+        u = ADAPTER_SCALE * (u + (up_a[...] if c == 2 else up_b[...]) if c >= 2 else u)
         slot = quarter ^ c
         keep[slot, :, :up_step] = jnp.where(first, u[:, :up_step], u[:, up_step:])
         send[slot, :, :up_step] = jnp.where(first, u[:, up_step:], u[:, :up_step])
@@ -196,29 +256,6 @@
                 down_out[j, :, at * down_step : (at + 1) * down_step] = part[:, up_step:]
 
 
-def cut_kernel(frozen, out, sems):
-    half, half_width = out.shape[1:]
-    copies = [
-        pltpu.make_async_copy(frozen.at[j + 1, 0, pl.ds(half, half), pl.ds(half_width, half_width)], out.at[j], sems.at[j])
-        for j in range(2)
-    ]
-    for copy in copies:
-        copy.start()
-    for copy in copies:
-        copy.wait()
-
-
-def cut(frozen):
-    half, half_width = frozen.shape[2] // 2, frozen.shape[3] // 2
-    return pl.pallas_call(
-        cut_kernel,
-        out_shape=jax.ShapeDtypeStruct((2, half, half_width), BF),
-        in_specs=[pl.BlockSpec(memory_space=pl.ANY)],
-        out_specs=VMEM,
-        scratch_shapes=[pltpu.SemaphoreType.DMA((2,))],
-    )(frozen)
-
-
 def call(kernel, outs, *args):
     return pl.pallas_call(
         kernel,
@@ -242,7 +279,9 @@
     own = keep[0] + got[0] + got[1] + got[2]
     bit = 2
     while bit < seqs:
-        own = own + swap(own, bit * dps | 1, total)
+        if 2 * bit >= seqs:
+            own = own.astype(BF)
+        own = own.astype(F32) + swap(own, bit * dps | 1, total).astype(F32)
         bit *= 2
     piece = own.astype(BF)
     mine = jnp.stack([piece] + [swap(piece, partner[s], total) for s in (1, 2, 3)])
@@ -255,24 +294,36 @@
     half, half_width = count // 2, width // 2
     forward = [(i, (i + 1) % seqs) for i in range(seqs)]
     backward = [(i, (i - 1) % seqs) for i in range(seqs)]
-    frozen_kv = lax.ppermute(cut(frozen), "seq", forward)
+    middle = half_width + half_width // 2
+    frozen_kv = [
+        lax.ppermute(frozen[1:, 0, half:, half_width:middle], "seq", forward),
+        lax.ppermute(frozen[1:, 0, half:, middle:], "seq", forward),
+    ]
     low_t = jnp.einsum("psw,gw->psg", down_weight, tokens[0], preferred_element_type=F32).astype(BF)
     low_kv = lax.ppermute(low_t[1:, :, half:], "seq", forward)
     sds = jax.ShapeDtypeStruct
-    own, up_part, rank_part = call(
+    own, up_part, rank = call(
         local_kernel,
         [sds((3, half, half_width), BF), sds((24, width), F32), sds((24, count), F32)],
         frozen, grad, low_t, up_weight,
     )
-    up_part, rank_part, cross = call(
-        far_kernel,
-        [sds((24, width), F32), sds((24, count), F32), sds((16, count), F32)],
-        own, frozen_kv, low_kv, grad, low_t, up_weight, up_part, rank_part,
+    up_side, rank_side, cross_side = sds((24, half_width // 2), F32), sds((24, count), F32), sds((16, count), F32)
+    up_a, rank, cross = call(
+        far_first, [up_side, rank_side, cross_side],
+        own, frozen_kv[0], low_kv, grad, low_t, up_weight, rank,
+    )
+    n = half_width // HEAD_DIM // 2
+    by_keys = sds((n, count, half), BF)
+    rank, cross, *kept = call(
+        far_second,
+        [rank_side, cross_side, sds((n, half, HEAD_DIM), BF), by_keys, by_keys, sds((8 * n, count), F32)],
+        own, frozen_kv[1], low_kv, grad, low_t, up_weight, rank, cross,
     )
     cross = lax.ppermute(cross, "seq", backward)
+    up_b, rank = call(far_rest, [up_side, rank_side], own, low_kv, grad, low_t, up_weight, rank, *kept)
     columns = (width + tokens.shape[2]) // 8
     piece = sds((4, 24, columns), F32)
-    keep, send = call(down_kernel, [piece, piece], tokens, rank_part, cross, up_part)
+    keep, send = call(down_kernel, [piece, piece], tokens, rank, cross, up_part, up_a, up_b)
     mine, other = total_sum(keep, send, seqs, dps)
     return tuple(
         call(spread_kernel, [sds((3, RANK, tokens.shape[2]), F32), sds((3, RANK, width), F32)], mine, other)

time: 48 us -> 46.2 us (0.963)
  waiting for transfers between devices: 22.7 us -> 16 us
  starting transfers between devices: 15.3 us -> 18.6 us
  local copies, waits for them, and re-layouts: 0.12 us -> 2.29 us
  Pallas kernels: 7.25 us -> 6.65 us
    ppermute x1, waiting for transfers between devices: 3.51 us -> 0.01 us  [on_device(): low_kv = lax.ppermute(low_t[1:, :, half:], 'seq', forward)]
    ppermute x10, waiting for transfers between devices: 17.3 us -> 14.3 us  [swap(): return lax.ppermute(x, AXES, [(i, i ^ bits) for i in range(total)])]
    pallas_call x1 -> x0, Pallas kernels: 1.84 us -> none  [cut(): pl.pallas_call(cut_kernel, out_shape=jax.ShapeDtypeStruct((2, half, half_...]
    ppermute x1 -> x2, starting transfers between devices: 2.99 us -> 4.48 us  [the longest x1 2.99 us: on_device(): lax.ppermute(frozen[1:, 0, half:, half_width:middle], 'seq', forward)]
    pallas_call x4 -> x6, Pallas kernels: 5.41 us -> 6.65 us  [call(): pl.pallas_call(kernel, out_shape=outs, in_specs=[VMEM] * len(args), out_s...]
    squeeze x0 -> x1, local copies, waits for them, and re-layouts: none -> 1.13 us  [on_device(): frozen[1:, 0, half:, half_width:middle]]
    ppermute x10, starting transfers between devices: 8.99 us -> 10.1 us  [swap(): return lax.ppermute(x, AXES, [(i, i ^ bits) for i in range(total)])]
    unnamed x10 -> x12, local copies, waits for them, and re-layouts: 0.03 us -> 1.07 us
  transfers between devices with their start and end apart: 13 -> 14, of which waited for: 11 -> 11; matrix products, arithmetic and copies ran while one was open for 4% -> 4% of each run, Pallas kernels for 6% -> 10%
where the time goes in v5:
time: 46.2 us; the launch traced here: 46 us
  starting transfers between devices  18.6 us (40%)
  waiting for transfers between devices  16 us (35%)
  Pallas kernels  6.65 us (14%)
  local copies, waits for them, and re-layouts  2.29 us (5%)
  matrix products  1.6 us (3%)
  between operations  0.76 us (2%)
    ppermute x10, waiting for transfers between devices, swap(): return lax.ppermute(x, AXES, [(i, i ^ bits) for i in range(total)])  14.3 us
    ppermute x10, starting transfers between devices, swap(): return lax.ppermute(x, AXES, [(i, i ^ bits) for i in range(total)])  10.1 us
    pallas_call x6, Pallas kernels, call(): pl.pallas_call(kernel, out_shape=outs, in_specs=[VMEM] * len(args), out_s...  6.65 us
    ppermute x1, starting transfers between devices, on_device(): lax.ppermute(frozen[1:, 0, half:, half_width:middle], 'seq', forward)  2.99 us
    ppermute x1, starting transfers between devices, on_device(): cross = lax.ppermute(cross, 'seq', backward)  2.48 us
    dot_general x1, matrix products, on_device(): jnp.einsum('psw,gw->psg', down_weight, tokens[0], preferred_element_type=...  1.6 us
    ppermute x1, starting transfers between devices, on_device(): low_kv = lax.ppermute(low_t[1:, :, half:], 'seq', forward)  1.56 us
    ppermute x1, starting transfers between devices, on_device(): lax.ppermute(frozen[1:, 0, half:, middle:], 'seq', forward)  1.49 us
  transfers between devices with their start and end apart: 14, of which 11 were waited for; matrix products, arithmetic and copies ran while one was open for 4% of the time, Pallas kernels for 10%

profile of v5, /device:TPU:0, one launch (start us, length us, event | category | flops | bytes accessed | tf_op | source)
XLA Modules:
  0.0 46.0 jit_solution(10065492252341184543)
XLA Ops:
  0.7 1.1 %slice_bitcast_fusion = (bf16[2,64,512]{2,1,0:T(8,128)(2,1)S(1)}, bf16[2,64,512]{2,1,0:T(8,128)(2,1)S(1)}) fusion(bf16[3,1,128,2048]{3,2,0,1:T(8,128)(2,1)} %bitcast.29), kind=kLoop, calls=%fused_computation.3 | loop fusion | bytes 524288 | tf_op jit(solution)/shard_map/squeeze | solution.py:299
  1.8 3.0 %collective-permute-start.2 = (bf16[2,64,512]{2,1,0:T(8,128)(2,1)S(1)}, bf16[2,64,512]{2,1,0:T(8,128)(2,1)S(1)}, u32[]{:S(2)}, u32[]{:S(2)}) collective-permute-start(bf16[2,64,512]{2,1,0:T(8,128)(2,1)S(1)} %get-tuple-element.36), channel_id=1, source_target_pairs={{0,4},{4,8},{8,12},{12,16},{16,20},{20,24},{24,28},{28,0},{1,5},{5... | collective-permute-start | bytes 393224 | tf_op jit(solution)/shard_map/ppermute | solution.py:299
  4.8 1.6 %convolution_convert_fusion.low_t = bf16[3,8,128]{2,1,0:T(8,128)(2,1)S(1)} fusion(bf16[3,8,4096]{2,1,0:T(8,128)(2,1)S(1)} %copy-done, bf16[1,128,4096]{2,1,0:T(8,128)(2,1)} %tokens.1), kind=kOutput, calls=%fused_computation | convolution fusion | flops 25168896 | bytes 1251328 | tf_op jit(solution)/shard_map/psw,gw->psg/dot_general | solution.py:302
  6.5 1.6 %collective-permute-start = (bf16[2,8,64]{2,1,0:T(8,128)(2,1)S(1)}, bf16[2,8,64]{2,1,0:T(8,128)(2,1)S(1)}, u32[]{:S(2)}, u32[]{:S(2)}) collective-permute-start(bf16[2,8,64]{2,1,0:T(8,128)(2,1)S(1)} %slice.31), channel_id=1, source_target_pairs={{0,4},{4,8},{8,12},{12,16},{16,20},{20,24},{24,28},{28,0},{1,5},{5... | collective-permute-start | bytes 6152 | tf_op jit(solution)/shard_map/ppermute | solution.py:303
  8.0 1.5 %collective-permute-start.1 = (bf16[2,64,512]{2,1,0:T(8,128)(2,1)S(1)}, bf16[2,64,512]{2,1,0:T(8,128)(2,1)S(1)}, u32[]{:S(2)}, u32[]{:S(2)}) collective-permute-start(bf16[2,64,512]{2,1,0:T(8,128)(2,1)S(1)} %get-tuple-element.37), channel_id=1, source_target_pairs={{0,4},{4,8},{8,12},{12,16},{16,20},{20,24},{24,28},{28,0},{1,5},{5... | collective-permute-start | bytes 393224 | tf_op jit(solution)/shard_map/ppermute | solution.py:300
  9.5 1.0 %copy-done.3 = bf16[1,128,2048]{2,1,0:T(8,128)(2,1)S(1)} copy-done((bf16[1,128,2048]{2,1,0:T(8,128)(2,1)S(1)}, bf16[1,128,2048]{2,1,0:T(8,128)(2,1)}, u32[]{:S(2)}) %copy-start.3) | copy-done | bytes 524312
  10.6 3.2 %shard_map.68 = (bf16[3,64,1024]{2,1,0:T(8,128)(2,1)S(1)}, f32[24,2048]{1,0:T(8,128)S(1)}, f32[24,128]{1,0:T(8,128)S(1)}) custom-call(bf16[3,1,128,2048]{3,2,1,0:T(8,128)(2,1)S(1)} %copy-done.2, bf16[1,128,2048]{2,1,0:T(8,128)(2,1)S(1)} %copy-done.3, bf16[3,8,128]{2,1,0:T(8,128)(2,1)S(1)} %convolution_convert_fusion.low_t, bf16[3,8,2048]{2,1,0:T(8,128)(2,1)S(1)} %copy-done.5), custom_call_target="tpu_custom_call" | custom-call | flops 1000000000 | bytes 1000000 | tf_op jit(solution)/shard_map/pallas_call | solution.py:260
  13.8 1.1 %shard_map.69 = (f32[24,512]{1,0:T(8,128)S(1)}, f32[24,128]{1,0:T(8,128)S(1)}, f32[16,128]{1,0:T(8,128)S(1)}) custom-call(bf16[3,64,1024]{2,1,0:T(8,128)(2,1)S(1)} %get-tuple-element.18.own, bf16[2,64,512]{2,1,0:T(8,128)(2,1)S(1)} %collective-permute-done.2.frozen_kv, bf16[2,8,64]{2,1,0:T(8,128)(2,1)S(1)} %collective-permute-done.low_kv, ...), custom_call_target="tpu_custom_call" | custom-call | flops 1000000000 | bytes 1000000 | tf_op jit(solution)/shard_map/pallas_call | solution.py:260
  14.9 0.8 %collective-permute-done.1.frozen_kv = bf16[2,64,512]{2,1,0:T(8,128)(2,1)S(1)} collective-permute-done((bf16[2,64,512]{2,1,0:T(8,128)(2,1)S(1)}, bf16[2,64,512]{2,1,0:T(8,128)(2,1)S(1)}, u32[]{:S(2)}, u32[]{:S(2)}) %collective-permute-start.1) | collective-permute-done | bytes 131104 | tf_op jit(solution)/shard_map/ppermute | solution.py:300
  15.7 0.8 %shard_map.70 = (f32[24,128]{1,0:T(8,128)S(1)}, f32[16,128]{1,0:T(8,128)S(1)}, bf16[4,64,128]{2,1,0:T(8,128)(2,1)S(1)}, bf16[4,128,64]{2,1,0:T(8,128)(2,1)S(1)},...) custom-call(bf16[3,64,1024]{2,1,0:T(8,128)(2,1)S(1)} %get-tuple-element.18.own, ...), custom_call_target="tpu_custom_call" | custom-call | flops 1000000000 | bytes 1000000 | tf_op jit(solution)/shard_map/pallas_call | solution.py:260
  16.5 2.5 %collective-permute-start.3 = (f32[16,128]{1,0:T(8,128)S(1)}, f32[16,128]{1,0:T(8,128)S(1)}, u32[]{:S(2)}, u32[]{:S(2)}) collective-permute-start(f32[16,128]{1,0:T(8,128)S(1)} %get-tuple-element.28), channel_id=1, source_target_pairs={{0,28},{4,0},{8,4},{12,8},{16,12},{20,16},{24,20},{28,24},{1,29},{... | collective-permute-start | bytes 24584 | tf_op jit(solution)/shard_map/ppermute | solution.py:322
  18.9 0.5 %shard_map.71 = (f32[24,512]{1,0:T(8,128)S(1)}, f32[24,128]{1,0:T(8,128)S(1)}) custom-call(bf16[3,64,1024]{2,1,0:T(8,128)(2,1)S(1)} %get-tuple-element.18.own, bf16[2,8,64]{2,1,0:T(8,128)(2,1)S(1)} %collective-permute-done.low_kv, bf16[1,128,2048]{2,1,0:T(8,128)(2,1)S(1)} %copy-done.4, bf16[3,8,128]{2,1,0:T(8,128)(2,1)S(1)} %convolution_convert_fusion.low_t, ...), custom_call_target="tpu_custom_call" | custom-call | flops 1000000000 | bytes 1000000 | tf_op jit(solution)/shard_map/pallas_call | solution.py:260
  19.4 0.9 %collective-permute-done.3.cross = f32[16,128]{1,0:T(8,128)S(1)} collective-permute-done((f32[16,128]{1,0:T(8,128)S(1)}, f32[16,128]{1,0:T(8,128)S(1)}, u32[]{:S(2)}, u32[]{:S(2)}) %collective-permute-start.3) | collective-permute-done | bytes 8224 | tf_op jit(solution)/shard_map/ppermute | solution.py:322
  20.3 0.3 shard_map.72
  20.7 1.6 %collective-permute-done.4 = f32[4,24,768]{2,1,0:T(8,128)S(1)} collective-permute-done((f32[4,24,768]{2,1,0:T(8,128)S(1)}, f32[4,24,768]{2,1,0:T(8,128)S(1)}, u32[]{:S(2)}, u32[]{:S(2)}) %collective-permute-start.4) | collective-permute-done | bytes 294944 | tf_op jit(solution)/shard_map/ppermute | solution.py:271
  22.3 1.3 %collective-permute-start.5 = (bf16[24,768]{1,0:T(8,128)(2,1)S(1)}, bf16[24,768]{1,0:T(8,128)(2,1)S(1)}, u32[]{:S(2)}, u32[]{:S(2)}) collective-permute-start(bf16[24,768]{1,0:T(8,128)(2,1)S(1)} %get-tuple-element.38), channel_id=1, source_target_pairs={{0,5},{1,4},{2,7},{3,6},{4,1},{5,0},{6,3},{7,2},{8,13},{9,12},{10,... | collective-permute-start | bytes 110600 | tf_op jit(solution)/shard_map/ppermute | solution.py:271
  23.6 1.5 %collective-permute-start.7 = (bf16[24,768]{1,0:T(8,128)(2,1)S(1)}, bf16[24,768]{1,0:T(8,128)(2,1)S(1)}, u32[]{:S(2)}, u32[]{:S(2)}) collective-permute-start(bf16[24,768]{1,0:T(8,128)(2,1)S(1)} %get-tuple-element.39), channel_id=1, source_target_pairs={{0,6},{1,7},{2,4},{3,5},{4,2},{5,3},{6,0},{7,1},{8,14},{9,15},{10,... | collective-permute-start | bytes 110600 | tf_op jit(solution)/shard_map/ppermute | solution.py:271
  25.3 0.5 %collective-permute-done.5 = bf16[24,768]{1,0:T(8,128)(2,1)S(1)} collective-permute-done((bf16[24,768]{1,0:T(8,128)(2,1)S(1)}, bf16[24,768]{1,0:T(8,128)(2,1)S(1)}, u32[]{:S(2)}, u32[]{:S(2)}) %collective-permute-start.5) | collective-permute-done | bytes 36896 | tf_op jit(solution)/shard_map/ppermute | solution.py:271
  25.8 2.7 %collective-permute-done.7 = bf16[24,768]{1,0:T(8,128)(2,1)S(1)} collective-permute-done((bf16[24,768]{1,0:T(8,128)(2,1)S(1)}, bf16[24,768]{1,0:T(8,128)(2,1)S(1)}, u32[]{:S(2)}, u32[]{:S(2)}) %collective-permute-start.7) | collective-permute-done | bytes 36896 | tf_op jit(solution)/shard_map/ppermute | solution.py:271
  28.5 0.7 %collective-permute-done.6 = bf16[24,768]{1,0:T(8,128)(2,1)S(1)} collective-permute-done((bf16[24,768]{1,0:T(8,128)(2,1)S(1)}, bf16[24,768]{1,0:T(8,128)(2,1)S(1)}, u32[]{:S(2)}, u32[]{:S(2)}) %collective-permute-start.6) | collective-permute-done | bytes 36896 | tf_op jit(solution)/shard_map/ppermute | solution.py:271
  29.3 1.2 %collective-permute-start.8 = (f32[24,768]{1,0:T(8,128)S(1)}, f32[24,768]{1,0:T(8,128)S(1)}, u32[]{:S(2)}, u32[]{:S(2)}) collective-permute-start(f32[24,768]{1,0:T(8,128)S(1)} %fusion.3), channel_id=1, source_target_pairs={{0,9},{1,8},{2,11},{3,10},{4,13},{5,12},{6,15},{7,14},{8,1},{9,0},... | collective-permute-start | bytes 221192 | tf_op jit(solution)/shard_map/ppermute | solution.py:271
  30.4 3.2 %collective-permute-done.8 = f32[24,768]{1,0:T(8,128)S(1)} collective-permute-done((f32[24,768]{1,0:T(8,128)S(1)}, f32[24,768]{1,0:T(8,128)S(1)}, u32[]{:S(2)}, u32[]{:S(2)}) %collective-permute-start.8) | collective-permute-done | bytes 73760 | tf_op jit(solution)/shard_map/ppermute | solution.py:271
  33.6 2.2 %collective-permute-start.9 = (bf16[24,768]{1,0:T(8,128)(2,1)S(1)}, bf16[24,768]{1,0:T(8,128)(2,1)S(1)}, u32[]{:S(2)}, u32[]{:S(2)}) collective-permute-start(bf16[24,768]{1,0:T(8,128)(2,1)S(1)} %add_convert_fusion.1), channel_id=1, source_target_pairs={{0,17},{1,16},{2,19},{3,18},{4,21},{5,20},{6,23},{7,22},{8,25},{9,... | collective-permute-start | bytes 110600 | tf_op jit(solution)/shard_map/ppermute | solution.py:271
  35.8 2.3 %collective-permute-done.9 = bf16[24,768]{1,0:T(8,128)(2,1)S(1)} collective-permute-done((bf16[24,768]{1,0:T(8,128)(2,1)S(1)}, bf16[24,768]{1,0:T(8,128)(2,1)S(1)}, u32[]{:S(2)}, u32[]{:S(2)}) %collective-permute-start.9) | collective-permute-done | bytes 36896 | tf_op jit(solution)/shard_map/ppermute | solution.py:271
  38.1 1.4 %collective-permute-start.12 = (bf16[24,768]{1,0:T(8,128)(2,1)S(1)}, bf16[24,768]{1,0:T(8,128)(2,1)S(1)}, u32[]{:S(2)}, u32[]{:S(2)}) collective-permute-start(bf16[24,768]{1,0:T(8,128)(2,1)S(1)} %add_convert_fusion), channel_id=1, source_target_pairs={{0,6},{1,7},{2,4},{3,5},{4,2},{5,3},{6,0},{7,1},{8,14},{9,15},{10,... | collective-permute-start | bytes 110600 | tf_op jit(solution)/shard_map/ppermute | solution.py:271
  39.5 0.4 collective-permute-start.11
  40.0 1.4 %collective-permute-start.10 = (bf16[24,768]{1,0:T(8,128)(2,1)S(1)}, bf16[24,768]{1,0:T(8,128)(2,1)S(1)}, u32[]{:S(2)}, u32[]{:S(2)}) collective-permute-start(bf16[24,768]{1,0:T(8,128)(2,1)S(1)} %add_convert_fusion), channel_id=1, source_target_pairs={{0,5},{1,4},{2,7},{3,6},{4,1},{5,0},{6,3},{7,2},{8,13},{9,12},{10,... | collective-permute-start | bytes 110600 | tf_op jit(solution)/shard_map/ppermute | solution.py:271
  41.4 1.8 %collective-permute-done.12 = bf16[24,768]{1,0:T(8,128)(2,1)S(1)} collective-permute-done((bf16[24,768]{1,0:T(8,128)(2,1)S(1)}, bf16[24,768]{1,0:T(8,128)(2,1)S(1)}, u32[]{:S(2)}, u32[]{:S(2)}) %collective-permute-start.12) | collective-permute-done | bytes 36896 | tf_op jit(solution)/shard_map/ppermute | solution.py:271
  43.1 0.5 %collective-permute-done.11 = bf16[24,768]{1,0:T(8,128)(2,1)S(1)} collective-permute-done((bf16[24,768]{1,0:T(8,128)(2,1)S(1)}, bf16[24,768]{1,0:T(8,128)(2,1)S(1)}, u32[]{:S(2)}, u32[]{:S(2)}) %collective-permute-start.11) | collective-permute-done | bytes 36896 | tf_op jit(solution)/shard_map/ppermute | solution.py:271
  43.7 0.4 collective-permute-start.13
  44.1 1.0 %collective-permute-done.13.other = bf16[4,24,768]{2,1,0:T(8,128)(2,1)S(1)} collective-permute-done((bf16[4,24,768]{2,1,0:T(8,128)(2,1)S(1)}, bf16[4,24,768]{2,1,0:T(8,128)(2,1)S(1)}, u32[]{:S(2)}, u32[]{:S(2)}) %collective-permute-start.13) | collective-permute-done | bytes 147488 | tf_op jit(solution)/shard_map/ppermute | solution.py:271
  45.1 0.9 %shard_map.73 = (f32[3,8,4096]{2,1,0:T(8,128)}, f32[3,8,2048]{2,1,0:T(8,128)}) custom-call(bf16[4,24,768]{2,1,0:T(8,128)(2,1)S(1)} %pad_maximum_fusion.mine, bf16[4,24,768]{2,1,0:T(8,128)(2,1)S(1)} %collective-permute-done.13.other), custom_call_target="tpu_custom_call" | custom-call | flops 1000000000 | bytes 1000000 | tf_op jit(solution)/shard_map/pallas_call | solution.py:260
  (23 shorter events, 0.5 us)
Async XLA Ops:
  0.6 4.2 %copy-start = (bf16[3,8,4096]{2,1,0:T(8,128)(2,1)S(1)}, bf16[3,8,4096]{2,1,0:T(8,128)(2,1)}, u32[]{:S(2)}) copy-start(bf16[3,8,4096]{2,1,0:T(8,128)(2,1)} %param.8) | copy-start | bytes 589828
  0.6 8.9 %copy-start.2 = (bf16[3,1,128,2048]{3,2,1,0:T(8,128)(2,1)S(1)}, bf16[3,1,128,2048]{3,2,1,0:T(8,128)(2,1)}, u32[]{:S(2)}) copy-start(bf16[3,1,128,2048]{3,2,1,0:T(8,128)(2,1)} %frozen.1) | copy-start | bytes 4718596
  0.7 8.9 %copy-start.5 = (bf16[3,8,2048]{2,1,0:T(8,128)(2,1)S(1)}, bf16[3,8,2048]{2,1,0:T(8,128)(2,1)}, u32[]{:S(2)}) copy-start(bf16[3,8,2048]{2,1,0:T(8,128)(2,1)} %up.7) | copy-start | bytes 294916
  1.8 12.0 %collective-permute-start.2 = (bf16[2,64,512]{2,1,0:T(8,128)(2,1)S(1)}, bf16[2,64,512]{2,1,0:T(8,128)(2,1)S(1)}, u32[]{:S(2)}, u32[]{:S(2)}) collective-permute-start(bf16[2,64,512]{2,1,0:T(8,128)(2,1)S(1)} %get-tuple-element.36), channel_id=1, source_target_pairs={{0,4},{4,8},{8,12},{12,16},{16,20},{20,24},{24,28},{28,0},{1,5},{5... | collective-permute-start | bytes 393224 | tf_op jit(solution)/shard_map/ppermute | solution.py:299
  6.5 7.3 %collective-permute-start = (bf16[2,8,64]{2,1,0:T(8,128)(2,1)S(1)}, bf16[2,8,64]{2,1,0:T(8,128)(2,1)S(1)}, u32[]{:S(2)}, u32[]{:S(2)}) collective-permute-start(bf16[2,8,64]{2,1,0:T(8,128)(2,1)S(1)} %slice.31), channel_id=1, source_target_pairs={{0,4},{4,8},{8,12},{12,16},{16,20},{20,24},{24,28},{28,0},{1,5},{5... | collective-permute-start | bytes 6152 | tf_op jit(solution)/shard_map/ppermute | solution.py:303
  8.0 7.7 %collective-permute-start.1 = (bf16[2,64,512]{2,1,0:T(8,128)(2,1)S(1)}, bf16[2,64,512]{2,1,0:T(8,128)(2,1)S(1)}, u32[]{:S(2)}, u32[]{:S(2)}) collective-permute-start(bf16[2,64,512]{2,1,0:T(8,128)(2,1)S(1)} %get-tuple-element.37), channel_id=1, source_target_pairs={{0,4},{4,8},{8,12},{12,16},{16,20},{20,24},{24,28},{28,0},{1,5},{5... | collective-permute-start | bytes 393224 | tf_op jit(solution)/shard_map/ppermute | solution.py:300
  9.5 1.0 %copy-start.3 = (bf16[1,128,2048]{2,1,0:T(8,128)(2,1)S(1)}, bf16[1,128,2048]{2,1,0:T(8,128)(2,1)}, u32[]{:S(2)}) copy-start(bf16[1,128,2048]{2,1,0:T(8,128)(2,1)} %grad.7) | copy-start | bytes 1572868
  15.7 3.2 %copy-start.4 = (bf16[1,128,2048]{2,1,0:T(8,128)(2,1)S(1)}, bf16[1,128,2048]{2,1,0:T(8,128)(2,1)}, u32[]{:S(2)}) copy-start(bf16[1,128,2048]{2,1,0:T(8,128)(2,1)} %grad.7) | copy-start | bytes 1572868
  16.5 3.9 %collective-permute-start.3 = (f32[16,128]{1,0:T(8,128)S(1)}, f32[16,128]{1,0:T(8,128)S(1)}, u32[]{:S(2)}, u32[]{:S(2)}) collective-permute-start(f32[16,128]{1,0:T(8,128)S(1)} %get-tuple-element.28), channel_id=1, source_target_pairs={{0,28},{4,0},{8,4},{12,8},{16,12},{20,16},{24,20},{28,24},{1,29},{... | collective-permute-start | bytes 24584 | tf_op jit(solution)/shard_map/ppermute | solution.py:322
  18.9 1.4 %copy-start.1 = (bf16[1,128,4096]{2,1,0:T(8,128)(2,1)S(1)}, bf16[1,128,4096]{2,1,0:T(8,128)(2,1)}, u32[]{:S(2)}) copy-start(bf16[1,128,4096]{2,1,0:T(8,128)(2,1)} %tokens.1) | copy-start | bytes 3145732
  20.6 1.6 %collective-permute-start.4 = (f32[4,24,768]{2,1,0:T(8,128)S(1)}, f32[4,24,768]{2,1,0:T(8,128)S(1)}, u32[]{:S(2)}, u32[]{:S(2)}) collective-permute-start(f32[4,24,768]{2,1,0:T(8,128)S(1)} %get-tuple-element.33), channel_id=1, source_target_pairs={{0,1},{1,0},{2,3},{3,2},{4,5},{5,4},{6,7},{7,6},{8,9},{9,8},{10,11... | collective-permute-start | bytes 884744 | tf_op jit(solution)/shard_map/ppermute | solution.py:271
  22.3 3.5 %collective-permute-start.5 = (bf16[24,768]{1,0:T(8,128)(2,1)S(1)}, bf16[24,768]{1,0:T(8,128)(2,1)S(1)}, u32[]{:S(2)}, u32[]{:S(2)}) collective-permute-start(bf16[24,768]{1,0:T(8,128)(2,1)S(1)} %get-tuple-element.38), channel_id=1, source_target_pairs={{0,5},{1,4},{2,7},{3,6},{4,1},{5,0},{6,3},{7,2},{8,13},{9,12},{10,... | collective-permute-start | bytes 110600 | tf_op jit(solution)/shard_map/ppermute | solution.py:271
  23.6 4.9 %collective-permute-start.7 = (bf16[24,768]{1,0:T(8,128)(2,1)S(1)}, bf16[24,768]{1,0:T(8,128)(2,1)S(1)}, u32[]{:S(2)}, u32[]{:S(2)}) collective-permute-start(bf16[24,768]{1,0:T(8,128)(2,1)S(1)} %get-tuple-element.39), channel_id=1, source_target_pairs={{0,6},{1,7},{2,4},{3,5},{4,2},{5,3},{6,0},{7,1},{8,14},{9,15},{10,... | collective-permute-start | bytes 110600 | tf_op jit(solution)/shard_map/ppermute | solution.py:271
  25.1 4.1 %collective-permute-start.6 = (bf16[24,768]{1,0:T(8,128)(2,1)S(1)}, bf16[24,768]{1,0:T(8,128)(2,1)S(1)}, u32[]{:S(2)}, u32[]{:S(2)}) collective-permute-start(bf16[24,768]{1,0:T(8,128)(2,1)S(1)} %get-tuple-element.40), channel_id=1, source_target_pairs={{0,3},{1,2},{2,1},{3,0},{4,7},{5,6},{6,5},{7,4},{8,11},{9,10},{10,... | collective-permute-start | bytes 110600 | tf_op jit(solution)/shard_map/ppermute | solution.py:271
  29.3 4.3 %collective-permute-start.8 = (f32[24,768]{1,0:T(8,128)S(1)}, f32[24,768]{1,0:T(8,128)S(1)}, u32[]{:S(2)}, u32[]{:S(2)}) collective-permute-start(f32[24,768]{1,0:T(8,128)S(1)} %fusion.3), channel_id=1, source_target_pairs={{0,9},{1,8},{2,11},{3,10},{4,13},{5,12},{6,15},{7,14},{8,1},{9,0},... | collective-permute-start | bytes 221192 | tf_op jit(solution)/shard_map/ppermute | solution.py:271
  33.6 4.4 %collective-permute-start.9 = (bf16[24,768]{1,0:T(8,128)(2,1)S(1)}, bf16[24,768]{1,0:T(8,128)(2,1)S(1)}, u32[]{:S(2)}, u32[]{:S(2)}) collective-permute-start(bf16[24,768]{1,0:T(8,128)(2,1)S(1)} %add_convert_fusion.1), channel_id=1, source_target_pairs={{0,17},{1,16},{2,19},{3,18},{4,21},{5,20},{6,23},{7,22},{8,25},{9,... | collective-permute-start | bytes 110600 | tf_op jit(solution)/shard_map/ppermute | solution.py:271
  38.1 5.0 %collective-permute-start.12 = (bf16[24,768]{1,0:T(8,128)(2,1)S(1)}, bf16[24,768]{1,0:T(8,128)(2,1)S(1)}, u32[]{:S(2)}, u32[]{:S(2)}) collective-permute-start(bf16[24,768]{1,0:T(8,128)(2,1)S(1)} %add_convert_fusion), channel_id=1, source_target_pairs={{0,6},{1,7},{2,4},{3,5},{4,2},{5,3},{6,0},{7,1},{8,14},{9,15},{10,... | collective-permute-start | bytes 110600 | tf_op jit(solution)/shard_map/ppermute | solution.py:271
  39.5 4.2 %collective-permute-start.11 = (bf16[24,768]{1,0:T(8,128)(2,1)S(1)}, bf16[24,768]{1,0:T(8,128)(2,1)S(1)}, u32[]{:S(2)}, u32[]{:S(2)}) collective-permute-start(bf16[24,768]{1,0:T(8,128)(2,1)S(1)} %add_convert_fusion), channel_id=1, source_target_pairs={{0,3},{1,2},{2,1},{3,0},{4,7},{5,6},{6,5},{7,4},{8,11},{9,10},{10,... | collective-permute-start | bytes 110600 | tf_op jit(solution)/shard_map/ppermute | solution.py:271
  40.0 3.7 %collective-permute-start.10 = (bf16[24,768]{1,0:T(8,128)(2,1)S(1)}, bf16[24,768]{1,0:T(8,128)(2,1)S(1)}, u32[]{:S(2)}, u32[]{:S(2)}) collective-permute-start(bf16[24,768]{1,0:T(8,128)(2,1)S(1)} %add_convert_fusion), channel_id=1, source_target_pairs={{0,5},{1,4},{2,7},{3,6},{4,1},{5,0},{6,3},{7,2},{8,13},{9,12},{10,... | collective-permute-start | bytes 110600 | tf_op jit(solution)/shard_map/ppermute | solution.py:271
  43.7 1.4 %collective-permute-start.13 = (bf16[4,24,768]{2,1,0:T(8,128)(2,1)S(1)}, bf16[4,24,768]{2,1,0:T(8,128)(2,1)S(1)}, u32[]{:S(2)}, u32[]{:S(2)}) collective-permute-start(bf16[4,24,768]{2,1,0:T(8,128)(2,1)S(1)} %pad_maximum_fusion.mine), channel_id=1, source_target_pairs={{0,1},{1,0},{2,3},{3,2},{4,5},{5,4},{6,7},{7,6},{8,9},{9,8},{10,11... | collective-permute-start | bytes 442376 | tf_op jit(solution)/shard_map/ppermute | solution.py:271

commit v6 on v5

--- a/solution.py
+++ b/solution.py
@@ -12,8 +12,8 @@
 BF = jnp.bfloat16
 F32 = jnp.float32
 AXES = ("seq", "dp")
+COST = pl.CostEstimate(flops=10**9, bytes_accessed=10**6, transcendentals=0)
 VMEM = pl.BlockSpec(memory_space=pltpu.VMEM)
-TOGETHER = 8
 LIMIT = 48 * 1024 * 1024
 
 
@@ -88,47 +88,90 @@
     )
 
 
-def local_kernel(frozen, grad, low_t, up, far_out, up_out, rank_out):
+def low_kernel(tokens, down, low_out, near_out, buffer, sems):
+    chunks = buffer.shape[0]
+    step = buffer.shape[2]
+    copies = [
+        pltpu.make_async_copy(tokens.at[0, :, pl.ds(c * step, step)], buffer.at[c], sems.at[c])
+        for c in range(chunks)
+    ]
+    for copy in copies:
+        copy.start()
+    low = 0.0
+    for c, copy in enumerate(copies):
+        copy.wait()
+        low = low + nt(down[:, c * step : (c + 1) * step], buffer[c])
+    half = near_out.shape[2]
+    for j in range(3):
+        part = low[8 * j : 8 * j + 8].astype(BF)
+        low_out[j] = part
+        if j > 0:
+            near_out[j - 1] = part[:, half:]
+
+
+def low_rank(tokens, down_weight):
+    count, model = tokens.shape[1:]
+    chunks = 4
+    return pl.pallas_call(
+        low_kernel,
+        out_shape=[
+            jax.ShapeDtypeStruct((3, RANK, count), BF),
+            jax.ShapeDtypeStruct((2, RANK, count // 2), BF),
+        ],
+        in_specs=[pl.BlockSpec(memory_space=pltpu.HBM), VMEM],
+        out_specs=[VMEM, VMEM],
+        scratch_shapes=[pltpu.VMEM((chunks, count, model // chunks), BF), pltpu.SemaphoreType.DMA((chunks,))],
+    )(tokens, down_weight.reshape(3 * RANK, model))
+
+
+def plain_kernel(frozen, grad, low_t, up, far_out, up_out, rank_out, plain_grad, sem):
     count, width = grad.shape[1:]
     half, half_width = count // 2, width // 2
+    copy = pltpu.make_async_copy(grad.at[0, :, pl.ds(0, half_width)], plain_grad, sem)
+    copy.start()
     low = [low_t[j] for j in range(3)]
     low_f = [x.astype(F32) for x in low]
-    near_f = [x[:, half:] for x in low_f]
-    ranks = [jnp.zeros((RANK, count), F32)] * 3
-    full_mask = causal(count, count, 0)
-    half_mask = causal(half, half, 0)
-    for first in range(0, half_width, TOGETHER * HEAD_DIM):
-        items, places = [], []
-        for start in range(first, first + TOGETHER * HEAD_DIM, HEAD_DIM):
-            cols = slice(start, start + HEAD_DIM)
-            ups = [up[j, :, cols] for j in range(3)]
-            q, k, v = [project(frozen[j, 0, :, cols], low[j], ups[j]) for j in range(3)]
-            items.append((q, k, v, grad[0, :, cols], ups, low_f))
-            places.append(cols)
-        for cols, (grads, parts) in zip(places, heads(items, full_mask)):
-            for j in range(3):
-                up_out[8 * j : 8 * j + 8, cols] = grads[j]
-            ranks = [a + b for a, b in zip(ranks, parts)]
-    near_ranks = [jnp.zeros((RANK, half), F32)] * 3
-    for first in range(half_width, width, TOGETHER * HEAD_DIM):
-        items, places = [], []
-        for start in range(first, first + TOGETHER * HEAD_DIM, HEAD_DIM):
-            cols = slice(start, start + HEAD_DIM)
-            ups = [up[j, :, cols] for j in range(3)]
-            whole = [project(frozen[j, 0, :, cols], low[j], ups[j]) for j in range(3)]
-            for j in range(3):
-                far_out[j, :, start - half_width : start - half_width + HEAD_DIM] = whole[j][:half]
-            q, k, v = [x[half:] for x in whole]
-            items.append((q, k, v, grad[0, half:, cols], ups, near_f))
-            places.append(cols)
-        for cols, (grads, parts) in zip(places, heads(items, half_mask)):
-            for j in range(3):
-                up_out[8 * j : 8 * j + 8, cols] = grads[j]
-            near_ranks = [a + b for a, b in zip(near_ranks, parts)]
+    far = [x[:, :half] for x in low]
+    starts = range(0, half_width, HEAD_DIM)
+    held = []
+    for start in starts:
+        cols = slice(start, start + HEAD_DIM)
+        held.append([project(frozen[j, 0, :, cols], low[j], up[j, :, cols]) for j in range(3)])
+    for start in starts:
+        cols = slice(half_width + start, half_width + start + HEAD_DIM)
+        for j in range(3):
+            far_out[j, :, start : start + HEAD_DIM] = project(frozen[j, 0, :half, cols], far[j], up[j, :, cols])
+    copy.wait()
+    items = []
+    for start, (q, k, v) in zip(starts, held):
+        cols = slice(start, start + HEAD_DIM)
+        items.append((q, k, v, plain_grad[:, cols], [up[j, :, cols] for j in range(3)], low_f))
+    parts = heads(items, causal(count, count, 0))
+    for start, (grads, _) in zip(starts, parts):
+        for j in range(3):
+            up_out[8 * j : 8 * j + 8, start : start + HEAD_DIM] = grads[j]
     for j in range(3):
-        rank_out[8 * j : 8 * j + 8, :] = ranks[j] + jnp.concatenate(
-            [jnp.zeros((RANK, half), F32), near_ranks[j]], axis=1
-        )
+        rank_out[8 * j : 8 * j + 8, :] = sum(ranks[j] for _, ranks in parts)
+
+
+def near_kernel(frozen, grad, low_t, up, up_out, rank_out):
+    count, width = grad.shape[1:]
+    half, half_width = count // 2, width // 2
+    low = [low_t[j][:, half:] for j in range(3)]
+    low_f = [x.astype(F32) for x in low]
+    starts = range(half_width, width, HEAD_DIM)
+    items = []
+    for start in starts:
+        cols = slice(start, start + HEAD_DIM)
+        ups = [up[j, :, cols] for j in range(3)]
+        q, k, v = [project(frozen[j, 0, half:, cols], low[j], ups[j]) for j in range(3)]
+        items.append((q, k, v, grad[0, half:, cols], ups, low_f))
+    parts = heads(items, causal(half, half, 0))
+    for start, (grads, _) in zip(starts, parts):
+        for j in range(3):
+            up_out[8 * j : 8 * j + 8, start - half_width : start - half_width + HEAD_DIM] = grads[j]
+    for j in range(3):
+        rank_out[8 * j : 8 * j + 8, :] = right(sum(ranks[j] for _, ranks in parts))
 
 
 def far_items(own, near_kv, low_kv, grad, low_t, up, first):
@@ -222,18 +265,24 @@
     return bits & 1, (dp & 2) | (seq & 1)
 
 
-def down_kernel(tokens, rank_in, cross, up_in, up_a, up_b, keep, send):
+def down_kernel(tokens, rank_in, rank_near, cross, up_plain, up_near, up_a, up_b, keep, send):
     half, quarter = position()
     first = half == 0
-    ranks = rank_in[...] + jnp.concatenate([jnp.zeros((RANK, rank_in.shape[1]), F32), cross[...]], axis=0)
+    ranks = rank_in[...] + rank_near[...] + jnp.concatenate(
+        [jnp.zeros((RANK, rank_in.shape[1]), F32), cross[...]], axis=0
+    )
     both = rows(hi_lo(ranks))
     n = ranks.shape[0]
-    up_step, down_step = up_in.shape[1] // 8, tokens.shape[2] // 8
+    up_step, down_step = up_a.shape[1] // 2, tokens.shape[2] // 8
     for c in range(4):
         d = nn(both, tokens[0, :, 2 * c * down_step : 2 * (c + 1) * down_step])
         d = ADAPTER_SCALE * (d[:n] + d[n:])
-        u = up_in[:, 2 * c * up_step : 2 * (c + 1) * up_step]
-        u = ADAPTER_SCALE * (u + (up_a[...] if c == 2 else up_b[...]) if c >= 2 else u)
+        cols = slice((c % 2) * 2 * up_step, (c % 2 + 1) * 2 * up_step)
+        if c < 2:
+            u = up_plain[:, cols]
+        else:
+            u = up_near[:, cols] + (up_a if c == 2 else up_b)[...]
+        u = ADAPTER_SCALE * u
         slot = quarter ^ c
         keep[slot, :, :up_step] = jnp.where(first, u[:, :up_step], u[:, up_step:])
         send[slot, :, :up_step] = jnp.where(first, u[:, up_step:], u[:, :up_step])
@@ -263,7 +312,7 @@
         in_specs=[VMEM] * len(args),
         out_specs=jax.tree.map(lambda _: VMEM, outs),
         compiler_params=pltpu.CompilerParams(vmem_limit_bytes=LIMIT),
-        cost_estimate=pl.CostEstimate(flops=10**9, bytes_accessed=10**6, transcendentals=0),
+        cost_estimate=COST,
     )(*args)
 
 
@@ -299,15 +348,20 @@
         lax.ppermute(frozen[1:, 0, half:, half_width:middle], "seq", forward),
         lax.ppermute(frozen[1:, 0, half:, middle:], "seq", forward),
     ]
-    low_t = jnp.einsum("psw,gw->psg", down_weight, tokens[0], preferred_element_type=F32).astype(BF)
-    low_kv = lax.ppermute(low_t[1:, :, half:], "seq", forward)
+    low_t, low_near = low_rank(tokens, down_weight)
+    low_kv = lax.ppermute(low_near, "seq", forward)
     sds = jax.ShapeDtypeStruct
-    own, up_part, rank = call(
-        local_kernel,
-        [sds((3, half, half_width), BF), sds((24, width), F32), sds((24, count), F32)],
-        frozen, grad, low_t, up_weight,
-    )
-    up_side, rank_side, cross_side = sds((24, half_width // 2), F32), sds((24, count), F32), sds((16, count), F32)
+    up_half, up_side = sds((24, half_width), F32), sds((24, half_width // 2), F32)
+    rank_side, cross_side = sds((24, count), F32), sds((16, count), F32)
+    own, up_plain, rank = pl.pallas_call(
+        plain_kernel,
+        out_shape=[sds((3, half, half_width), BF), up_half, rank_side],
+        in_specs=[VMEM, pl.BlockSpec(memory_space=pltpu.HBM), VMEM, VMEM],
+        out_specs=[VMEM] * 3,
+        scratch_shapes=[pltpu.VMEM((count, half_width), BF), pltpu.SemaphoreType.DMA],
+        compiler_params=pltpu.CompilerParams(vmem_limit_bytes=LIMIT),
+        cost_estimate=COST,
+    )(frozen, grad, low_t, up_weight)
     up_a, rank, cross = call(
         far_first, [up_side, rank_side, cross_side],
         own, frozen_kv[0], low_kv, grad, low_t, up_weight, rank,
@@ -319,11 +373,13 @@
         [rank_side, cross_side, sds((n, half, HEAD_DIM), BF), by_keys, by_keys, sds((8 * n, count), F32)],
         own, frozen_kv[1], low_kv, grad, low_t, up_weight, rank, cross,
     )
+    rank, *held = lax.optimization_barrier((rank, grad, low_t, up_weight))
     cross = lax.ppermute(cross, "seq", backward)
+    up_near, rank_near = call(near_kernel, [up_half, rank_side], frozen, *held)
     up_b, rank = call(far_rest, [up_side, rank_side], own, low_kv, grad, low_t, up_weight, rank, *kept)
     columns = (width + tokens.shape[2]) // 8
     piece = sds((4, 24, columns), F32)
-    keep, send = call(down_kernel, [piece, piece], tokens, rank, cross, up_part, up_a, up_b)
+    keep, send = call(down_kernel, [piece, piece], tokens, rank, rank_near, cross, up_plain, up_near, up_a, up_b)
     mine, other = total_sum(keep, send, seqs, dps)
     return tuple(
         call(spread_kernel, [sds((3, RANK, tokens.shape[2]), F32), sds((3, RANK, width), F32)], mine, other)

time: 46.2 us -> 49.4 us (1.069)
  Pallas kernels: 6.65 us -> 10.5 us
  starting transfers between devices: 18.6 us -> 16.5 us
  waiting for transfers between devices: 16 us -> 17.6 us
  matrix products: 1.6 us -> 0 us
  local copies, waits for them, and re-layouts: 2.29 us -> 3.61 us
    pallas_call x0 -> x2, Pallas kernels: none -> 5.57 us  [the longest x1 3.44 us: low_rank(): pl.pallas_call(low_kernel, out_shape=[jax.ShapeDtypeStruct((3, RANK, coun...]
    ppermute x10, waiting for transfers between devices: 14.3 us -> 16.4 us  [swap(): return lax.ppermute(x, AXES, [(i, i ^ bits) for i in range(total)])]
    ppermute x10, starting transfers between devices: 10.1 us -> 8.31 us  [swap(): return lax.ppermute(x, AXES, [(i, i ^ bits) for i in range(total)])]
    pallas_call x6, Pallas kernels: 6.65 us -> 4.94 us  [call(): pl.pallas_call(kernel, out_shape=outs, in_specs=[VMEM] * len(args), out_s...]
    dot_general x1 -> x0, matrix products: 1.6 us -> none  [on_device(): jnp.einsum('psw,gw->psg', down_weight, tokens[0], preferred_element_type=...]
    unnamed x12 -> x10, local copies, waits for them, and re-layouts: 1.07 us -> 2.48 us
    ppermute x1, waiting for transfers between devices: 0.89 us -> 0.01 us  [on_device(): cross = lax.ppermute(cross, 'seq', backward)]
  transfers between devices with their start and end apart: 14 -> 14, of which waited for: 11 -> 10; matrix products, arithmetic and copies ran while one was open for 4% -> 0% of each run, Pallas kernels for 10% -> 18%
where the time goes in v6:
time: 49.4 us; the launch traced here: 49.1 us
  waiting for transfers between devices  17.6 us (36%)
  starting transfers between devices  16.5 us (33%)
  Pallas kernels  10.5 us (21%)
  local copies, waits for them, and re-layouts  3.61 us (7%)
  between operations  0.79 us (2%)
    ppermute x10, waiting for transfers between devices, swap(): return lax.ppermute(x, AXES, [(i, i ^ bits) for i in range(total)])  16.4 us
    ppermute x10, starting transfers between devices, swap(): return lax.ppermute(x, AXES, [(i, i ^ bits) for i in range(total)])  8.31 us
    pallas_call x6, Pallas kernels, call(): pl.pallas_call(kernel, out_shape=outs, in_specs=[VMEM] * len(args), out_s...  4.94 us
    pallas_call x1, Pallas kernels, low_rank(): pl.pallas_call(low_kernel, out_shape=[jax.ShapeDtypeStruct((3, RANK, coun...  3.44 us
    ppermute x1, starting transfers between devices, on_device(): lax.ppermute(frozen[1:, 0, half:, half_width:middle], 'seq', forward)  2.99 us
    unnamed x10, local copies, waits for them, and re-layouts  2.48 us
    pallas_call x1, Pallas kernels, on_device(): pl.pallas_call(plain_kernel, out_shape=[sds((3, half, half_width), BF), u...  2.13 us
    ppermute x1, starting transfers between devices, on_device(): cross = lax.ppermute(cross, 'seq', backward)  2.08 us
  transfers between devices with their start and end apart: 14, of which 10 were waited for; matrix products, arithmetic and copies ran while one was open for 0% of the time, Pallas kernels for 18%

profile of v6, /device:TPU:0, one launch (start us, length us, event | category | flops | bytes accessed | tf_op | source)
XLA Modules:
  0.0 49.1 jit_solution(14708945497115268769)
XLA Ops:
  0.6 1.1 %slice_bitcast_fusion = (bf16[2,64,512]{2,1,0:T(8,128)(2,1)S(1)}, bf16[2,64,512]{2,1,0:T(8,128)(2,1)S(1)}) fusion(bf16[3,1,128,2048]{3,2,0,1:T(8,128)(2,1)} %bitcast.24), kind=kLoop, calls=%fused_computation.1 | loop fusion | bytes 524288 | tf_op jit(solution)/shard_map/squeeze | solution.py:348
  1.8 3.0 %collective-permute-start.2 = (bf16[2,64,512]{2,1,0:T(8,128)(2,1)S(1)}, bf16[2,64,512]{2,1,0:T(8,128)(2,1)S(1)}, u32[]{:S(2)}, u32[]{:S(2)}) collective-permute-start(bf16[2,64,512]{2,1,0:T(8,128)(2,1)S(1)} %get-tuple-element.52), channel_id=1, source_target_pairs={{0,4},{4,8},{8,12},{12,16},{16,20},{20,24},{24,28},{28,0},{1,5},{5... | collective-permute-start | bytes 393224 | tf_op jit(solution)/shard_map/ppermute | solution.py:348
  4.8 3.4 %shard_map.68 = (bf16[3,8,128]{2,1,0:T(8,128)(2,1)}, bf16[2,8,64]{2,1,0:T(8,128)(2,1)}) custom-call(bf16[1,128,4096]{2,1,0:T(8,128)(2,1)} %tokens.3, bf16[24,4096]{1,0:T(8,128)(2,1)} %bitcast.25), custom_call_target="tpu_custom_call" | custom-call | tf_op jit(solution)/shard_map/pallas_call | solution.py:115
  8.2 1.6 %collective-permute-start = (bf16[2,8,64]{2,1,0:T(8,128)(2,1)}, bf16[2,8,64]{2,1,0:T(8,128)(2,1)S(1)}, u32[]{:S(2)}, u32[]{:S(2)}) collective-permute-start(bf16[2,8,64]{2,1,0:T(8,128)(2,1)} %get-tuple-element.28), channel_id=1, source_target_pairs={{0,4},{4,8},{8,12},{12,16},{16,20},{20,24},{24,28},{28,0},{1,5},{5... | collective-permute-start | bytes 6152 | tf_op jit(solution)/shard_map/ppermute | solution.py:352
  9.8 1.5 %collective-permute-start.1 = (bf16[2,64,512]{2,1,0:T(8,128)(2,1)S(1)}, bf16[2,64,512]{2,1,0:T(8,128)(2,1)S(1)}, u32[]{:S(2)}, u32[]{:S(2)}) collective-permute-start(bf16[2,64,512]{2,1,0:T(8,128)(2,1)S(1)} %get-tuple-element.53), channel_id=1, source_target_pairs={{0,4},{4,8},{8,12},{12,16},{16,20},{20,24},{24,28},{28,0},{1,5},{5... | collective-permute-start | bytes 393224 | tf_op jit(solution)/shard_map/ppermute | solution.py:349
  11.3 1.0 %copy-done.2 = bf16[1,128,2048]{2,1,0:T(8,128)(2,1)S(1)} copy-done((bf16[1,128,2048]{2,1,0:T(8,128)(2,1)S(1)}, bf16[1,128,2048]{2,1,0:T(8,128)(2,1)}, u32[]{:S(2)}) %copy-start.2) | copy-done | bytes 524312
  12.3 0.7 %copy-done.4 = bf16[3,8,128]{2,1,0:T(8,128)(2,1)S(1)} copy-done((bf16[3,8,128]{2,1,0:T(8,128)(2,1)S(1)}, bf16[3,8,128]{2,1,0:T(8,128)(2,1)}, u32[]{:S(2)}) %copy-start.4) | copy-done | bytes 6168
  13.0 2.1 %shard_map.69 = (bf16[3,64,1024]{2,1,0:T(8,128)(2,1)S(1)}, f32[24,1024]{1,0:T(8,128)S(1)}, f32[24,128]{1,0:T(8,128)S(1)}) custom-call(bf16[3,1,128,2048]{3,2,1,0:T(8,128)(2,1)S(1)} %copy-done.1, bf16[1,128,2048]{2,1,0:T(8,128)(2,1)S(1)} %copy-done.2, bf16[3,8,128]{2,1,0:T(8,128)(2,1)S(1)} %copy-done.4, bf16[3,8,2048]{2,1,0:T(8,128)(2,1)S(1)} %copy-done.3), custom_call_target="tpu_custom_call" | custom-call | flops 1000000000 | bytes 1000000 | tf_op jit(solution)/shard_map/pallas_call | solution.py:356
  15.2 1.1 %shard_map.70 = (f32[24,512]{1,0:T(8,128)S(1)}, f32[24,128]{1,0:T(8,128)S(1)}, f32[16,128]{1,0:T(8,128)S(1)}) custom-call(bf16[3,64,1024]{2,1,0:T(8,128)(2,1)S(1)} %get-tuple-element.27.own, bf16[2,64,512]{2,1,0:T(8,128)(2,1)S(1)} %collective-permute-done.2.frozen_kv, bf16[2,8,64]{2,1,0:T(8,128)(2,1)S(1)} %collective-permute-done.low_kv, ...), custom_call_target="tpu_custom_call" | custom-call | flops 1000000000 | bytes 1000000 | tf_op jit(solution)/shard_map/pallas_call | solution.py:309
  16.3 1.2 %collective-permute-done.1.frozen_kv = bf16[2,64,512]{2,1,0:T(8,128)(2,1)S(1)} collective-permute-done((bf16[2,64,512]{2,1,0:T(8,128)(2,1)S(1)}, bf16[2,64,512]{2,1,0:T(8,128)(2,1)S(1)}, u32[]{:S(2)}, u32[]{:S(2)}) %collective-permute-start.1) | collective-permute-done | bytes 131104 | tf_op jit(solution)/shard_map/ppermute | solution.py:349
  17.5 0.8 %shard_map.71 = (f32[24,128]{1,0:T(8,128)S(1)}, f32[16,128]{1,0:T(8,128)S(1)}, bf16[4,64,128]{2,1,0:T(8,128)(2,1)S(1)}, bf16[4,128,64]{2,1,0:T(8,128)(2,1)S(1)},...) custom-call(bf16[3,64,1024]{2,1,0:T(8,128)(2,1)S(1)} %get-tuple-element.27.own, ...), custom_call_target="tpu_custom_call" | custom-call | flops 1000000000 | bytes 1000000 | tf_op jit(solution)/shard_map/pallas_call | solution.py:309
  18.2 2.1 %collective-permute-start.3 = (f32[16,128]{1,0:T(8,128)S(1)}, f32[16,128]{1,0:T(8,128)S(1)}, u32[]{:S(2)}, u32[]{:S(2)}) collective-permute-start(f32[16,128]{1,0:T(8,128)S(1)} %get-tuple-element.43), channel_id=1, source_target_pairs={{0,28},{4,0},{8,4},{12,8},{16,12},{20,16},{24,20},{28,24},{1,29},{... | collective-permute-start | bytes 24584 | tf_op jit(solution)/shard_map/ppermute | solution.py:377
  20.3 1.5 %shard_map.73 = (f32[24,1024]{1,0:T(8,128)S(1)}, f32[24,128]{1,0:T(8,128)S(1)}) custom-call(bf16[3,1,128,2048]{3,2,1,0:T(8,128)(2,1)S(1)} %copy-done.1, bf16[1,128,2048]{2,1,0:T(8,128)(2,1)S(1)} %copy-done.2, bf16[3,8,128]{2,1,0:T(8,128)(2,1)S(1)} %copy-done.4, bf16[3,8,2048]{2,1,0:T(8,128)(2,1)S(1)} %copy-done.3), custom_call_target="tpu_custom_call" | custom-call | flops 1000000000 | bytes 1000000 | tf_op jit(solution)/shard_map/pallas_call | solution.py:309
  21.8 0.5 shard_map.72
  22.3 0.7 %copy-done = bf16[1,128,4096]{2,1,0:T(8,128)(2,1)S(1)} copy-done((bf16[1,128,4096]{2,1,0:T(8,128)(2,1)S(1)}, bf16[1,128,4096]{2,1,0:T(8,128)(2,1)}, u32[]{:S(2)}) %copy-start) | copy-done | bytes 1048600
  23.1 0.3 shard_map.74
  23.4 1.6 %collective-permute-done.4 = f32[4,24,768]{2,1,0:T(8,128)S(1)} collective-permute-done((f32[4,24,768]{2,1,0:T(8,128)S(1)}, f32[4,24,768]{2,1,0:T(8,128)S(1)}, u32[]{:S(2)}, u32[]{:S(2)}) %collective-permute-start.4) | collective-permute-done | bytes 294944 | tf_op jit(solution)/shard_map/ppermute | solution.py:320
  25.1 2.7 %collective-permute-start.7 = (bf16[24,768]{1,0:T(8,128)(2,1)S(1)}, bf16[24,768]{1,0:T(8,128)(2,1)S(1)}, u32[]{:S(2)}, u32[]{:S(2)}) collective-permute-start(bf16[24,768]{1,0:T(8,128)(2,1)S(1)} %get-tuple-element.55), channel_id=1, source_target_pairs={{0,6},{1,7},{2,4},{3,5},{4,2},{5,3},{6,0},{7,1},{8,14},{9,15},{10,... | collective-permute-start | bytes 110600 | tf_op jit(solution)/shard_map/ppermute | solution.py:320
  27.9 0.2 collective-permute-start.6
  28.1 0.5 %collective-permute-done.5 = bf16[24,768]{1,0:T(8,128)(2,1)S(1)} collective-permute-done((bf16[24,768]{1,0:T(8,128)(2,1)S(1)}, bf16[24,768]{1,0:T(8,128)(2,1)S(1)}, u32[]{:S(2)}, u32[]{:S(2)}) %collective-permute-start.5) | collective-permute-done | bytes 36896 | tf_op jit(solution)/shard_map/ppermute | solution.py:320
  28.6 2.1 %collective-permute-done.7 = bf16[24,768]{1,0:T(8,128)(2,1)S(1)} collective-permute-done((bf16[24,768]{1,0:T(8,128)(2,1)S(1)}, bf16[24,768]{1,0:T(8,128)(2,1)S(1)}, u32[]{:S(2)}, u32[]{:S(2)}) %collective-permute-start.7) | collective-permute-done | bytes 36896 | tf_op jit(solution)/shard_map/ppermute | solution.py:320
  30.7 0.7 %collective-permute-done.6 = bf16[24,768]{1,0:T(8,128)(2,1)S(1)} collective-permute-done((bf16[24,768]{1,0:T(8,128)(2,1)S(1)}, bf16[24,768]{1,0:T(8,128)(2,1)S(1)}, u32[]{:S(2)}, u32[]{:S(2)}) %collective-permute-start.6) | collective-permute-done | bytes 36896 | tf_op jit(solution)/shard_map/ppermute | solution.py:320
  31.4 0.4 collective-permute-start.8
  31.8 3.9 %collective-permute-done.8 = f32[24,768]{1,0:T(8,128)S(1)} collective-permute-done((f32[24,768]{1,0:T(8,128)S(1)}, f32[24,768]{1,0:T(8,128)S(1)}, u32[]{:S(2)}, u32[]{:S(2)}) %collective-permute-start.8) | collective-permute-done | bytes 73760 | tf_op jit(solution)/shard_map/ppermute | solution.py:320
  35.8 1.4 %collective-permute-start.9 = (bf16[24,768]{1,0:T(8,128)(2,1)S(1)}, bf16[24,768]{1,0:T(8,128)(2,1)S(1)}, u32[]{:S(2)}, u32[]{:S(2)}) collective-permute-start(bf16[24,768]{1,0:T(8,128)(2,1)S(1)} %add_convert_fusion.1), channel_id=1, source_target_pairs={{0,17},{1,16},{2,19},{3,18},{4,21},{5,20},{6,23},{7,22},{8,25},{9,... | collective-permute-start | bytes 110600 | tf_op jit(solution)/shard_map/ppermute | solution.py:320
  37.2 3.9 %collective-permute-done.9 = bf16[24,768]{1,0:T(8,128)(2,1)S(1)} collective-permute-done((bf16[24,768]{1,0:T(8,128)(2,1)S(1)}, bf16[24,768]{1,0:T(8,128)(2,1)S(1)}, u32[]{:S(2)}, u32[]{:S(2)}) %collective-permute-start.9) | collective-permute-done | bytes 36896 | tf_op jit(solution)/shard_map/ppermute | solution.py:320
  41.1 1.7 %collective-permute-start.12 = (bf16[24,768]{1,0:T(8,128)(2,1)S(1)}, bf16[24,768]{1,0:T(8,128)(2,1)S(1)}, u32[]{:S(2)}, u32[]{:S(2)}) collective-permute-start(bf16[24,768]{1,0:T(8,128)(2,1)S(1)} %add_convert_fusion), channel_id=1, source_target_pairs={{0,6},{1,7},{2,4},{3,5},{4,2},{5,3},{6,0},{7,1},{8,14},{9,15},{10,... | collective-permute-start | bytes 110600 | tf_op jit(solution)/shard_map/ppermute | solution.py:320
  42.9 1.4 %collective-permute-start.10 = (bf16[24,768]{1,0:T(8,128)(2,1)S(1)}, bf16[24,768]{1,0:T(8,128)(2,1)S(1)}, u32[]{:S(2)}, u32[]{:S(2)}) collective-permute-start(bf16[24,768]{1,0:T(8,128)(2,1)S(1)} %add_convert_fusion), channel_id=1, source_target_pairs={{0,5},{1,4},{2,7},{3,6},{4,1},{5,0},{6,3},{7,2},{8,13},{9,12},{10,... | collective-permute-start | bytes 110600 | tf_op jit(solution)/shard_map/ppermute | solution.py:320
  44.3 1.7 %collective-permute-done.12 = bf16[24,768]{1,0:T(8,128)(2,1)S(1)} collective-permute-done((bf16[24,768]{1,0:T(8,128)(2,1)S(1)}, bf16[24,768]{1,0:T(8,128)(2,1)S(1)}, u32[]{:S(2)}, u32[]{:S(2)}) %collective-permute-start.12) | collective-permute-done | bytes 36896 | tf_op jit(solution)/shard_map/ppermute | solution.py:320
  46.0 0.8 %collective-permute-done.11 = bf16[24,768]{1,0:T(8,128)(2,1)S(1)} collective-permute-done((bf16[24,768]{1,0:T(8,128)(2,1)S(1)}, bf16[24,768]{1,0:T(8,128)(2,1)S(1)}, u32[]{:S(2)}, u32[]{:S(2)}) %collective-permute-start.11) | collective-permute-done | bytes 36896 | tf_op jit(solution)/shard_map/ppermute | solution.py:320
  47.0 1.3 %collective-permute-done.13.other = bf16[4,24,768]{2,1,0:T(8,128)(2,1)S(1)} collective-permute-done((bf16[4,24,768]{2,1,0:T(8,128)(2,1)S(1)}, bf16[4,24,768]{2,1,0:T(8,128)(2,1)S(1)}, u32[]{:S(2)}, u32[]{:S(2)}) %collective-permute-start.13) | collective-permute-done | bytes 147488 | tf_op jit(solution)/shard_map/ppermute | solution.py:320
  48.2 0.9 %shard_map.75 = (f32[3,8,4096]{2,1,0:T(8,128)}, f32[3,8,2048]{2,1,0:T(8,128)}) custom-call(bf16[4,24,768]{2,1,0:T(8,128)(2,1)S(1)} %pad_maximum_fusion.mine, bf16[4,24,768]{2,1,0:T(8,128)(2,1)S(1)} %collective-permute-done.13.other), custom_call_target="tpu_custom_call" | custom-call | flops 1000000000 | bytes 1000000 | tf_op jit(solution)/shard_map/pallas_call | solution.py:309
  (21 shorter events, 0.6 us)
Async XLA Ops:
  0.6 10.7 %copy-start.1 = (bf16[3,1,128,2048]{3,2,1,0:T(8,128)(2,1)S(1)}, bf16[3,1,128,2048]{3,2,1,0:T(8,128)(2,1)}, u32[]{:S(2)}) copy-start(bf16[3,1,128,2048]{3,2,1,0:T(8,128)(2,1)} %frozen.3) | copy-start | bytes 4718596
  0.6 10.7 %copy-start.3 = (bf16[3,8,2048]{2,1,0:T(8,128)(2,1)S(1)}, bf16[3,8,2048]{2,1,0:T(8,128)(2,1)}, u32[]{:S(2)}) copy-start(bf16[3,8,2048]{2,1,0:T(8,128)(2,1)} %up.8) | copy-start | bytes 294916
  1.8 13.4 %collective-permute-start.2 = (bf16[2,64,512]{2,1,0:T(8,128)(2,1)S(1)}, bf16[2,64,512]{2,1,0:T(8,128)(2,1)S(1)}, u32[]{:S(2)}, u32[]{:S(2)}) collective-permute-start(bf16[2,64,512]{2,1,0:T(8,128)(2,1)S(1)} %get-tuple-element.52), channel_id=1, source_target_pairs={{0,4},{4,8},{8,12},{12,16},{16,20},{20,24},{24,28},{28,0},{1,5},{5... | collective-permute-start | bytes 393224 | tf_op jit(solution)/shard_map/ppermute | solution.py:348
  8.2 7.0 %collective-permute-start = (bf16[2,8,64]{2,1,0:T(8,128)(2,1)}, bf16[2,8,64]{2,1,0:T(8,128)(2,1)S(1)}, u32[]{:S(2)}, u32[]{:S(2)}) collective-permute-start(bf16[2,8,64]{2,1,0:T(8,128)(2,1)} %get-tuple-element.28), channel_id=1, source_target_pairs={{0,4},{4,8},{8,12},{12,16},{16,20},{20,24},{24,28},{28,0},{1,5},{5... | collective-permute-start | bytes 6152 | tf_op jit(solution)/shard_map/ppermute | solution.py:352
  9.8 7.7 %collective-permute-start.1 = (bf16[2,64,512]{2,1,0:T(8,128)(2,1)S(1)}, bf16[2,64,512]{2,1,0:T(8,128)(2,1)S(1)}, u32[]{:S(2)}, u32[]{:S(2)}) collective-permute-start(bf16[2,64,512]{2,1,0:T(8,128)(2,1)S(1)} %get-tuple-element.53), channel_id=1, source_target_pairs={{0,4},{4,8},{8,12},{12,16},{16,20},{20,24},{24,28},{28,0},{1,5},{5... | collective-permute-start | bytes 393224 | tf_op jit(solution)/shard_map/ppermute | solution.py:349
  11.3 1.0 %copy-start.2 = (bf16[1,128,2048]{2,1,0:T(8,128)(2,1)S(1)}, bf16[1,128,2048]{2,1,0:T(8,128)(2,1)}, u32[]{:S(2)}) copy-start(bf16[1,128,2048]{2,1,0:T(8,128)(2,1)} %grad.8) | copy-start | bytes 1572868
  12.3 0.7 %copy-start.4 = (bf16[3,8,128]{2,1,0:T(8,128)(2,1)S(1)}, bf16[3,8,128]{2,1,0:T(8,128)(2,1)}, u32[]{:S(2)}) copy-start(bf16[3,8,128]{2,1,0:T(8,128)(2,1)} %get-tuple-element.40.low_t) | copy-start | bytes 18436
  18.2 4.1 %collective-permute-start.3 = (f32[16,128]{1,0:T(8,128)S(1)}, f32[16,128]{1,0:T(8,128)S(1)}, u32[]{:S(2)}, u32[]{:S(2)}) collective-permute-start(f32[16,128]{1,0:T(8,128)S(1)} %get-tuple-element.43), channel_id=1, source_target_pairs={{0,28},{4,0},{8,4},{12,8},{16,12},{20,16},{24,20},{28,24},{1,29},{... | collective-permute-start | bytes 24584 | tf_op jit(solution)/shard_map/ppermute | solution.py:377
  21.8 1.2 %copy-start = (bf16[1,128,4096]{2,1,0:T(8,128)(2,1)S(1)}, bf16[1,128,4096]{2,1,0:T(8,128)(2,1)}, u32[]{:S(2)}) copy-start(bf16[1,128,4096]{2,1,0:T(8,128)(2,1)} %tokens.3) | copy-start | bytes 3145732
  23.4 1.6 %collective-permute-start.4 = (f32[4,24,768]{2,1,0:T(8,128)S(1)}, f32[4,24,768]{2,1,0:T(8,128)S(1)}, u32[]{:S(2)}, u32[]{:S(2)}) collective-permute-start(f32[4,24,768]{2,1,0:T(8,128)S(1)} %get-tuple-element.49), channel_id=1, source_target_pairs={{0,1},{1,0},{2,3},{3,2},{4,5},{5,4},{6,7},{7,6},{8,9},{9,8},{10,11... | collective-permute-start | bytes 884744 | tf_op jit(solution)/shard_map/ppermute | solution.py:320
  25.1 3.5 %collective-permute-start.5 = (bf16[24,768]{1,0:T(8,128)(2,1)S(1)}, bf16[24,768]{1,0:T(8,128)(2,1)S(1)}, u32[]{:S(2)}, u32[]{:S(2)}) collective-permute-start(bf16[24,768]{1,0:T(8,128)(2,1)S(1)} %get-tuple-element.54), channel_id=1, source_target_pairs={{0,5},{1,4},{2,7},{3,6},{4,1},{5,0},{6,3},{7,2},{8,13},{9,12},{10,... | collective-permute-start | bytes 110600 | tf_op jit(solution)/shard_map/ppermute | solution.py:320
  25.1 5.5 %collective-permute-start.7 = (bf16[24,768]{1,0:T(8,128)(2,1)S(1)}, bf16[24,768]{1,0:T(8,128)(2,1)S(1)}, u32[]{:S(2)}, u32[]{:S(2)}) collective-permute-start(bf16[24,768]{1,0:T(8,128)(2,1)S(1)} %get-tuple-element.55), channel_id=1, source_target_pairs={{0,6},{1,7},{2,4},{3,5},{4,2},{5,3},{6,0},{7,1},{8,14},{9,15},{10,... | collective-permute-start | bytes 110600 | tf_op jit(solution)/shard_map/ppermute | solution.py:320
  27.9 3.5 %collective-permute-start.6 = (bf16[24,768]{1,0:T(8,128)(2,1)S(1)}, bf16[24,768]{1,0:T(8,128)(2,1)S(1)}, u32[]{:S(2)}, u32[]{:S(2)}) collective-permute-start(bf16[24,768]{1,0:T(8,128)(2,1)S(1)} %get-tuple-element.56), channel_id=1, source_target_pairs={{0,3},{1,2},{2,1},{3,0},{4,7},{5,6},{6,5},{7,4},{8,11},{9,10},{10,... | collective-permute-start | bytes 110600 | tf_op jit(solution)/shard_map/ppermute | solution.py:320
  31.4 4.3 %collective-permute-start.8 = (f32[24,768]{1,0:T(8,128)S(1)}, f32[24,768]{1,0:T(8,128)S(1)}, u32[]{:S(2)}, u32[]{:S(2)}) collective-permute-start(f32[24,768]{1,0:T(8,128)S(1)} %fusion.2), channel_id=1, source_target_pairs={{0,9},{1,8},{2,11},{3,10},{4,13},{5,12},{6,15},{7,14},{8,1},{9,0},... | collective-permute-start | bytes 221192 | tf_op jit(solution)/shard_map/ppermute | solution.py:320
  35.8 5.3 %collective-permute-start.9 = (bf16[24,768]{1,0:T(8,128)(2,1)S(1)}, bf16[24,768]{1,0:T(8,128)(2,1)S(1)}, u32[]{:S(2)}, u32[]{:S(2)}) collective-permute-start(bf16[24,768]{1,0:T(8,128)(2,1)S(1)} %add_convert_fusion.1), channel_id=1, source_target_pairs={{0,17},{1,16},{2,19},{3,18},{4,21},{5,20},{6,23},{7,22},{8,25},{9,... | collective-permute-start | bytes 110600 | tf_op jit(solution)/shard_map/ppermute | solution.py:320
  41.1 4.9 %collective-permute-start.12 = (bf16[24,768]{1,0:T(8,128)(2,1)S(1)}, bf16[24,768]{1,0:T(8,128)(2,1)S(1)}, u32[]{:S(2)}, u32[]{:S(2)}) collective-permute-start(bf16[24,768]{1,0:T(8,128)(2,1)S(1)} %add_convert_fusion), channel_id=1, source_target_pairs={{0,6},{1,7},{2,4},{3,5},{4,2},{5,3},{6,0},{7,1},{8,14},{9,15},{10,... | collective-permute-start | bytes 110600 | tf_op jit(solution)/shard_map/ppermute | solution.py:320
  42.7 4.0 %collective-permute-start.11 = (bf16[24,768]{1,0:T(8,128)(2,1)S(1)}, bf16[24,768]{1,0:T(8,128)(2,1)S(1)}, u32[]{:S(2)}, u32[]{:S(2)}) collective-permute-start(bf16[24,768]{1,0:T(8,128)(2,1)S(1)} %add_convert_fusion), channel_id=1, source_target_pairs={{0,3},{1,2},{2,1},{3,0},{4,7},{5,6},{6,5},{7,4},{8,11},{9,10},{10,... | collective-permute-start | bytes 110600 | tf_op jit(solution)/shard_map/ppermute | solution.py:320
  42.9 3.8 %collective-permute-start.10 = (bf16[24,768]{1,0:T(8,128)(2,1)S(1)}, bf16[24,768]{1,0:T(8,128)(2,1)S(1)}, u32[]{:S(2)}, u32[]{:S(2)}) collective-permute-start(bf16[24,768]{1,0:T(8,128)(2,1)S(1)} %add_convert_fusion), channel_id=1, source_target_pairs={{0,5},{1,4},{2,7},{3,6},{4,1},{5,0},{6,3},{7,2},{8,13},{9,12},{10,... | collective-permute-start | bytes 110600 | tf_op jit(solution)/shard_map/ppermute | solution.py:320
  46.8 1.4 %collective-permute-start.13 = (bf16[4,24,768]{2,1,0:T(8,128)(2,1)S(1)}, bf16[4,24,768]{2,1,0:T(8,128)(2,1)S(1)}, u32[]{:S(2)}, u32[]{:S(2)}) collective-permute-start(bf16[4,24,768]{2,1,0:T(8,128)(2,1)S(1)} %pad_maximum_fusion.mine), channel_id=1, source_target_pairs={{0,1},{1,0},{2,3},{3,2},{4,5},{5,4},{6,7},{7,6},{8,9},{9,8},{10,11... | collective-permute-start | bytes 442376 | tf_op jit(solution)/shard_map/ppermute | solution.py:320

commit v7 on v5

--- a/solution.py
+++ b/solution.py
@@ -1,3 +1,5 @@
+import functools
+
 import jax
 import jax.numpy as jnp
 from jax import lax
@@ -12,8 +14,8 @@
 BF = jnp.bfloat16
 F32 = jnp.float32
 AXES = ("seq", "dp")
+COST = pl.CostEstimate(flops=10**6, bytes_accessed=10**4, transcendentals=0)
 VMEM = pl.BlockSpec(memory_space=pltpu.VMEM)
-TOGETHER = 8
 LIMIT = 48 * 1024 * 1024
 
 
@@ -88,51 +90,33 @@
     )
 
 
-def local_kernel(frozen, grad, low_t, up, far_out, up_out, rank_out):
-    count, width = grad.shape[1:]
-    half, half_width = count // 2, width // 2
-    low = [low_t[j] for j in range(3)]
-    low_f = [x.astype(F32) for x in low]
-    near_f = [x[:, half:] for x in low_f]
-    ranks = [jnp.zeros((RANK, count), F32)] * 3
-    full_mask = causal(count, count, 0)
-    half_mask = causal(half, half, 0)
-    for first in range(0, half_width, TOGETHER * HEAD_DIM):
-        items, places = [], []
-        for start in range(first, first + TOGETHER * HEAD_DIM, HEAD_DIM):
-            cols = slice(start, start + HEAD_DIM)
-            ups = [up[j, :, cols] for j in range(3)]
-            q, k, v = [project(frozen[j, 0, :, cols], low[j], ups[j]) for j in range(3)]
-            items.append((q, k, v, grad[0, :, cols], ups, low_f))
-            places.append(cols)
-        for cols, (grads, parts) in zip(places, heads(items, full_mask)):
-            for j in range(3):
-                up_out[8 * j : 8 * j + 8, cols] = grads[j]
-            ranks = [a + b for a, b in zip(ranks, parts)]
-    near_ranks = [jnp.zeros((RANK, half), F32)] * 3
-    for first in range(half_width, width, TOGETHER * HEAD_DIM):
-        items, places = [], []
-        for start in range(first, first + TOGETHER * HEAD_DIM, HEAD_DIM):
-            cols = slice(start, start + HEAD_DIM)
-            ups = [up[j, :, cols] for j in range(3)]
-            whole = [project(frozen[j, 0, :, cols], low[j], ups[j]) for j in range(3)]
-            for j in range(3):
-                far_out[j, :, start - half_width : start - half_width + HEAD_DIM] = whole[j][:half]
-            q, k, v = [x[half:] for x in whole]
-            items.append((q, k, v, grad[0, half:, cols], ups, near_f))
-            places.append(cols)
-        for cols, (grads, parts) in zip(places, heads(items, half_mask)):
-            for j in range(3):
-                up_out[8 * j : 8 * j + 8, cols] = grads[j]
-            near_ranks = [a + b for a, b in zip(near_ranks, parts)]
+def project_kernel(frozen, low_t, up, out):
     for j in range(3):
-        rank_out[8 * j : 8 * j + 8, :] = ranks[j] + jnp.concatenate(
-            [jnp.zeros((RANK, half), F32), near_ranks[j]], axis=1
-        )
-
-
-def far_items(own, near_kv, low_kv, grad, low_t, up, first):
-    half = own.shape[1]
+        for start in range(0, out.shape[2], 512):
+            cols = slice(start, start + 512)
+            out[j, :, cols] = project(frozen[j, 0, :, cols], low_t[j], up[j, :, cols])
+
+
+def group_kernel(first, start, projected, grad, low_t, up, up_out, rank_out):
+    count = grad.shape[1]
+    low = [low_t[j].astype(F32)[:, first:] for j in range(3)]
+    starts = range(0, up_out.shape[1], HEAD_DIM)
+    items = []
+    for h in starts:
+        cols = slice(start + h, start + h + HEAD_DIM)
+        q, k, v = [projected[j, first:, cols] for j in range(3)]
+        items.append((q, k, v, grad[0, first:, cols], [up[j, :, cols] for j in range(3)], low))
+    parts = heads(items, causal(count - first, count - first, 0))
+    for h, (grads, _) in zip(starts, parts):
+        for j in range(3):
+            up_out[8 * j : 8 * j + 8, h : h + HEAD_DIM] = grads[j]
+    for j in range(3):
+        part = sum(ranks[j] for _, ranks in parts)
+        rank_out[8 * j : 8 * j + 8, :] = right(part) if first else part
+
+
+def far_items(projected, near_kv, low_kv, grad, low_t, up, first):
+    half = projected.shape[1] // 2
     half_width = up.shape[2] // 2
     far_f = [low_t[j].astype(F32)[:, :half] for j in range(3)]
     lows = [far_f[0]] + [
@@ -140,11 +124,11 @@
     ]
     items = []
     for h, near in enumerate(near_kv):
-        here = slice(first + h * HEAD_DIM, first + (h + 1) * HEAD_DIM)
-        cols = slice(half_width + here.start, half_width + here.stop)
+        start = half_width + first + h * HEAD_DIM
+        cols = slice(start, start + HEAD_DIM)
         ups = [up[j, :, cols] for j in range(3)]
-        k, v = [jnp.concatenate([near[j], own[j + 1, :, here]], axis=0) for j in range(2)]
-        items.append((own[0, :, here], k, v, grad[0, :half, cols], ups, lows))
+        k, v = [jnp.concatenate([near[j], projected[j + 1, :half, cols]], axis=0) for j in range(2)]
+        items.append((projected[0, :half, cols], k, v, grad[0, :half, cols], ups, lows))
     return items
 
 
@@ -168,9 +152,9 @@
     return jnp.concatenate([jnp.zeros_like(x), x], axis=1)
 
 
-def far_first(own, frozen_kv, low_kv, grad, low_t, up, rank_in, up_out, rank_out, cross_out):
-    half = own.shape[1]
-    items = far_items(own, near_rows(frozen_kv, low_kv, up, 0), low_kv, grad, low_t, up, 0)
+def far_first(projected, frozen_kv, low_kv, grad, low_t, up, rank_in, up_out, rank_out, cross_out):
+    half = projected.shape[1] // 2
+    items = far_items(projected, near_rows(frozen_kv, low_kv, up, 0), low_kv, grad, low_t, up, 0)
     parts = heads(items, causal(2 * half, half, half))
     for h, (grads, _) in enumerate(parts):
         for j in range(3):
@@ -183,12 +167,12 @@
 
 
 def far_second(
-    own, frozen_kv, low_kv, grad, low_t, up, rank_in, cross_in, rank_out, cross_out, near_out, pb_out, ds_out, aq_out
+    projected, frozen_kv, low_kv, grad, low_t, up, rank_in, cross_in, rank_out, cross_out, near_out, pb_out, ds_out, aq_out
 ):
-    half = own.shape[1]
-    first = own.shape[2] - frozen_kv.shape[2]
+    half = projected.shape[1] // 2
+    first = projected.shape[2] // 2 - frozen_kv.shape[2]
     near = near_rows(frozen_kv, low_kv, up, first)
-    items = far_items(own, near, low_kv, grad, low_t, up, first)
+    items = far_items(projected, near, low_kv, grad, low_t, up, first)
     found = scores(items, causal(2 * half, half, half))
     rank_out[:8, :] = rank_in[:8, :]
     for j in (1, 2):
@@ -202,10 +186,10 @@
         aq_out[8 * h : 8 * h + 8, :] = f[2]
 
 
-def far_rest(own, low_kv, grad, low_t, up, rank_in, near, pb, ds, aq, up_out, rank_out):
+def far_rest(projected, low_kv, grad, low_t, up, rank_in, near, pb, ds, aq, up_out, rank_out):
     n = near.shape[0]
-    first = own.shape[2] - n * HEAD_DIM
-    items = far_items(own, [[near[h]] * 2 for h in range(n)], low_kv, grad, low_t, up, first)
+    first = projected.shape[2] // 2 - n * HEAD_DIM
+    items = far_items(projected, [[near[h]] * 2 for h in range(n)], low_kv, grad, low_t, up, first)
     parts = rest(items, [(pb[h], ds[h], aq[8 * h : 8 * h + 8, :]) for h in range(n)])
     for h, (grads, _) in enumerate(parts):
         for j in range(3):
@@ -222,18 +206,24 @@
     return bits & 1, (dp & 2) | (seq & 1)
 
 
-def down_kernel(tokens, rank_in, cross, up_in, up_a, up_b, keep, send):
+def down_kernel(tokens, rank_in, rank_near, cross, up_plain, up_near, up_a, up_b, keep, send):
     half, quarter = position()
     first = half == 0
-    ranks = rank_in[...] + jnp.concatenate([jnp.zeros((RANK, rank_in.shape[1]), F32), cross[...]], axis=0)
+    ranks = rank_in[...] + rank_near[...] + jnp.concatenate(
+        [jnp.zeros((RANK, rank_in.shape[1]), F32), cross[...]], axis=0
+    )
     both = rows(hi_lo(ranks))
     n = ranks.shape[0]
-    up_step, down_step = up_in.shape[1] // 8, tokens.shape[2] // 8
+    up_step, down_step = up_a.shape[1] // 2, tokens.shape[2] // 8
     for c in range(4):
         d = nn(both, tokens[0, :, 2 * c * down_step : 2 * (c + 1) * down_step])
         d = ADAPTER_SCALE * (d[:n] + d[n:])
-        u = up_in[:, 2 * c * up_step : 2 * (c + 1) * up_step]
-        u = ADAPTER_SCALE * (u + (up_a[...] if c == 2 else up_b[...]) if c >= 2 else u)
+        cols = slice((c % 2) * 2 * up_step, (c % 2 + 1) * 2 * up_step)
+        if c < 2:
+            u = up_plain[:, cols]
+        else:
+            u = up_near[:, cols] + (up_a if c == 2 else up_b)[...]
+        u = ADAPTER_SCALE * u
         slot = quarter ^ c
         keep[slot, :, :up_step] = jnp.where(first, u[:, :up_step], u[:, up_step:])
         send[slot, :, :up_step] = jnp.where(first, u[:, up_step:], u[:, :up_step])
@@ -263,7 +253,7 @@
         in_specs=[VMEM] * len(args),
         out_specs=jax.tree.map(lambda _: VMEM, outs),
         compiler_params=pltpu.CompilerParams(vmem_limit_bytes=LIMIT),
-        cost_estimate=pl.CostEstimate(flops=10**9, bytes_accessed=10**6, transcendentals=0),
+        cost_estimate=COST,
     )(*args)
 
 
@@ -302,28 +292,32 @@
     low_t = jnp.einsum("psw,gw->psg", down_weight, tokens[0], preferred_element_type=F32).astype(BF)
     low_kv = lax.ppermute(low_t[1:, :, half:], "seq", forward)
     sds = jax.ShapeDtypeStruct
-    own, up_part, rank = call(
-        local_kernel,
-        [sds((3, half, half_width), BF), sds((24, width), F32), sds((24, count), F32)],
-        frozen, grad, low_t, up_weight,
-    )
-    up_side, rank_side, cross_side = sds((24, half_width // 2), F32), sds((24, count), F32), sds((16, count), F32)
+    up_half, up_side = sds((24, half_width), F32), sds((24, half_width // 2), F32)
+    rank_side, cross_side = sds((24, count), F32), sds((16, count), F32)
+    projected = call(project_kernel, sds((3, count, width), BF), frozen, low_t, up_weight)
+    up_plain, rank = call(
+        functools.partial(group_kernel, 0, 0), [up_half, rank_side], projected, grad, low_t, up_weight
+    )
     up_a, rank, cross = call(
         far_first, [up_side, rank_side, cross_side],
-        own, frozen_kv[0], low_kv, grad, low_t, up_weight, rank,
+        projected, frozen_kv[0], low_kv, grad, low_t, up_weight, rank,
     )
     n = half_width // HEAD_DIM // 2
     by_keys = sds((n, count, half), BF)
     rank, cross, *kept = call(
         far_second,
         [rank_side, cross_side, sds((n, half, HEAD_DIM), BF), by_keys, by_keys, sds((8 * n, count), F32)],
-        own, frozen_kv[1], low_kv, grad, low_t, up_weight, rank, cross,
-    )
+        projected, frozen_kv[1], low_kv, grad, low_t, up_weight, rank, cross,
+    )
+    rank, *held = lax.optimization_barrier((rank, grad, low_t, up_weight))
     cross = lax.ppermute(cross, "seq", backward)
-    up_b, rank = call(far_rest, [up_side, rank_side], own, low_kv, grad, low_t, up_weight, rank, *kept)
+    up_near, rank_near = call(
+        functools.partial(group_kernel, half, half_width), [up_half, rank_side], projected, *held
+    )
+    up_b, rank = call(far_rest, [up_side, rank_side], projected, low_kv, grad, low_t, up_weight, rank, *kept)
     columns = (width + tokens.shape[2]) // 8
     piece = sds((4, 24, columns), F32)
-    keep, send = call(down_kernel, [piece, piece], tokens, rank, cross, up_part, up_a, up_b)
+    keep, send = call(down_kernel, [piece, piece], tokens, rank, rank_near, cross, up_plain, up_near, up_a, up_b)
     mine, other = total_sum(keep, send, seqs, dps)
     return tuple(
         call(spread_kernel, [sds((3, RANK, tokens.shape[2]), F32), sds((3, RANK, width), F32)], mine, other)

time: 46.2 us -> 46 us (level)
  waiting for transfers between devices: 16 us -> 18.8 us
  starting transfers between devices: 18.6 us -> 16 us
  local copies, waits for them, and re-layouts: 2.29 us -> 1.7 us
    ppermute x1, waiting for transfers between devices: 0.01 us -> 2.6 us  [on_device(): low_kv = lax.ppermute(low_t[1:, :, half:], 'seq', forward)]
    ppermute x10, starting transfers between devices: 10.1 us -> 8.27 us  [swap(): return lax.ppermute(x, AXES, [(i, i ^ bits) for i in range(total)])]
    ppermute x10, waiting for transfers between devices: 14.3 us -> 15.9 us  [swap(): return lax.ppermute(x, AXES, [(i, i ^ bits) for i in range(total)])]
    ppermute x1, starting transfers between devices: 2.48 us -> 1.65 us  [on_device(): cross = lax.ppermute(cross, 'seq', backward)]
    ppermute x1, waiting for transfers between devices: 0.81 us -> 0.01 us  [on_device(): lax.ppermute(frozen[1:, 0, half:, middle:], 'seq', forward)]
    ppermute x1, waiting for transfers between devices: 0.89 us -> 0.29 us  [on_device(): cross = lax.ppermute(cross, 'seq', backward)]
    unnamed x12 -> x10, local copies, waits for them, and re-layouts: 1.07 us -> 0.48 us
    pallas_call x6 -> x8, Pallas kernels: 6.65 us -> 6.89 us  [call(): pl.pallas_call(kernel, out_shape=outs, in_specs=[VMEM] * len(args), out_s...]
  transfers between devices with their start and end apart: 14 -> 14, of which waited for: 11 -> 11; matrix products, arithmetic and copies ran while one was open for 4% -> 4% of each run, Pallas kernels for 10% -> 11%
where the time goes in v7:
time: 46 us; the launch traced here: 45.8 us
  waiting for transfers between devices  18.8 us (41%)
  starting transfers between devices  16 us (35%)
  Pallas kernels  6.89 us (15%)
  local copies, waits for them, and re-layouts  1.7 us (4%)
  matrix products  1.6 us (3%)
  between operations  0.78 us (2%)
    ppermute x10, waiting for transfers between devices, swap(): return lax.ppermute(x, AXES, [(i, i ^ bits) for i in range(total)])  15.9 us
    ppermute x10, starting transfers between devices, swap(): return lax.ppermute(x, AXES, [(i, i ^ bits) for i in range(total)])  8.27 us
    pallas_call x8, Pallas kernels, call(): pl.pallas_call(kernel, out_shape=outs, in_specs=[VMEM] * len(args), out_s...  6.89 us
    ppermute x1, starting transfers between devices, on_device(): lax.ppermute(frozen[1:, 0, half:, half_width:middle], 'seq', forward)  2.99 us
    ppermute x1, waiting for transfers between devices, on_device(): low_kv = lax.ppermute(low_t[1:, :, half:], 'seq', forward)  2.6 us
    ppermute x1, starting transfers between devices, on_device(): cross = lax.ppermute(cross, 'seq', backward)  1.65 us
    dot_general x1, matrix products, on_device(): jnp.einsum('psw,gw->psg', down_weight, tokens[0], preferred_element_type=...  1.6 us
    ppermute x1, starting transfers between devices, on_device(): lax.ppermute(frozen[1:, 0, half:, middle:], 'seq', forward)  1.55 us
  transfers between devices with their start and end apart: 14, of which 11 were waited for; matrix products, arithmetic and copies ran while one was open for 4% of the time, Pallas kernels for 11%

profile of v7, /device:TPU:0, one launch (start us, length us, event | category | flops | bytes accessed | tf_op | source)
XLA Modules:
  0.0 45.8 jit_solution(9601938358483394554)
XLA Ops:
  0.7 1.1 %slice_bitcast_fusion = (bf16[2,64,512]{2,1,0:T(8,128)(2,1)S(1)}, bf16[2,64,512]{2,1,0:T(8,128)(2,1)S(1)}) fusion(bf16[3,1,128,2048]{3,2,0,1:T(8,128)(2,1)} %bitcast.29), kind=kLoop, calls=%fused_computation.3 | loop fusion | bytes 524288 | tf_op jit(solution)/shard_map/squeeze | solution.py:289
  1.8 3.0 %collective-permute-start.2 = (bf16[2,64,512]{2,1,0:T(8,128)(2,1)S(1)}, bf16[2,64,512]{2,1,0:T(8,128)(2,1)S(1)}, u32[]{:S(2)}, u32[]{:S(2)}) collective-permute-start(bf16[2,64,512]{2,1,0:T(8,128)(2,1)S(1)} %get-tuple-element.46), channel_id=1, source_target_pairs={{0,4},{4,8},{8,12},{12,16},{16,20},{20,24},{24,28},{28,0},{1,5},{5... | collective-permute-start | bytes 393224 | tf_op jit(solution)/shard_map/ppermute | solution.py:289
  4.8 1.5 %collective-permute-start.1 = (bf16[2,64,512]{2,1,0:T(8,128)(2,1)S(1)}, bf16[2,64,512]{2,1,0:T(8,128)(2,1)S(1)}, u32[]{:S(2)}, u32[]{:S(2)}) collective-permute-start(bf16[2,64,512]{2,1,0:T(8,128)(2,1)S(1)} %get-tuple-element.47), channel_id=1, source_target_pairs={{0,4},{4,8},{8,12},{12,16},{16,20},{20,24},{24,28},{28,0},{1,5},{5... | collective-permute-start | bytes 393224 | tf_op jit(solution)/shard_map/ppermute | solution.py:290
  6.3 1.6 %convolution_convert_fusion.low_t = bf16[3,8,128]{2,1,0:T(8,128)(2,1)S(1)} fusion(bf16[3,8,4096]{2,1,0:T(8,128)(2,1)S(1)} %copy-done, bf16[1,128,4096]{2,1,0:T(8,128)(2,1)} %tokens.1), kind=kOutput, calls=%fused_computation | convolution fusion | flops 25168896 | bytes 1251328 | tf_op jit(solution)/shard_map/psw,gw->psg/dot_general | solution.py:292
  8.0 1.5 %collective-permute-start = (bf16[2,8,64]{2,1,0:T(8,128)(2,1)S(1)}, bf16[2,8,64]{2,1,0:T(8,128)(2,1)S(1)}, u32[]{:S(2)}, u32[]{:S(2)}) collective-permute-start(bf16[2,8,64]{2,1,0:T(8,128)(2,1)S(1)} %slice.31), channel_id=1, source_target_pairs={{0,4},{4,8},{8,12},{12,16},{16,20},{20,24},{24,28},{28,0},{1,5},{5... | collective-permute-start | bytes 6152 | tf_op jit(solution)/shard_map/ppermute | solution.py:293
  9.5 0.6 %shard_map.68.projected = bf16[3,128,2048]{2,1,0:T(8,128)(2,1)S(1)} custom-call(bf16[3,1,128,2048]{3,2,1,0:T(8,128)(2,1)S(1)} %copy-done.4, bf16[3,8,128]{2,1,0:T(8,128)(2,1)S(1)} %convolution_convert_fusion.low_t, bf16[3,8,2048]{2,1,0:T(8,128)(2,1)S(1)} %copy-done.3), custom_call_target="tpu_custom_call" | custom-call | flops 1000000 | bytes 10000 | tf_op jit(solution)/shard_map/pallas_call | solution.py:250
  10.1 1.6 %shard_map.69 = (f32[24,1024]{1,0:T(8,128)S(1)}, f32[24,128]{1,0:T(8,128)S(1)}) custom-call(bf16[3,128,2048]{2,1,0:T(8,128)(2,1)S(1)} %shard_map.68.projected, bf16[1,128,2048]{2,1,0:T(8,128)(2,1)S(1)} %copy-done.1, bf16[3,8,128]{2,1,0:T(8,128)(2,1)S(1)} %convolution_convert_fusion.low_t, bf16[3,8,2048]{2,1,0:T(8,128)(2,1)S(1)} %copy-done.3), custom_call_target="tpu_custom_call" | custom-call | flops 1000000 | bytes 10000 | tf_op jit(solution)/shard_map/pallas_call | solution.py:250
  11.7 2.6 %collective-permute-done.low_kv = bf16[2,8,64]{2,1,0:T(8,128)(2,1)S(1)} collective-permute-done((bf16[2,8,64]{2,1,0:T(8,128)(2,1)S(1)}, bf16[2,8,64]{2,1,0:T(8,128)(2,1)S(1)}, u32[]{:S(2)}, u32[]{:S(2)}) %collective-permute-start) | collective-permute-done | bytes 2080 | tf_op jit(solution)/shard_map/ppermute | solution.py:293
  14.3 1.1 %shard_map.70 = (f32[24,512]{1,0:T(8,128)S(1)}, f32[24,128]{1,0:T(8,128)S(1)}, f32[16,128]{1,0:T(8,128)S(1)}) custom-call(bf16[3,128,2048]{2,1,0:T(8,128)(2,1)S(1)} %shard_map.68.projected, bf16[2,64,512]{2,1,0:T(8,128)(2,1)S(1)} %collective-permute-done.2.frozen_kv, bf16[2,8,64]{2,1,0:T(8,128)(2,1)S(1)} %collective-permute-done.low_kv, ...), custom_call_target="tpu_custom_call" | custom-call | flops 1000000 | bytes 10000 | tf_op jit(solution)/shard_map/pallas_call | solution.py:250
  15.4 0.8 %shard_map.71 = (f32[24,128]{1,0:T(8,128)S(1)}, f32[16,128]{1,0:T(8,128)S(1)}, bf16[4,64,128]{2,1,0:T(8,128)(2,1)S(1)}, bf16[4,128,64]{2,1,0:T(8,128)(2,1)S(1)},...) custom-call(bf16[3,128,2048]{2,1,0:T(8,128)(2,1)S(1)} %shard_map.68.projected, ...), custom_call_target="tpu_custom_call" | custom-call | flops 1000000 | bytes 10000 | tf_op jit(solution)/shard_map/pallas_call | solution.py:250
  16.2 1.6 %collective-permute-start.3 = (f32[16,128]{1,0:T(8,128)S(1)}, f32[16,128]{1,0:T(8,128)S(1)}, u32[]{:S(2)}, u32[]{:S(2)}) collective-permute-start(f32[16,128]{1,0:T(8,128)S(1)} %get-tuple-element.37), channel_id=1, source_target_pairs={{0,28},{4,0},{8,4},{12,8},{16,12},{20,16},{24,20},{28,24},{1,29},{... | collective-permute-start | bytes 24584 | tf_op jit(solution)/shard_map/ppermute | solution.py:313
  17.8 1.2 %shard_map.73 = (f32[24,1024]{1,0:T(8,128)S(1)}, f32[24,128]{1,0:T(8,128)S(1)}) custom-call(bf16[3,128,2048]{2,1,0:T(8,128)(2,1)S(1)} %shard_map.68.projected, bf16[1,128,2048]{2,1,0:T(8,128)(2,1)S(1)} %copy-done.1, bf16[3,8,128]{2,1,0:T(8,128)(2,1)S(1)} %convolution_convert_fusion.low_t, bf16[3,8,2048]{2,1,0:T(8,128)(2,1)S(1)} %copy-done.3), custom_call_target="tpu_custom_call" | custom-call | flops 1000000 | bytes 10000 | tf_op jit(solution)/shard_map/pallas_call | solution.py:250
  19.1 0.5 %shard_map.72 = (f32[24,512]{1,0:T(8,128)S(1)}, f32[24,128]{1,0:T(8,128)S(1)}) custom-call(bf16[3,128,2048]{2,1,0:T(8,128)(2,1)S(1)} %shard_map.68.projected, bf16[2,8,64]{2,1,0:T(8,128)(2,1)S(1)} %collective-permute-done.low_kv, bf16[1,128,2048]{2,1,0:T(8,128)(2,1)S(1)} %copy-done.1, bf16[3,8,128]{2,1,0:T(8,128)(2,1)S(1)} %convolution_convert_fusion.low_t, ...), custom_call_target="tpu_custom_call" | custom-call | flops 1000000 | bytes 10000 | tf_op jit(solution)/shard_map/pallas_call | solution.py:250
  19.6 0.3 collective-permute-done.3.cross
  19.9 0.5 copy-done.2
  20.3 0.3 shard_map.74
  20.7 1.6 %collective-permute-done.4 = f32[4,24,768]{2,1,0:T(8,128)S(1)} collective-permute-done((f32[4,24,768]{2,1,0:T(8,128)S(1)}, f32[4,24,768]{2,1,0:T(8,128)S(1)}, u32[]{:S(2)}, u32[]{:S(2)}) %collective-permute-start.4) | collective-permute-done | bytes 294944 | tf_op jit(solution)/shard_map/ppermute | solution.py:261
  22.3 0.2 collective-permute-start.5
  22.6 2.6 %collective-permute-start.7 = (bf16[24,768]{1,0:T(8,128)(2,1)S(1)}, bf16[24,768]{1,0:T(8,128)(2,1)S(1)}, u32[]{:S(2)}, u32[]{:S(2)}) collective-permute-start(bf16[24,768]{1,0:T(8,128)(2,1)S(1)} %get-tuple-element.49), channel_id=1, source_target_pairs={{0,6},{1,7},{2,4},{3,5},{4,2},{5,3},{6,0},{7,1},{8,14},{9,15},{10,... | collective-permute-start | bytes 110600 | tf_op jit(solution)/shard_map/ppermute | solution.py:261
  25.3 0.5 %collective-permute-done.5 = bf16[24,768]{1,0:T(8,128)(2,1)S(1)} collective-permute-done((bf16[24,768]{1,0:T(8,128)(2,1)S(1)}, bf16[24,768]{1,0:T(8,128)(2,1)S(1)}, u32[]{:S(2)}, u32[]{:S(2)}) %collective-permute-start.5) | collective-permute-done | bytes 36896 | tf_op jit(solution)/shard_map/ppermute | solution.py:261
  25.9 2.1 %collective-permute-done.7 = bf16[24,768]{1,0:T(8,128)(2,1)S(1)} collective-permute-done((bf16[24,768]{1,0:T(8,128)(2,1)S(1)}, bf16[24,768]{1,0:T(8,128)(2,1)S(1)}, u32[]{:S(2)}, u32[]{:S(2)}) %collective-permute-start.7) | collective-permute-done | bytes 36896 | tf_op jit(solution)/shard_map/ppermute | solution.py:261
  27.9 0.7 %collective-permute-done.6 = bf16[24,768]{1,0:T(8,128)(2,1)S(1)} collective-permute-done((bf16[24,768]{1,0:T(8,128)(2,1)S(1)}, bf16[24,768]{1,0:T(8,128)(2,1)S(1)}, u32[]{:S(2)}, u32[]{:S(2)}) %collective-permute-start.6) | collective-permute-done | bytes 36896 | tf_op jit(solution)/shard_map/ppermute | solution.py:261
  28.8 4.3 %collective-permute-done.8 = f32[24,768]{1,0:T(8,128)S(1)} collective-permute-done((f32[24,768]{1,0:T(8,128)S(1)}, f32[24,768]{1,0:T(8,128)S(1)}, u32[]{:S(2)}, u32[]{:S(2)}) %collective-permute-start.8) | collective-permute-done | bytes 73760 | tf_op jit(solution)/shard_map/ppermute | solution.py:261
  33.0 1.7 %collective-permute-start.9 = (bf16[24,768]{1,0:T(8,128)(2,1)S(1)}, bf16[24,768]{1,0:T(8,128)(2,1)S(1)}, u32[]{:S(2)}, u32[]{:S(2)}) collective-permute-start(bf16[24,768]{1,0:T(8,128)(2,1)S(1)} %add_convert_fusion.1), channel_id=1, source_target_pairs={{0,17},{1,16},{2,19},{3,18},{4,21},{5,20},{6,23},{7,22},{8,25},{9,... | collective-permute-start | bytes 110600 | tf_op jit(solution)/shard_map/ppermute | solution.py:261
  34.7 2.8 %collective-permute-done.9 = bf16[24,768]{1,0:T(8,128)(2,1)S(1)} collective-permute-done((bf16[24,768]{1,0:T(8,128)(2,1)S(1)}, bf16[24,768]{1,0:T(8,128)(2,1)S(1)}, u32[]{:S(2)}, u32[]{:S(2)}) %collective-permute-start.9) | collective-permute-done | bytes 36896 | tf_op jit(solution)/shard_map/ppermute | solution.py:261
  37.5 1.5 %collective-permute-start.12 = (bf16[24,768]{1,0:T(8,128)(2,1)S(1)}, bf16[24,768]{1,0:T(8,128)(2,1)S(1)}, u32[]{:S(2)}, u32[]{:S(2)}) collective-permute-start(bf16[24,768]{1,0:T(8,128)(2,1)S(1)} %add_convert_fusion), channel_id=1, source_target_pairs={{0,6},{1,7},{2,4},{3,5},{4,2},{5,3},{6,0},{7,1},{8,14},{9,15},{10,... | collective-permute-start | bytes 110600 | tf_op jit(solution)/shard_map/ppermute | solution.py:261
  39.0 0.7 %collective-permute-start.11 = (bf16[24,768]{1,0:T(8,128)(2,1)S(1)}, bf16[24,768]{1,0:T(8,128)(2,1)S(1)}, u32[]{:S(2)}, u32[]{:S(2)}) collective-permute-start(bf16[24,768]{1,0:T(8,128)(2,1)S(1)} %add_convert_fusion), channel_id=1, source_target_pairs={{0,3},{1,2},{2,1},{3,0},{4,7},{5,6},{6,5},{7,4},{8,11},{9,10},{10,... | collective-permute-start | bytes 110600 | tf_op jit(solution)/shard_map/ppermute | solution.py:261
  39.7 1.1 %collective-permute-start.10 = (bf16[24,768]{1,0:T(8,128)(2,1)S(1)}, bf16[24,768]{1,0:T(8,128)(2,1)S(1)}, u32[]{:S(2)}, u32[]{:S(2)}) collective-permute-start(bf16[24,768]{1,0:T(8,128)(2,1)S(1)} %add_convert_fusion), channel_id=1, source_target_pairs={{0,5},{1,4},{2,7},{3,6},{4,1},{5,0},{6,3},{7,2},{8,13},{9,12},{10,... | collective-permute-start | bytes 110600 | tf_op jit(solution)/shard_map/ppermute | solution.py:261
  40.8 2.1 %collective-permute-done.12 = bf16[24,768]{1,0:T(8,128)(2,1)S(1)} collective-permute-done((bf16[24,768]{1,0:T(8,128)(2,1)S(1)}, bf16[24,768]{1,0:T(8,128)(2,1)S(1)}, u32[]{:S(2)}, u32[]{:S(2)}) %collective-permute-start.12) | collective-permute-done | bytes 36896 | tf_op jit(solution)/shard_map/ppermute | solution.py:261
  42.8 0.6 %collective-permute-done.11 = bf16[24,768]{1,0:T(8,128)(2,1)S(1)} collective-permute-done((bf16[24,768]{1,0:T(8,128)(2,1)S(1)}, bf16[24,768]{1,0:T(8,128)(2,1)S(1)}, u32[]{:S(2)}, u32[]{:S(2)}) %collective-permute-start.11) | collective-permute-done | bytes 36896 | tf_op jit(solution)/shard_map/ppermute | solution.py:261
  43.7 1.3 %collective-permute-done.13.other = bf16[4,24,768]{2,1,0:T(8,128)(2,1)S(1)} collective-permute-done((bf16[4,24,768]{2,1,0:T(8,128)(2,1)S(1)}, bf16[4,24,768]{2,1,0:T(8,128)(2,1)S(1)}, u32[]{:S(2)}, u32[]{:S(2)}) %collective-permute-start.13) | collective-permute-done | bytes 147488 | tf_op jit(solution)/shard_map/ppermute | solution.py:261
  44.9 0.9 %shard_map.75 = (f32[3,8,4096]{2,1,0:T(8,128)}, f32[3,8,2048]{2,1,0:T(8,128)}) custom-call(bf16[4,24,768]{2,1,0:T(8,128)(2,1)S(1)} %pad_maximum_fusion.mine, bf16[4,24,768]{2,1,0:T(8,128)(2,1)S(1)} %collective-permute-done.13.other), custom_call_target="tpu_custom_call" | custom-call | flops 1000000 | bytes 10000 | tf_op jit(solution)/shard_map/pallas_call | solution.py:250
  (23 shorter events, 0.8 us)
Async XLA Ops:
  0.6 5.7 %copy-start = (bf16[3,8,4096]{2,1,0:T(8,128)(2,1)S(1)}, bf16[3,8,4096]{2,1,0:T(8,128)(2,1)}, u32[]{:S(2)}) copy-start(bf16[3,8,4096]{2,1,0:T(8,128)(2,1)} %param.8) | copy-start | bytes 589828
  0.6 8.9 %copy-start.4 = (bf16[3,1,128,2048]{3,2,1,0:T(8,128)(2,1)S(1)}, bf16[3,1,128,2048]{3,2,1,0:T(8,128)(2,1)}, u32[]{:S(2)}) copy-start(bf16[3,1,128,2048]{3,2,1,0:T(8,128)(2,1)} %frozen.1) | copy-start | bytes 4718596
  0.7 8.9 %copy-start.3 = (bf16[3,8,2048]{2,1,0:T(8,128)(2,1)S(1)}, bf16[3,8,2048]{2,1,0:T(8,128)(2,1)}, u32[]{:S(2)}) copy-start(bf16[3,8,2048]{2,1,0:T(8,128)(2,1)} %up.10) | copy-start | bytes 294916
  1.8 12.5 %collective-permute-start.2 = (bf16[2,64,512]{2,1,0:T(8,128)(2,1)S(1)}, bf16[2,64,512]{2,1,0:T(8,128)(2,1)S(1)}, u32[]{:S(2)}, u32[]{:S(2)}) collective-permute-start(bf16[2,64,512]{2,1,0:T(8,128)(2,1)S(1)} %get-tuple-element.46), channel_id=1, source_target_pairs={{0,4},{4,8},{8,12},{12,16},{16,20},{20,24},{24,28},{28,0},{1,5},{5... | collective-permute-start | bytes 393224 | tf_op jit(solution)/shard_map/ppermute | solution.py:289
  4.8 10.6 %collective-permute-start.1 = (bf16[2,64,512]{2,1,0:T(8,128)(2,1)S(1)}, bf16[2,64,512]{2,1,0:T(8,128)(2,1)S(1)}, u32[]{:S(2)}, u32[]{:S(2)}) collective-permute-start(bf16[2,64,512]{2,1,0:T(8,128)(2,1)S(1)} %get-tuple-element.47), channel_id=1, source_target_pairs={{0,4},{4,8},{8,12},{12,16},{16,20},{20,24},{24,28},{28,0},{1,5},{5... | collective-permute-start | bytes 393224 | tf_op jit(solution)/shard_map/ppermute | solution.py:290
  8.0 2.1 %copy-start.1 = (bf16[1,128,2048]{2,1,0:T(8,128)(2,1)S(1)}, bf16[1,128,2048]{2,1,0:T(8,128)(2,1)}, u32[]{:S(2)}) copy-start(bf16[1,128,2048]{2,1,0:T(8,128)(2,1)} %grad.8) | copy-start | bytes 1572868
  8.0 6.3 %collective-permute-start = (bf16[2,8,64]{2,1,0:T(8,128)(2,1)S(1)}, bf16[2,8,64]{2,1,0:T(8,128)(2,1)S(1)}, u32[]{:S(2)}, u32[]{:S(2)}) collective-permute-start(bf16[2,8,64]{2,1,0:T(8,128)(2,1)S(1)} %slice.31), channel_id=1, source_target_pairs={{0,4},{4,8},{8,12},{12,16},{16,20},{20,24},{24,28},{28,0},{1,5},{5... | collective-permute-start | bytes 6152 | tf_op jit(solution)/shard_map/ppermute | solution.py:293
  16.2 3.7 %collective-permute-start.3 = (f32[16,128]{1,0:T(8,128)S(1)}, f32[16,128]{1,0:T(8,128)S(1)}, u32[]{:S(2)}, u32[]{:S(2)}) collective-permute-start(f32[16,128]{1,0:T(8,128)S(1)} %get-tuple-element.37), channel_id=1, source_target_pairs={{0,28},{4,0},{8,4},{12,8},{16,12},{20,16},{24,20},{28,24},{1,29},{... | collective-permute-start | bytes 24584 | tf_op jit(solution)/shard_map/ppermute | solution.py:313
  19.1 1.2 %copy-start.2 = (bf16[1,128,4096]{2,1,0:T(8,128)(2,1)S(1)}, bf16[1,128,4096]{2,1,0:T(8,128)(2,1)}, u32[]{:S(2)}) copy-start(bf16[1,128,4096]{2,1,0:T(8,128)(2,1)} %tokens.1) | copy-start | bytes 3145732
  20.6 1.6 %collective-permute-start.4 = (f32[4,24,768]{2,1,0:T(8,128)S(1)}, f32[4,24,768]{2,1,0:T(8,128)S(1)}, u32[]{:S(2)}, u32[]{:S(2)}) collective-permute-start(f32[4,24,768]{2,1,0:T(8,128)S(1)} %get-tuple-element.43), channel_id=1, source_target_pairs={{0,1},{1,0},{2,3},{3,2},{4,5},{5,4},{6,7},{7,6},{8,9},{9,8},{10,11... | collective-permute-start | bytes 884744 | tf_op jit(solution)/shard_map/ppermute | solution.py:261
  22.3 3.5 %collective-permute-start.5 = (bf16[24,768]{1,0:T(8,128)(2,1)S(1)}, bf16[24,768]{1,0:T(8,128)(2,1)S(1)}, u32[]{:S(2)}, u32[]{:S(2)}) collective-permute-start(bf16[24,768]{1,0:T(8,128)(2,1)S(1)} %get-tuple-element.48), channel_id=1, source_target_pairs={{0,5},{1,4},{2,7},{3,6},{4,1},{5,0},{6,3},{7,2},{8,13},{9,12},{10,... | collective-permute-start | bytes 110600 | tf_op jit(solution)/shard_map/ppermute | solution.py:261
  22.6 5.4 %collective-permute-start.7 = (bf16[24,768]{1,0:T(8,128)(2,1)S(1)}, bf16[24,768]{1,0:T(8,128)(2,1)S(1)}, u32[]{:S(2)}, u32[]{:S(2)}) collective-permute-start(bf16[24,768]{1,0:T(8,128)(2,1)S(1)} %get-tuple-element.49), channel_id=1, source_target_pairs={{0,6},{1,7},{2,4},{3,5},{4,2},{5,3},{6,0},{7,1},{8,14},{9,15},{10,... | collective-permute-start | bytes 110600 | tf_op jit(solution)/shard_map/ppermute | solution.py:261
  25.1 3.5 %collective-permute-start.6 = (bf16[24,768]{1,0:T(8,128)(2,1)S(1)}, bf16[24,768]{1,0:T(8,128)(2,1)S(1)}, u32[]{:S(2)}, u32[]{:S(2)}) collective-permute-start(bf16[24,768]{1,0:T(8,128)(2,1)S(1)} %get-tuple-element.50), channel_id=1, source_target_pairs={{0,3},{1,2},{2,1},{3,0},{4,7},{5,6},{6,5},{7,4},{8,11},{9,10},{10,... | collective-permute-start | bytes 110600 | tf_op jit(solution)/shard_map/ppermute | solution.py:261
  28.7 4.3 %collective-permute-start.8 = (f32[24,768]{1,0:T(8,128)S(1)}, f32[24,768]{1,0:T(8,128)S(1)}, u32[]{:S(2)}, u32[]{:S(2)}) collective-permute-start(f32[24,768]{1,0:T(8,128)S(1)} %fusion.3), channel_id=1, source_target_pairs={{0,9},{1,8},{2,11},{3,10},{4,13},{5,12},{6,15},{7,14},{8,1},{9,0},... | collective-permute-start | bytes 221192 | tf_op jit(solution)/shard_map/ppermute | solution.py:261
  33.0 4.5 %collective-permute-start.9 = (bf16[24,768]{1,0:T(8,128)(2,1)S(1)}, bf16[24,768]{1,0:T(8,128)(2,1)S(1)}, u32[]{:S(2)}, u32[]{:S(2)}) collective-permute-start(bf16[24,768]{1,0:T(8,128)(2,1)S(1)} %add_convert_fusion.1), channel_id=1, source_target_pairs={{0,17},{1,16},{2,19},{3,18},{4,21},{5,20},{6,23},{7,22},{8,25},{9,... | collective-permute-start | bytes 110600 | tf_op jit(solution)/shard_map/ppermute | solution.py:261
  37.5 5.3 %collective-permute-start.12 = (bf16[24,768]{1,0:T(8,128)(2,1)S(1)}, bf16[24,768]{1,0:T(8,128)(2,1)S(1)}, u32[]{:S(2)}, u32[]{:S(2)}) collective-permute-start(bf16[24,768]{1,0:T(8,128)(2,1)S(1)} %add_convert_fusion), channel_id=1, source_target_pairs={{0,6},{1,7},{2,4},{3,5},{4,2},{5,3},{6,0},{7,1},{8,14},{9,15},{10,... | collective-permute-start | bytes 110600 | tf_op jit(solution)/shard_map/ppermute | solution.py:261
  39.0 4.5 %collective-permute-start.11 = (bf16[24,768]{1,0:T(8,128)(2,1)S(1)}, bf16[24,768]{1,0:T(8,128)(2,1)S(1)}, u32[]{:S(2)}, u32[]{:S(2)}) collective-permute-start(bf16[24,768]{1,0:T(8,128)(2,1)S(1)} %add_convert_fusion), channel_id=1, source_target_pairs={{0,3},{1,2},{2,1},{3,0},{4,7},{5,6},{6,5},{7,4},{8,11},{9,10},{10,... | collective-permute-start | bytes 110600 | tf_op jit(solution)/shard_map/ppermute | solution.py:261
  39.7 3.8 %collective-permute-start.10 = (bf16[24,768]{1,0:T(8,128)(2,1)S(1)}, bf16[24,768]{1,0:T(8,128)(2,1)S(1)}, u32[]{:S(2)}, u32[]{:S(2)}) collective-permute-start(bf16[24,768]{1,0:T(8,128)(2,1)S(1)} %add_convert_fusion), channel_id=1, source_target_pairs={{0,5},{1,4},{2,7},{3,6},{4,1},{5,0},{6,3},{7,2},{8,13},{9,12},{10,... | collective-permute-start | bytes 110600 | tf_op jit(solution)/shard_map/ppermute | solution.py:261
  43.5 1.4 %collective-permute-start.13 = (bf16[4,24,768]{2,1,0:T(8,128)(2,1)S(1)}, bf16[4,24,768]{2,1,0:T(8,128)(2,1)S(1)}, u32[]{:S(2)}, u32[]{:S(2)}) collective-permute-start(bf16[4,24,768]{2,1,0:T(8,128)(2,1)S(1)} %pad_maximum_fusion.mine), channel_id=1, source_target_pairs={{0,1},{1,0},{2,3},{3,2},{4,5},{5,4},{6,7},{7,6},{8,9},{9,8},{10,11... | collective-permute-start | bytes 442376 | tf_op jit(solution)/shard_map/ppermute | solution.py:261

commit v8 on v7

--- a/solution.py
+++ b/solution.py
@@ -115,7 +115,7 @@
         rank_out[8 * j : 8 * j + 8, :] = right(part) if first else part
 
 
-def far_items(projected, near_kv, low_kv, grad, low_t, up, first):
+def far_items(projected, near_kv, low_kv, grad, low_t, up):
     half = projected.shape[1] // 2
     half_width = up.shape[2] // 2
     far_f = [low_t[j].astype(F32)[:, :half] for j in range(3)]
@@ -124,7 +124,7 @@
     ]
     items = []
     for h, near in enumerate(near_kv):
-        start = half_width + first + h * HEAD_DIM
+        start = half_width + h * HEAD_DIM
         cols = slice(start, start + HEAD_DIM)
         ups = [up[j, :, cols] for j in range(3)]
         k, v = [jnp.concatenate([near[j], projected[j + 1, :half, cols]], axis=0) for j in range(2)]
@@ -132,12 +132,12 @@
     return items
 
 
-def near_rows(frozen_kv, low_kv, up, first):
+def near_rows(frozen_kv, low_kv, up):
     half_width = up.shape[2] // 2
     near = []
     for h in range(frozen_kv.shape[2] // HEAD_DIM):
         here = slice(h * HEAD_DIM, (h + 1) * HEAD_DIM)
-        start = half_width + first + h * HEAD_DIM
+        start = half_width + h * HEAD_DIM
         near.append(
             [project(frozen_kv[j, :, here], low_kv[j], up[j + 1, :, start : start + HEAD_DIM]) for j in range(2)]
         )
@@ -152,33 +152,18 @@
     return jnp.concatenate([jnp.zeros_like(x), x], axis=1)
 
 
-def far_first(projected, frozen_kv, low_kv, grad, low_t, up, rank_in, up_out, rank_out, cross_out):
-    half = projected.shape[1] // 2
-    items = far_items(projected, near_rows(frozen_kv, low_kv, up, 0), low_kv, grad, low_t, up, 0)
-    parts = heads(items, causal(2 * half, half, half))
-    for h, (grads, _) in enumerate(parts):
-        for j in range(3):
-            up_out[8 * j : 8 * j + 8, h * HEAD_DIM : (h + 1) * HEAD_DIM] = grads[j]
-    for j in range(3):
-        part = sum(ranks[j] for _, ranks in parts)
-        rank_out[8 * j : 8 * j + 8, :] = rank_in[8 * j : 8 * j + 8, :] + left(part[:, -half:])
-        if j > 0:
-            cross_out[8 * j - 8 : 8 * j, :] = right(part[:, :half])
-
-
-def far_second(
-    projected, frozen_kv, low_kv, grad, low_t, up, rank_in, cross_in, rank_out, cross_out, near_out, pb_out, ds_out, aq_out
+def far_scores(
+    projected, frozen_kv, low_kv, grad, low_t, up, rank_in, rank_out, cross_out, near_out, pb_out, ds_out, aq_out
 ):
     half = projected.shape[1] // 2
-    first = projected.shape[2] // 2 - frozen_kv.shape[2]
-    near = near_rows(frozen_kv, low_kv, up, first)
-    items = far_items(projected, near, low_kv, grad, low_t, up, first)
+    near = near_rows(frozen_kv, low_kv, up)
+    items = far_items(projected, near, low_kv, grad, low_t, up)
     found = scores(items, causal(2 * half, half, half))
-    rank_out[:8, :] = rank_in[:8, :]
     for j in (1, 2):
         part = sum(f[j + 2] for f in found)
+        cross_out[8 * j - 8 : 8 * j, :] = right(part[:, :half])
         rank_out[8 * j : 8 * j + 8, :] = rank_in[8 * j : 8 * j + 8, :] + left(part[:, half:])
-        cross_out[8 * j - 8 : 8 * j, :] = cross_in[8 * j - 8 : 8 * j, :] + right(part[:, :half])
+    rank_out[:8, :] = rank_in[:8, :]
     for h, f in enumerate(found):
         near_out[h] = near[h][0]
         pb_out[h] = f[0]
@@ -188,8 +173,7 @@
 
 def far_rest(projected, low_kv, grad, low_t, up, rank_in, near, pb, ds, aq, up_out, rank_out):
     n = near.shape[0]
-    first = projected.shape[2] // 2 - n * HEAD_DIM
-    items = far_items(projected, [[near[h]] * 2 for h in range(n)], low_kv, grad, low_t, up, first)
+    items = far_items(projected, [[near[h]] * 2 for h in range(n)], low_kv, grad, low_t, up)
     parts = rest(items, [(pb[h], ds[h], aq[8 * h : 8 * h + 8, :]) for h in range(n)])
     for h, (grads, _) in enumerate(parts):
         for j in range(3):
@@ -206,7 +190,7 @@
     return bits & 1, (dp & 2) | (seq & 1)
 
 
-def down_kernel(tokens, rank_in, rank_near, cross, up_plain, up_near, up_a, up_b, keep, send):
+def down_kernel(tokens, rank_in, rank_near, cross, up_plain, up_near, up_far, keep, send):
     half, quarter = position()
     first = half == 0
     ranks = rank_in[...] + rank_near[...] + jnp.concatenate(
@@ -214,7 +198,7 @@
     )
     both = rows(hi_lo(ranks))
     n = ranks.shape[0]
-    up_step, down_step = up_a.shape[1] // 2, tokens.shape[2] // 8
+    up_step, down_step = up_plain.shape[1] // 4, tokens.shape[2] // 8
     for c in range(4):
         d = nn(both, tokens[0, :, 2 * c * down_step : 2 * (c + 1) * down_step])
         d = ADAPTER_SCALE * (d[:n] + d[n:])
@@ -222,7 +206,7 @@
         if c < 2:
             u = up_plain[:, cols]
         else:
-            u = up_near[:, cols] + (up_a if c == 2 else up_b)[...]
+            u = up_near[:, cols] + up_far[:, cols]
         u = ADAPTER_SCALE * u
         slot = quarter ^ c
         keep[slot, :, :up_step] = jnp.where(first, u[:, :up_step], u[:, up_step:])
@@ -231,19 +215,29 @@
         send[slot, :, up_step:] = jnp.where(first, d[:, down_step:], d[:, :down_step])
 
 
-def spread_kernel(mine, other, down_out, up_out):
+def spread(pieces, own, down_out, up_out):
     half, quarter = position()
+    half = half if own else 1 - half
     up_step, down_step = up_out.shape[2] // 8, down_out.shape[2] // 8
     for c in range(4):
-        slot = quarter ^ c
-        a, b = mine[slot].astype(F32), other[slot].astype(F32)
-        for h in range(2):
-            x = jnp.where(half == h, a, b)
-            at = 2 * c + h
-            for j in range(3):
-                part = x[8 * j : 8 * j + 8]
-                up_out[j, :, at * up_step : (at + 1) * up_step] = part[:, :up_step]
-                down_out[j, :, at * down_step : (at + 1) * down_step] = part[:, up_step:]
+        x = pieces[quarter ^ c].astype(F32)
+        at = 2 * c + half
+        ups = pl.ds(pl.multiple_of(at * up_step, up_step), up_step)
+        downs = pl.ds(pl.multiple_of(at * down_step, down_step), down_step)
+        for j in range(3):
+            part = x[8 * j : 8 * j + 8]
+            up_out[j, :, ups] = part[:, :up_step]
+            down_out[j, :, downs] = part[:, up_step:]
+
+
+def first_spread(pieces, down_out, up_out):
+    spread(pieces, True, down_out, up_out)
+
+
+def last_spread(pieces, down_in, up_in, down_out, up_out):
+    down_out[...] = down_in[...]
+    up_out[...] = up_in[...]
+    spread(pieces, False, down_out, up_out)
 
 
 def call(kernel, outs, *args):
@@ -269,10 +263,16 @@
     own = keep[0] + got[0] + got[1] + got[2]
     bit = 2
     while bit < seqs:
-        if 2 * bit >= seqs:
+        steps = [bit, 2 * bit, 3 * bit] if 2 * bit < seqs else [bit]
+        bit *= len(steps) + 1
+        if bit >= seqs:
             own = own.astype(BF)
-        own = own.astype(F32) + swap(own, bit * dps | 1, total).astype(F32)
-        bit *= 2
+        parts = [swap(own, step * dps | (step & (step - 1) == 0), total) for step in steps]
+        own = own.astype(F32)
+        if len(parts) == 3:
+            own = (own + parts[0].astype(F32)) + (parts[1].astype(F32) + parts[2].astype(F32))
+        else:
+            own = own + parts[0].astype(F32)
     piece = own.astype(BF)
     mine = jnp.stack([piece] + [swap(piece, partner[s], total) for s in (1, 2, 3)])
     return mine, swap(mine, 1, total)
@@ -284,44 +284,37 @@
     half, half_width = count // 2, width // 2
     forward = [(i, (i + 1) % seqs) for i in range(seqs)]
     backward = [(i, (i - 1) % seqs) for i in range(seqs)]
-    middle = half_width + half_width // 2
-    frozen_kv = [
-        lax.ppermute(frozen[1:, 0, half:, half_width:middle], "seq", forward),
-        lax.ppermute(frozen[1:, 0, half:, middle:], "seq", forward),
-    ]
+    frozen_kv = lax.ppermute(frozen[1:, 0, half:, half_width:], "seq", forward)
     low_t = jnp.einsum("psw,gw->psg", down_weight, tokens[0], preferred_element_type=F32).astype(BF)
     low_kv = lax.ppermute(low_t[1:, :, half:], "seq", forward)
     sds = jax.ShapeDtypeStruct
-    up_half, up_side = sds((24, half_width), F32), sds((24, half_width // 2), F32)
-    rank_side, cross_side = sds((24, count), F32), sds((16, count), F32)
+    up_half, rank_side = sds((24, half_width), F32), sds((24, count), F32)
     projected = call(project_kernel, sds((3, count, width), BF), frozen, low_t, up_weight)
     up_plain, rank = call(
         functools.partial(group_kernel, 0, 0), [up_half, rank_side], projected, grad, low_t, up_weight
     )
-    up_a, rank, cross = call(
-        far_first, [up_side, rank_side, cross_side],
-        projected, frozen_kv[0], low_kv, grad, low_t, up_weight, rank,
-    )
-    n = half_width // HEAD_DIM // 2
+    n = half_width // HEAD_DIM
     by_keys = sds((n, count, half), BF)
     rank, cross, *kept = call(
-        far_second,
-        [rank_side, cross_side, sds((n, half, HEAD_DIM), BF), by_keys, by_keys, sds((8 * n, count), F32)],
-        projected, frozen_kv[1], low_kv, grad, low_t, up_weight, rank, cross,
+        far_scores,
+        [
+            rank_side, sds((16, count), F32), sds((n, half, HEAD_DIM), BF), by_keys, by_keys,
+            sds((8 * n, count), F32),
+        ],
+        projected, frozen_kv, low_kv, grad, low_t, up_weight, rank,
     )
     rank, *held = lax.optimization_barrier((rank, grad, low_t, up_weight))
     cross = lax.ppermute(cross, "seq", backward)
     up_near, rank_near = call(
         functools.partial(group_kernel, half, half_width), [up_half, rank_side], projected, *held
     )
-    up_b, rank = call(far_rest, [up_side, rank_side], projected, low_kv, grad, low_t, up_weight, rank, *kept)
+    up_far, rank = call(far_rest, [up_half, rank_side], projected, low_kv, grad, low_t, up_weight, rank, *kept)
     columns = (width + tokens.shape[2]) // 8
     piece = sds((4, 24, columns), F32)
-    keep, send = call(down_kernel, [piece, piece], tokens, rank, rank_near, cross, up_plain, up_near, up_a, up_b)
+    keep, send = call(down_kernel, [piece, piece], tokens, rank, rank_near, cross, up_plain, up_near, up_far)
     mine, other = total_sum(keep, send, seqs, dps)
-    return tuple(
-        call(spread_kernel, [sds((3, RANK, tokens.shape[2]), F32), sds((3, RANK, width), F32)], mine, other)
-    )
+    outs = [sds((3, RANK, tokens.shape[2]), F32), sds((3, RANK, width), F32)]
+    return tuple(call(last_spread, outs, other, *call(first_spread, outs, mine)))
 
 
 def solution(mesh):

time: 46 us -> 44.3 us (0.963)
  waiting for transfers between devices: 18.8 us -> 16.2 us
  starting transfers between devices: 16 us -> 17.3 us
  Pallas kernels: 6.89 us -> 6.3 us
    ppermute x10 -> x11, waiting for transfers between devices: 15.9 us -> 12.2 us  [swap(): return lax.ppermute(x, AXES, [(i, i ^ bits) for i in range(total)])]
    ppermute x10 -> x11, starting transfers between devices: 8.27 us -> 11 us  [swap(): return lax.ppermute(x, AXES, [(i, i ^ bits) for i in range(total)])]
    ppermute x2 -> x1, starting transfers between devices: 4.54 us -> 2.99 us  [on_device(): frozen_kv = lax.ppermute(frozen[1:, 0, half:, half_width:], 'seq', forward)]
    ppermute x1, waiting for transfers between devices: 2.6 us -> 3.96 us  [on_device(): low_kv = lax.ppermute(low_t[1:, :, half:], 'seq', forward)]
    pallas_call x8, Pallas kernels: 6.89 us -> 6.3 us  [call(): pl.pallas_call(kernel, out_shape=outs, in_specs=[VMEM] * len(args), out_s...]
  transfers between devices with their start and end apart: 14 -> 14, of which waited for: 11 -> 10; matrix products, arithmetic and copies ran while one was open for 4% -> 4% of each run, Pallas kernels for 11% -> 9%
where the time goes in v8:
time: 44.3 us; the launch traced here: 44.1 us
  starting transfers between devices  17.3 us (39%)
  waiting for transfers between devices  16.2 us (37%)
  Pallas kernels  6.3 us (14%)
  local copies, waits for them, and re-layouts  1.8 us (4%)
  matrix products  1.6 us (4%)
  between operations  0.75 us (2%)
    ppermute x11, waiting for transfers between devices, swap(): return lax.ppermute(x, AXES, [(i, i ^ bits) for i in range(total)])  12.2 us
    ppermute x11, starting transfers between devices, swap(): return lax.ppermute(x, AXES, [(i, i ^ bits) for i in range(total)])  11 us
    pallas_call x8, Pallas kernels, call(): pl.pallas_call(kernel, out_shape=outs, in_specs=[VMEM] * len(args), out_s...  6.3 us
    ppermute x1, waiting for transfers between devices, on_device(): low_kv = lax.ppermute(low_t[1:, :, half:], 'seq', forward)  3.96 us
    ppermute x1, starting transfers between devices, on_device(): frozen_kv = lax.ppermute(frozen[1:, 0, half:, half_width:], 'seq', forward)  2.99 us
    ppermute x1, starting transfers between devices, on_device(): cross = lax.ppermute(cross, 'seq', backward)  1.77 us
    dot_general x1, matrix products, on_device(): jnp.einsum('psw,gw->psg', down_weight, tokens[0], preferred_element_type=...  1.6 us
    ppermute x1, starting transfers between devices, on_device(): low_kv = lax.ppermute(low_t[1:, :, half:], 'seq', forward)  1.56 us
  transfers between devices with their start and end apart: 14, of which 10 were waited for; matrix products, arithmetic and copies ran while one was open for 4% of the time, Pallas kernels for 9%

profile of v8, /device:TPU:0, one launch (start us, length us, event | category | flops | bytes accessed | tf_op | source)
XLA Modules:
  0.0 44.1 jit_solution(11330822489809986738)
XLA Ops:
  0.7 1.1 %slice_bitcast_fusion = bf16[2,64,1024]{2,1,0:T(8,128)(2,1)S(1)} fusion(bf16[3,1,128,2048]{3,2,0,1:T(8,128)(2,1)} %bitcast.28), kind=kLoop, calls=%fused_computation.2 | loop fusion | bytes 524288 | tf_op jit(solution)/shard_map/squeeze | solution.py:287
  1.8 3.0 %collective-permute-start.1 = (bf16[2,64,1024]{2,1,0:T(8,128)(2,1)S(1)}, bf16[2,64,1024]{2,1,0:T(8,128)(2,1)S(1)}, u32[]{:S(2)}, u32[]{:S(2)}) collective-permute-start(bf16[2,64,1024]{2,1,0:T(8,128)(2,1)S(1)} %slice_bitcast_fusion), channel_id=1, source_target_pairs={{0,4},{4,8},{8,12},{12,16},{16,20},{20,24},{24,28},{28,0},{1,5},{5... | collective-permute-start | bytes 786440 | tf_op jit(solution)/shard_map/ppermute | solution.py:287
  4.8 1.6 %convolution_convert_fusion.low_t = bf16[3,8,128]{2,1,0:T(8,128)(2,1)S(1)} fusion(bf16[3,8,4096]{2,1,0:T(8,128)(2,1)S(1)} %copy-done, bf16[1,128,4096]{2,1,0:T(8,128)(2,1)} %tokens.1), kind=kOutput, calls=%fused_computation | convolution fusion | flops 25168896 | bytes 1251328 | tf_op jit(solution)/shard_map/psw,gw->psg/dot_general | solution.py:288
  6.5 1.6 %collective-permute-start = (bf16[2,8,64]{2,1,0:T(8,128)(2,1)S(1)}, bf16[2,8,64]{2,1,0:T(8,128)(2,1)S(1)}, u32[]{:S(2)}, u32[]{:S(2)}) collective-permute-start(bf16[2,8,64]{2,1,0:T(8,128)(2,1)S(1)} %slice.27), channel_id=1, source_target_pairs={{0,4},{4,8},{8,12},{12,16},{16,20},{20,24},{24,28},{28,0},{1,5},{5... | collective-permute-start | bytes 6152 | tf_op jit(solution)/shard_map/ppermute | solution.py:289
  8.0 0.6 %shard_map.68.projected = bf16[3,128,2048]{2,1,0:T(8,128)(2,1)S(1)} custom-call(bf16[3,1,128,2048]{3,2,1,0:T(8,128)(2,1)S(1)} %copy-done.4, bf16[3,8,128]{2,1,0:T(8,128)(2,1)S(1)} %convolution_convert_fusion.low_t, bf16[3,8,2048]{2,1,0:T(8,128)(2,1)S(1)} %copy-done.3), custom_call_target="tpu_custom_call" | custom-call | flops 1000000 | bytes 10000 | tf_op jit(solution)/shard_map/pallas_call | solution.py:244
  8.6 1.6 %shard_map.69 = (f32[24,1024]{1,0:T(8,128)S(1)}, f32[24,128]{1,0:T(8,128)S(1)}) custom-call(bf16[3,128,2048]{2,1,0:T(8,128)(2,1)S(1)} %shard_map.68.projected, bf16[1,128,2048]{2,1,0:T(8,128)(2,1)S(1)} %copy-done.1, bf16[3,8,128]{2,1,0:T(8,128)(2,1)S(1)} %convolution_convert_fusion.low_t, bf16[3,8,2048]{2,1,0:T(8,128)(2,1)S(1)} %copy-done.3), custom_call_target="tpu_custom_call" | custom-call | flops 1000000 | bytes 10000 | tf_op jit(solution)/shard_map/pallas_call | solution.py:244
  10.2 4.0 %collective-permute-done.low_kv = bf16[2,8,64]{2,1,0:T(8,128)(2,1)S(1)} collective-permute-done((bf16[2,8,64]{2,1,0:T(8,128)(2,1)S(1)}, bf16[2,8,64]{2,1,0:T(8,128)(2,1)S(1)}, u32[]{:S(2)}, u32[]{:S(2)}) %collective-permute-start) | collective-permute-done | bytes 2080 | tf_op jit(solution)/shard_map/ppermute | solution.py:289
  14.2 1.1 %shard_map.70 = (f32[24,128]{1,0:T(8,128)S(1)}, f32[16,128]{1,0:T(8,128)S(1)}, bf16[8,64,128]{2,1,0:T(8,128)(2,1)S(1)}, bf16[8,128,64]{2,1,0:T(8,128)(2,1)S(1)},...) custom-call(bf16[3,128,2048]{2,1,0:T(8,128)(2,1)S(1)} %shard_map.68.projected, ...), custom_call_target="tpu_custom_call" | custom-call | flops 1000000 | bytes 10000 | tf_op jit(solution)/shard_map/pallas_call | solution.py:244
  15.3 1.8 %collective-permute-start.2 = (f32[16,128]{1,0:T(8,128)S(1)}, f32[16,128]{1,0:T(8,128)S(1)}, u32[]{:S(2)}, u32[]{:S(2)}) collective-permute-start(f32[16,128]{1,0:T(8,128)S(1)} %get-tuple-element.34), channel_id=1, source_target_pairs={{0,28},{4,0},{8,4},{12,8},{16,12},{20,16},{24,20},{28,24},{1,29},{... | collective-permute-start | bytes 24584 | tf_op jit(solution)/shard_map/ppermute | solution.py:307
  17.0 1.2 %shard_map.72 = (f32[24,1024]{1,0:T(8,128)S(1)}, f32[24,128]{1,0:T(8,128)S(1)}) custom-call(bf16[3,128,2048]{2,1,0:T(8,128)(2,1)S(1)} %shard_map.68.projected, bf16[1,128,2048]{2,1,0:T(8,128)(2,1)S(1)} %copy-done.1, bf16[3,8,128]{2,1,0:T(8,128)(2,1)S(1)} %convolution_convert_fusion.low_t, bf16[3,8,2048]{2,1,0:T(8,128)(2,1)S(1)} %copy-done.3), custom_call_target="tpu_custom_call" | custom-call | flops 1000000 | bytes 10000 | tf_op jit(solution)/shard_map/pallas_call | solution.py:244
  18.3 0.6 %shard_map.71 = (f32[24,1024]{1,0:T(8,128)S(1)}, f32[24,128]{1,0:T(8,128)S(1)}) custom-call(bf16[3,128,2048]{2,1,0:T(8,128)(2,1)S(1)} %shard_map.68.projected, bf16[2,8,64]{2,1,0:T(8,128)(2,1)S(1)} %collective-permute-done.low_kv, bf16[1,128,2048]{2,1,0:T(8,128)(2,1)S(1)} %copy-done.1, bf16[3,8,128]{2,1,0:T(8,128)(2,1)S(1)} %convolution_convert_fusion.low_t, ...), custom_call_target="tpu_custom_call" | custom-call | flops 1000000 | bytes 10000 | tf_op jit(solution)/shard_map/pallas_call | solution.py:244
  19.0 0.6 %copy-done.2 = bf16[1,128,4096]{2,1,0:T(8,128)(2,1)S(1)} copy-done((bf16[1,128,4096]{2,1,0:T(8,128)(2,1)S(1)}, bf16[1,128,4096]{2,1,0:T(8,128)(2,1)}, u32[]{:S(2)}) %copy-start.2) | copy-done | bytes 1048600
  19.5 0.3 shard_map.73
  19.9 1.6 %collective-permute-done.3 = f32[4,24,768]{2,1,0:T(8,128)S(1)} collective-permute-done((f32[4,24,768]{2,1,0:T(8,128)S(1)}, f32[4,24,768]{2,1,0:T(8,128)S(1)}, u32[]{:S(2)}, u32[]{:S(2)}) %collective-permute-start.3) | collective-permute-done | bytes 294944 | tf_op jit(solution)/shard_map/ppermute | solution.py:255
  21.5 0.1 collective-permute-start.4
  21.6 2.7 %collective-permute-start.6 = (bf16[24,768]{1,0:T(8,128)(2,1)S(1)}, bf16[24,768]{1,0:T(8,128)(2,1)S(1)}, u32[]{:S(2)}, u32[]{:S(2)}) collective-permute-start(bf16[24,768]{1,0:T(8,128)(2,1)S(1)} %get-tuple-element.45), channel_id=1, source_target_pairs={{0,6},{1,7},{2,4},{3,5},{4,2},{5,3},{6,0},{7,1},{8,14},{9,15},{10,... | collective-permute-start | bytes 110600 | tf_op jit(solution)/shard_map/ppermute | solution.py:255
  24.3 0.2 collective-permute-start.5
  24.5 0.5 %collective-permute-done.4 = bf16[24,768]{1,0:T(8,128)(2,1)S(1)} collective-permute-done((bf16[24,768]{1,0:T(8,128)(2,1)S(1)}, bf16[24,768]{1,0:T(8,128)(2,1)S(1)}, u32[]{:S(2)}, u32[]{:S(2)}) %collective-permute-start.4) | collective-permute-done | bytes 36896 | tf_op jit(solution)/shard_map/ppermute | solution.py:255
  25.1 2.1 %collective-permute-done.6 = bf16[24,768]{1,0:T(8,128)(2,1)S(1)} collective-permute-done((bf16[24,768]{1,0:T(8,128)(2,1)S(1)}, bf16[24,768]{1,0:T(8,128)(2,1)S(1)}, u32[]{:S(2)}, u32[]{:S(2)}) %collective-permute-start.6) | collective-permute-done | bytes 36896 | tf_op jit(solution)/shard_map/ppermute | solution.py:255
  27.1 0.7 %collective-permute-done.5 = bf16[24,768]{1,0:T(8,128)(2,1)S(1)} collective-permute-done((bf16[24,768]{1,0:T(8,128)(2,1)S(1)}, bf16[24,768]{1,0:T(8,128)(2,1)S(1)}, u32[]{:S(2)}, u32[]{:S(2)}) %collective-permute-start.5) | collective-permute-done | bytes 36896 | tf_op jit(solution)/shard_map/ppermute | solution.py:255
  27.9 3.4 %collective-permute-start.9 = (bf16[24,768]{1,0:T(8,128)(2,1)S(1)}, bf16[24,768]{1,0:T(8,128)(2,1)S(1)}, u32[]{:S(2)}, u32[]{:S(2)}) collective-permute-start(bf16[24,768]{1,0:T(8,128)(2,1)S(1)} %fusion.4), channel_id=1, source_target_pairs={{0,24},{1,25},{2,26},{3,27},{4,28},{5,29},{6,30},{7,31},{8,16},{9,... | collective-permute-start | bytes 110600 | tf_op jit(solution)/shard_map/ppermute | solution.py:255
  31.3 0.8 %collective-permute-start.7 = (bf16[24,768]{1,0:T(8,128)(2,1)S(1)}, bf16[24,768]{1,0:T(8,128)(2,1)S(1)}, u32[]{:S(2)}, u32[]{:S(2)}) collective-permute-start(bf16[24,768]{1,0:T(8,128)(2,1)S(1)} %fusion.4), channel_id=1, source_target_pairs={{0,9},{1,8},{2,11},{3,10},{4,13},{5,12},{6,15},{7,14},{8,1},{9,0},... | collective-permute-start | bytes 110600 | tf_op jit(solution)/shard_map/ppermute | solution.py:255
  32.1 1.6 %collective-permute-done.9 = bf16[24,768]{1,0:T(8,128)(2,1)S(1)} collective-permute-done((bf16[24,768]{1,0:T(8,128)(2,1)S(1)}, bf16[24,768]{1,0:T(8,128)(2,1)S(1)}, u32[]{:S(2)}, u32[]{:S(2)}) %collective-permute-start.9) | collective-permute-done | bytes 36896 | tf_op jit(solution)/shard_map/ppermute | solution.py:255
  33.7 2.3 %collective-permute-done.8 = bf16[24,768]{1,0:T(8,128)(2,1)S(1)} collective-permute-done((bf16[24,768]{1,0:T(8,128)(2,1)S(1)}, bf16[24,768]{1,0:T(8,128)(2,1)S(1)}, u32[]{:S(2)}, u32[]{:S(2)}) %collective-permute-start.8) | collective-permute-done | bytes 36896 | tf_op jit(solution)/shard_map/ppermute | solution.py:255
  36.0 1.6 %collective-permute-start.12 = (bf16[24,768]{1,0:T(8,128)(2,1)S(1)}, bf16[24,768]{1,0:T(8,128)(2,1)S(1)}, u32[]{:S(2)}, u32[]{:S(2)}) collective-permute-start(bf16[24,768]{1,0:T(8,128)(2,1)S(1)} %add_convert_fusion), channel_id=1, source_target_pairs={{0,6},{1,7},{2,4},{3,5},{4,2},{5,3},{6,0},{7,1},{8,14},{9,15},{10,... | collective-permute-start | bytes 110600 | tf_op jit(solution)/shard_map/ppermute | solution.py:255
  37.6 0.5 %collective-permute-start.11 = (bf16[24,768]{1,0:T(8,128)(2,1)S(1)}, bf16[24,768]{1,0:T(8,128)(2,1)S(1)}, u32[]{:S(2)}, u32[]{:S(2)}) collective-permute-start(bf16[24,768]{1,0:T(8,128)(2,1)S(1)} %add_convert_fusion), channel_id=1, source_target_pairs={{0,3},{1,2},{2,1},{3,0},{4,7},{5,6},{6,5},{7,4},{8,11},{9,10},{10,... | collective-permute-start | bytes 110600 | tf_op jit(solution)/shard_map/ppermute | solution.py:255
  38.0 1.2 %collective-permute-start.10 = (bf16[24,768]{1,0:T(8,128)(2,1)S(1)}, bf16[24,768]{1,0:T(8,128)(2,1)S(1)}, u32[]{:S(2)}, u32[]{:S(2)}) collective-permute-start(bf16[24,768]{1,0:T(8,128)(2,1)S(1)} %add_convert_fusion), channel_id=1, source_target_pairs={{0,5},{1,4},{2,7},{3,6},{4,1},{5,0},{6,3},{7,2},{8,13},{9,12},{10,... | collective-permute-start | bytes 110600 | tf_op jit(solution)/shard_map/ppermute | solution.py:255
  39.3 1.7 %collective-permute-done.12 = bf16[24,768]{1,0:T(8,128)(2,1)S(1)} collective-permute-done((bf16[24,768]{1,0:T(8,128)(2,1)S(1)}, bf16[24,768]{1,0:T(8,128)(2,1)S(1)}, u32[]{:S(2)}, u32[]{:S(2)}) %collective-permute-start.12) | collective-permute-done | bytes 36896 | tf_op jit(solution)/shard_map/ppermute | solution.py:255
  41.0 0.8 %collective-permute-done.11 = bf16[24,768]{1,0:T(8,128)(2,1)S(1)} collective-permute-done((bf16[24,768]{1,0:T(8,128)(2,1)S(1)}, bf16[24,768]{1,0:T(8,128)(2,1)S(1)}, u32[]{:S(2)}, u32[]{:S(2)}) %collective-permute-start.11) | collective-permute-done | bytes 36896 | tf_op jit(solution)/shard_map/ppermute | solution.py:255
  41.7 0.5 %collective-permute-start.13 = (bf16[4,24,768]{2,1,0:T(8,128)(2,1)S(1)}, bf16[4,24,768]{2,1,0:T(8,128)(2,1)S(1)}, u32[]{:S(2)}, u32[]{:S(2)}) collective-permute-start(bf16[4,24,768]{2,1,0:T(8,128)(2,1)S(1)} %pad_maximum_fusion.pieces), channel_id=1, source_target_pairs={{0,1},{1,0},{2,3},{3,2},{4,5},{5,4},{6,7},{7,6},{8,9},{9,8},{10,11... | collective-permute-start | bytes 442376 | tf_op jit(solution)/shard_map/ppermute | solution.py:255
  42.2 1.0 %collective-permute-done.13.pieces = bf16[4,24,768]{2,1,0:T(8,128)(2,1)S(1)} collective-permute-done((bf16[4,24,768]{2,1,0:T(8,128)(2,1)S(1)}, bf16[4,24,768]{2,1,0:T(8,128)(2,1)S(1)}, u32[]{:S(2)}, u32[]{:S(2)}) %collective-permute-start.13) | collective-permute-done | bytes 147488 | tf_op jit(solution)/shard_map/ppermute | solution.py:255
  43.2 0.9 %shard_map.75 = (f32[3,8,4096]{2,1,0:T(8,128)}, f32[3,8,2048]{2,1,0:T(8,128)}) custom-call(bf16[4,24,768]{2,1,0:T(8,128)(2,1)S(1)} %collective-permute-done.13.pieces, f32[3,8,4096]{2,1,0:T(8,128)S(1)} %get-tuple-element.40.down_in, f32[3,8,2048]{2,1,0:T(8,128)S(1)} %get-tuple-element.41.up_in), custom_call_target="tpu_custom_call" | custom-call | flops 1000000 | bytes 10000 | tf_op jit(solution)/shard_map/pallas_call | solution.py:244
  (22 shorter events, 0.4 us)
Async XLA Ops:
  0.6 4.1 %copy-start = (bf16[3,8,4096]{2,1,0:T(8,128)(2,1)S(1)}, bf16[3,8,4096]{2,1,0:T(8,128)(2,1)}, u32[]{:S(2)}) copy-start(bf16[3,8,4096]{2,1,0:T(8,128)(2,1)} %param.8) | copy-start | bytes 589828
  0.6 7.4 %copy-start.4 = (bf16[3,1,128,2048]{3,2,1,0:T(8,128)(2,1)S(1)}, bf16[3,1,128,2048]{3,2,1,0:T(8,128)(2,1)}, u32[]{:S(2)}) copy-start(bf16[3,1,128,2048]{3,2,1,0:T(8,128)(2,1)} %frozen.1) | copy-start | bytes 4718596
  0.7 7.4 %copy-start.3 = (bf16[3,8,2048]{2,1,0:T(8,128)(2,1)S(1)}, bf16[3,8,2048]{2,1,0:T(8,128)(2,1)}, u32[]{:S(2)}) copy-start(bf16[3,8,2048]{2,1,0:T(8,128)(2,1)} %up.8) | copy-start | bytes 294916
  1.8 12.4 %collective-permute-start.1 = (bf16[2,64,1024]{2,1,0:T(8,128)(2,1)S(1)}, bf16[2,64,1024]{2,1,0:T(8,128)(2,1)S(1)}, u32[]{:S(2)}, u32[]{:S(2)}) collective-permute-start(bf16[2,64,1024]{2,1,0:T(8,128)(2,1)S(1)} %slice_bitcast_fusion), channel_id=1, source_target_pairs={{0,4},{4,8},{8,12},{12,16},{16,20},{20,24},{24,28},{28,0},{1,5},{5... | collective-permute-start | bytes 786440 | tf_op jit(solution)/shard_map/ppermute | solution.py:287
  6.5 2.2 %copy-start.1 = (bf16[1,128,2048]{2,1,0:T(8,128)(2,1)S(1)}, bf16[1,128,2048]{2,1,0:T(8,128)(2,1)}, u32[]{:S(2)}) copy-start(bf16[1,128,2048]{2,1,0:T(8,128)(2,1)} %grad.6) | copy-start | bytes 1572868
  6.5 7.7 %collective-permute-start = (bf16[2,8,64]{2,1,0:T(8,128)(2,1)S(1)}, bf16[2,8,64]{2,1,0:T(8,128)(2,1)S(1)}, u32[]{:S(2)}, u32[]{:S(2)}) collective-permute-start(bf16[2,8,64]{2,1,0:T(8,128)(2,1)S(1)} %slice.27), channel_id=1, source_target_pairs={{0,4},{4,8},{8,12},{12,16},{16,20},{20,24},{24,28},{28,0},{1,5},{5... | collective-permute-start | bytes 6152 | tf_op jit(solution)/shard_map/ppermute | solution.py:289
  15.3 3.7 %collective-permute-start.2 = (f32[16,128]{1,0:T(8,128)S(1)}, f32[16,128]{1,0:T(8,128)S(1)}, u32[]{:S(2)}, u32[]{:S(2)}) collective-permute-start(f32[16,128]{1,0:T(8,128)S(1)} %get-tuple-element.34), channel_id=1, source_target_pairs={{0,28},{4,0},{8,4},{12,8},{16,12},{20,16},{24,20},{28,24},{1,29},{... | collective-permute-start | bytes 24584 | tf_op jit(solution)/shard_map/ppermute | solution.py:307
  18.3 1.2 %copy-start.2 = (bf16[1,128,4096]{2,1,0:T(8,128)(2,1)S(1)}, bf16[1,128,4096]{2,1,0:T(8,128)(2,1)}, u32[]{:S(2)}) copy-start(bf16[1,128,4096]{2,1,0:T(8,128)(2,1)} %tokens.1) | copy-start | bytes 3145732
  19.8 1.6 %collective-permute-start.3 = (f32[4,24,768]{2,1,0:T(8,128)S(1)}, f32[4,24,768]{2,1,0:T(8,128)S(1)}, u32[]{:S(2)}, u32[]{:S(2)}) collective-permute-start(f32[4,24,768]{2,1,0:T(8,128)S(1)} %get-tuple-element.39), channel_id=1, source_target_pairs={{0,1},{1,0},{2,3},{3,2},{4,5},{5,4},{6,7},{7,6},{8,9},{9,8},{10,11... | collective-permute-start | bytes 884744 | tf_op jit(solution)/shard_map/ppermute | solution.py:255
  21.5 3.5 %collective-permute-start.4 = (bf16[24,768]{1,0:T(8,128)(2,1)S(1)}, bf16[24,768]{1,0:T(8,128)(2,1)S(1)}, u32[]{:S(2)}, u32[]{:S(2)}) collective-permute-start(bf16[24,768]{1,0:T(8,128)(2,1)S(1)} %get-tuple-element.44), channel_id=1, source_target_pairs={{0,5},{1,4},{2,7},{3,6},{4,1},{5,0},{6,3},{7,2},{8,13},{9,12},{10,... | collective-permute-start | bytes 110600 | tf_op jit(solution)/shard_map/ppermute | solution.py:255
  21.6 5.5 %collective-permute-start.6 = (bf16[24,768]{1,0:T(8,128)(2,1)S(1)}, bf16[24,768]{1,0:T(8,128)(2,1)S(1)}, u32[]{:S(2)}, u32[]{:S(2)}) collective-permute-start(bf16[24,768]{1,0:T(8,128)(2,1)S(1)} %get-tuple-element.45), channel_id=1, source_target_pairs={{0,6},{1,7},{2,4},{3,5},{4,2},{5,3},{6,0},{7,1},{8,14},{9,15},{10,... | collective-permute-start | bytes 110600 | tf_op jit(solution)/shard_map/ppermute | solution.py:255
  24.3 3.5 %collective-permute-start.5 = (bf16[24,768]{1,0:T(8,128)(2,1)S(1)}, bf16[24,768]{1,0:T(8,128)(2,1)S(1)}, u32[]{:S(2)}, u32[]{:S(2)}) collective-permute-start(bf16[24,768]{1,0:T(8,128)(2,1)S(1)} %get-tuple-element.46), channel_id=1, source_target_pairs={{0,3},{1,2},{2,1},{3,0},{4,7},{5,6},{6,5},{7,4},{8,11},{9,10},{10,... | collective-permute-start | bytes 110600 | tf_op jit(solution)/shard_map/ppermute | solution.py:255
  27.9 5.8 %collective-permute-start.9 = (bf16[24,768]{1,0:T(8,128)(2,1)S(1)}, bf16[24,768]{1,0:T(8,128)(2,1)S(1)}, u32[]{:S(2)}, u32[]{:S(2)}) collective-permute-start(bf16[24,768]{1,0:T(8,128)(2,1)S(1)} %fusion.4), channel_id=1, source_target_pairs={{0,24},{1,25},{2,26},{3,27},{4,28},{5,29},{6,30},{7,31},{8,16},{9,... | collective-permute-start | bytes 110600 | tf_op jit(solution)/shard_map/ppermute | solution.py:255
  31.3 4.7 %collective-permute-start.8 = (bf16[24,768]{1,0:T(8,128)(2,1)S(1)}, bf16[24,768]{1,0:T(8,128)(2,1)S(1)}, u32[]{:S(2)}, u32[]{:S(2)}) collective-permute-start(bf16[24,768]{1,0:T(8,128)(2,1)S(1)} %fusion.4), channel_id=1, source_target_pairs={{0,17},{1,16},{2,19},{3,18},{4,21},{5,20},{6,23},{7,22},{8,25},{9,... | collective-permute-start | bytes 110600 | tf_op jit(solution)/shard_map/ppermute | solution.py:255
  31.3 4.7 %collective-permute-start.7 = (bf16[24,768]{1,0:T(8,128)(2,1)S(1)}, bf16[24,768]{1,0:T(8,128)(2,1)S(1)}, u32[]{:S(2)}, u32[]{:S(2)}) collective-permute-start(bf16[24,768]{1,0:T(8,128)(2,1)S(1)} %fusion.4), channel_id=1, source_target_pairs={{0,9},{1,8},{2,11},{3,10},{4,13},{5,12},{6,15},{7,14},{8,1},{9,0},... | collective-permute-start | bytes 110600 | tf_op jit(solution)/shard_map/ppermute | solution.py:255
  36.0 5.0 %collective-permute-start.12 = (bf16[24,768]{1,0:T(8,128)(2,1)S(1)}, bf16[24,768]{1,0:T(8,128)(2,1)S(1)}, u32[]{:S(2)}, u32[]{:S(2)}) collective-permute-start(bf16[24,768]{1,0:T(8,128)(2,1)S(1)} %add_convert_fusion), channel_id=1, source_target_pairs={{0,6},{1,7},{2,4},{3,5},{4,2},{5,3},{6,0},{7,1},{8,14},{9,15},{10,... | collective-permute-start | bytes 110600 | tf_op jit(solution)/shard_map/ppermute | solution.py:255
  37.6 4.2 %collective-permute-start.11 = (bf16[24,768]{1,0:T(8,128)(2,1)S(1)}, bf16[24,768]{1,0:T(8,128)(2,1)S(1)}, u32[]{:S(2)}, u32[]{:S(2)}) collective-permute-start(bf16[24,768]{1,0:T(8,128)(2,1)S(1)} %add_convert_fusion), channel_id=1, source_target_pairs={{0,3},{1,2},{2,1},{3,0},{4,7},{5,6},{6,5},{7,4},{8,11},{9,10},{10,... | collective-permute-start | bytes 110600 | tf_op jit(solution)/shard_map/ppermute | solution.py:255
  38.0 3.7 %collective-permute-start.10 = (bf16[24,768]{1,0:T(8,128)(2,1)S(1)}, bf16[24,768]{1,0:T(8,128)(2,1)S(1)}, u32[]{:S(2)}, u32[]{:S(2)}) collective-permute-start(bf16[24,768]{1,0:T(8,128)(2,1)S(1)} %add_convert_fusion), channel_id=1, source_target_pairs={{0,5},{1,4},{2,7},{3,6},{4,1},{5,0},{6,3},{7,2},{8,13},{9,12},{10,... | collective-permute-start | bytes 110600 | tf_op jit(solution)/shard_map/ppermute | solution.py:255
  41.7 1.5 %collective-permute-start.13 = (bf16[4,24,768]{2,1,0:T(8,128)(2,1)S(1)}, bf16[4,24,768]{2,1,0:T(8,128)(2,1)S(1)}, u32[]{:S(2)}, u32[]{:S(2)}) collective-permute-start(bf16[4,24,768]{2,1,0:T(8,128)(2,1)S(1)} %pad_maximum_fusion.pieces), channel_id=1, source_target_pairs={{0,1},{1,0},{2,3},{3,2},{4,5},{5,4},{6,7},{7,6},{8,9},{9,8},{10,11... | collective-permute-start | bytes 442376 | tf_op jit(solution)/shard_map/ppermute | solution.py:255

commit v9 on v8

--- a/solution.py
+++ b/solution.py
@@ -115,71 +115,106 @@
         rank_out[8 * j : 8 * j + 8, :] = right(part) if first else part
 
 
-def far_items(projected, near_kv, low_kv, grad, low_t, up):
+def left(x):
+    return jnp.concatenate([x, jnp.zeros_like(x)], axis=1)
+
+
+def right(x):
+    return jnp.concatenate([jnp.zeros_like(x), x], axis=1)
+
+
+def shifted_columns(up):
+    half_width = up.shape[2] // 2
+    return [slice(start, start + HEAD_DIM) for start in range(half_width, 2 * half_width, HEAD_DIM)]
+
+
+def far_ready(projected, grad, up, e_out, dp_out, top_out, sum_out, bk_out, bv_out):
     half = projected.shape[1] // 2
-    half_width = up.shape[2] // 2
+    mask = causal(half, half, 0)
+    for h, cols in enumerate(shifted_columns(up)):
+        q, k, v = [projected[j, :half, cols] for j in range(3)]
+        g = grad[0, :half, cols]
+        st = jnp.where(mask, nt(k, q) * SCALE, -jnp.inf)
+        top = jnp.max(st, axis=0, keepdims=True)
+        e = jnp.exp(st - top)
+        e_out[h] = e
+        dp_out[h] = nt(v, g)
+        top_out[h : h + 1, :] = top
+        sum_out[h : h + 1, :] = jnp.sum(e, axis=0, keepdims=True)
+        bk_out[h] = rows(hi_lo(nt(up[1, :, cols], q)))
+        bv_out[h] = rows(hi_lo(nt(up[2, :, cols], g)))
+
+
+def far_scores(
+    projected, frozen_kv, low_kv, grad, up, e, dp, top, total, bk, bv,
+    cross_out, near_out, pb_out, ds_out, factor_out, dot_out,
+):
+    half = projected.shape[1] // 2
+    columns = shifted_columns(up)
+    near = []
+    for h, cols in enumerate(columns):
+        here = slice(h * HEAD_DIM, (h + 1) * HEAD_DIM)
+        near.append([project(frozen_kv[j, :, here], low_kv[j], up[j + 1, :, cols]) for j in range(2)])
+    sts = [nt(near[h][0], projected[0, :half, cols]) for h, cols in enumerate(columns)]
+    dps = [nt(near[h][1], grad[0, :half, cols]) for h, cols in enumerate(columns)]
+    found = []
+    for h, (st, dpn) in enumerate(zip(sts, dps)):
+        st = st * SCALE
+        far_top = top[h : h + 1, :]
+        highest = jnp.maximum(far_top, jnp.max(st, axis=0, keepdims=True))
+        en = jnp.exp(st - highest)
+        rescale = jnp.exp(far_top - highest)
+        inverse = 1.0 / (total[h : h + 1, :] * rescale + jnp.sum(en, axis=0, keepdims=True))
+        factor = rescale * inverse
+        p = en * inverse
+        pb = p.astype(BF)
+        far_pb = (e[h] * factor).astype(BF).astype(F32)
+        dot = jnp.sum(pb.astype(F32) * dpn, axis=0, keepdims=True)
+        dot = dot + jnp.sum(far_pb * dp[h], axis=0, keepdims=True)
+        ds = (p * (dpn - dot) * SCALE).astype(BF)
+        factor_out[h : h + 1, :] = factor
+        dot_out[h : h + 1, :] = dot
+        found.append((pb, ds))
+    by_k = sum(nt(bk[h], ds) for h, (_, ds) in enumerate(found))
+    by_v = sum(nt(bv[h], pb) for h, (pb, _) in enumerate(found))
+    cross_out[:8, :] = right(by_k[:8] + by_k[8:])
+    cross_out[8:, :] = right(by_v[:8] + by_v[8:])
+    for h, (pb, ds) in enumerate(found):
+        near_out[h] = near[h][0]
+        pb_out[h] = pb
+        ds_out[h] = ds
+
+
+def far_rest(
+    projected, low_kv, grad, low_t, up, e, dp, bk, bv, near, near_pb, near_ds, factor, dot, up_out, rank_out
+):
+    half = projected.shape[1] // 2
     far_f = [low_t[j].astype(F32)[:, :half] for j in range(3)]
     lows = [far_f[0]] + [
         jnp.concatenate([low_kv[j].astype(F32), far_f[j + 1]], axis=1) for j in range(2)
     ]
-    items = []
-    for h, near in enumerate(near_kv):
-        start = half_width + h * HEAD_DIM
-        cols = slice(start, start + HEAD_DIM)
-        ups = [up[j, :, cols] for j in range(3)]
-        k, v = [jnp.concatenate([near[j], projected[j + 1, :half, cols]], axis=0) for j in range(2)]
-        items.append((projected[0, :half, cols], k, v, grad[0, :half, cols], ups, lows))
-    return items
-
-
-def near_rows(frozen_kv, low_kv, up):
-    half_width = up.shape[2] // 2
-    near = []
-    for h in range(frozen_kv.shape[2] // HEAD_DIM):
-        here = slice(h * HEAD_DIM, (h + 1) * HEAD_DIM)
-        start = half_width + h * HEAD_DIM
-        near.append(
-            [project(frozen_kv[j, :, here], low_kv[j], up[j + 1, :, start : start + HEAD_DIM]) for j in range(2)]
+    items, found, far_ds, far_pb = [], [], [], []
+    for h, cols in enumerate(shifted_columns(up)):
+        p = e[h] * factor[h : h + 1, :]
+        pb = p.astype(BF)
+        ds = (p * (dp[h] - dot[h : h + 1, :]) * SCALE).astype(BF)
+        far_pb.append(pb)
+        far_ds.append(ds)
+        whole_ds = jnp.concatenate([near_ds[h], ds], axis=0)
+        k = jnp.concatenate([near[h], projected[1, :half, cols]], axis=0)
+        items.append(
+            (projected[0, :half, cols], k, None, grad[0, :half, cols], [up[j, :, cols] for j in range(3)], lows)
         )
-    return near
-
-
-def left(x):
-    return jnp.concatenate([x, jnp.zeros_like(x)], axis=1)
-
-
-def right(x):
-    return jnp.concatenate([jnp.zeros_like(x), x], axis=1)
-
-
-def far_scores(
-    projected, frozen_kv, low_kv, grad, low_t, up, rank_in, rank_out, cross_out, near_out, pb_out, ds_out, aq_out
-):
-    half = projected.shape[1] // 2
-    near = near_rows(frozen_kv, low_kv, up)
-    items = far_items(projected, near, low_kv, grad, low_t, up)
-    found = scores(items, causal(2 * half, half, half))
-    for j in (1, 2):
-        part = sum(f[j + 2] for f in found)
-        cross_out[8 * j - 8 : 8 * j, :] = right(part[:, :half])
-        rank_out[8 * j : 8 * j + 8, :] = rank_in[8 * j : 8 * j + 8, :] + left(part[:, half:])
-    rank_out[:8, :] = rank_in[:8, :]
-    for h, f in enumerate(found):
-        near_out[h] = near[h][0]
-        pb_out[h] = f[0]
-        ds_out[h] = f[1]
-        aq_out[8 * h : 8 * h + 8, :] = f[2]
-
-
-def far_rest(projected, low_kv, grad, low_t, up, rank_in, near, pb, ds, aq, up_out, rank_out):
-    n = near.shape[0]
-    items = far_items(projected, [[near[h]] * 2 for h in range(n)], low_kv, grad, low_t, up)
-    parts = rest(items, [(pb[h], ds[h], aq[8 * h : 8 * h + 8, :]) for h in range(n)])
+        found.append((jnp.concatenate([near_pb[h], pb], axis=0), whole_ds, nt(lows[0].astype(BF), whole_ds)))
+    by_k = sum(nt(bk[h], ds) for h, ds in enumerate(far_ds))
+    by_v = sum(nt(bv[h], pb) for h, pb in enumerate(far_pb))
+    parts = rest(items, found)
     for h, (grads, _) in enumerate(parts):
         for j in range(3):
             up_out[8 * j : 8 * j + 8, h * HEAD_DIM : (h + 1) * HEAD_DIM] = grads[j]
-    rank_out[:8, :] = rank_in[:8, :] + left(sum(rank for _, rank in parts))
-    rank_out[8:, :] = rank_in[8:, :]
+    rank_out[:8, :] = left(sum(rank for _, rank in parts))
+    rank_out[8:16, :] = left(by_k[:8] + by_k[8:])
+    rank_out[16:, :] = left(by_v[:8] + by_v[8:])
 
 
 def position():
@@ -190,12 +225,11 @@
     return bits & 1, (dp & 2) | (seq & 1)
 
 
-def down_kernel(tokens, rank_in, rank_near, cross, up_plain, up_near, up_far, keep, send):
+def down_kernel(tokens, rank_plain, rank_near, rank_far, cross, up_plain, up_near, up_far, keep, send):
     half, quarter = position()
     first = half == 0
-    ranks = rank_in[...] + rank_near[...] + jnp.concatenate(
-        [jnp.zeros((RANK, rank_in.shape[1]), F32), cross[...]], axis=0
-    )
+    ranks = rank_plain[...] + rank_near[...] + rank_far[...]
+    ranks = ranks + jnp.concatenate([jnp.zeros((RANK, ranks.shape[1]), F32), cross[...]], axis=0)
     both = rows(hi_lo(ranks))
     n = ranks.shape[0]
     up_step, down_step = up_plain.shape[1] // 4, tokens.shape[2] // 8
@@ -270,7 +304,7 @@
         parts = [swap(own, step * dps | (step & (step - 1) == 0), total) for step in steps]
         own = own.astype(F32)
         if len(parts) == 3:
-            own = (own + parts[0].astype(F32)) + (parts[1].astype(F32) + parts[2].astype(F32))
+            own = (own + parts[0].astype(F32)) + (parts[2].astype(F32) + parts[1].astype(F32))
         else:
             own = own + parts[0].astype(F32)
     piece = own.astype(BF)
@@ -290,28 +324,33 @@
     sds = jax.ShapeDtypeStruct
     up_half, rank_side = sds((24, half_width), F32), sds((24, count), F32)
     projected = call(project_kernel, sds((3, count, width), BF), frozen, low_t, up_weight)
-    up_plain, rank = call(
+    up_plain, rank_plain = call(
         functools.partial(group_kernel, 0, 0), [up_half, rank_side], projected, grad, low_t, up_weight
     )
     n = half_width // HEAD_DIM
-    by_keys = sds((n, count, half), BF)
-    rank, cross, *kept = call(
+    square, line, pairs = sds((n, half, half), F32), sds((n, half), F32), sds((n, 2 * RANK, half), BF)
+    e, dp, top, total, bk, bv = call(
+        far_ready, [square, square, line, line, pairs, pairs], projected, grad, up_weight
+    )
+    bk, rank_plain = lax.optimization_barrier((bk, rank_plain))
+    squares = sds((n, half, half), BF)
+    cross, near, pb, ds, factor, dot = call(
         far_scores,
-        [
-            rank_side, sds((16, count), F32), sds((n, half, HEAD_DIM), BF), by_keys, by_keys,
-            sds((8 * n, count), F32),
-        ],
-        projected, frozen_kv, low_kv, grad, low_t, up_weight, rank,
-    )
-    rank, *held = lax.optimization_barrier((rank, grad, low_t, up_weight))
+        [sds((2 * RANK, count), F32), sds((n, half, HEAD_DIM), BF), squares, squares, line, line],
+        projected, frozen_kv, low_kv, grad, up_weight, e, dp, top, total, bk, bv,
+    )
+    factor, *held = lax.optimization_barrier((factor, grad, low_t, up_weight))
     cross = lax.ppermute(cross, "seq", backward)
     up_near, rank_near = call(
         functools.partial(group_kernel, half, half_width), [up_half, rank_side], projected, *held
     )
-    up_far, rank = call(far_rest, [up_half, rank_side], projected, low_kv, grad, low_t, up_weight, rank, *kept)
+    up_far, rank_far = call(
+        far_rest, [up_half, rank_side],
+        projected, low_kv, grad, low_t, up_weight, e, dp, bk, bv, near, pb, ds, factor, dot,
+    )
     columns = (width + tokens.shape[2]) // 8
     piece = sds((4, 24, columns), F32)
-    keep, send = call(down_kernel, [piece, piece], tokens, rank, rank_near, cross, up_plain, up_near, up_far)
+    keep, send = call(down_kernel, [piece, piece], tokens, rank_plain, rank_near, rank_far, cross, up_plain, up_near, up_far)
     mine, other = total_sum(keep, send, seqs, dps)
     outs = [sds((3, RANK, tokens.shape[2]), F32), sds((3, RANK, width), F32)]
     return tuple(call(last_spread, outs, other, *call(first_spread, outs, mine)))

time: 44.3 us -> 43.2 us (0.975)
  waiting for transfers between devices: 16.2 us -> 15.4 us
  starting transfers between devices: 17.3 us -> 16.8 us
  Pallas kernels: 6.3 us -> 6.76 us
    pallas_call x8 -> x9, Pallas kernels: 6.3 us -> 6.76 us  [call(): pl.pallas_call(kernel, out_shape=outs, in_specs=[VMEM] * len(args), out_s...]
    ppermute x1, waiting for transfers between devices: 3.96 us -> 3.52 us  [on_device(): low_kv = lax.ppermute(low_t[1:, :, half:], 'seq', forward)]
  transfers between devices with their start and end apart: 14 -> 14, of which waited for: 10 -> 11; matrix products, arithmetic and copies ran while one was open for 4% -> 4% of each run, Pallas kernels for 9% -> 11%
where the time goes in v9:
time: 43.2 us; the launch traced here: 43 us
  starting transfers between devices  16.8 us (39%)
  waiting for transfers between devices  15.4 us (36%)
  Pallas kernels  6.76 us (16%)
  matrix products  1.6 us (4%)
  local copies, waits for them, and re-layouts  1.55 us (4%)
  between operations  0.76 us (2%)
    ppermute x11, waiting for transfers between devices, swap(): return lax.ppermute(x, AXES, [(i, i ^ bits) for i in range(total)])  11.8 us
    ppermute x11, starting transfers between devices, swap(): return lax.ppermute(x, AXES, [(i, i ^ bits) for i in range(total)])  10.5 us
    pallas_call x9, Pallas kernels, call(): pl.pallas_call(kernel, out_shape=outs, in_specs=[VMEM] * len(args), out_s...  6.76 us
    ppermute x1, waiting for transfers between devices, on_device(): low_kv = lax.ppermute(low_t[1:, :, half:], 'seq', forward)  3.52 us
    ppermute x1, starting transfers between devices, on_device(): frozen_kv = lax.ppermute(frozen[1:, 0, half:, half_width:], 'seq', forward)  2.99 us
    ppermute x1, starting transfers between devices, on_device(): cross = lax.ppermute(cross, 'seq', backward)  1.77 us
    dot_general x1, matrix products, on_device(): jnp.einsum('psw,gw->psg', down_weight, tokens[0], preferred_element_type=...  1.6 us
    ppermute x1, starting transfers between devices, on_device(): low_kv = lax.ppermute(low_t[1:, :, half:], 'seq', forward)  1.56 us
  transfers between devices with their start and end apart: 14, of which 11 were waited for; matrix products, arithmetic and copies ran while one was open for 4% of the time, Pallas kernels for 11%

profile of v9, /device:TPU:0, one launch (start us, length us, event | category | flops | bytes accessed | tf_op | source)
XLA Modules:
  0.0 43.0 jit_solution(2365176597251153153)
XLA Ops:
  0.7 1.1 %slice_bitcast_fusion = bf16[2,64,1024]{2,1,0:T(8,128)(2,1)S(1)} fusion(bf16[3,1,128,2048]{3,2,0,1:T(8,128)(2,1)} %bitcast.28), kind=kLoop, calls=%fused_computation.2 | loop fusion | bytes 524288 | tf_op jit(solution)/shard_map/squeeze | solution.py:321
  1.8 3.0 %collective-permute-start = (bf16[2,64,1024]{2,1,0:T(8,128)(2,1)S(1)}, bf16[2,64,1024]{2,1,0:T(8,128)(2,1)S(1)}, u32[]{:S(2)}, u32[]{:S(2)}) collective-permute-start(bf16[2,64,1024]{2,1,0:T(8,128)(2,1)S(1)} %slice_bitcast_fusion), channel_id=1, source_target_pairs={{0,4},{4,8},{8,12},{12,16},{16,20},{20,24},{24,28},{28,0},{1,5},{5... | collective-permute-start | bytes 786440 | tf_op jit(solution)/shard_map/ppermute | solution.py:321
  4.8 1.6 %convolution_convert_fusion.low_t = bf16[3,8,128]{2,1,0:T(8,128)(2,1)S(1)} fusion(bf16[3,8,4096]{2,1,0:T(8,128)(2,1)S(1)} %copy-done, bf16[1,128,4096]{2,1,0:T(8,128)(2,1)} %tokens.1), kind=kOutput, calls=%fused_computation | convolution fusion | flops 25168896 | bytes 1251328 | tf_op jit(solution)/shard_map/psw,gw->psg/dot_general | solution.py:322
  6.5 1.6 %collective-permute-start.1 = (bf16[2,8,64]{2,1,0:T(8,128)(2,1)S(1)}, bf16[2,8,64]{2,1,0:T(8,128)(2,1)S(1)}, u32[]{:S(2)}, u32[]{:S(2)}) collective-permute-start(bf16[2,8,64]{2,1,0:T(8,128)(2,1)S(1)} %slice.28), channel_id=1, source_target_pairs={{0,4},{4,8},{8,12},{12,16},{16,20},{20,24},{24,28},{28,0},{1,5},{5... | collective-permute-start | bytes 6152 | tf_op jit(solution)/shard_map/ppermute | solution.py:323
  8.0 0.6 %shard_map.68.projected = bf16[3,128,2048]{2,1,0:T(8,128)(2,1)S(1)} custom-call(bf16[3,1,128,2048]{3,2,1,0:T(8,128)(2,1)S(1)} %copy-done.4, bf16[3,8,128]{2,1,0:T(8,128)(2,1)S(1)} %convolution_convert_fusion.low_t, bf16[3,8,2048]{2,1,0:T(8,128)(2,1)S(1)} %copy-done.3), custom_call_target="tpu_custom_call" | custom-call | flops 1000000 | bytes 10000 | tf_op jit(solution)/shard_map/pallas_call | solution.py:278
  8.6 1.6 %shard_map.70 = (f32[24,1024]{1,0:T(8,128)S(1)}, f32[24,128]{1,0:T(8,128)S(1)}) custom-call(bf16[3,128,2048]{2,1,0:T(8,128)(2,1)S(1)} %shard_map.68.projected, bf16[1,128,2048]{2,1,0:T(8,128)(2,1)S(1)} %copy-done.1, bf16[3,8,128]{2,1,0:T(8,128)(2,1)S(1)} %convolution_convert_fusion.low_t, bf16[3,8,2048]{2,1,0:T(8,128)(2,1)S(1)} %copy-done.3), custom_call_target="tpu_custom_call" | custom-call | flops 1000000 | bytes 10000 | tf_op jit(solution)/shard_map/pallas_call | solution.py:278
  10.2 0.4 %shard_map.69 = (f32[8,64,64]{2,1,0:T(8,128)S(1)}, f32[8,64,64]{2,1,0:T(8,128)S(1)}, f32[8,64]{1,0:T(8,128)S(1)}, f32[8,64]{1,0:T(8,128)S(1)}, bf16[8,16,64]{2,1...) custom-call(bf16[3,128,2048]{2,1,0:T(8,128)(2,1)S(1)} %shard_map.68.projected, bf16[1,128,2048]{2,1,0:T(8,128)(2,1)S(1)} %copy-done.1, ...), custom_call_target="tpu_custom_call" | custom-call | flops 1000000 | bytes 10000 | tf_op jit(solution)/shard_map/pallas_call | solution.py:278
  10.7 3.5 %collective-permute-done.1.low_kv = bf16[2,8,64]{2,1,0:T(8,128)(2,1)S(1)} collective-permute-done((bf16[2,8,64]{2,1,0:T(8,128)(2,1)S(1)}, bf16[2,8,64]{2,1,0:T(8,128)(2,1)S(1)}, u32[]{:S(2)}, u32[]{:S(2)}) %collective-permute-start.1) | collective-permute-done | bytes 2080 | tf_op jit(solution)/shard_map/ppermute | solution.py:323
  14.2 0.8 %shard_map.71 = (f32[16,128]{1,0:T(8,128)S(1)}, bf16[8,64,128]{2,1,0:T(8,128)(2,1)S(1)}, bf16[8,64,64]{2,1,0:T(8,128)(2,1)S(1)}, bf16[8,64,64]{2,1,0:T(8,128)(2,...) custom-call(bf16[3,128,2048]{2,1,0:T(8,128)(2,1)S(1)} %shard_map.68.projected, ...), custom_call_target="tpu_custom_call" | custom-call | flops 1000000 | bytes 10000 | tf_op jit(solution)/shard_map/pallas_call | solution.py:278
  15.0 1.8 %collective-permute-start.2 = (f32[16,128]{1,0:T(8,128)S(1)}, f32[16,128]{1,0:T(8,128)S(1)}, u32[]{:S(2)}, u32[]{:S(2)}) collective-permute-start(f32[16,128]{1,0:T(8,128)S(1)} %get-tuple-element.50), channel_id=1, source_target_pairs={{0,28},{4,0},{8,4},{12,8},{16,12},{20,16},{24,20},{28,24},{1,29},{... | collective-permute-start | bytes 24584 | tf_op jit(solution)/shard_map/ppermute | solution.py:343
  16.8 1.2 %shard_map.72 = (f32[24,1024]{1,0:T(8,128)S(1)}, f32[24,128]{1,0:T(8,128)S(1)}) custom-call(bf16[3,128,2048]{2,1,0:T(8,128)(2,1)S(1)} %shard_map.68.projected, bf16[1,128,2048]{2,1,0:T(8,128)(2,1)S(1)} %copy-done.1, bf16[3,8,128]{2,1,0:T(8,128)(2,1)S(1)} %convolution_convert_fusion.low_t, bf16[3,8,2048]{2,1,0:T(8,128)(2,1)S(1)} %copy-done.3), custom_call_target="tpu_custom_call" | custom-call | flops 1000000 | bytes 10000 | tf_op jit(solution)/shard_map/pallas_call | solution.py:278
  18.1 0.9 %shard_map.73 = (f32[24,1024]{1,0:T(8,128)S(1)}, f32[24,128]{1,0:T(8,128)S(1)}) custom-call(bf16[3,128,2048]{2,1,0:T(8,128)(2,1)S(1)} %shard_map.68.projected, bf16[2,8,64]{2,1,0:T(8,128)(2,1)S(1)} %collective-permute-done.1.low_kv, bf16[1,128,2048]{2,1,0:T(8,128)(2,1)S(1)} %copy-done.1, bf16[3,8,128]{2,1,0:T(8,128)(2,1)S(1)} %convolution_convert_fusion.low_t, ...), custom_call_target="tpu_custom_call" | custom-call | flops 1000000 | bytes 10000 | tf_op jit(solution)/shard_map/pallas_call | solution.py:278
  19.0 0.3 copy-done.2
  19.3 0.3 shard_map.74
  19.6 1.6 %collective-permute-done.3 = f32[4,24,768]{2,1,0:T(8,128)S(1)} collective-permute-done((f32[4,24,768]{2,1,0:T(8,128)S(1)}, f32[4,24,768]{2,1,0:T(8,128)S(1)}, u32[]{:S(2)}, u32[]{:S(2)}) %collective-permute-start.3) | collective-permute-done | bytes 294944 | tf_op jit(solution)/shard_map/ppermute | solution.py:289
  21.4 2.7 %collective-permute-start.6 = (bf16[24,768]{1,0:T(8,128)(2,1)S(1)}, bf16[24,768]{1,0:T(8,128)(2,1)S(1)}, u32[]{:S(2)}, u32[]{:S(2)}) collective-permute-start(bf16[24,768]{1,0:T(8,128)(2,1)S(1)} %get-tuple-element.61), channel_id=1, source_target_pairs={{0,6},{1,7},{2,4},{3,5},{4,2},{5,3},{6,0},{7,1},{8,14},{9,15},{10,... | collective-permute-start | bytes 110600 | tf_op jit(solution)/shard_map/ppermute | solution.py:289
  24.3 0.5 %collective-permute-done.4 = bf16[24,768]{1,0:T(8,128)(2,1)S(1)} collective-permute-done((bf16[24,768]{1,0:T(8,128)(2,1)S(1)}, bf16[24,768]{1,0:T(8,128)(2,1)S(1)}, u32[]{:S(2)}, u32[]{:S(2)}) %collective-permute-start.4) | collective-permute-done | bytes 36896 | tf_op jit(solution)/shard_map/ppermute | solution.py:289
  24.8 2.1 %collective-permute-done.6 = bf16[24,768]{1,0:T(8,128)(2,1)S(1)} collective-permute-done((bf16[24,768]{1,0:T(8,128)(2,1)S(1)}, bf16[24,768]{1,0:T(8,128)(2,1)S(1)}, u32[]{:S(2)}, u32[]{:S(2)}) %collective-permute-start.6) | collective-permute-done | bytes 36896 | tf_op jit(solution)/shard_map/ppermute | solution.py:289
  26.9 0.7 %collective-permute-done.5 = bf16[24,768]{1,0:T(8,128)(2,1)S(1)} collective-permute-done((bf16[24,768]{1,0:T(8,128)(2,1)S(1)}, bf16[24,768]{1,0:T(8,128)(2,1)S(1)}, u32[]{:S(2)}, u32[]{:S(2)}) %collective-permute-start.5) | collective-permute-done | bytes 36896 | tf_op jit(solution)/shard_map/ppermute | solution.py:289
  27.6 0.5 %collective-permute-start.9 = (bf16[24,768]{1,0:T(8,128)(2,1)S(1)}, bf16[24,768]{1,0:T(8,128)(2,1)S(1)}, u32[]{:S(2)}, u32[]{:S(2)}) collective-permute-start(bf16[24,768]{1,0:T(8,128)(2,1)S(1)} %fusion.4), channel_id=1, source_target_pairs={{0,17},{1,16},{2,19},{3,18},{4,21},{5,20},{6,23},{7,22},{8,25},{9,... | collective-permute-start | bytes 110600 | tf_op jit(solution)/shard_map/ppermute | solution.py:289
  28.2 3.0 %collective-permute-start.8 = (bf16[24,768]{1,0:T(8,128)(2,1)S(1)}, bf16[24,768]{1,0:T(8,128)(2,1)S(1)}, u32[]{:S(2)}, u32[]{:S(2)}) collective-permute-start(bf16[24,768]{1,0:T(8,128)(2,1)S(1)} %fusion.4), channel_id=1, source_target_pairs={{0,24},{1,25},{2,26},{3,27},{4,28},{5,29},{6,30},{7,31},{8,16},{9,... | collective-permute-start | bytes 110600 | tf_op jit(solution)/shard_map/ppermute | solution.py:289
  31.4 0.7 %collective-permute-done.9 = bf16[24,768]{1,0:T(8,128)(2,1)S(1)} collective-permute-done((bf16[24,768]{1,0:T(8,128)(2,1)S(1)}, bf16[24,768]{1,0:T(8,128)(2,1)S(1)}, u32[]{:S(2)}, u32[]{:S(2)}) %collective-permute-start.9) | collective-permute-done | bytes 36896 | tf_op jit(solution)/shard_map/ppermute | solution.py:289
  32.1 1.8 %collective-permute-done.8 = bf16[24,768]{1,0:T(8,128)(2,1)S(1)} collective-permute-done((bf16[24,768]{1,0:T(8,128)(2,1)S(1)}, bf16[24,768]{1,0:T(8,128)(2,1)S(1)}, u32[]{:S(2)}, u32[]{:S(2)}) %collective-permute-start.8) | collective-permute-done | bytes 36896 | tf_op jit(solution)/shard_map/ppermute | solution.py:289
  33.9 1.0 %collective-permute-done.7 = bf16[24,768]{1,0:T(8,128)(2,1)S(1)} collective-permute-done((bf16[24,768]{1,0:T(8,128)(2,1)S(1)}, bf16[24,768]{1,0:T(8,128)(2,1)S(1)}, u32[]{:S(2)}, u32[]{:S(2)}) %collective-permute-start.7) | collective-permute-done | bytes 36896 | tf_op jit(solution)/shard_map/ppermute | solution.py:289
  34.9 1.5 %collective-permute-start.12 = (bf16[24,768]{1,0:T(8,128)(2,1)S(1)}, bf16[24,768]{1,0:T(8,128)(2,1)S(1)}, u32[]{:S(2)}, u32[]{:S(2)}) collective-permute-start(bf16[24,768]{1,0:T(8,128)(2,1)S(1)} %add_convert_fusion), channel_id=1, source_target_pairs={{0,6},{1,7},{2,4},{3,5},{4,2},{5,3},{6,0},{7,1},{8,14},{9,15},{10,... | collective-permute-start | bytes 110600 | tf_op jit(solution)/shard_map/ppermute | solution.py:289
  36.4 0.5 %collective-permute-start.11 = (bf16[24,768]{1,0:T(8,128)(2,1)S(1)}, bf16[24,768]{1,0:T(8,128)(2,1)S(1)}, u32[]{:S(2)}, u32[]{:S(2)}) collective-permute-start(bf16[24,768]{1,0:T(8,128)(2,1)S(1)} %add_convert_fusion), channel_id=1, source_target_pairs={{0,3},{1,2},{2,1},{3,0},{4,7},{5,6},{6,5},{7,4},{8,11},{9,10},{10,... | collective-permute-start | bytes 110600 | tf_op jit(solution)/shard_map/ppermute | solution.py:289
  37.0 1.2 %collective-permute-start.10 = (bf16[24,768]{1,0:T(8,128)(2,1)S(1)}, bf16[24,768]{1,0:T(8,128)(2,1)S(1)}, u32[]{:S(2)}, u32[]{:S(2)}) collective-permute-start(bf16[24,768]{1,0:T(8,128)(2,1)S(1)} %add_convert_fusion), channel_id=1, source_target_pairs={{0,5},{1,4},{2,7},{3,6},{4,1},{5,0},{6,3},{7,2},{8,13},{9,12},{10,... | collective-permute-start | bytes 110600 | tf_op jit(solution)/shard_map/ppermute | solution.py:289
  38.2 1.7 %collective-permute-done.12 = bf16[24,768]{1,0:T(8,128)(2,1)S(1)} collective-permute-done((bf16[24,768]{1,0:T(8,128)(2,1)S(1)}, bf16[24,768]{1,0:T(8,128)(2,1)S(1)}, u32[]{:S(2)}, u32[]{:S(2)}) %collective-permute-start.12) | collective-permute-done | bytes 36896 | tf_op jit(solution)/shard_map/ppermute | solution.py:289
  39.9 0.8 %collective-permute-done.11 = bf16[24,768]{1,0:T(8,128)(2,1)S(1)} collective-permute-done((bf16[24,768]{1,0:T(8,128)(2,1)S(1)}, bf16[24,768]{1,0:T(8,128)(2,1)S(1)}, u32[]{:S(2)}, u32[]{:S(2)}) %collective-permute-start.11) | collective-permute-done | bytes 36896 | tf_op jit(solution)/shard_map/ppermute | solution.py:289
  40.6 0.5 %collective-permute-start.13 = (bf16[4,24,768]{2,1,0:T(8,128)(2,1)S(1)}, bf16[4,24,768]{2,1,0:T(8,128)(2,1)S(1)}, u32[]{:S(2)}, u32[]{:S(2)}) collective-permute-start(bf16[4,24,768]{2,1,0:T(8,128)(2,1)S(1)} %pad_maximum_fusion.pieces), channel_id=1, source_target_pairs={{0,1},{1,0},{2,3},{3,2},{4,5},{5,4},{6,7},{7,6},{8,9},{9,8},{10,11... | collective-permute-start | bytes 442376 | tf_op jit(solution)/shard_map/ppermute | solution.py:289
  41.1 1.0 %collective-permute-done.13.pieces = bf16[4,24,768]{2,1,0:T(8,128)(2,1)S(1)} collective-permute-done((bf16[4,24,768]{2,1,0:T(8,128)(2,1)S(1)}, bf16[4,24,768]{2,1,0:T(8,128)(2,1)S(1)}, u32[]{:S(2)}, u32[]{:S(2)}) %collective-permute-start.13) | collective-permute-done | bytes 147488 | tf_op jit(solution)/shard_map/ppermute | solution.py:289
  42.1 0.9 %shard_map.76 = (f32[3,8,4096]{2,1,0:T(8,128)}, f32[3,8,2048]{2,1,0:T(8,128)}) custom-call(bf16[4,24,768]{2,1,0:T(8,128)(2,1)S(1)} %collective-permute-done.13.pieces, f32[3,8,4096]{2,1,0:T(8,128)S(1)} %get-tuple-element.56.down_in, f32[3,8,2048]{2,1,0:T(8,128)S(1)} %get-tuple-element.57.up_in), custom_call_target="tpu_custom_call" | custom-call | flops 1000000 | bytes 10000 | tf_op jit(solution)/shard_map/pallas_call | solution.py:278
  (23 shorter events, 0.9 us)
Async XLA Ops:
  0.6 4.1 %copy-start = (bf16[3,8,4096]{2,1,0:T(8,128)(2,1)S(1)}, bf16[3,8,4096]{2,1,0:T(8,128)(2,1)}, u32[]{:S(2)}) copy-start(bf16[3,8,4096]{2,1,0:T(8,128)(2,1)} %param.8) | copy-start | bytes 589828
  0.6 7.4 %copy-start.4 = (bf16[3,1,128,2048]{3,2,1,0:T(8,128)(2,1)S(1)}, bf16[3,1,128,2048]{3,2,1,0:T(8,128)(2,1)}, u32[]{:S(2)}) copy-start(bf16[3,1,128,2048]{3,2,1,0:T(8,128)(2,1)} %frozen.1) | copy-start | bytes 4718596
  0.7 7.4 %copy-start.3 = (bf16[3,8,2048]{2,1,0:T(8,128)(2,1)S(1)}, bf16[3,8,2048]{2,1,0:T(8,128)(2,1)}, u32[]{:S(2)}) copy-start(bf16[3,8,2048]{2,1,0:T(8,128)(2,1)} %up.10) | copy-start | bytes 294916
  1.8 12.4 %collective-permute-start = (bf16[2,64,1024]{2,1,0:T(8,128)(2,1)S(1)}, bf16[2,64,1024]{2,1,0:T(8,128)(2,1)S(1)}, u32[]{:S(2)}, u32[]{:S(2)}) collective-permute-start(bf16[2,64,1024]{2,1,0:T(8,128)(2,1)S(1)} %slice_bitcast_fusion), channel_id=1, source_target_pairs={{0,4},{4,8},{8,12},{12,16},{16,20},{20,24},{24,28},{28,0},{1,5},{5... | collective-permute-start | bytes 786440 | tf_op jit(solution)/shard_map/ppermute | solution.py:321
  6.5 2.2 %copy-start.1 = (bf16[1,128,2048]{2,1,0:T(8,128)(2,1)S(1)}, bf16[1,128,2048]{2,1,0:T(8,128)(2,1)}, u32[]{:S(2)}) copy-start(bf16[1,128,2048]{2,1,0:T(8,128)(2,1)} %grad.8) | copy-start | bytes 1572868
  6.5 7.7 %collective-permute-start.1 = (bf16[2,8,64]{2,1,0:T(8,128)(2,1)S(1)}, bf16[2,8,64]{2,1,0:T(8,128)(2,1)S(1)}, u32[]{:S(2)}, u32[]{:S(2)}) collective-permute-start(bf16[2,8,64]{2,1,0:T(8,128)(2,1)S(1)} %slice.28), channel_id=1, source_target_pairs={{0,4},{4,8},{8,12},{12,16},{16,20},{20,24},{24,28},{28,0},{1,5},{5... | collective-permute-start | bytes 6152 | tf_op jit(solution)/shard_map/ppermute | solution.py:323
  15.0 3.9 %collective-permute-start.2 = (f32[16,128]{1,0:T(8,128)S(1)}, f32[16,128]{1,0:T(8,128)S(1)}, u32[]{:S(2)}, u32[]{:S(2)}) collective-permute-start(f32[16,128]{1,0:T(8,128)S(1)} %get-tuple-element.50), channel_id=1, source_target_pairs={{0,28},{4,0},{8,4},{12,8},{16,12},{20,16},{24,20},{28,24},{1,29},{... | collective-permute-start | bytes 24584 | tf_op jit(solution)/shard_map/ppermute | solution.py:343
  18.0 1.2 %copy-start.2 = (bf16[1,128,4096]{2,1,0:T(8,128)(2,1)S(1)}, bf16[1,128,4096]{2,1,0:T(8,128)(2,1)}, u32[]{:S(2)}) copy-start(bf16[1,128,4096]{2,1,0:T(8,128)(2,1)} %tokens.1) | copy-start | bytes 3145732
  19.6 1.6 %collective-permute-start.3 = (f32[4,24,768]{2,1,0:T(8,128)S(1)}, f32[4,24,768]{2,1,0:T(8,128)S(1)}, u32[]{:S(2)}, u32[]{:S(2)}) collective-permute-start(f32[4,24,768]{2,1,0:T(8,128)S(1)} %get-tuple-element.55), channel_id=1, source_target_pairs={{0,1},{1,0},{2,3},{3,2},{4,5},{5,4},{6,7},{7,6},{8,9},{9,8},{10,11... | collective-permute-start | bytes 884744 | tf_op jit(solution)/shard_map/ppermute | solution.py:289
  21.3 3.5 %collective-permute-start.4 = (bf16[24,768]{1,0:T(8,128)(2,1)S(1)}, bf16[24,768]{1,0:T(8,128)(2,1)S(1)}, u32[]{:S(2)}, u32[]{:S(2)}) collective-permute-start(bf16[24,768]{1,0:T(8,128)(2,1)S(1)} %get-tuple-element.60), channel_id=1, source_target_pairs={{0,5},{1,4},{2,7},{3,6},{4,1},{5,0},{6,3},{7,2},{8,13},{9,12},{10,... | collective-permute-start | bytes 110600 | tf_op jit(solution)/shard_map/ppermute | solution.py:289
  21.4 5.5 %collective-permute-start.6 = (bf16[24,768]{1,0:T(8,128)(2,1)S(1)}, bf16[24,768]{1,0:T(8,128)(2,1)S(1)}, u32[]{:S(2)}, u32[]{:S(2)}) collective-permute-start(bf16[24,768]{1,0:T(8,128)(2,1)S(1)} %get-tuple-element.61), channel_id=1, source_target_pairs={{0,6},{1,7},{2,4},{3,5},{4,2},{5,3},{6,0},{7,1},{8,14},{9,15},{10,... | collective-permute-start | bytes 110600 | tf_op jit(solution)/shard_map/ppermute | solution.py:289
  24.1 3.5 %collective-permute-start.5 = (bf16[24,768]{1,0:T(8,128)(2,1)S(1)}, bf16[24,768]{1,0:T(8,128)(2,1)S(1)}, u32[]{:S(2)}, u32[]{:S(2)}) collective-permute-start(bf16[24,768]{1,0:T(8,128)(2,1)S(1)} %get-tuple-element.62), channel_id=1, source_target_pairs={{0,3},{1,2},{2,1},{3,0},{4,7},{5,6},{6,5},{7,4},{8,11},{9,10},{10,... | collective-permute-start | bytes 110600 | tf_op jit(solution)/shard_map/ppermute | solution.py:289
  27.6 4.5 %collective-permute-start.9 = (bf16[24,768]{1,0:T(8,128)(2,1)S(1)}, bf16[24,768]{1,0:T(8,128)(2,1)S(1)}, u32[]{:S(2)}, u32[]{:S(2)}) collective-permute-start(bf16[24,768]{1,0:T(8,128)(2,1)S(1)} %fusion.4), channel_id=1, source_target_pairs={{0,17},{1,16},{2,19},{3,18},{4,21},{5,20},{6,23},{7,22},{8,25},{9,... | collective-permute-start | bytes 110600 | tf_op jit(solution)/shard_map/ppermute | solution.py:289
  28.2 5.8 %collective-permute-start.8 = (bf16[24,768]{1,0:T(8,128)(2,1)S(1)}, bf16[24,768]{1,0:T(8,128)(2,1)S(1)}, u32[]{:S(2)}, u32[]{:S(2)}) collective-permute-start(bf16[24,768]{1,0:T(8,128)(2,1)S(1)} %fusion.4), channel_id=1, source_target_pairs={{0,24},{1,25},{2,26},{3,27},{4,28},{5,29},{6,30},{7,31},{8,16},{9,... | collective-permute-start | bytes 110600 | tf_op jit(solution)/shard_map/ppermute | solution.py:289
  31.1 3.8 %collective-permute-start.7 = (bf16[24,768]{1,0:T(8,128)(2,1)S(1)}, bf16[24,768]{1,0:T(8,128)(2,1)S(1)}, u32[]{:S(2)}, u32[]{:S(2)}) collective-permute-start(bf16[24,768]{1,0:T(8,128)(2,1)S(1)} %fusion.4), channel_id=1, source_target_pairs={{0,9},{1,8},{2,11},{3,10},{4,13},{5,12},{6,15},{7,14},{8,1},{9,0},... | collective-permute-start | bytes 110600 | tf_op jit(solution)/shard_map/ppermute | solution.py:289
  34.9 5.0 %collective-permute-start.12 = (bf16[24,768]{1,0:T(8,128)(2,1)S(1)}, bf16[24,768]{1,0:T(8,128)(2,1)S(1)}, u32[]{:S(2)}, u32[]{:S(2)}) collective-permute-start(bf16[24,768]{1,0:T(8,128)(2,1)S(1)} %add_convert_fusion), channel_id=1, source_target_pairs={{0,6},{1,7},{2,4},{3,5},{4,2},{5,3},{6,0},{7,1},{8,14},{9,15},{10,... | collective-permute-start | bytes 110600 | tf_op jit(solution)/shard_map/ppermute | solution.py:289
  36.4 4.2 %collective-permute-start.11 = (bf16[24,768]{1,0:T(8,128)(2,1)S(1)}, bf16[24,768]{1,0:T(8,128)(2,1)S(1)}, u32[]{:S(2)}, u32[]{:S(2)}) collective-permute-start(bf16[24,768]{1,0:T(8,128)(2,1)S(1)} %add_convert_fusion), channel_id=1, source_target_pairs={{0,3},{1,2},{2,1},{3,0},{4,7},{5,6},{6,5},{7,4},{8,11},{9,10},{10,... | collective-permute-start | bytes 110600 | tf_op jit(solution)/shard_map/ppermute | solution.py:289
  37.0 3.7 %collective-permute-start.10 = (bf16[24,768]{1,0:T(8,128)(2,1)S(1)}, bf16[24,768]{1,0:T(8,128)(2,1)S(1)}, u32[]{:S(2)}, u32[]{:S(2)}) collective-permute-start(bf16[24,768]{1,0:T(8,128)(2,1)S(1)} %add_convert_fusion), channel_id=1, source_target_pairs={{0,5},{1,4},{2,7},{3,6},{4,1},{5,0},{6,3},{7,2},{8,13},{9,12},{10,... | collective-permute-start | bytes 110600 | tf_op jit(solution)/shard_map/ppermute | solution.py:289
  40.6 1.5 %collective-permute-start.13 = (bf16[4,24,768]{2,1,0:T(8,128)(2,1)S(1)}, bf16[4,24,768]{2,1,0:T(8,128)(2,1)S(1)}, u32[]{:S(2)}, u32[]{:S(2)}) collective-permute-start(bf16[4,24,768]{2,1,0:T(8,128)(2,1)S(1)} %pad_maximum_fusion.pieces), channel_id=1, source_target_pairs={{0,1},{1,0},{2,3},{3,2},{4,5},{5,4},{6,7},{7,6},{8,9},{9,8},{10,11... | collective-permute-start | bytes 442376 | tf_op jit(solution)/shard_map/ppermute | solution.py:289

commit v10 on v9

--- a/solution.py
+++ b/solution.py
@@ -151,10 +151,8 @@
 ):
     half = projected.shape[1] // 2
     columns = shifted_columns(up)
-    near = []
-    for h, cols in enumerate(columns):
-        here = slice(h * HEAD_DIM, (h + 1) * HEAD_DIM)
-        near.append([project(frozen_kv[j, :, here], low_kv[j], up[j + 1, :, cols]) for j in range(2)])
+    wide = [project(frozen_kv[j], low_kv[j], up[j + 1, :, columns[0].start :]) for j in range(2)]
+    near = [[x[:, h * HEAD_DIM : (h + 1) * HEAD_DIM] for x in wide] for h in range(len(columns))]
     sts = [nt(near[h][0], projected[0, :half, cols]) for h, cols in enumerate(columns)]
     dps = [nt(near[h][1], grad[0, :half, cols]) for h, cols in enumerate(columns)]
     found = []
@@ -294,7 +292,7 @@
     partner = {1: dps | 1, 2: 3, 3: dps | 2}
     keep = keep + swap(send, 1, total)
     got = [swap(keep[s].astype(BF), partner[s], total).astype(F32) for s in (1, 2, 3)]
-    own = keep[0] + got[0] + got[1] + got[2]
+    own = keep[0] + got[2] + got[0] + got[1]
     bit = 2
     while bit < seqs:
         steps = [bit, 2 * bit, 3 * bit] if 2 * bit < seqs else [bit]
@@ -332,18 +330,17 @@
     e, dp, top, total, bk, bv = call(
         far_ready, [square, square, line, line, pairs, pairs], projected, grad, up_weight
     )
-    bk, rank_plain = lax.optimization_barrier((bk, rank_plain))
+    up_near, rank_near = call(
+        functools.partial(group_kernel, half, half_width), [up_half, rank_side], projected, grad, low_t, up_weight
+    )
+    bk, rank_plain, rank_near = lax.optimization_barrier((bk, rank_plain, rank_near))
     squares = sds((n, half, half), BF)
     cross, near, pb, ds, factor, dot = call(
         far_scores,
         [sds((2 * RANK, count), F32), sds((n, half, HEAD_DIM), BF), squares, squares, line, line],
         projected, frozen_kv, low_kv, grad, up_weight, e, dp, top, total, bk, bv,
     )
-    factor, *held = lax.optimization_barrier((factor, grad, low_t, up_weight))
     cross = lax.ppermute(cross, "seq", backward)
-    up_near, rank_near = call(
-        functools.partial(group_kernel, half, half_width), [up_half, rank_side], projected, *held
-    )
     up_far, rank_far = call(
         far_rest, [up_half, rank_side],
         projected, low_kv, grad, low_t, up_weight, e, dp, bk, bv, near, pb, ds, factor, dot,

time: 43.2 us -> 42.8 us (level)
  waiting for transfers between devices: 15.4 us -> 14.2 us
  starting transfers between devices: 16.8 us -> 17.9 us
    ppermute x1, waiting for transfers between devices: 3.52 us -> 2.25 us  [on_device(): low_kv = lax.ppermute(low_t[1:, :, half:], 'seq', forward)]
    ppermute x11, starting transfers between devices: 10.5 us -> 11.6 us  [swap(): return lax.ppermute(x, AXES, [(i, i ^ bits) for i in range(total)])]
    ppermute x1, waiting for transfers between devices: 0.01 us -> 1.02 us  [on_device(): cross = lax.ppermute(cross, 'seq', backward)]
    ppermute x11, waiting for transfers between devices: 11.8 us -> 11 us  [swap(): return lax.ppermute(x, AXES, [(i, i ^ bits) for i in range(total)])]
  transfers between devices with their start and end apart: 14 -> 14, of which waited for: 11 -> 10; matrix products, arithmetic and copies ran while one was open for 4% -> 4% of each run, Pallas kernels for 11% -> 11%
where the time goes in v10:
time: 42.8 us; the launch traced here: 42.6 us
  starting transfers between devices  17.9 us (42%)
  waiting for transfers between devices  14.2 us (33%)
  Pallas kernels  6.77 us (16%)
  matrix products  1.6 us (4%)
  local copies, waits for them, and re-layouts  1.22 us (3%)
  between operations  0.75 us (2%)
    ppermute x11, starting transfers between devices, swap(): return lax.ppermute(x, AXES, [(i, i ^ bits) for i in range(total)])  11.6 us
    ppermute x11, waiting for transfers between devices, swap(): return lax.ppermute(x, AXES, [(i, i ^ bits) for i in range(total)])  11 us
    pallas_call x9, Pallas kernels, call(): pl.pallas_call(kernel, out_shape=outs, in_specs=[VMEM] * len(args), out_s...  6.77 us
    ppermute x1, starting transfers between devices, on_device(): frozen_kv = lax.ppermute(frozen[1:, 0, half:, half_width:], 'seq', forward)  2.99 us
    ppermute x1, waiting for transfers between devices, on_device(): low_kv = lax.ppermute(low_t[1:, :, half:], 'seq', forward)  2.25 us
    ppermute x1, starting transfers between devices, on_device(): cross = lax.ppermute(cross, 'seq', backward)  1.78 us
    dot_general x1, matrix products, on_device(): jnp.einsum('psw,gw->psg', down_weight, tokens[0], preferred_element_type=...  1.6 us
    ppermute x1, starting transfers between devices, on_device(): low_kv = lax.ppermute(low_t[1:, :, half:], 'seq', forward)  1.56 us
  transfers between devices with their start and end apart: 14, of which 10 were waited for; matrix products, arithmetic and copies ran while one was open for 4% of the time, Pallas kernels for 11%

profile of v10, /device:TPU:0, one launch (start us, length us, event | category | flops | bytes accessed | tf_op | source)
XLA Modules:
  0.0 42.6 jit_solution(6391081232308431208)
XLA Ops:
  0.7 1.1 %slice_bitcast_fusion = bf16[2,64,1024]{2,1,0:T(8,128)(2,1)S(1)} fusion(bf16[3,1,128,2048]{3,2,0,1:T(8,128)(2,1)} %bitcast.28), kind=kLoop, calls=%fused_computation.2 | loop fusion | bytes 524288 | tf_op jit(solution)/shard_map/squeeze | solution.py:319
  1.8 3.0 %collective-permute-start.1 = (bf16[2,64,1024]{2,1,0:T(8,128)(2,1)S(1)}, bf16[2,64,1024]{2,1,0:T(8,128)(2,1)S(1)}, u32[]{:S(2)}, u32[]{:S(2)}) collective-permute-start(bf16[2,64,1024]{2,1,0:T(8,128)(2,1)S(1)} %slice_bitcast_fusion), channel_id=1, source_target_pairs={{0,4},{4,8},{8,12},{12,16},{16,20},{20,24},{24,28},{28,0},{1,5},{5... | collective-permute-start | bytes 786440 | tf_op jit(solution)/shard_map/ppermute | solution.py:319
  4.8 1.6 %convolution_convert_fusion.low_t = bf16[3,8,128]{2,1,0:T(8,128)(2,1)S(1)} fusion(bf16[3,8,4096]{2,1,0:T(8,128)(2,1)S(1)} %copy-done, bf16[1,128,4096]{2,1,0:T(8,128)(2,1)} %tokens.1), kind=kOutput, calls=%fused_computation | convolution fusion | flops 25168896 | bytes 1251328 | tf_op jit(solution)/shard_map/psw,gw->psg/dot_general | solution.py:320
  6.5 1.6 %collective-permute-start = (bf16[2,8,64]{2,1,0:T(8,128)(2,1)S(1)}, bf16[2,8,64]{2,1,0:T(8,128)(2,1)S(1)}, u32[]{:S(2)}, u32[]{:S(2)}) collective-permute-start(bf16[2,8,64]{2,1,0:T(8,128)(2,1)S(1)} %slice.27), channel_id=1, source_target_pairs={{0,4},{4,8},{8,12},{12,16},{16,20},{20,24},{24,28},{28,0},{1,5},{5... | collective-permute-start | bytes 6152 | tf_op jit(solution)/shard_map/ppermute | solution.py:321
  8.0 0.6 %shard_map.68.projected = bf16[3,128,2048]{2,1,0:T(8,128)(2,1)S(1)} custom-call(bf16[3,1,128,2048]{3,2,1,0:T(8,128)(2,1)S(1)} %copy-done.4, bf16[3,8,128]{2,1,0:T(8,128)(2,1)S(1)} %convolution_convert_fusion.low_t, bf16[3,8,2048]{2,1,0:T(8,128)(2,1)S(1)} %copy-done.3), custom_call_target="tpu_custom_call" | custom-call | flops 1000000 | bytes 10000 | tf_op jit(solution)/shard_map/pallas_call | solution.py:276
  8.6 1.2 %shard_map.71 = (f32[24,1024]{1,0:T(8,128)S(1)}, f32[24,128]{1,0:T(8,128)S(1)}) custom-call(bf16[3,128,2048]{2,1,0:T(8,128)(2,1)S(1)} %shard_map.68.projected, bf16[1,128,2048]{2,1,0:T(8,128)(2,1)S(1)} %copy-done.1, bf16[3,8,128]{2,1,0:T(8,128)(2,1)S(1)} %convolution_convert_fusion.low_t, bf16[3,8,2048]{2,1,0:T(8,128)(2,1)S(1)} %copy-done.3), custom_call_target="tpu_custom_call" | custom-call | flops 1000000 | bytes 10000 | tf_op jit(solution)/shard_map/pallas_call | solution.py:276
  9.9 1.6 %shard_map.70 = (f32[24,1024]{1,0:T(8,128)S(1)}, f32[24,128]{1,0:T(8,128)S(1)}) custom-call(bf16[3,128,2048]{2,1,0:T(8,128)(2,1)S(1)} %shard_map.68.projected, bf16[1,128,2048]{2,1,0:T(8,128)(2,1)S(1)} %copy-done.1, bf16[3,8,128]{2,1,0:T(8,128)(2,1)S(1)} %convolution_convert_fusion.low_t, bf16[3,8,2048]{2,1,0:T(8,128)(2,1)S(1)} %copy-done.3), custom_call_target="tpu_custom_call" | custom-call | flops 1000000 | bytes 10000 | tf_op jit(solution)/shard_map/pallas_call | solution.py:276
  11.5 0.4 %shard_map.69 = (f32[8,64,64]{2,1,0:T(8,128)S(1)}, f32[8,64,64]{2,1,0:T(8,128)S(1)}, f32[8,64]{1,0:T(8,128)S(1)}, f32[8,64]{1,0:T(8,128)S(1)}, bf16[8,16,64]{2,1...) custom-call(bf16[3,128,2048]{2,1,0:T(8,128)(2,1)S(1)} %shard_map.68.projected, bf16[1,128,2048]{2,1,0:T(8,128)(2,1)S(1)} %copy-done.1, ...), custom_call_target="tpu_custom_call" | custom-call | flops 1000000 | bytes 10000 | tf_op jit(solution)/shard_map/pallas_call | solution.py:276
  11.9 2.3 %collective-permute-done.low_kv = bf16[2,8,64]{2,1,0:T(8,128)(2,1)S(1)} collective-permute-done((bf16[2,8,64]{2,1,0:T(8,128)(2,1)S(1)}, bf16[2,8,64]{2,1,0:T(8,128)(2,1)S(1)}, u32[]{:S(2)}, u32[]{:S(2)}) %collective-permute-start) | collective-permute-done | bytes 2080 | tf_op jit(solution)/shard_map/ppermute | solution.py:321
  14.2 0.8 %shard_map.72 = (f32[16,128]{1,0:T(8,128)S(1)}, bf16[8,64,128]{2,1,0:T(8,128)(2,1)S(1)}, bf16[8,64,64]{2,1,0:T(8,128)(2,1)S(1)}, bf16[8,64,64]{2,1,0:T(8,128)(2,...) custom-call(bf16[3,128,2048]{2,1,0:T(8,128)(2,1)S(1)} %shard_map.68.projected, ...), custom_call_target="tpu_custom_call" | custom-call | flops 1000000 | bytes 10000 | tf_op jit(solution)/shard_map/pallas_call | solution.py:276
  15.0 1.8 %collective-permute-start.2 = (f32[16,128]{1,0:T(8,128)S(1)}, f32[16,128]{1,0:T(8,128)S(1)}, u32[]{:S(2)}, u32[]{:S(2)}) collective-permute-start(f32[16,128]{1,0:T(8,128)S(1)} %get-tuple-element.44), channel_id=1, source_target_pairs={{0,28},{4,0},{8,4},{12,8},{16,12},{20,16},{24,20},{28,24},{1,29},{... | collective-permute-start | bytes 24584 | tf_op jit(solution)/shard_map/ppermute | solution.py:343
  16.8 0.9 %shard_map.73 = (f32[24,1024]{1,0:T(8,128)S(1)}, f32[24,128]{1,0:T(8,128)S(1)}) custom-call(bf16[3,128,2048]{2,1,0:T(8,128)(2,1)S(1)} %shard_map.68.projected, bf16[2,8,64]{2,1,0:T(8,128)(2,1)S(1)} %collective-permute-done.low_kv, bf16[1,128,2048]{2,1,0:T(8,128)(2,1)S(1)} %copy-done.1, bf16[3,8,128]{2,1,0:T(8,128)(2,1)S(1)} %convolution_convert_fusion.low_t, ...), custom_call_target="tpu_custom_call" | custom-call | flops 1000000 | bytes 10000 | tf_op jit(solution)/shard_map/pallas_call | solution.py:276
  17.7 1.0 %collective-permute-done.2.cross = f32[16,128]{1,0:T(8,128)S(1)} collective-permute-done((f32[16,128]{1,0:T(8,128)S(1)}, f32[16,128]{1,0:T(8,128)S(1)}, u32[]{:S(2)}, u32[]{:S(2)}) %collective-permute-start.2) | collective-permute-done | bytes 8224 | tf_op jit(solution)/shard_map/ppermute | solution.py:343
  18.7 0.3 shard_map.74
  19.1 1.6 %collective-permute-done.3 = f32[4,24,768]{2,1,0:T(8,128)S(1)} collective-permute-done((f32[4,24,768]{2,1,0:T(8,128)S(1)}, f32[4,24,768]{2,1,0:T(8,128)S(1)}, u32[]{:S(2)}, u32[]{:S(2)}) %collective-permute-start.3) | collective-permute-done | bytes 294944 | tf_op jit(solution)/shard_map/ppermute | solution.py:287
  20.7 1.2 %collective-permute-start.4 = (bf16[24,768]{1,0:T(8,128)(2,1)S(1)}, bf16[24,768]{1,0:T(8,128)(2,1)S(1)}, u32[]{:S(2)}, u32[]{:S(2)}) collective-permute-start(bf16[24,768]{1,0:T(8,128)(2,1)S(1)} %get-tuple-element.54), channel_id=1, source_target_pairs={{0,6},{1,7},{2,4},{3,5},{4,2},{5,3},{6,0},{7,1},{8,14},{9,15},{10,... | collective-permute-start | bytes 110600 | tf_op jit(solution)/shard_map/ppermute | solution.py:287
  21.9 0.2 collective-permute-start.6
  22.1 1.9 %collective-permute-start.5 = (bf16[24,768]{1,0:T(8,128)(2,1)S(1)}, bf16[24,768]{1,0:T(8,128)(2,1)S(1)}, u32[]{:S(2)}, u32[]{:S(2)}) collective-permute-start(bf16[24,768]{1,0:T(8,128)(2,1)S(1)} %get-tuple-element.56), channel_id=1, source_target_pairs={{0,5},{1,4},{2,7},{3,6},{4,1},{5,0},{6,3},{7,2},{8,13},{9,12},{10,... | collective-permute-start | bytes 110600 | tf_op jit(solution)/shard_map/ppermute | solution.py:287
  24.0 1.8 %collective-permute-done.4 = bf16[24,768]{1,0:T(8,128)(2,1)S(1)} collective-permute-done((bf16[24,768]{1,0:T(8,128)(2,1)S(1)}, bf16[24,768]{1,0:T(8,128)(2,1)S(1)}, u32[]{:S(2)}, u32[]{:S(2)}) %collective-permute-start.4) | collective-permute-done | bytes 36896 | tf_op jit(solution)/shard_map/ppermute | solution.py:287
  25.7 0.3 collective-permute-done.6
  26.1 2.1 %collective-permute-start.9 = (bf16[24,768]{1,0:T(8,128)(2,1)S(1)}, bf16[24,768]{1,0:T(8,128)(2,1)S(1)}, u32[]{:S(2)}, u32[]{:S(2)}) collective-permute-start(bf16[24,768]{1,0:T(8,128)(2,1)S(1)} %fusion.4), channel_id=1, source_target_pairs={{0,17},{1,16},{2,19},{3,18},{4,21},{5,20},{6,23},{7,22},{8,25},{9,... | collective-permute-start | bytes 110600 | tf_op jit(solution)/shard_map/ppermute | solution.py:287
  28.2 2.5 %collective-permute-start.8 = (bf16[24,768]{1,0:T(8,128)(2,1)S(1)}, bf16[24,768]{1,0:T(8,128)(2,1)S(1)}, u32[]{:S(2)}, u32[]{:S(2)}) collective-permute-start(bf16[24,768]{1,0:T(8,128)(2,1)S(1)} %fusion.4), channel_id=1, source_target_pairs={{0,24},{1,25},{2,26},{3,27},{4,28},{5,29},{6,30},{7,31},{8,16},{9,... | collective-permute-start | bytes 110600 | tf_op jit(solution)/shard_map/ppermute | solution.py:287
  30.7 0.2 collective-permute-start.7
  30.9 3.3 %collective-permute-done.8 = bf16[24,768]{1,0:T(8,128)(2,1)S(1)} collective-permute-done((bf16[24,768]{1,0:T(8,128)(2,1)S(1)}, bf16[24,768]{1,0:T(8,128)(2,1)S(1)}, u32[]{:S(2)}, u32[]{:S(2)}) %collective-permute-start.8) | collective-permute-done | bytes 36896 | tf_op jit(solution)/shard_map/ppermute | solution.py:287
  34.1 0.6 %collective-permute-done.7 = bf16[24,768]{1,0:T(8,128)(2,1)S(1)} collective-permute-done((bf16[24,768]{1,0:T(8,128)(2,1)S(1)}, bf16[24,768]{1,0:T(8,128)(2,1)S(1)}, u32[]{:S(2)}, u32[]{:S(2)}) %collective-permute-start.7) | collective-permute-done | bytes 36896 | tf_op jit(solution)/shard_map/ppermute | solution.py:287
  34.7 1.4 %collective-permute-start.12 = (bf16[24,768]{1,0:T(8,128)(2,1)S(1)}, bf16[24,768]{1,0:T(8,128)(2,1)S(1)}, u32[]{:S(2)}, u32[]{:S(2)}) collective-permute-start(bf16[24,768]{1,0:T(8,128)(2,1)S(1)} %add_convert_fusion), channel_id=1, source_target_pairs={{0,6},{1,7},{2,4},{3,5},{4,2},{5,3},{6,0},{7,1},{8,14},{9,15},{10,... | collective-permute-start | bytes 110600 | tf_op jit(solution)/shard_map/ppermute | solution.py:287
  36.2 1.8 %collective-permute-start.10 = (bf16[24,768]{1,0:T(8,128)(2,1)S(1)}, bf16[24,768]{1,0:T(8,128)(2,1)S(1)}, u32[]{:S(2)}, u32[]{:S(2)}) collective-permute-start(bf16[24,768]{1,0:T(8,128)(2,1)S(1)} %add_convert_fusion), channel_id=1, source_target_pairs={{0,5},{1,4},{2,7},{3,6},{4,1},{5,0},{6,3},{7,2},{8,13},{9,12},{10,... | collective-permute-start | bytes 110600 | tf_op jit(solution)/shard_map/ppermute | solution.py:287
  38.0 1.8 %collective-permute-done.12 = bf16[24,768]{1,0:T(8,128)(2,1)S(1)} collective-permute-done((bf16[24,768]{1,0:T(8,128)(2,1)S(1)}, bf16[24,768]{1,0:T(8,128)(2,1)S(1)}, u32[]{:S(2)}, u32[]{:S(2)}) %collective-permute-start.12) | collective-permute-done | bytes 36896 | tf_op jit(solution)/shard_map/ppermute | solution.py:287
  39.8 0.5 %collective-permute-done.11 = bf16[24,768]{1,0:T(8,128)(2,1)S(1)} collective-permute-done((bf16[24,768]{1,0:T(8,128)(2,1)S(1)}, bf16[24,768]{1,0:T(8,128)(2,1)S(1)}, u32[]{:S(2)}, u32[]{:S(2)}) %collective-permute-start.11) | collective-permute-done | bytes 36896 | tf_op jit(solution)/shard_map/ppermute | solution.py:287
  40.3 0.2 collective-permute-start.13
  40.5 1.2 %collective-permute-done.13.pieces = bf16[4,24,768]{2,1,0:T(8,128)(2,1)S(1)} collective-permute-done((bf16[4,24,768]{2,1,0:T(8,128)(2,1)S(1)}, bf16[4,24,768]{2,1,0:T(8,128)(2,1)S(1)}, u32[]{:S(2)}, u32[]{:S(2)}) %collective-permute-start.13) | collective-permute-done | bytes 147488 | tf_op jit(solution)/shard_map/ppermute | solution.py:287
  41.8 0.9 %shard_map.76 = (f32[3,8,4096]{2,1,0:T(8,128)}, f32[3,8,2048]{2,1,0:T(8,128)}) custom-call(bf16[4,24,768]{2,1,0:T(8,128)(2,1)S(1)} %collective-permute-done.13.pieces, f32[3,8,4096]{2,1,0:T(8,128)S(1)} %get-tuple-element.50.down_in, f32[3,8,2048]{2,1,0:T(8,128)S(1)} %get-tuple-element.51.up_in), custom_call_target="tpu_custom_call" | custom-call | flops 1000000 | bytes 10000 | tf_op jit(solution)/shard_map/pallas_call | solution.py:276
  (23 shorter events, 0.4 us)
Async XLA Ops:
  0.6 4.1 %copy-start = (bf16[3,8,4096]{2,1,0:T(8,128)(2,1)S(1)}, bf16[3,8,4096]{2,1,0:T(8,128)(2,1)}, u32[]{:S(2)}) copy-start(bf16[3,8,4096]{2,1,0:T(8,128)(2,1)} %param.8) | copy-start | bytes 589828
  0.6 7.4 %copy-start.4 = (bf16[3,1,128,2048]{3,2,1,0:T(8,128)(2,1)S(1)}, bf16[3,1,128,2048]{3,2,1,0:T(8,128)(2,1)}, u32[]{:S(2)}) copy-start(bf16[3,1,128,2048]{3,2,1,0:T(8,128)(2,1)} %frozen.1) | copy-start | bytes 4718596
  0.7 7.4 %copy-start.3 = (bf16[3,8,2048]{2,1,0:T(8,128)(2,1)S(1)}, bf16[3,8,2048]{2,1,0:T(8,128)(2,1)}, u32[]{:S(2)}) copy-start(bf16[3,8,2048]{2,1,0:T(8,128)(2,1)} %up.11) | copy-start | bytes 294916
  1.8 12.4 %collective-permute-start.1 = (bf16[2,64,1024]{2,1,0:T(8,128)(2,1)S(1)}, bf16[2,64,1024]{2,1,0:T(8,128)(2,1)S(1)}, u32[]{:S(2)}, u32[]{:S(2)}) collective-permute-start(bf16[2,64,1024]{2,1,0:T(8,128)(2,1)S(1)} %slice_bitcast_fusion), channel_id=1, source_target_pairs={{0,4},{4,8},{8,12},{12,16},{16,20},{20,24},{24,28},{28,0},{1,5},{5... | collective-permute-start | bytes 786440 | tf_op jit(solution)/shard_map/ppermute | solution.py:319
  6.5 2.2 %copy-start.1 = (bf16[1,128,2048]{2,1,0:T(8,128)(2,1)S(1)}, bf16[1,128,2048]{2,1,0:T(8,128)(2,1)}, u32[]{:S(2)}) copy-start(bf16[1,128,2048]{2,1,0:T(8,128)(2,1)} %grad.9) | copy-start | bytes 1572868
  6.5 7.7 %collective-permute-start = (bf16[2,8,64]{2,1,0:T(8,128)(2,1)S(1)}, bf16[2,8,64]{2,1,0:T(8,128)(2,1)S(1)}, u32[]{:S(2)}, u32[]{:S(2)}) collective-permute-start(bf16[2,8,64]{2,1,0:T(8,128)(2,1)S(1)} %slice.27), channel_id=1, source_target_pairs={{0,4},{4,8},{8,12},{12,16},{16,20},{20,24},{24,28},{28,0},{1,5},{5... | collective-permute-start | bytes 6152 | tf_op jit(solution)/shard_map/ppermute | solution.py:321
  15.0 3.7 %collective-permute-start.2 = (f32[16,128]{1,0:T(8,128)S(1)}, f32[16,128]{1,0:T(8,128)S(1)}, u32[]{:S(2)}, u32[]{:S(2)}) collective-permute-start(f32[16,128]{1,0:T(8,128)S(1)} %get-tuple-element.44), channel_id=1, source_target_pairs={{0,28},{4,0},{8,4},{12,8},{16,12},{20,16},{24,20},{28,24},{1,29},{... | collective-permute-start | bytes 24584 | tf_op jit(solution)/shard_map/ppermute | solution.py:343
  16.8 1.9 %copy-start.2 = (bf16[1,128,4096]{2,1,0:T(8,128)(2,1)S(1)}, bf16[1,128,4096]{2,1,0:T(8,128)(2,1)}, u32[]{:S(2)}) copy-start(bf16[1,128,4096]{2,1,0:T(8,128)(2,1)} %tokens.1) | copy-start | bytes 3145732
  19.0 1.6 %collective-permute-start.3 = (f32[4,24,768]{2,1,0:T(8,128)S(1)}, f32[4,24,768]{2,1,0:T(8,128)S(1)}, u32[]{:S(2)}, u32[]{:S(2)}) collective-permute-start(f32[4,24,768]{2,1,0:T(8,128)S(1)} %get-tuple-element.49), channel_id=1, source_target_pairs={{0,1},{1,0},{2,3},{3,2},{4,5},{5,4},{6,7},{7,6},{8,9},{9,8},{10,11... | collective-permute-start | bytes 884744 | tf_op jit(solution)/shard_map/ppermute | solution.py:287
  20.7 5.0 %collective-permute-start.4 = (bf16[24,768]{1,0:T(8,128)(2,1)S(1)}, bf16[24,768]{1,0:T(8,128)(2,1)S(1)}, u32[]{:S(2)}, u32[]{:S(2)}) collective-permute-start(bf16[24,768]{1,0:T(8,128)(2,1)S(1)} %get-tuple-element.54), channel_id=1, source_target_pairs={{0,6},{1,7},{2,4},{3,5},{4,2},{5,3},{6,0},{7,1},{8,14},{9,15},{10,... | collective-permute-start | bytes 110600 | tf_op jit(solution)/shard_map/ppermute | solution.py:287
  21.9 4.1 %collective-permute-start.6 = (bf16[24,768]{1,0:T(8,128)(2,1)S(1)}, bf16[24,768]{1,0:T(8,128)(2,1)S(1)}, u32[]{:S(2)}, u32[]{:S(2)}) collective-permute-start(bf16[24,768]{1,0:T(8,128)(2,1)S(1)} %get-tuple-element.55), channel_id=1, source_target_pairs={{0,3},{1,2},{2,1},{3,0},{4,7},{5,6},{6,5},{7,4},{8,11},{9,10},{10,... | collective-permute-start | bytes 110600 | tf_op jit(solution)/shard_map/ppermute | solution.py:287
  22.1 3.9 %collective-permute-start.5 = (bf16[24,768]{1,0:T(8,128)(2,1)S(1)}, bf16[24,768]{1,0:T(8,128)(2,1)S(1)}, u32[]{:S(2)}, u32[]{:S(2)}) collective-permute-start(bf16[24,768]{1,0:T(8,128)(2,1)S(1)} %get-tuple-element.56), channel_id=1, source_target_pairs={{0,5},{1,4},{2,7},{3,6},{4,1},{5,0},{6,3},{7,2},{8,13},{9,12},{10,... | collective-permute-start | bytes 110600 | tf_op jit(solution)/shard_map/ppermute | solution.py:287
  26.1 4.8 %collective-permute-start.9 = (bf16[24,768]{1,0:T(8,128)(2,1)S(1)}, bf16[24,768]{1,0:T(8,128)(2,1)S(1)}, u32[]{:S(2)}, u32[]{:S(2)}) collective-permute-start(bf16[24,768]{1,0:T(8,128)(2,1)S(1)} %fusion.4), channel_id=1, source_target_pairs={{0,17},{1,16},{2,19},{3,18},{4,21},{5,20},{6,23},{7,22},{8,25},{9,... | collective-permute-start | bytes 110600 | tf_op jit(solution)/shard_map/ppermute | solution.py:287
  28.2 6.0 %collective-permute-start.8 = (bf16[24,768]{1,0:T(8,128)(2,1)S(1)}, bf16[24,768]{1,0:T(8,128)(2,1)S(1)}, u32[]{:S(2)}, u32[]{:S(2)}) collective-permute-start(bf16[24,768]{1,0:T(8,128)(2,1)S(1)} %fusion.4), channel_id=1, source_target_pairs={{0,24},{1,25},{2,26},{3,27},{4,28},{5,29},{6,30},{7,31},{8,16},{9,... | collective-permute-start | bytes 110600 | tf_op jit(solution)/shard_map/ppermute | solution.py:287
  30.7 4.0 %collective-permute-start.7 = (bf16[24,768]{1,0:T(8,128)(2,1)S(1)}, bf16[24,768]{1,0:T(8,128)(2,1)S(1)}, u32[]{:S(2)}, u32[]{:S(2)}) collective-permute-start(bf16[24,768]{1,0:T(8,128)(2,1)S(1)} %fusion.4), channel_id=1, source_target_pairs={{0,9},{1,8},{2,11},{3,10},{4,13},{5,12},{6,15},{7,14},{8,1},{9,0},... | collective-permute-start | bytes 110600 | tf_op jit(solution)/shard_map/ppermute | solution.py:287
  34.7 5.0 %collective-permute-start.12 = (bf16[24,768]{1,0:T(8,128)(2,1)S(1)}, bf16[24,768]{1,0:T(8,128)(2,1)S(1)}, u32[]{:S(2)}, u32[]{:S(2)}) collective-permute-start(bf16[24,768]{1,0:T(8,128)(2,1)S(1)} %add_convert_fusion), channel_id=1, source_target_pairs={{0,6},{1,7},{2,4},{3,5},{4,2},{5,3},{6,0},{7,1},{8,14},{9,15},{10,... | collective-permute-start | bytes 110600 | tf_op jit(solution)/shard_map/ppermute | solution.py:287
  36.1 4.2 %collective-permute-start.11 = (bf16[24,768]{1,0:T(8,128)(2,1)S(1)}, bf16[24,768]{1,0:T(8,128)(2,1)S(1)}, u32[]{:S(2)}, u32[]{:S(2)}) collective-permute-start(bf16[24,768]{1,0:T(8,128)(2,1)S(1)} %add_convert_fusion), channel_id=1, source_target_pairs={{0,3},{1,2},{2,1},{3,0},{4,7},{5,6},{6,5},{7,4},{8,11},{9,10},{10,... | collective-permute-start | bytes 110600 | tf_op jit(solution)/shard_map/ppermute | solution.py:287
  36.2 4.1 %collective-permute-start.10 = (bf16[24,768]{1,0:T(8,128)(2,1)S(1)}, bf16[24,768]{1,0:T(8,128)(2,1)S(1)}, u32[]{:S(2)}, u32[]{:S(2)}) collective-permute-start(bf16[24,768]{1,0:T(8,128)(2,1)S(1)} %add_convert_fusion), channel_id=1, source_target_pairs={{0,5},{1,4},{2,7},{3,6},{4,1},{5,0},{6,3},{7,2},{8,13},{9,12},{10,... | collective-permute-start | bytes 110600 | tf_op jit(solution)/shard_map/ppermute | solution.py:287
  40.3 1.4 %collective-permute-start.13 = (bf16[4,24,768]{2,1,0:T(8,128)(2,1)S(1)}, bf16[4,24,768]{2,1,0:T(8,128)(2,1)S(1)}, u32[]{:S(2)}, u32[]{:S(2)}) collective-permute-start(bf16[4,24,768]{2,1,0:T(8,128)(2,1)S(1)} %pad_maximum_fusion.pieces), channel_id=1, source_target_pairs={{0,1},{1,0},{2,3},{3,2},{4,5},{5,4},{6,7},{7,6},{8,9},{9,8},{10,11... | collective-permute-start | bytes 442376 | tf_op jit(solution)/shard_map/ppermute | solution.py:287

commit v11 on v10

--- a/solution.py
+++ b/solution.py
@@ -217,10 +217,7 @@
 
 def position():
     seq, dp = lax.axis_index("seq"), lax.axis_index("dp")
-    bits = seq ^ dp
-    for shift in (4, 2, 1):
-        bits = bits ^ (bits >> shift)
-    return bits & 1, (dp & 2) | (seq & 1)
+    return (seq ^ dp) & 1, (dp & 2) | (seq & 1)
 
 
 def down_kernel(tokens, rank_plain, rank_near, rank_far, cross, up_plain, up_near, up_far, keep, send):
@@ -289,7 +286,7 @@
 
 def total_sum(keep, send, seqs, dps):
     total = seqs * dps
-    partner = {1: dps | 1, 2: 3, 3: dps | 2}
+    partner = {1: dps | 1, 2: 2, 3: dps | 3}
     keep = keep + swap(send, 1, total)
     got = [swap(keep[s].astype(BF), partner[s], total).astype(F32) for s in (1, 2, 3)]
     own = keep[0] + got[2] + got[0] + got[1]
@@ -299,7 +296,7 @@
         bit *= len(steps) + 1
         if bit >= seqs:
             own = own.astype(BF)
-        parts = [swap(own, step * dps | (step & (step - 1) == 0), total) for step in steps]
+        parts = [swap(own, step * dps, total) for step in steps]
         own = own.astype(F32)
         if len(parts) == 3:
             own = (own + parts[0].astype(F32)) + (parts[2].astype(F32) + parts[1].astype(F32))

time: 42.8 us -> 42.2 us (0.986)
  transfers between devices with their start and end apart: 14 -> 14, of which waited for: 10 -> 11; matrix products, arithmetic and copies ran while one was open for 4% -> 4% of each run, Pallas kernels for 11% -> 11%
where the time goes in v11:
time: 42.2 us; the launch traced here: 42.1 us
  starting transfers between devices  17.8 us (42%)
  waiting for transfers between devices  13.8 us (33%)
  Pallas kernels  6.76 us (16%)
  matrix products  1.6 us (4%)
  local copies, waits for them, and re-layouts  1.22 us (3%)
  between operations  0.76 us (2%)
    ppermute x11, starting transfers between devices, swap(): return lax.ppermute(x, AXES, [(i, i ^ bits) for i in range(total)])  11.4 us
    ppermute x11, waiting for transfers between devices, swap(): return lax.ppermute(x, AXES, [(i, i ^ bits) for i in range(total)])  10.6 us
    pallas_call x9, Pallas kernels, call(): pl.pallas_call(kernel, out_shape=outs, in_specs=[VMEM] * len(args), out_s...  6.76 us
    ppermute x1, starting transfers between devices, on_device(): frozen_kv = lax.ppermute(frozen[1:, 0, half:, half_width:], 'seq', forward)  2.99 us
    ppermute x1, waiting for transfers between devices, on_device(): low_kv = lax.ppermute(low_t[1:, :, half:], 'seq', forward)  2.25 us
    ppermute x1, starting transfers between devices, on_device(): cross = lax.ppermute(cross, 'seq', backward)  1.78 us
    dot_general x1, matrix products, on_device(): jnp.einsum('psw,gw->psg', down_weight, tokens[0], preferred_element_type=...  1.6 us
    ppermute x1, starting transfers between devices, on_device(): low_kv = lax.ppermute(low_t[1:, :, half:], 'seq', forward)  1.56 us
  transfers between devices with their start and end apart: 14, of which 11 were waited for; matrix products, arithmetic and copies ran while one was open for 4% of the time, Pallas kernels for 11%

profile of v11, /device:TPU:0, one launch (start us, length us, event | category | flops | bytes accessed | tf_op | source)
XLA Modules:
  0.0 42.1 jit_solution(12034505921670467251)
XLA Ops:
  0.7 1.1 %slice_bitcast_fusion = bf16[2,64,1024]{2,1,0:T(8,128)(2,1)S(1)} fusion(bf16[3,1,128,2048]{3,2,0,1:T(8,128)(2,1)} %bitcast.28), kind=kLoop, calls=%fused_computation.2 | loop fusion | bytes 524288 | tf_op jit(solution)/shard_map/squeeze | solution.py:316
  1.8 3.0 %collective-permute-start.1 = (bf16[2,64,1024]{2,1,0:T(8,128)(2,1)S(1)}, bf16[2,64,1024]{2,1,0:T(8,128)(2,1)S(1)}, u32[]{:S(2)}, u32[]{:S(2)}) collective-permute-start(bf16[2,64,1024]{2,1,0:T(8,128)(2,1)S(1)} %slice_bitcast_fusion), channel_id=1, source_target_pairs={{0,4},{4,8},{8,12},{12,16},{16,20},{20,24},{24,28},{28,0},{1,5},{5... | collective-permute-start | bytes 786440 | tf_op jit(solution)/shard_map/ppermute | solution.py:316
  4.8 1.6 %convolution_convert_fusion.low_t = bf16[3,8,128]{2,1,0:T(8,128)(2,1)S(1)} fusion(bf16[3,8,4096]{2,1,0:T(8,128)(2,1)S(1)} %copy-done, bf16[1,128,4096]{2,1,0:T(8,128)(2,1)} %tokens.1), kind=kOutput, calls=%fused_computation | convolution fusion | flops 25168896 | bytes 1251328 | tf_op jit(solution)/shard_map/psw,gw->psg/dot_general | solution.py:317
  6.5 1.6 %collective-permute-start = (bf16[2,8,64]{2,1,0:T(8,128)(2,1)S(1)}, bf16[2,8,64]{2,1,0:T(8,128)(2,1)S(1)}, u32[]{:S(2)}, u32[]{:S(2)}) collective-permute-start(bf16[2,8,64]{2,1,0:T(8,128)(2,1)S(1)} %slice.27), channel_id=1, source_target_pairs={{0,4},{4,8},{8,12},{12,16},{16,20},{20,24},{24,28},{28,0},{1,5},{5... | collective-permute-start | bytes 6152 | tf_op jit(solution)/shard_map/ppermute | solution.py:318
  8.0 0.6 %shard_map.68.projected = bf16[3,128,2048]{2,1,0:T(8,128)(2,1)S(1)} custom-call(bf16[3,1,128,2048]{3,2,1,0:T(8,128)(2,1)S(1)} %copy-done.4, bf16[3,8,128]{2,1,0:T(8,128)(2,1)S(1)} %convolution_convert_fusion.low_t, bf16[3,8,2048]{2,1,0:T(8,128)(2,1)S(1)} %copy-done.3), custom_call_target="tpu_custom_call" | custom-call | flops 1000000 | bytes 10000 | tf_op jit(solution)/shard_map/pallas_call | solution.py:273
  8.6 1.2 %shard_map.71 = (f32[24,1024]{1,0:T(8,128)S(1)}, f32[24,128]{1,0:T(8,128)S(1)}) custom-call(bf16[3,128,2048]{2,1,0:T(8,128)(2,1)S(1)} %shard_map.68.projected, bf16[1,128,2048]{2,1,0:T(8,128)(2,1)S(1)} %copy-done.1, bf16[3,8,128]{2,1,0:T(8,128)(2,1)S(1)} %convolution_convert_fusion.low_t, bf16[3,8,2048]{2,1,0:T(8,128)(2,1)S(1)} %copy-done.3), custom_call_target="tpu_custom_call" | custom-call | flops 1000000 | bytes 10000 | tf_op jit(solution)/shard_map/pallas_call | solution.py:273
  9.9 1.6 %shard_map.70 = (f32[24,1024]{1,0:T(8,128)S(1)}, f32[24,128]{1,0:T(8,128)S(1)}) custom-call(bf16[3,128,2048]{2,1,0:T(8,128)(2,1)S(1)} %shard_map.68.projected, bf16[1,128,2048]{2,1,0:T(8,128)(2,1)S(1)} %copy-done.1, bf16[3,8,128]{2,1,0:T(8,128)(2,1)S(1)} %convolution_convert_fusion.low_t, bf16[3,8,2048]{2,1,0:T(8,128)(2,1)S(1)} %copy-done.3), custom_call_target="tpu_custom_call" | custom-call | flops 1000000 | bytes 10000 | tf_op jit(solution)/shard_map/pallas_call | solution.py:273
  11.5 0.4 %shard_map.69 = (f32[8,64,64]{2,1,0:T(8,128)S(1)}, f32[8,64,64]{2,1,0:T(8,128)S(1)}, f32[8,64]{1,0:T(8,128)S(1)}, f32[8,64]{1,0:T(8,128)S(1)}, bf16[8,16,64]{2,1...) custom-call(bf16[3,128,2048]{2,1,0:T(8,128)(2,1)S(1)} %shard_map.68.projected, bf16[1,128,2048]{2,1,0:T(8,128)(2,1)S(1)} %copy-done.1, ...), custom_call_target="tpu_custom_call" | custom-call | flops 1000000 | bytes 10000 | tf_op jit(solution)/shard_map/pallas_call | solution.py:273
  11.9 2.3 %collective-permute-done.low_kv = bf16[2,8,64]{2,1,0:T(8,128)(2,1)S(1)} collective-permute-done((bf16[2,8,64]{2,1,0:T(8,128)(2,1)S(1)}, bf16[2,8,64]{2,1,0:T(8,128)(2,1)S(1)}, u32[]{:S(2)}, u32[]{:S(2)}) %collective-permute-start) | collective-permute-done | bytes 2080 | tf_op jit(solution)/shard_map/ppermute | solution.py:318
  14.2 0.8 %shard_map.72 = (f32[16,128]{1,0:T(8,128)S(1)}, bf16[8,64,128]{2,1,0:T(8,128)(2,1)S(1)}, bf16[8,64,64]{2,1,0:T(8,128)(2,1)S(1)}, bf16[8,64,64]{2,1,0:T(8,128)(2,...) custom-call(bf16[3,128,2048]{2,1,0:T(8,128)(2,1)S(1)} %shard_map.68.projected, ...), custom_call_target="tpu_custom_call" | custom-call | flops 1000000 | bytes 10000 | tf_op jit(solution)/shard_map/pallas_call | solution.py:273
  15.0 1.8 %collective-permute-start.2 = (f32[16,128]{1,0:T(8,128)S(1)}, f32[16,128]{1,0:T(8,128)S(1)}, u32[]{:S(2)}, u32[]{:S(2)}) collective-permute-start(f32[16,128]{1,0:T(8,128)S(1)} %get-tuple-element.44), channel_id=1, source_target_pairs={{0,28},{4,0},{8,4},{12,8},{16,12},{20,16},{24,20},{28,24},{1,29},{... | collective-permute-start | bytes 24584 | tf_op jit(solution)/shard_map/ppermute | solution.py:340
  16.8 0.9 %shard_map.73 = (f32[24,1024]{1,0:T(8,128)S(1)}, f32[24,128]{1,0:T(8,128)S(1)}) custom-call(bf16[3,128,2048]{2,1,0:T(8,128)(2,1)S(1)} %shard_map.68.projected, bf16[2,8,64]{2,1,0:T(8,128)(2,1)S(1)} %collective-permute-done.low_kv, bf16[1,128,2048]{2,1,0:T(8,128)(2,1)S(1)} %copy-done.1, bf16[3,8,128]{2,1,0:T(8,128)(2,1)S(1)} %convolution_convert_fusion.low_t, ...), custom_call_target="tpu_custom_call" | custom-call | flops 1000000 | bytes 10000 | tf_op jit(solution)/shard_map/pallas_call | solution.py:273
  17.7 1.0 %collective-permute-done.2.cross = f32[16,128]{1,0:T(8,128)S(1)} collective-permute-done((f32[16,128]{1,0:T(8,128)S(1)}, f32[16,128]{1,0:T(8,128)S(1)}, u32[]{:S(2)}, u32[]{:S(2)}) %collective-permute-start.2) | collective-permute-done | bytes 8224 | tf_op jit(solution)/shard_map/ppermute | solution.py:340
  18.7 0.3 shard_map.74
  19.1 1.6 %collective-permute-done.3 = f32[4,24,768]{2,1,0:T(8,128)S(1)} collective-permute-done((f32[4,24,768]{2,1,0:T(8,128)S(1)}, f32[4,24,768]{2,1,0:T(8,128)S(1)}, u32[]{:S(2)}, u32[]{:S(2)}) %collective-permute-start.3) | collective-permute-done | bytes 294944 | tf_op jit(solution)/shard_map/ppermute | solution.py:284
  20.7 0.9 %collective-permute-start.4 = (bf16[24,768]{1,0:T(8,128)(2,1)S(1)}, bf16[24,768]{1,0:T(8,128)(2,1)S(1)}, u32[]{:S(2)}, u32[]{:S(2)}) collective-permute-start(bf16[24,768]{1,0:T(8,128)(2,1)S(1)} %get-tuple-element.54), channel_id=1, source_target_pairs={{0,7},{1,6},{2,5},{3,4},{4,3},{5,2},{6,1},{7,0},{8,15},{9,14},{10,... | collective-permute-start | bytes 110600 | tf_op jit(solution)/shard_map/ppermute | solution.py:284
  21.6 0.7 %collective-permute-start.6 = (bf16[24,768]{1,0:T(8,128)(2,1)S(1)}, bf16[24,768]{1,0:T(8,128)(2,1)S(1)}, u32[]{:S(2)}, u32[]{:S(2)}) collective-permute-start(bf16[24,768]{1,0:T(8,128)(2,1)S(1)} %get-tuple-element.55), channel_id=1, source_target_pairs={{0,2},{1,3},{2,0},{3,1},{4,6},{5,7},{6,4},{7,5},{8,10},{9,11},{10,... | collective-permute-start | bytes 110600 | tf_op jit(solution)/shard_map/ppermute | solution.py:284
  22.4 1.3 %collective-permute-start.5 = (bf16[24,768]{1,0:T(8,128)(2,1)S(1)}, bf16[24,768]{1,0:T(8,128)(2,1)S(1)}, u32[]{:S(2)}, u32[]{:S(2)}) collective-permute-start(bf16[24,768]{1,0:T(8,128)(2,1)S(1)} %get-tuple-element.56), channel_id=1, source_target_pairs={{0,5},{1,4},{2,7},{3,6},{4,1},{5,0},{6,3},{7,2},{8,13},{9,12},{10,... | collective-permute-start | bytes 110600 | tf_op jit(solution)/shard_map/ppermute | solution.py:284
  23.7 1.5 %collective-permute-done.4 = bf16[24,768]{1,0:T(8,128)(2,1)S(1)} collective-permute-done((bf16[24,768]{1,0:T(8,128)(2,1)S(1)}, bf16[24,768]{1,0:T(8,128)(2,1)S(1)}, u32[]{:S(2)}, u32[]{:S(2)}) %collective-permute-start.4) | collective-permute-done | bytes 36896 | tf_op jit(solution)/shard_map/ppermute | solution.py:284
  25.2 0.9 %collective-permute-done.6 = bf16[24,768]{1,0:T(8,128)(2,1)S(1)} collective-permute-done((bf16[24,768]{1,0:T(8,128)(2,1)S(1)}, bf16[24,768]{1,0:T(8,128)(2,1)S(1)}, u32[]{:S(2)}, u32[]{:S(2)}) %collective-permute-start.6) | collective-permute-done | bytes 36896 | tf_op jit(solution)/shard_map/ppermute | solution.py:284
  26.2 2.1 %collective-permute-start.9 = (bf16[24,768]{1,0:T(8,128)(2,1)S(1)}, bf16[24,768]{1,0:T(8,128)(2,1)S(1)}, u32[]{:S(2)}, u32[]{:S(2)}) collective-permute-start(bf16[24,768]{1,0:T(8,128)(2,1)S(1)} %fusion.4), channel_id=1, source_target_pairs={{0,16},{1,17},{2,18},{3,19},{4,20},{5,21},{6,22},{7,23},{8,24},{9,... | collective-permute-start | bytes 110600 | tf_op jit(solution)/shard_map/ppermute | solution.py:284
  28.4 2.3 %collective-permute-start.8 = (bf16[24,768]{1,0:T(8,128)(2,1)S(1)}, bf16[24,768]{1,0:T(8,128)(2,1)S(1)}, u32[]{:S(2)}, u32[]{:S(2)}) collective-permute-start(bf16[24,768]{1,0:T(8,128)(2,1)S(1)} %fusion.4), channel_id=1, source_target_pairs={{0,24},{1,25},{2,26},{3,27},{4,28},{5,29},{6,30},{7,31},{8,16},{9,... | collective-permute-start | bytes 110600 | tf_op jit(solution)/shard_map/ppermute | solution.py:284
  30.7 0.5 %collective-permute-start.7 = (bf16[24,768]{1,0:T(8,128)(2,1)S(1)}, bf16[24,768]{1,0:T(8,128)(2,1)S(1)}, u32[]{:S(2)}, u32[]{:S(2)}) collective-permute-start(bf16[24,768]{1,0:T(8,128)(2,1)S(1)} %fusion.4), channel_id=1, source_target_pairs={{0,8},{1,9},{2,10},{3,11},{4,12},{5,13},{6,14},{7,15},{8,0},{9,1},... | collective-permute-start | bytes 110600 | tf_op jit(solution)/shard_map/ppermute | solution.py:284
  31.2 2.9 %collective-permute-done.8 = bf16[24,768]{1,0:T(8,128)(2,1)S(1)} collective-permute-done((bf16[24,768]{1,0:T(8,128)(2,1)S(1)}, bf16[24,768]{1,0:T(8,128)(2,1)S(1)}, u32[]{:S(2)}, u32[]{:S(2)}) %collective-permute-start.8) | collective-permute-done | bytes 36896 | tf_op jit(solution)/shard_map/ppermute | solution.py:284
  34.1 0.5 %collective-permute-done.7 = bf16[24,768]{1,0:T(8,128)(2,1)S(1)} collective-permute-done((bf16[24,768]{1,0:T(8,128)(2,1)S(1)}, bf16[24,768]{1,0:T(8,128)(2,1)S(1)}, u32[]{:S(2)}, u32[]{:S(2)}) %collective-permute-start.7) | collective-permute-done | bytes 36896 | tf_op jit(solution)/shard_map/ppermute | solution.py:284
  34.8 1.6 %collective-permute-start.11 = (bf16[24,768]{1,0:T(8,128)(2,1)S(1)}, bf16[24,768]{1,0:T(8,128)(2,1)S(1)}, u32[]{:S(2)}, u32[]{:S(2)}) collective-permute-start(bf16[24,768]{1,0:T(8,128)(2,1)S(1)} %add_convert_fusion), channel_id=1, source_target_pairs={{0,2},{1,3},{2,0},{3,1},{4,6},{5,7},{6,4},{7,5},{8,10},{9,11},{10,... | collective-permute-start | bytes 110600 | tf_op jit(solution)/shard_map/ppermute | solution.py:284
  36.3 1.3 %collective-permute-start.10 = (bf16[24,768]{1,0:T(8,128)(2,1)S(1)}, bf16[24,768]{1,0:T(8,128)(2,1)S(1)}, u32[]{:S(2)}, u32[]{:S(2)}) collective-permute-start(bf16[24,768]{1,0:T(8,128)(2,1)S(1)} %add_convert_fusion), channel_id=1, source_target_pairs={{0,5},{1,4},{2,7},{3,6},{4,1},{5,0},{6,3},{7,2},{8,13},{9,12},{10,... | collective-permute-start | bytes 110600 | tf_op jit(solution)/shard_map/ppermute | solution.py:284
  37.7 1.5 %collective-permute-done.12 = bf16[24,768]{1,0:T(8,128)(2,1)S(1)} collective-permute-done((bf16[24,768]{1,0:T(8,128)(2,1)S(1)}, bf16[24,768]{1,0:T(8,128)(2,1)S(1)}, u32[]{:S(2)}, u32[]{:S(2)}) %collective-permute-start.12) | collective-permute-done | bytes 36896 | tf_op jit(solution)/shard_map/ppermute | solution.py:284
  39.1 0.3 collective-permute-done.11
  39.7 0.4 collective-permute-start.13
  40.2 1.0 %collective-permute-done.13.pieces = bf16[4,24,768]{2,1,0:T(8,128)(2,1)S(1)} collective-permute-done((bf16[4,24,768]{2,1,0:T(8,128)(2,1)S(1)}, bf16[4,24,768]{2,1,0:T(8,128)(2,1)S(1)}, u32[]{:S(2)}, u32[]{:S(2)}) %collective-permute-start.13) | collective-permute-done | bytes 147488 | tf_op jit(solution)/shard_map/ppermute | solution.py:284
  41.2 0.9 %shard_map.76 = (f32[3,8,4096]{2,1,0:T(8,128)}, f32[3,8,2048]{2,1,0:T(8,128)}) custom-call(bf16[4,24,768]{2,1,0:T(8,128)(2,1)S(1)} %collective-permute-done.13.pieces, f32[3,8,4096]{2,1,0:T(8,128)S(1)} %get-tuple-element.50.down_in, f32[3,8,2048]{2,1,0:T(8,128)S(1)} %get-tuple-element.51.up_in), custom_call_target="tpu_custom_call" | custom-call | flops 1000000 | bytes 10000 | tf_op jit(solution)/shard_map/pallas_call | solution.py:273
  (23 shorter events, 0.7 us)
Async XLA Ops:
  0.6 4.1 %copy-start = (bf16[3,8,4096]{2,1,0:T(8,128)(2,1)S(1)}, bf16[3,8,4096]{2,1,0:T(8,128)(2,1)}, u32[]{:S(2)}) copy-start(bf16[3,8,4096]{2,1,0:T(8,128)(2,1)} %param.8) | copy-start | bytes 589828
  0.6 7.4 %copy-start.4 = (bf16[3,1,128,2048]{3,2,1,0:T(8,128)(2,1)S(1)}, bf16[3,1,128,2048]{3,2,1,0:T(8,128)(2,1)}, u32[]{:S(2)}) copy-start(bf16[3,1,128,2048]{3,2,1,0:T(8,128)(2,1)} %frozen.1) | copy-start | bytes 4718596
  0.7 7.4 %copy-start.3 = (bf16[3,8,2048]{2,1,0:T(8,128)(2,1)S(1)}, bf16[3,8,2048]{2,1,0:T(8,128)(2,1)}, u32[]{:S(2)}) copy-start(bf16[3,8,2048]{2,1,0:T(8,128)(2,1)} %up.11) | copy-start | bytes 294916
  1.8 12.4 %collective-permute-start.1 = (bf16[2,64,1024]{2,1,0:T(8,128)(2,1)S(1)}, bf16[2,64,1024]{2,1,0:T(8,128)(2,1)S(1)}, u32[]{:S(2)}, u32[]{:S(2)}) collective-permute-start(bf16[2,64,1024]{2,1,0:T(8,128)(2,1)S(1)} %slice_bitcast_fusion), channel_id=1, source_target_pairs={{0,4},{4,8},{8,12},{12,16},{16,20},{20,24},{24,28},{28,0},{1,5},{5... | collective-permute-start | bytes 786440 | tf_op jit(solution)/shard_map/ppermute | solution.py:316
  6.5 2.2 %copy-start.1 = (bf16[1,128,2048]{2,1,0:T(8,128)(2,1)S(1)}, bf16[1,128,2048]{2,1,0:T(8,128)(2,1)}, u32[]{:S(2)}) copy-start(bf16[1,128,2048]{2,1,0:T(8,128)(2,1)} %grad.9) | copy-start | bytes 1572868
  6.5 7.7 %collective-permute-start = (bf16[2,8,64]{2,1,0:T(8,128)(2,1)S(1)}, bf16[2,8,64]{2,1,0:T(8,128)(2,1)S(1)}, u32[]{:S(2)}, u32[]{:S(2)}) collective-permute-start(bf16[2,8,64]{2,1,0:T(8,128)(2,1)S(1)} %slice.27), channel_id=1, source_target_pairs={{0,4},{4,8},{8,12},{12,16},{16,20},{20,24},{24,28},{28,0},{1,5},{5... | collective-permute-start | bytes 6152 | tf_op jit(solution)/shard_map/ppermute | solution.py:318
  15.0 3.7 %collective-permute-start.2 = (f32[16,128]{1,0:T(8,128)S(1)}, f32[16,128]{1,0:T(8,128)S(1)}, u32[]{:S(2)}, u32[]{:S(2)}) collective-permute-start(f32[16,128]{1,0:T(8,128)S(1)} %get-tuple-element.44), channel_id=1, source_target_pairs={{0,28},{4,0},{8,4},{12,8},{16,12},{20,16},{24,20},{28,24},{1,29},{... | collective-permute-start | bytes 24584 | tf_op jit(solution)/shard_map/ppermute | solution.py:340
  16.8 1.9 %copy-start.2 = (bf16[1,128,4096]{2,1,0:T(8,128)(2,1)S(1)}, bf16[1,128,4096]{2,1,0:T(8,128)(2,1)}, u32[]{:S(2)}) copy-start(bf16[1,128,4096]{2,1,0:T(8,128)(2,1)} %tokens.1) | copy-start | bytes 3145732
  19.0 1.6 %collective-permute-start.3 = (f32[4,24,768]{2,1,0:T(8,128)S(1)}, f32[4,24,768]{2,1,0:T(8,128)S(1)}, u32[]{:S(2)}, u32[]{:S(2)}) collective-permute-start(f32[4,24,768]{2,1,0:T(8,128)S(1)} %get-tuple-element.49), channel_id=1, source_target_pairs={{0,1},{1,0},{2,3},{3,2},{4,5},{5,4},{6,7},{7,6},{8,9},{9,8},{10,11... | collective-permute-start | bytes 884744 | tf_op jit(solution)/shard_map/ppermute | solution.py:284
  20.7 4.5 %collective-permute-start.4 = (bf16[24,768]{1,0:T(8,128)(2,1)S(1)}, bf16[24,768]{1,0:T(8,128)(2,1)S(1)}, u32[]{:S(2)}, u32[]{:S(2)}) collective-permute-start(bf16[24,768]{1,0:T(8,128)(2,1)S(1)} %get-tuple-element.54), channel_id=1, source_target_pairs={{0,7},{1,6},{2,5},{3,4},{4,3},{5,2},{6,1},{7,0},{8,15},{9,14},{10,... | collective-permute-start | bytes 110600 | tf_op jit(solution)/shard_map/ppermute | solution.py:284
  21.6 4.5 %collective-permute-start.6 = (bf16[24,768]{1,0:T(8,128)(2,1)S(1)}, bf16[24,768]{1,0:T(8,128)(2,1)S(1)}, u32[]{:S(2)}, u32[]{:S(2)}) collective-permute-start(bf16[24,768]{1,0:T(8,128)(2,1)S(1)} %get-tuple-element.55), channel_id=1, source_target_pairs={{0,2},{1,3},{2,0},{3,1},{4,6},{5,7},{6,4},{7,5},{8,10},{9,11},{10,... | collective-permute-start | bytes 110600 | tf_op jit(solution)/shard_map/ppermute | solution.py:284
  22.4 3.8 %collective-permute-start.5 = (bf16[24,768]{1,0:T(8,128)(2,1)S(1)}, bf16[24,768]{1,0:T(8,128)(2,1)S(1)}, u32[]{:S(2)}, u32[]{:S(2)}) collective-permute-start(bf16[24,768]{1,0:T(8,128)(2,1)S(1)} %get-tuple-element.56), channel_id=1, source_target_pairs={{0,5},{1,4},{2,7},{3,6},{4,1},{5,0},{6,3},{7,2},{8,13},{9,12},{10,... | collective-permute-start | bytes 110600 | tf_op jit(solution)/shard_map/ppermute | solution.py:284
  26.2 5.0 %collective-permute-start.9 = (bf16[24,768]{1,0:T(8,128)(2,1)S(1)}, bf16[24,768]{1,0:T(8,128)(2,1)S(1)}, u32[]{:S(2)}, u32[]{:S(2)}) collective-permute-start(bf16[24,768]{1,0:T(8,128)(2,1)S(1)} %fusion.4), channel_id=1, source_target_pairs={{0,16},{1,17},{2,18},{3,19},{4,20},{5,21},{6,22},{7,23},{8,24},{9,... | collective-permute-start | bytes 110600 | tf_op jit(solution)/shard_map/ppermute | solution.py:284
  28.4 5.8 %collective-permute-start.8 = (bf16[24,768]{1,0:T(8,128)(2,1)S(1)}, bf16[24,768]{1,0:T(8,128)(2,1)S(1)}, u32[]{:S(2)}, u32[]{:S(2)}) collective-permute-start(bf16[24,768]{1,0:T(8,128)(2,1)S(1)} %fusion.4), channel_id=1, source_target_pairs={{0,24},{1,25},{2,26},{3,27},{4,28},{5,29},{6,30},{7,31},{8,16},{9,... | collective-permute-start | bytes 110600 | tf_op jit(solution)/shard_map/ppermute | solution.py:284
  30.7 4.0 %collective-permute-start.7 = (bf16[24,768]{1,0:T(8,128)(2,1)S(1)}, bf16[24,768]{1,0:T(8,128)(2,1)S(1)}, u32[]{:S(2)}, u32[]{:S(2)}) collective-permute-start(bf16[24,768]{1,0:T(8,128)(2,1)S(1)} %fusion.4), channel_id=1, source_target_pairs={{0,8},{1,9},{2,10},{3,11},{4,12},{5,13},{6,14},{7,15},{8,0},{9,1},... | collective-permute-start | bytes 110600 | tf_op jit(solution)/shard_map/ppermute | solution.py:284
  34.7 4.5 %collective-permute-start.12 = (bf16[24,768]{1,0:T(8,128)(2,1)S(1)}, bf16[24,768]{1,0:T(8,128)(2,1)S(1)}, u32[]{:S(2)}, u32[]{:S(2)}) collective-permute-start(bf16[24,768]{1,0:T(8,128)(2,1)S(1)} %add_convert_fusion), channel_id=1, source_target_pairs={{0,7},{1,6},{2,5},{3,4},{4,3},{5,2},{6,1},{7,0},{8,15},{9,14},{10,... | collective-permute-start | bytes 110600 | tf_op jit(solution)/shard_map/ppermute | solution.py:284
  34.8 4.7 %collective-permute-start.11 = (bf16[24,768]{1,0:T(8,128)(2,1)S(1)}, bf16[24,768]{1,0:T(8,128)(2,1)S(1)}, u32[]{:S(2)}, u32[]{:S(2)}) collective-permute-start(bf16[24,768]{1,0:T(8,128)(2,1)S(1)} %add_convert_fusion), channel_id=1, source_target_pairs={{0,2},{1,3},{2,0},{3,1},{4,6},{5,7},{6,4},{7,5},{8,10},{9,11},{10,... | collective-permute-start | bytes 110600 | tf_op jit(solution)/shard_map/ppermute | solution.py:284
  36.3 3.4 %collective-permute-start.10 = (bf16[24,768]{1,0:T(8,128)(2,1)S(1)}, bf16[24,768]{1,0:T(8,128)(2,1)S(1)}, u32[]{:S(2)}, u32[]{:S(2)}) collective-permute-start(bf16[24,768]{1,0:T(8,128)(2,1)S(1)} %add_convert_fusion), channel_id=1, source_target_pairs={{0,5},{1,4},{2,7},{3,6},{4,1},{5,0},{6,3},{7,2},{8,13},{9,12},{10,... | collective-permute-start | bytes 110600 | tf_op jit(solution)/shard_map/ppermute | solution.py:284
  39.7 1.4 %collective-permute-start.13 = (bf16[4,24,768]{2,1,0:T(8,128)(2,1)S(1)}, bf16[4,24,768]{2,1,0:T(8,128)(2,1)S(1)}, u32[]{:S(2)}, u32[]{:S(2)}) collective-permute-start(bf16[4,24,768]{2,1,0:T(8,128)(2,1)S(1)} %pad_maximum_fusion.pieces), channel_id=1, source_target_pairs={{0,1},{1,0},{2,3},{3,2},{4,5},{5,4},{6,7},{7,6},{8,9},{9,8},{10,11... | collective-permute-start | bytes 442376 | tf_op jit(solution)/shard_map/ppermute | solution.py:284

commit v12 on v11

--- a/solution.py
+++ b/solution.py
@@ -123,22 +123,37 @@
     return jnp.concatenate([jnp.zeros_like(x), x], axis=1)
 
 
-def shifted_columns(up):
+def shifted_pairs(up):
     half_width = up.shape[2] // 2
-    return [slice(start, start + HEAD_DIM) for start in range(half_width, 2 * half_width, HEAD_DIM)]
-
-
-def far_ready(projected, grad, up, e_out, dp_out, top_out, sum_out, bk_out, bv_out):
+    return [slice(start, start + 2 * HEAD_DIM) for start in range(half_width, 2 * half_width, 2 * HEAD_DIM)]
+
+
+def block_diagonal(x):
+    none = jnp.zeros_like(x[:, :HEAD_DIM])
+    return jnp.concatenate(
+        [
+            jnp.concatenate([x[:, :HEAD_DIM], none], axis=1),
+            jnp.concatenate([none, x[:, HEAD_DIM:]], axis=1),
+        ],
+        axis=0,
+    )
+
+
+def far_ready(projected, grad, up, q_out, g_out, e_out, dp_out, top_out, sum_out, bk_out, bv_out):
     half = projected.shape[1] // 2
-    mask = causal(half, half, 0)
-    for h, cols in enumerate(shifted_columns(up)):
-        q, k, v = [projected[j, :half, cols] for j in range(3)]
-        g = grad[0, :half, cols]
-        st = jnp.where(mask, nt(k, q) * SCALE, -jnp.inf)
+    key = lax.broadcasted_iota(jnp.int32, (half, 2 * half), 0)
+    query = lax.broadcasted_iota(jnp.int32, (half, 2 * half), 1)
+    mask = key <= jnp.where(query >= half, query - half, query)
+    for h, cols in enumerate(shifted_pairs(up)):
+        q = block_diagonal(projected[0, :half, cols])
+        g = block_diagonal(grad[0, :half, cols])
+        st = jnp.where(mask, nt(projected[1, :half, cols], q) * SCALE, -jnp.inf)
         top = jnp.max(st, axis=0, keepdims=True)
         e = jnp.exp(st - top)
+        q_out[h] = q
+        g_out[h] = g
         e_out[h] = e
-        dp_out[h] = nt(v, g)
+        dp_out[h] = nt(projected[2, :half, cols], g)
         top_out[h : h + 1, :] = top
         sum_out[h : h + 1, :] = jnp.sum(e, axis=0, keepdims=True)
         bk_out[h] = rows(hi_lo(nt(up[1, :, cols], q)))
@@ -146,15 +161,14 @@
 
 
 def far_scores(
-    projected, frozen_kv, low_kv, grad, up, e, dp, top, total, bk, bv,
+    frozen_kv, low_kv, up, q, g, e, dp, top, total, bk, bv,
     cross_out, near_out, pb_out, ds_out, factor_out, dot_out,
 ):
-    half = projected.shape[1] // 2
-    columns = shifted_columns(up)
-    wide = [project(frozen_kv[j], low_kv[j], up[j + 1, :, columns[0].start :]) for j in range(2)]
-    near = [[x[:, h * HEAD_DIM : (h + 1) * HEAD_DIM] for x in wide] for h in range(len(columns))]
-    sts = [nt(near[h][0], projected[0, :half, cols]) for h, cols in enumerate(columns)]
-    dps = [nt(near[h][1], grad[0, :half, cols]) for h, cols in enumerate(columns)]
+    pairs = shifted_pairs(up)
+    wide = [project(frozen_kv[j], low_kv[j], up[j + 1, :, pairs[0].start :]) for j in range(2)]
+    here = [slice(h * 2 * HEAD_DIM, (h + 1) * 2 * HEAD_DIM) for h in range(len(pairs))]
+    sts = [nt(wide[0][:, cols], q[h]) for h, cols in enumerate(here)]
+    dps = [nt(wide[1][:, cols], g[h]) for h, cols in enumerate(here)]
     found = []
     for h, (st, dpn) in enumerate(zip(sts, dps)):
         st = st * SCALE
@@ -177,40 +191,54 @@
     by_v = sum(nt(bv[h], pb) for h, (pb, _) in enumerate(found))
     cross_out[:8, :] = right(by_k[:8] + by_k[8:])
     cross_out[8:, :] = right(by_v[:8] + by_v[8:])
+    near_out[...] = wide[0]
     for h, (pb, ds) in enumerate(found):
-        near_out[h] = near[h][0]
         pb_out[h] = pb
         ds_out[h] = ds
 
 
 def far_rest(
-    projected, low_kv, grad, low_t, up, e, dp, bk, bv, near, near_pb, near_ds, factor, dot, up_out, rank_out
+    projected, low_kv, low_t, up, q, g, e, dp, bk, bv, near, near_pb, near_ds, factor, dot, up_out, rank_out
 ):
     half = projected.shape[1] // 2
     far_f = [low_t[j].astype(F32)[:, :half] for j in range(3)]
-    lows = [far_f[0]] + [
-        jnp.concatenate([low_kv[j].astype(F32), far_f[j + 1]], axis=1) for j in range(2)
-    ]
-    items, found, far_ds, far_pb = [], [], [], []
-    for h, cols in enumerate(shifted_columns(up)):
+    low_q = rows([left(far_f[0]), right(far_f[0])])
+    low_k, low_v = [jnp.concatenate([low_kv[j].astype(F32), far_f[j + 1]], axis=1) for j in range(2)]
+    first_head = lax.broadcasted_iota(jnp.int32, (3 * RANK, 2 * half), 1) < half
+    pairs = shifted_pairs(up)
+    here = [slice(h * 2 * HEAD_DIM, (h + 1) * 2 * HEAD_DIM) for h in range(len(pairs))]
+    far_ds, far_pb, whole_ds, whole_pb, keys = [], [], [], [], []
+    for h, cols in enumerate(pairs):
         p = e[h] * factor[h : h + 1, :]
-        pb = p.astype(BF)
-        ds = (p * (dp[h] - dot[h : h + 1, :]) * SCALE).astype(BF)
-        far_pb.append(pb)
-        far_ds.append(ds)
-        whole_ds = jnp.concatenate([near_ds[h], ds], axis=0)
-        k = jnp.concatenate([near[h], projected[1, :half, cols]], axis=0)
-        items.append(
-            (projected[0, :half, cols], k, None, grad[0, :half, cols], [up[j, :, cols] for j in range(3)], lows)
-        )
-        found.append((jnp.concatenate([near_pb[h], pb], axis=0), whole_ds, nt(lows[0].astype(BF), whole_ds)))
+        far_pb.append(p.astype(BF))
+        far_ds.append((p * (dp[h] - dot[h : h + 1, :]) * SCALE).astype(BF))
+        whole_pb.append(jnp.concatenate([near_pb[h], far_pb[h]], axis=0))
+        whole_ds.append(jnp.concatenate([near_ds[h], far_ds[h]], axis=0))
+        keys.append(jnp.concatenate([near[:, here[h]], projected[1, :half, cols]], axis=0))
     by_k = sum(nt(bk[h], ds) for h, ds in enumerate(far_ds))
     by_v = sum(nt(bv[h], pb) for h, pb in enumerate(far_pb))
-    parts = rest(items, found)
-    for h, (grads, _) in enumerate(parts):
-        for j in range(3):
-            up_out[8 * j : 8 * j + 8, h * HEAD_DIM : (h + 1) * HEAD_DIM] = grads[j]
-    rank_out[:8, :] = left(sum(rank for _, rank in parts))
+    aq = [nt(low_q, ds) for ds in whole_ds]
+    av = [nn(low_v.astype(BF), pb) for pb in whole_pb]
+    by_q = []
+    for h, cols in enumerate(pairs):
+        both = []
+        for t in range(2):
+            head = slice(t * HEAD_DIM, (t + 1) * HEAD_DIM)
+            both += [low_k] + hi_lo(nt(up[0, :, cols][:, head], keys[h][:, head]))
+        x = nn(rows(both), whole_ds[h])
+        by_q.append(jnp.where(first_head, x[: 3 * RANK], x[3 * RANK :]))
+    rank_q = 0.0
+    for h in range(len(pairs)):
+        uk = nn(rows(hi_lo(by_q[h][:8])), q[h])
+        uv = nn(rows(hi_lo(av[h])), g[h])
+        up_out[8:16, here[h]] = uk[:8] + uk[8:]
+        up_out[16:, here[h]] = uv[:8] + uv[8:]
+        for t in range(2):
+            uq = nn(rows(hi_lo(aq[h][8 * t : 8 * t + 8])), keys[h][:, t * HEAD_DIM : (t + 1) * HEAD_DIM])
+            start = here[h].start + t * HEAD_DIM
+            up_out[:8, start : start + HEAD_DIM] = uq[:8] + uq[8:]
+        rank_q = rank_q + by_q[h][8:16] + by_q[h][16:24]
+    rank_out[:8, :] = left(rank_q[:, :half] + rank_q[:, half:])
     rank_out[8:16, :] = left(by_k[:8] + by_k[8:])
     rank_out[16:, :] = left(by_v[:8] + by_v[8:])
 
@@ -303,8 +331,8 @@
         else:
             own = own + parts[0].astype(F32)
     piece = own.astype(BF)
-    mine = jnp.stack([piece] + [swap(piece, partner[s], total) for s in (1, 2, 3)])
-    return mine, swap(mine, 1, total)
+    mine = [piece] + [swap(piece, partner[s], total) for s in (1, 2, 3)]
+    return jnp.stack(mine), jnp.stack([swap(x, 1, total) for x in mine])
 
 
 def on_device(tokens, frozen, grad, down_weight, up_weight):
@@ -322,25 +350,26 @@
     up_plain, rank_plain = call(
         functools.partial(group_kernel, 0, 0), [up_half, rank_side], projected, grad, low_t, up_weight
     )
-    n = half_width // HEAD_DIM
-    square, line, pairs = sds((n, half, half), F32), sds((n, half), F32), sds((n, 2 * RANK, half), BF)
-    e, dp, top, total, bk, bv = call(
-        far_ready, [square, square, line, line, pairs, pairs], projected, grad, up_weight
+    n = half_width // HEAD_DIM // 2
+    diagonal, line, pairs = sds((n, 2 * half, 2 * HEAD_DIM), BF), sds((n, 2 * half), F32), sds((n, 2 * RANK, 2 * half), BF)
+    square = sds((n, half, 2 * half), F32)
+    q, g, e, dp, top, total, bk, bv = call(
+        far_ready, [diagonal, diagonal, square, square, line, line, pairs, pairs], projected, grad, up_weight
     )
     up_near, rank_near = call(
         functools.partial(group_kernel, half, half_width), [up_half, rank_side], projected, grad, low_t, up_weight
     )
     bk, rank_plain, rank_near = lax.optimization_barrier((bk, rank_plain, rank_near))
-    squares = sds((n, half, half), BF)
+    squares = sds((n, half, 2 * half), BF)
     cross, near, pb, ds, factor, dot = call(
         far_scores,
-        [sds((2 * RANK, count), F32), sds((n, half, HEAD_DIM), BF), squares, squares, line, line],
-        projected, frozen_kv, low_kv, grad, up_weight, e, dp, top, total, bk, bv,
+        [sds((2 * RANK, count), F32), sds((half, half_width), BF), squares, squares, line, line],
+        frozen_kv, low_kv, up_weight, q, g, e, dp, top, total, bk, bv,
     )
     cross = lax.ppermute(cross, "seq", backward)
     up_far, rank_far = call(
         far_rest, [up_half, rank_side],
-        projected, low_kv, grad, low_t, up_weight, e, dp, bk, bv, near, pb, ds, factor, dot,
+        projected, low_kv, low_t, up_weight, q, g, e, dp, bk, bv, near, pb, ds, factor, dot,
     )
     columns = (width + tokens.shape[2]) // 8
     piece = sds((4, 24, columns), F32)

time: 42.2 us -> 41.9 us (level)
  waiting for transfers between devices: 13.8 us -> 13.3 us
    ppermute x11 -> x14, waiting for transfers between devices: 10.6 us -> 10.1 us  [swap(): return lax.ppermute(x, AXES, [(i, i ^ bits) for i in range(total)])]
    ppermute x11 -> x14, starting transfers between devices: 11.4 us -> 11.6 us  [swap(): return lax.ppermute(x, AXES, [(i, i ^ bits) for i in range(total)])]
  transfers between devices with their start and end apart: 14 -> 17, of which waited for: 11 -> 12; matrix products, arithmetic and copies ran while one was open for 4% -> 4% of each run, Pallas kernels for 11% -> 12%
where the time goes in v12:
time: 41.9 us; the launch traced here: 41.7 us
  starting transfers between devices  17.9 us (43%)
  waiting for transfers between devices  13.3 us (32%)
  Pallas kernels  6.73 us (16%)
  matrix products  1.6 us (4%)
  local copies, waits for them, and re-layouts  1.22 us (3%)
  between operations  0.77 us (2%)
    ppermute x14, starting transfers between devices, swap(): return lax.ppermute(x, AXES, [(i, i ^ bits) for i in range(total)])  11.6 us
    ppermute x14, waiting for transfers between devices, swap(): return lax.ppermute(x, AXES, [(i, i ^ bits) for i in range(total)])  10.1 us
    pallas_call x9, Pallas kernels, call(): pl.pallas_call(kernel, out_shape=outs, in_specs=[VMEM] * len(args), out_s...  6.73 us
    ppermute x1, starting transfers between devices, on_device(): frozen_kv = lax.ppermute(frozen[1:, 0, half:, half_width:], 'seq', forward)  2.99 us
    ppermute x1, waiting for transfers between devices, on_device(): low_kv = lax.ppermute(low_t[1:, :, half:], 'seq', forward)  2.23 us
    ppermute x1, starting transfers between devices, on_device(): cross = lax.ppermute(cross, 'seq', backward)  1.78 us
    dot_general x1, matrix products, on_device(): jnp.einsum('psw,gw->psg', down_weight, tokens[0], preferred_element_type=...  1.6 us
    ppermute x1, starting transfers between devices, on_device(): low_kv = lax.ppermute(low_t[1:, :, half:], 'seq', forward)  1.56 us
  transfers between devices with their start and end apart: 17, of which 12 were waited for; matrix products, arithmetic and copies ran while one was open for 4% of the time, Pallas kernels for 12%

profile of v12, /device:TPU:0, one launch (start us, length us, event | category | flops | bytes accessed | tf_op | source)
XLA Modules:
  0.0 41.7 jit_solution(15824222234059669691)
XLA Ops:
  0.7 1.1 %slice_bitcast_fusion = bf16[2,64,1024]{2,1,0:T(8,128)(2,1)S(1)} fusion(bf16[3,1,128,2048]{3,2,0,1:T(8,128)(2,1)} %bitcast.32), kind=kLoop, calls=%fused_computation.2 | loop fusion | bytes 524288 | tf_op jit(solution)/shard_map/squeeze | solution.py:344
  1.8 3.0 %collective-permute-start.1 = (bf16[2,64,1024]{2,1,0:T(8,128)(2,1)S(1)}, bf16[2,64,1024]{2,1,0:T(8,128)(2,1)S(1)}, u32[]{:S(2)}, u32[]{:S(2)}) collective-permute-start(bf16[2,64,1024]{2,1,0:T(8,128)(2,1)S(1)} %slice_bitcast_fusion), channel_id=1, source_target_pairs={{0,4},{4,8},{8,12},{12,16},{16,20},{20,24},{24,28},{28,0},{1,5},{5... | collective-permute-start | bytes 786440 | tf_op jit(solution)/shard_map/ppermute | solution.py:344
  4.8 1.6 %convolution_convert_fusion.low_t = bf16[3,8,128]{2,1,0:T(8,128)(2,1)S(1)} fusion(bf16[3,8,4096]{2,1,0:T(8,128)(2,1)S(1)} %copy-done, bf16[1,128,4096]{2,1,0:T(8,128)(2,1)} %tokens.1), kind=kOutput, calls=%fused_computation | convolution fusion | flops 25168896 | bytes 1251328 | tf_op jit(solution)/shard_map/psw,gw->psg/dot_general | solution.py:345
  6.5 1.6 %collective-permute-start = (bf16[2,8,64]{2,1,0:T(8,128)(2,1)S(1)}, bf16[2,8,64]{2,1,0:T(8,128)(2,1)S(1)}, u32[]{:S(2)}, u32[]{:S(2)}) collective-permute-start(bf16[2,8,64]{2,1,0:T(8,128)(2,1)S(1)} %slice.27), channel_id=1, source_target_pairs={{0,4},{4,8},{8,12},{12,16},{16,20},{20,24},{24,28},{28,0},{1,5},{5... | collective-permute-start | bytes 6152 | tf_op jit(solution)/shard_map/ppermute | solution.py:346
  8.0 0.6 %shard_map.68.projected = bf16[3,128,2048]{2,1,0:T(8,128)(2,1)S(1)} custom-call(bf16[3,1,128,2048]{3,2,1,0:T(8,128)(2,1)S(1)} %copy-done.4, bf16[3,8,128]{2,1,0:T(8,128)(2,1)S(1)} %convolution_convert_fusion.low_t, bf16[3,8,2048]{2,1,0:T(8,128)(2,1)S(1)} %copy-done.3), custom_call_target="tpu_custom_call" | custom-call | flops 1000000 | bytes 10000 | tf_op jit(solution)/shard_map/pallas_call | solution.py:301
  8.6 1.2 %shard_map.71 = (f32[24,1024]{1,0:T(8,128)S(1)}, f32[24,128]{1,0:T(8,128)S(1)}) custom-call(bf16[3,128,2048]{2,1,0:T(8,128)(2,1)S(1)} %shard_map.68.projected, bf16[1,128,2048]{2,1,0:T(8,128)(2,1)S(1)} %copy-done.1, bf16[3,8,128]{2,1,0:T(8,128)(2,1)S(1)} %convolution_convert_fusion.low_t, bf16[3,8,2048]{2,1,0:T(8,128)(2,1)S(1)} %copy-done.3), custom_call_target="tpu_custom_call" | custom-call | flops 1000000 | bytes 10000 | tf_op jit(solution)/shard_map/pallas_call | solution.py:301
  9.9 1.6 %shard_map.70 = (f32[24,1024]{1,0:T(8,128)S(1)}, f32[24,128]{1,0:T(8,128)S(1)}) custom-call(bf16[3,128,2048]{2,1,0:T(8,128)(2,1)S(1)} %shard_map.68.projected, bf16[1,128,2048]{2,1,0:T(8,128)(2,1)S(1)} %copy-done.1, bf16[3,8,128]{2,1,0:T(8,128)(2,1)S(1)} %convolution_convert_fusion.low_t, bf16[3,8,2048]{2,1,0:T(8,128)(2,1)S(1)} %copy-done.3), custom_call_target="tpu_custom_call" | custom-call | flops 1000000 | bytes 10000 | tf_op jit(solution)/shard_map/pallas_call | solution.py:301
  11.5 0.5 %shard_map.69 = (bf16[4,128,256]{2,1,0:T(8,128)(2,1)S(1)}, bf16[4,128,256]{2,1,0:T(8,128)(2,1)S(1)}, f32[4,64,128]{2,1,0:T(8,128)S(1)}, f32[4,64,128]{2,1,0:T(8,...) custom-call(bf16[3,128,2048]{2,1,0:T(8,128)(2,1)S(1)} %shard_map.68., ...), custom_call_target="tpu_custom_call" | custom-call | flops 1000000 | bytes 10000 | tf_op jit(solution)/shard_map/pallas_call | solution.py:301
  12.0 2.2 %collective-permute-done.low_kv = bf16[2,8,64]{2,1,0:T(8,128)(2,1)S(1)} collective-permute-done((bf16[2,8,64]{2,1,0:T(8,128)(2,1)S(1)}, bf16[2,8,64]{2,1,0:T(8,128)(2,1)S(1)}, u32[]{:S(2)}, u32[]{:S(2)}) %collective-permute-start) | collective-permute-done | bytes 2080 | tf_op jit(solution)/shard_map/ppermute | solution.py:346
  14.2 0.7 %shard_map.72 = (f32[16,128]{1,0:T(8,128)S(1)}, bf16[64,1024]{1,0:T(8,128)(2,1)S(1)}, bf16[4,64,128]{2,1,0:T(8,128)(2,1)S(1)}, bf16[4,64,128]{2,1,0:T(8,128)(2,1...) custom-call(bf16[2,64,1024]{2,1,0:T(8,128)(2,1)S(1)} %collective-permute-done.1.frozen_kv, ...), custom_call_target="tpu_custom_call" | custom-call | flops 1000000 | bytes 10000 | tf_op jit(solution)/shard_map/pallas_call | solution.py:301
  14.9 1.8 %collective-permute-start.2 = (f32[16,128]{1,0:T(8,128)S(1)}, f32[16,128]{1,0:T(8,128)S(1)}, u32[]{:S(2)}, u32[]{:S(2)}) collective-permute-start(f32[16,128]{1,0:T(8,128)S(1)} %get-tuple-element.48), channel_id=1, source_target_pairs={{0,28},{4,0},{8,4},{12,8},{16,12},{20,16},{24,20},{28,24},{1,29},{... | collective-permute-start | bytes 24584 | tf_op jit(solution)/shard_map/ppermute | solution.py:369
  16.7 0.9 %shard_map.73 = (f32[24,1024]{1,0:T(8,128)S(1)}, f32[24,128]{1,0:T(8,128)S(1)}) custom-call(bf16[3,128,2048]{2,1,0:T(8,128)(2,1)S(1)} %shard_map.68.projected, bf16[2,8,64]{2,1,0:T(8,128)(2,1)S(1)} %collective-permute-done.low_kv, bf16[3,8,128]{2,1,0:T(8,128)(2,1)S(1)} %convolution_convert_fusion.low_t, bf16[3,8,2048]{2,1,0:T(8,128)(2,1)S(1)} %copy-done.3, ...), custom_call_target="tpu_custom_call" | custom-call | flops 1000000 | bytes 10000 | tf_op jit(solution)/shard_map/pallas_call | solution.py:301
  17.6 1.0 %collective-permute-done.2.cross = f32[16,128]{1,0:T(8,128)S(1)} collective-permute-done((f32[16,128]{1,0:T(8,128)S(1)}, f32[16,128]{1,0:T(8,128)S(1)}, u32[]{:S(2)}, u32[]{:S(2)}) %collective-permute-start.2) | collective-permute-done | bytes 8224 | tf_op jit(solution)/shard_map/ppermute | solution.py:369
  18.6 0.3 shard_map.74
  18.9 1.6 %collective-permute-done.3 = f32[4,24,768]{2,1,0:T(8,128)S(1)} collective-permute-done((f32[4,24,768]{2,1,0:T(8,128)S(1)}, f32[4,24,768]{2,1,0:T(8,128)S(1)}, u32[]{:S(2)}, u32[]{:S(2)}) %collective-permute-start.3) | collective-permute-done | bytes 294944 | tf_op jit(solution)/shard_map/ppermute | solution.py:312
  20.6 0.9 %collective-permute-start.4 = (bf16[24,768]{1,0:T(8,128)(2,1)S(1)}, bf16[24,768]{1,0:T(8,128)(2,1)S(1)}, u32[]{:S(2)}, u32[]{:S(2)}) collective-permute-start(bf16[24,768]{1,0:T(8,128)(2,1)S(1)} %get-tuple-element.58), channel_id=1, source_target_pairs={{0,7},{1,6},{2,5},{3,4},{4,3},{5,2},{6,1},{7,0},{8,15},{9,14},{10,... | collective-permute-start | bytes 110600 | tf_op jit(solution)/shard_map/ppermute | solution.py:312
  21.5 0.7 %collective-permute-start.6 = (bf16[24,768]{1,0:T(8,128)(2,1)S(1)}, bf16[24,768]{1,0:T(8,128)(2,1)S(1)}, u32[]{:S(2)}, u32[]{:S(2)}) collective-permute-start(bf16[24,768]{1,0:T(8,128)(2,1)S(1)} %get-tuple-element.59), channel_id=1, source_target_pairs={{0,2},{1,3},{2,0},{3,1},{4,6},{5,7},{6,4},{7,5},{8,10},{9,11},{10,... | collective-permute-start | bytes 110600 | tf_op jit(solution)/shard_map/ppermute | solution.py:312
  22.2 1.3 %collective-permute-start.5 = (bf16[24,768]{1,0:T(8,128)(2,1)S(1)}, bf16[24,768]{1,0:T(8,128)(2,1)S(1)}, u32[]{:S(2)}, u32[]{:S(2)}) collective-permute-start(bf16[24,768]{1,0:T(8,128)(2,1)S(1)} %get-tuple-element.60), channel_id=1, source_target_pairs={{0,5},{1,4},{2,7},{3,6},{4,1},{5,0},{6,3},{7,2},{8,13},{9,12},{10,... | collective-permute-start | bytes 110600 | tf_op jit(solution)/shard_map/ppermute | solution.py:312
  23.6 1.5 %collective-permute-done.4 = bf16[24,768]{1,0:T(8,128)(2,1)S(1)} collective-permute-done((bf16[24,768]{1,0:T(8,128)(2,1)S(1)}, bf16[24,768]{1,0:T(8,128)(2,1)S(1)}, u32[]{:S(2)}, u32[]{:S(2)}) %collective-permute-start.4) | collective-permute-done | bytes 36896 | tf_op jit(solution)/shard_map/ppermute | solution.py:312
  25.1 1.0 %collective-permute-done.6 = bf16[24,768]{1,0:T(8,128)(2,1)S(1)} collective-permute-done((bf16[24,768]{1,0:T(8,128)(2,1)S(1)}, bf16[24,768]{1,0:T(8,128)(2,1)S(1)}, u32[]{:S(2)}, u32[]{:S(2)}) %collective-permute-start.6) | collective-permute-done | bytes 36896 | tf_op jit(solution)/shard_map/ppermute | solution.py:312
  26.1 2.1 %collective-permute-start.9 = (bf16[24,768]{1,0:T(8,128)(2,1)S(1)}, bf16[24,768]{1,0:T(8,128)(2,1)S(1)}, u32[]{:S(2)}, u32[]{:S(2)}) collective-permute-start(bf16[24,768]{1,0:T(8,128)(2,1)S(1)} %fusion.4), channel_id=1, source_target_pairs={{0,16},{1,17},{2,18},{3,19},{4,20},{5,21},{6,22},{7,23},{8,24},{9,... | collective-permute-start | bytes 110600 | tf_op jit(solution)/shard_map/ppermute | solution.py:312
  28.2 2.3 %collective-permute-start.8 = (bf16[24,768]{1,0:T(8,128)(2,1)S(1)}, bf16[24,768]{1,0:T(8,128)(2,1)S(1)}, u32[]{:S(2)}, u32[]{:S(2)}) collective-permute-start(bf16[24,768]{1,0:T(8,128)(2,1)S(1)} %fusion.4), channel_id=1, source_target_pairs={{0,24},{1,25},{2,26},{3,27},{4,28},{5,29},{6,30},{7,31},{8,16},{9,... | collective-permute-start | bytes 110600 | tf_op jit(solution)/shard_map/ppermute | solution.py:312
  30.6 0.5 %collective-permute-start.7 = (bf16[24,768]{1,0:T(8,128)(2,1)S(1)}, bf16[24,768]{1,0:T(8,128)(2,1)S(1)}, u32[]{:S(2)}, u32[]{:S(2)}) collective-permute-start(bf16[24,768]{1,0:T(8,128)(2,1)S(1)} %fusion.4), channel_id=1, source_target_pairs={{0,8},{1,9},{2,10},{3,11},{4,12},{5,13},{6,14},{7,15},{8,0},{9,1},... | collective-permute-start | bytes 110600 | tf_op jit(solution)/shard_map/ppermute | solution.py:312
  31.0 3.0 %collective-permute-done.8 = bf16[24,768]{1,0:T(8,128)(2,1)S(1)} collective-permute-done((bf16[24,768]{1,0:T(8,128)(2,1)S(1)}, bf16[24,768]{1,0:T(8,128)(2,1)S(1)}, u32[]{:S(2)}, u32[]{:S(2)}) %collective-permute-start.8) | collective-permute-done | bytes 36896 | tf_op jit(solution)/shard_map/ppermute | solution.py:312
  34.0 0.5 %collective-permute-done.7 = bf16[24,768]{1,0:T(8,128)(2,1)S(1)} collective-permute-done((bf16[24,768]{1,0:T(8,128)(2,1)S(1)}, bf16[24,768]{1,0:T(8,128)(2,1)S(1)}, u32[]{:S(2)}, u32[]{:S(2)}) %collective-permute-start.7) | collective-permute-done | bytes 36896 | tf_op jit(solution)/shard_map/ppermute | solution.py:312
  34.6 1.6 %collective-permute-start.13 = (bf16[24,768]{1,0:T(8,128)(2,1)S(1)}, bf16[24,768]{1,0:T(8,128)(2,1)S(1)}, u32[]{:S(2)}, u32[]{:S(2)}) collective-permute-start(bf16[24,768]{1,0:T(8,128)(2,1)S(1)} %add_convert_fusion), channel_id=1, source_target_pairs={{0,2},{1,3},{2,0},{3,1},{4,6},{5,7},{6,4},{7,5},{8,10},{9,11},{10,... | collective-permute-start | bytes 110600 | tf_op jit(solution)/shard_map/ppermute | solution.py:312
  36.2 1.3 %collective-permute-start.11 = (bf16[24,768]{1,0:T(8,128)(2,1)S(1)}, bf16[24,768]{1,0:T(8,128)(2,1)S(1)}, u32[]{:S(2)}, u32[]{:S(2)}) collective-permute-start(bf16[24,768]{1,0:T(8,128)(2,1)S(1)} %add_convert_fusion), channel_id=1, source_target_pairs={{0,5},{1,4},{2,7},{3,6},{4,1},{5,0},{6,3},{7,2},{8,13},{9,12},{10,... | collective-permute-start | bytes 110600 | tf_op jit(solution)/shard_map/ppermute | solution.py:312
  37.5 1.5 %collective-permute-done.15 = bf16[24,768]{1,0:T(8,128)(2,1)S(1)} collective-permute-done((bf16[24,768]{1,0:T(8,128)(2,1)S(1)}, bf16[24,768]{1,0:T(8,128)(2,1)S(1)}, u32[]{:S(2)}, u32[]{:S(2)}) %collective-permute-start.15) | collective-permute-done | bytes 36896 | tf_op jit(solution)/shard_map/ppermute | solution.py:312
  39.0 0.3 collective-permute-done.13
  39.6 0.3 collective-permute-start.12
  40.2 0.3 collective-permute-done.14
  40.8 0.9 %shard_map.76 = (f32[3,8,4096]{2,1,0:T(8,128)}, f32[3,8,2048]{2,1,0:T(8,128)}) custom-call(bf16[4,24,768]{2,1,0:T(8,128)(2,1)S(1)} %pad_maximum_fusion.pieces, f32[3,8,4096]{2,1,0:T(8,128)S(1)} %get-tuple-element.54.down_in, f32[3,8,2048]{2,1,0:T(8,128)S(1)} %get-tuple-element.55.up_in), custom_call_target="tpu_custom_call" | custom-call | flops 1000000 | bytes 10000 | tf_op jit(solution)/shard_map/pallas_call | solution.py:301
  (30 shorter events, 1.2 us)
Async XLA Ops:
  0.6 4.1 %copy-start = (bf16[3,8,4096]{2,1,0:T(8,128)(2,1)S(1)}, bf16[3,8,4096]{2,1,0:T(8,128)(2,1)}, u32[]{:S(2)}) copy-start(bf16[3,8,4096]{2,1,0:T(8,128)(2,1)} %param.8) | copy-start | bytes 589828
  0.6 7.4 %copy-start.4 = (bf16[3,1,128,2048]{3,2,1,0:T(8,128)(2,1)S(1)}, bf16[3,1,128,2048]{3,2,1,0:T(8,128)(2,1)}, u32[]{:S(2)}) copy-start(bf16[3,1,128,2048]{3,2,1,0:T(8,128)(2,1)} %frozen.1) | copy-start | bytes 4718596
  0.7 7.4 %copy-start.3 = (bf16[3,8,2048]{2,1,0:T(8,128)(2,1)S(1)}, bf16[3,8,2048]{2,1,0:T(8,128)(2,1)}, u32[]{:S(2)}) copy-start(bf16[3,8,2048]{2,1,0:T(8,128)(2,1)} %up.11) | copy-start | bytes 294916
  1.8 12.4 %collective-permute-start.1 = (bf16[2,64,1024]{2,1,0:T(8,128)(2,1)S(1)}, bf16[2,64,1024]{2,1,0:T(8,128)(2,1)S(1)}, u32[]{:S(2)}, u32[]{:S(2)}) collective-permute-start(bf16[2,64,1024]{2,1,0:T(8,128)(2,1)S(1)} %slice_bitcast_fusion), channel_id=1, source_target_pairs={{0,4},{4,8},{8,12},{12,16},{16,20},{20,24},{24,28},{28,0},{1,5},{5... | collective-permute-start | bytes 786440 | tf_op jit(solution)/shard_map/ppermute | solution.py:344
  6.5 2.2 %copy-start.1 = (bf16[1,128,2048]{2,1,0:T(8,128)(2,1)S(1)}, bf16[1,128,2048]{2,1,0:T(8,128)(2,1)}, u32[]{:S(2)}) copy-start(bf16[1,128,2048]{2,1,0:T(8,128)(2,1)} %grad.5) | copy-start | bytes 1572868
  6.5 7.7 %collective-permute-start = (bf16[2,8,64]{2,1,0:T(8,128)(2,1)S(1)}, bf16[2,8,64]{2,1,0:T(8,128)(2,1)S(1)}, u32[]{:S(2)}, u32[]{:S(2)}) collective-permute-start(bf16[2,8,64]{2,1,0:T(8,128)(2,1)S(1)} %slice.27), channel_id=1, source_target_pairs={{0,4},{4,8},{8,12},{12,16},{16,20},{20,24},{24,28},{28,0},{1,5},{5... | collective-permute-start | bytes 6152 | tf_op jit(solution)/shard_map/ppermute | solution.py:346
  14.9 3.7 %copy-start.2 = (bf16[1,128,4096]{2,1,0:T(8,128)(2,1)S(1)}, bf16[1,128,4096]{2,1,0:T(8,128)(2,1)}, u32[]{:S(2)}) copy-start(bf16[1,128,4096]{2,1,0:T(8,128)(2,1)} %tokens.1) | copy-start | bytes 3145732
  14.9 3.7 %collective-permute-start.2 = (f32[16,128]{1,0:T(8,128)S(1)}, f32[16,128]{1,0:T(8,128)S(1)}, u32[]{:S(2)}, u32[]{:S(2)}) collective-permute-start(f32[16,128]{1,0:T(8,128)S(1)} %get-tuple-element.48), channel_id=1, source_target_pairs={{0,28},{4,0},{8,4},{12,8},{16,12},{20,16},{24,20},{28,24},{1,29},{... | collective-permute-start | bytes 24584 | tf_op jit(solution)/shard_map/ppermute | solution.py:369
  18.9 1.6 %collective-permute-start.3 = (f32[4,24,768]{2,1,0:T(8,128)S(1)}, f32[4,24,768]{2,1,0:T(8,128)S(1)}, u32[]{:S(2)}, u32[]{:S(2)}) collective-permute-start(f32[4,24,768]{2,1,0:T(8,128)S(1)} %get-tuple-element.53), channel_id=1, source_target_pairs={{0,1},{1,0},{2,3},{3,2},{4,5},{5,4},{6,7},{7,6},{8,9},{9,8},{10,11... | collective-permute-start | bytes 884744 | tf_op jit(solution)/shard_map/ppermute | solution.py:312
  20.6 4.5 %collective-permute-start.4 = (bf16[24,768]{1,0:T(8,128)(2,1)S(1)}, bf16[24,768]{1,0:T(8,128)(2,1)S(1)}, u32[]{:S(2)}, u32[]{:S(2)}) collective-permute-start(bf16[24,768]{1,0:T(8,128)(2,1)S(1)} %get-tuple-element.58), channel_id=1, source_target_pairs={{0,7},{1,6},{2,5},{3,4},{4,3},{5,2},{6,1},{7,0},{8,15},{9,14},{10,... | collective-permute-start | bytes 110600 | tf_op jit(solution)/shard_map/ppermute | solution.py:312
  21.5 4.5 %collective-permute-start.6 = (bf16[24,768]{1,0:T(8,128)(2,1)S(1)}, bf16[24,768]{1,0:T(8,128)(2,1)S(1)}, u32[]{:S(2)}, u32[]{:S(2)}) collective-permute-start(bf16[24,768]{1,0:T(8,128)(2,1)S(1)} %get-tuple-element.59), channel_id=1, source_target_pairs={{0,2},{1,3},{2,0},{3,1},{4,6},{5,7},{6,4},{7,5},{8,10},{9,11},{10,... | collective-permute-start | bytes 110600 | tf_op jit(solution)/shard_map/ppermute | solution.py:312
  22.2 3.8 %collective-permute-start.5 = (bf16[24,768]{1,0:T(8,128)(2,1)S(1)}, bf16[24,768]{1,0:T(8,128)(2,1)S(1)}, u32[]{:S(2)}, u32[]{:S(2)}) collective-permute-start(bf16[24,768]{1,0:T(8,128)(2,1)S(1)} %get-tuple-element.60), channel_id=1, source_target_pairs={{0,5},{1,4},{2,7},{3,6},{4,1},{5,0},{6,3},{7,2},{8,13},{9,12},{10,... | collective-permute-start | bytes 110600 | tf_op jit(solution)/shard_map/ppermute | solution.py:312
  26.1 4.9 %collective-permute-start.9 = (bf16[24,768]{1,0:T(8,128)(2,1)S(1)}, bf16[24,768]{1,0:T(8,128)(2,1)S(1)}, u32[]{:S(2)}, u32[]{:S(2)}) collective-permute-start(bf16[24,768]{1,0:T(8,128)(2,1)S(1)} %fusion.4), channel_id=1, source_target_pairs={{0,16},{1,17},{2,18},{3,19},{4,20},{5,21},{6,22},{7,23},{8,24},{9,... | collective-permute-start | bytes 110600 | tf_op jit(solution)/shard_map/ppermute | solution.py:312
  28.2 5.8 %collective-permute-start.8 = (bf16[24,768]{1,0:T(8,128)(2,1)S(1)}, bf16[24,768]{1,0:T(8,128)(2,1)S(1)}, u32[]{:S(2)}, u32[]{:S(2)}) collective-permute-start(bf16[24,768]{1,0:T(8,128)(2,1)S(1)} %fusion.4), channel_id=1, source_target_pairs={{0,24},{1,25},{2,26},{3,27},{4,28},{5,29},{6,30},{7,31},{8,16},{9,... | collective-permute-start | bytes 110600 | tf_op jit(solution)/shard_map/ppermute | solution.py:312
  30.6 4.0 %collective-permute-start.7 = (bf16[24,768]{1,0:T(8,128)(2,1)S(1)}, bf16[24,768]{1,0:T(8,128)(2,1)S(1)}, u32[]{:S(2)}, u32[]{:S(2)}) collective-permute-start(bf16[24,768]{1,0:T(8,128)(2,1)S(1)} %fusion.4), channel_id=1, source_target_pairs={{0,8},{1,9},{2,10},{3,11},{4,12},{5,13},{6,14},{7,15},{8,0},{9,1},... | collective-permute-start | bytes 110600 | tf_op jit(solution)/shard_map/ppermute | solution.py:312
  34.5 4.5 %collective-permute-start.15 = (bf16[24,768]{1,0:T(8,128)(2,1)S(1)}, bf16[24,768]{1,0:T(8,128)(2,1)S(1)}, u32[]{:S(2)}, u32[]{:S(2)}) collective-permute-start(bf16[24,768]{1,0:T(8,128)(2,1)S(1)} %add_convert_fusion), channel_id=1, source_target_pairs={{0,7},{1,6},{2,5},{3,4},{4,3},{5,2},{6,1},{7,0},{8,15},{9,14},{10,... | collective-permute-start | bytes 110600 | tf_op jit(solution)/shard_map/ppermute | solution.py:312
  34.6 4.7 %collective-permute-start.13 = (bf16[24,768]{1,0:T(8,128)(2,1)S(1)}, bf16[24,768]{1,0:T(8,128)(2,1)S(1)}, u32[]{:S(2)}, u32[]{:S(2)}) collective-permute-start(bf16[24,768]{1,0:T(8,128)(2,1)S(1)} %add_convert_fusion), channel_id=1, source_target_pairs={{0,2},{1,3},{2,0},{3,1},{4,6},{5,7},{6,4},{7,5},{8,10},{9,11},{10,... | collective-permute-start | bytes 110600 | tf_op jit(solution)/shard_map/ppermute | solution.py:312
  36.2 3.4 %collective-permute-start.11 = (bf16[24,768]{1,0:T(8,128)(2,1)S(1)}, bf16[24,768]{1,0:T(8,128)(2,1)S(1)}, u32[]{:S(2)}, u32[]{:S(2)}) collective-permute-start(bf16[24,768]{1,0:T(8,128)(2,1)S(1)} %add_convert_fusion), channel_id=1, source_target_pairs={{0,5},{1,4},{2,7},{3,6},{4,1},{5,0},{6,3},{7,2},{8,13},{9,12},{10,... | collective-permute-start | bytes 110600 | tf_op jit(solution)/shard_map/ppermute | solution.py:312
  37.5 2.5 %collective-permute-start.10 = (bf16[24,768]{1,0:T(8,128)(2,1)S(1)}, bf16[24,768]{1,0:T(8,128)(2,1)S(1)}, u32[]{:S(2)}, u32[]{:S(2)}) collective-permute-start(bf16[24,768]{1,0:T(8,128)(2,1)S(1)} %add_convert_fusion), channel_id=1, source_target_pairs={{0,1},{1,0},{2,3},{3,2},{4,5},{5,4},{6,7},{7,6},{8,9},{9,8},{10,11... | collective-permute-start | bytes 110600 | tf_op jit(solution)/shard_map/ppermute | solution.py:312
  39.0 1.2 %collective-permute-start.16 = (bf16[24,768]{1,0:T(8,128)(2,1)S(1)}, bf16[24,768]{1,0:T(8,128)(2,1)S(1)}, u32[]{:S(2)}, u32[]{:S(2)}) collective-permute-start(bf16[24,768]{1,0:T(8,128)(2,1)S(1)} %collective-permute-done.15), channel_id=1, source_target_pairs={{0,1},{1,0},{2,3},{3,2},{4,5},{5,4},{6,7},{7,6},{8,9},{9,8},{10,11... | collective-permute-start | bytes 110600 | tf_op jit(solution)/shard_map/ppermute | solution.py:312
  39.3 1.2 %collective-permute-start.14 = (bf16[24,768]{1,0:T(8,128)(2,1)S(1)}, bf16[24,768]{1,0:T(8,128)(2,1)S(1)}, u32[]{:S(2)}, u32[]{:S(2)}) collective-permute-start(bf16[24,768]{1,0:T(8,128)(2,1)S(1)} %collective-permute-done.13), channel_id=1, source_target_pairs={{0,1},{1,0},{2,3},{3,2},{4,5},{5,4},{6,7},{7,6},{8,9},{9,8},{10,11... | collective-permute-start | bytes 110600 | tf_op jit(solution)/shard_map/ppermute | solution.py:312
  39.6 1.2 %collective-permute-start.12 = (bf16[24,768]{1,0:T(8,128)(2,1)S(1)}, bf16[24,768]{1,0:T(8,128)(2,1)S(1)}, u32[]{:S(2)}, u32[]{:S(2)}) collective-permute-start(bf16[24,768]{1,0:T(8,128)(2,1)S(1)} %collective-permute-done.11), channel_id=1, source_target_pairs={{0,1},{1,0},{2,3},{3,2},{4,5},{5,4},{6,7},{7,6},{8,9},{9,8},{10,11... | collective-permute-start | bytes 110600 | tf_op jit(solution)/shard_map/ppermute | solution.py:312

commit v13 on v12

--- a/solution.py
+++ b/solution.py
@@ -276,9 +276,9 @@
     half, quarter = position()
     half = half if own else 1 - half
     up_step, down_step = up_out.shape[2] // 8, down_out.shape[2] // 8
-    for c in range(4):
-        x = pieces[quarter ^ c].astype(F32)
-        at = 2 * c + half
+    for away in range(4):
+        x = pieces[away][...].astype(F32)
+        at = 2 * (quarter ^ away) + half
         ups = pl.ds(pl.multiple_of(at * up_step, up_step), up_step)
         downs = pl.ds(pl.multiple_of(at * down_step, down_step), down_step)
         for j in range(3):
@@ -287,14 +287,14 @@
             down_out[j, :, downs] = part[:, up_step:]
 
 
-def first_spread(pieces, down_out, up_out):
-    spread(pieces, True, down_out, up_out)
-
-
-def last_spread(pieces, down_in, up_in, down_out, up_out):
+def first_spread(a, b, c, d, down_out, up_out):
+    spread((a, b, c, d), True, down_out, up_out)
+
+
+def last_spread(a, b, c, d, down_in, up_in, down_out, up_out):
     down_out[...] = down_in[...]
     up_out[...] = up_in[...]
-    spread(pieces, False, down_out, up_out)
+    spread((a, b, c, d), False, down_out, up_out)
 
 
 def call(kernel, outs, *args):
@@ -315,7 +315,7 @@
 def total_sum(keep, send, seqs, dps):
     total = seqs * dps
     partner = {1: dps | 1, 2: 2, 3: dps | 3}
-    keep = keep + swap(send, 1, total)
+    keep = keep + swap(send.astype(BF), 1, total).astype(F32)
     got = [swap(keep[s].astype(BF), partner[s], total).astype(F32) for s in (1, 2, 3)]
     own = keep[0] + got[2] + got[0] + got[1]
     bit = 2
@@ -332,7 +332,7 @@
             own = own + parts[0].astype(F32)
     piece = own.astype(BF)
     mine = [piece] + [swap(piece, partner[s], total) for s in (1, 2, 3)]
-    return jnp.stack(mine), jnp.stack([swap(x, 1, total) for x in mine])
+    return mine, [swap(x, 1, total) for x in mine]
 
 
 def on_device(tokens, frozen, grad, down_weight, up_weight):
@@ -376,7 +376,7 @@
     keep, send = call(down_kernel, [piece, piece], tokens, rank_plain, rank_near, rank_far, cross, up_plain, up_near, up_far)
     mine, other = total_sum(keep, send, seqs, dps)
     outs = [sds((3, RANK, tokens.shape[2]), F32), sds((3, RANK, width), F32)]
-    return tuple(call(last_spread, outs, other, *call(first_spread, outs, mine)))
+    return tuple(call(last_spread, outs, *other, *call(first_spread, outs, *mine)))
 
 
 def solution(mesh):

time: 41.9 us -> 41.7 us (level)
  no operation moved by 1% of the time
where the time goes in v13:
time: 41.7 us; the launch traced here: 41.5 us
  starting transfers between devices  17.9 us (43%)
  waiting for transfers between devices  13.2 us (32%)
  Pallas kernels  6.73 us (16%)
  matrix products  1.6 us (4%)
  local copies, waits for them, and re-layouts  1.22 us (3%)
  between operations  0.77 us (2%)
    ppermute x14, starting transfers between devices, swap(): return lax.ppermute(x, AXES, [(i, i ^ bits) for i in range(total)])  11.6 us
    ppermute x14, waiting for transfers between devices, swap(): return lax.ppermute(x, AXES, [(i, i ^ bits) for i in range(total)])  10 us
    pallas_call x9, Pallas kernels, call(): pl.pallas_call(kernel, out_shape=outs, in_specs=[VMEM] * len(args), out_s...  6.73 us
    ppermute x1, starting transfers between devices, on_device(): frozen_kv = lax.ppermute(frozen[1:, 0, half:, half_width:], 'seq', forward)  2.99 us
    ppermute x1, waiting for transfers between devices, on_device(): low_kv = lax.ppermute(low_t[1:, :, half:], 'seq', forward)  2.23 us
    ppermute x1, starting transfers between devices, on_device(): cross = lax.ppermute(cross, 'seq', backward)  1.78 us
    dot_general x1, matrix products, on_device(): jnp.einsum('psw,gw->psg', down_weight, tokens[0], preferred_element_type=...  1.6 us
    ppermute x1, starting transfers between devices, on_device(): low_kv = lax.ppermute(low_t[1:, :, half:], 'seq', forward)  1.56 us
  transfers between devices with their start and end apart: 17, of which 12 were waited for; matrix products, arithmetic and copies ran while one was open for 4% of the time, Pallas kernels for 12%

profile of v13, /device:TPU:0, one launch (start us, length us, event | category | flops | bytes accessed | tf_op | source)
XLA Modules:
  0.0 41.5 jit_solution(3603664804794376568)
XLA Ops:
  0.7 1.1 %slice_bitcast_fusion = bf16[2,64,1024]{2,1,0:T(8,128)(2,1)S(1)} fusion(bf16[3,1,128,2048]{3,2,0,1:T(8,128)(2,1)} %bitcast.24), kind=kLoop, calls=%fused_computation.3 | loop fusion | bytes 524288 | tf_op jit(solution)/shard_map/squeeze | solution.py:344
  1.8 3.0 %collective-permute-start.1 = (bf16[2,64,1024]{2,1,0:T(8,128)(2,1)S(1)}, bf16[2,64,1024]{2,1,0:T(8,128)(2,1)S(1)}, u32[]{:S(2)}, u32[]{:S(2)}) collective-permute-start(bf16[2,64,1024]{2,1,0:T(8,128)(2,1)S(1)} %slice_bitcast_fusion), channel_id=1, source_target_pairs={{0,4},{4,8},{8,12},{12,16},{16,20},{20,24},{24,28},{28,0},{1,5},{5... | collective-permute-start | bytes 786440 | tf_op jit(solution)/shard_map/ppermute | solution.py:344
  4.8 1.6 %convolution_convert_fusion.low_t = bf16[3,8,128]{2,1,0:T(8,128)(2,1)S(1)} fusion(bf16[3,8,4096]{2,1,0:T(8,128)(2,1)S(1)} %copy-done, bf16[1,128,4096]{2,1,0:T(8,128)(2,1)} %tokens.1), kind=kOutput, calls=%fused_computation | convolution fusion | flops 25168896 | bytes 1251328 | tf_op jit(solution)/shard_map/psw,gw->psg/dot_general | solution.py:345
  6.5 1.6 %collective-permute-start = (bf16[2,8,64]{2,1,0:T(8,128)(2,1)S(1)}, bf16[2,8,64]{2,1,0:T(8,128)(2,1)S(1)}, u32[]{:S(2)}, u32[]{:S(2)}) collective-permute-start(bf16[2,8,64]{2,1,0:T(8,128)(2,1)S(1)} %slice.27), channel_id=1, source_target_pairs={{0,4},{4,8},{8,12},{12,16},{16,20},{20,24},{24,28},{28,0},{1,5},{5... | collective-permute-start | bytes 6152 | tf_op jit(solution)/shard_map/ppermute | solution.py:346
  8.0 0.6 %shard_map.68.projected = bf16[3,128,2048]{2,1,0:T(8,128)(2,1)S(1)} custom-call(bf16[3,1,128,2048]{3,2,1,0:T(8,128)(2,1)S(1)} %copy-done.4, bf16[3,8,128]{2,1,0:T(8,128)(2,1)S(1)} %convolution_convert_fusion.low_t, bf16[3,8,2048]{2,1,0:T(8,128)(2,1)S(1)} %copy-done.3), custom_call_target="tpu_custom_call" | custom-call | flops 1000000 | bytes 10000 | tf_op jit(solution)/shard_map/pallas_call | solution.py:301
  8.6 1.2 %shard_map.71 = (f32[24,1024]{1,0:T(8,128)S(1)}, f32[24,128]{1,0:T(8,128)S(1)}) custom-call(bf16[3,128,2048]{2,1,0:T(8,128)(2,1)S(1)} %shard_map.68.projected, bf16[1,128,2048]{2,1,0:T(8,128)(2,1)S(1)} %copy-done.1, bf16[3,8,128]{2,1,0:T(8,128)(2,1)S(1)} %convolution_convert_fusion.low_t, bf16[3,8,2048]{2,1,0:T(8,128)(2,1)S(1)} %copy-done.3), custom_call_target="tpu_custom_call" | custom-call | flops 1000000 | bytes 10000 | tf_op jit(solution)/shard_map/pallas_call | solution.py:301
  9.9 1.6 %shard_map.70 = (f32[24,1024]{1,0:T(8,128)S(1)}, f32[24,128]{1,0:T(8,128)S(1)}) custom-call(bf16[3,128,2048]{2,1,0:T(8,128)(2,1)S(1)} %shard_map.68.projected, bf16[1,128,2048]{2,1,0:T(8,128)(2,1)S(1)} %copy-done.1, bf16[3,8,128]{2,1,0:T(8,128)(2,1)S(1)} %convolution_convert_fusion.low_t, bf16[3,8,2048]{2,1,0:T(8,128)(2,1)S(1)} %copy-done.3), custom_call_target="tpu_custom_call" | custom-call | flops 1000000 | bytes 10000 | tf_op jit(solution)/shard_map/pallas_call | solution.py:301
  11.5 0.5 %shard_map.69 = (bf16[4,128,256]{2,1,0:T(8,128)(2,1)S(1)}, bf16[4,128,256]{2,1,0:T(8,128)(2,1)S(1)}, f32[4,64,128]{2,1,0:T(8,128)S(1)}, f32[4,64,128]{2,1,0:T(8,...) custom-call(bf16[3,128,2048]{2,1,0:T(8,128)(2,1)S(1)} %shard_map.68., ...), custom_call_target="tpu_custom_call" | custom-call | flops 1000000 | bytes 10000 | tf_op jit(solution)/shard_map/pallas_call | solution.py:301
  12.0 2.2 %collective-permute-done.low_kv = bf16[2,8,64]{2,1,0:T(8,128)(2,1)S(1)} collective-permute-done((bf16[2,8,64]{2,1,0:T(8,128)(2,1)S(1)}, bf16[2,8,64]{2,1,0:T(8,128)(2,1)S(1)}, u32[]{:S(2)}, u32[]{:S(2)}) %collective-permute-start) | collective-permute-done | bytes 2080 | tf_op jit(solution)/shard_map/ppermute | solution.py:346
  14.2 0.7 %shard_map.72 = (f32[16,128]{1,0:T(8,128)S(1)}, bf16[64,1024]{1,0:T(8,128)(2,1)S(1)}, bf16[4,64,128]{2,1,0:T(8,128)(2,1)S(1)}, bf16[4,64,128]{2,1,0:T(8,128)(2,1...) custom-call(bf16[2,64,1024]{2,1,0:T(8,128)(2,1)S(1)} %collective-permute-done.1.frozen_kv, ...), custom_call_target="tpu_custom_call" | custom-call | flops 1000000 | bytes 10000 | tf_op jit(solution)/shard_map/pallas_call | solution.py:301
  14.9 1.8 %collective-permute-start.2 = (f32[16,128]{1,0:T(8,128)S(1)}, f32[16,128]{1,0:T(8,128)S(1)}, u32[]{:S(2)}, u32[]{:S(2)}) collective-permute-start(f32[16,128]{1,0:T(8,128)S(1)} %get-tuple-element.48), channel_id=1, source_target_pairs={{0,28},{4,0},{8,4},{12,8},{16,12},{20,16},{24,20},{28,24},{1,29},{... | collective-permute-start | bytes 24584 | tf_op jit(solution)/shard_map/ppermute | solution.py:369
  16.7 0.9 %shard_map.73 = (f32[24,1024]{1,0:T(8,128)S(1)}, f32[24,128]{1,0:T(8,128)S(1)}) custom-call(bf16[3,128,2048]{2,1,0:T(8,128)(2,1)S(1)} %shard_map.68.projected, bf16[2,8,64]{2,1,0:T(8,128)(2,1)S(1)} %collective-permute-done.low_kv, bf16[3,8,128]{2,1,0:T(8,128)(2,1)S(1)} %convolution_convert_fusion.low_t, bf16[3,8,2048]{2,1,0:T(8,128)(2,1)S(1)} %copy-done.3, ...), custom_call_target="tpu_custom_call" | custom-call | flops 1000000 | bytes 10000 | tf_op jit(solution)/shard_map/pallas_call | solution.py:301
  17.6 1.0 %collective-permute-done.2.cross = f32[16,128]{1,0:T(8,128)S(1)} collective-permute-done((f32[16,128]{1,0:T(8,128)S(1)}, f32[16,128]{1,0:T(8,128)S(1)}, u32[]{:S(2)}, u32[]{:S(2)}) %collective-permute-start.2) | collective-permute-done | bytes 8224 | tf_op jit(solution)/shard_map/ppermute | solution.py:369
  18.6 0.3 shard_map.74
  19.0 1.4 %collective-permute-done.3 = bf16[4,24,768]{2,1,0:T(8,128)(2,1)S(1)} collective-permute-done((bf16[4,24,768]{2,1,0:T(8,128)(2,1)S(1)}, bf16[4,24,768]{2,1,0:T(8,128)(2,1)S(1)}, u32[]{:S(2)}, u32[]{:S(2)}) %collective-permute-start.3) | collective-permute-done | bytes 147488 | tf_op jit(solution)/shard_map/ppermute | solution.py:312
  20.4 0.9 %collective-permute-start.4 = (bf16[24,768]{1,0:T(8,128)(2,1)S(1)}, bf16[24,768]{1,0:T(8,128)(2,1)S(1)}, u32[]{:S(2)}, u32[]{:S(2)}) collective-permute-start(bf16[24,768]{1,0:T(8,128)(2,1)S(1)} %get-tuple-element.58), channel_id=1, source_target_pairs={{0,7},{1,6},{2,5},{3,4},{4,3},{5,2},{6,1},{7,0},{8,15},{9,14},{10,... | collective-permute-start | bytes 110600 | tf_op jit(solution)/shard_map/ppermute | solution.py:312
  21.3 0.7 %collective-permute-start.6 = (bf16[24,768]{1,0:T(8,128)(2,1)S(1)}, bf16[24,768]{1,0:T(8,128)(2,1)S(1)}, u32[]{:S(2)}, u32[]{:S(2)}) collective-permute-start(bf16[24,768]{1,0:T(8,128)(2,1)S(1)} %get-tuple-element.59), channel_id=1, source_target_pairs={{0,2},{1,3},{2,0},{3,1},{4,6},{5,7},{6,4},{7,5},{8,10},{9,11},{10,... | collective-permute-start | bytes 110600 | tf_op jit(solution)/shard_map/ppermute | solution.py:312
  22.0 1.3 %collective-permute-start.5 = (bf16[24,768]{1,0:T(8,128)(2,1)S(1)}, bf16[24,768]{1,0:T(8,128)(2,1)S(1)}, u32[]{:S(2)}, u32[]{:S(2)}) collective-permute-start(bf16[24,768]{1,0:T(8,128)(2,1)S(1)} %get-tuple-element.60), channel_id=1, source_target_pairs={{0,5},{1,4},{2,7},{3,6},{4,1},{5,0},{6,3},{7,2},{8,13},{9,12},{10,... | collective-permute-start | bytes 110600 | tf_op jit(solution)/shard_map/ppermute | solution.py:312
  23.4 1.5 %collective-permute-done.4 = bf16[24,768]{1,0:T(8,128)(2,1)S(1)} collective-permute-done((bf16[24,768]{1,0:T(8,128)(2,1)S(1)}, bf16[24,768]{1,0:T(8,128)(2,1)S(1)}, u32[]{:S(2)}, u32[]{:S(2)}) %collective-permute-start.4) | collective-permute-done | bytes 36896 | tf_op jit(solution)/shard_map/ppermute | solution.py:312
  24.9 1.0 %collective-permute-done.6 = bf16[24,768]{1,0:T(8,128)(2,1)S(1)} collective-permute-done((bf16[24,768]{1,0:T(8,128)(2,1)S(1)}, bf16[24,768]{1,0:T(8,128)(2,1)S(1)}, u32[]{:S(2)}, u32[]{:S(2)}) %collective-permute-start.6) | collective-permute-done | bytes 36896 | tf_op jit(solution)/shard_map/ppermute | solution.py:312
  25.9 2.2 %collective-permute-start.9 = (bf16[24,768]{1,0:T(8,128)(2,1)S(1)}, bf16[24,768]{1,0:T(8,128)(2,1)S(1)}, u32[]{:S(2)}, u32[]{:S(2)}) collective-permute-start(bf16[24,768]{1,0:T(8,128)(2,1)S(1)} %fusion.4), channel_id=1, source_target_pairs={{0,16},{1,17},{2,18},{3,19},{4,20},{5,21},{6,22},{7,23},{8,24},{9,... | collective-permute-start | bytes 110600 | tf_op jit(solution)/shard_map/ppermute | solution.py:312
  28.1 2.3 %collective-permute-start.8 = (bf16[24,768]{1,0:T(8,128)(2,1)S(1)}, bf16[24,768]{1,0:T(8,128)(2,1)S(1)}, u32[]{:S(2)}, u32[]{:S(2)}) collective-permute-start(bf16[24,768]{1,0:T(8,128)(2,1)S(1)} %fusion.4), channel_id=1, source_target_pairs={{0,24},{1,25},{2,26},{3,27},{4,28},{5,29},{6,30},{7,31},{8,16},{9,... | collective-permute-start | bytes 110600 | tf_op jit(solution)/shard_map/ppermute | solution.py:312
  30.4 0.5 %collective-permute-start.7 = (bf16[24,768]{1,0:T(8,128)(2,1)S(1)}, bf16[24,768]{1,0:T(8,128)(2,1)S(1)}, u32[]{:S(2)}, u32[]{:S(2)}) collective-permute-start(bf16[24,768]{1,0:T(8,128)(2,1)S(1)} %fusion.4), channel_id=1, source_target_pairs={{0,8},{1,9},{2,10},{3,11},{4,12},{5,13},{6,14},{7,15},{8,0},{9,1},... | collective-permute-start | bytes 110600 | tf_op jit(solution)/shard_map/ppermute | solution.py:312
  30.9 3.0 %collective-permute-done.8 = bf16[24,768]{1,0:T(8,128)(2,1)S(1)} collective-permute-done((bf16[24,768]{1,0:T(8,128)(2,1)S(1)}, bf16[24,768]{1,0:T(8,128)(2,1)S(1)}, u32[]{:S(2)}, u32[]{:S(2)}) %collective-permute-start.8) | collective-permute-done | bytes 36896 | tf_op jit(solution)/shard_map/ppermute | solution.py:312
  33.8 0.5 %collective-permute-done.7 = bf16[24,768]{1,0:T(8,128)(2,1)S(1)} collective-permute-done((bf16[24,768]{1,0:T(8,128)(2,1)S(1)}, bf16[24,768]{1,0:T(8,128)(2,1)S(1)}, u32[]{:S(2)}, u32[]{:S(2)}) %collective-permute-start.7) | collective-permute-done | bytes 36896 | tf_op jit(solution)/shard_map/ppermute | solution.py:312
  34.4 1.6 %collective-permute-start.13 = (bf16[24,768]{1,0:T(8,128)(2,1)S(1)}, bf16[24,768]{1,0:T(8,128)(2,1)S(1)}, u32[]{:S(2)}, u32[]{:S(2)}) collective-permute-start(bf16[24,768]{1,0:T(8,128)(2,1)S(1)} %add_convert_fusion.a), channel_id=1, source_target_pairs={{0,2},{1,3},{2,0},{3,1},{4,6},{5,7},{6,4},{7,5},{8,10},{9,11},{10,... | collective-permute-start | bytes 110600 | tf_op jit(solution)/shard_map/ppermute | solution.py:312
  36.0 1.3 %collective-permute-start.11 = (bf16[24,768]{1,0:T(8,128)(2,1)S(1)}, bf16[24,768]{1,0:T(8,128)(2,1)S(1)}, u32[]{:S(2)}, u32[]{:S(2)}) collective-permute-start(bf16[24,768]{1,0:T(8,128)(2,1)S(1)} %add_convert_fusion.a), channel_id=1, source_target_pairs={{0,5},{1,4},{2,7},{3,6},{4,1},{5,0},{6,3},{7,2},{8,13},{9,12},{10,... | collective-permute-start | bytes 110600 | tf_op jit(solution)/shard_map/ppermute | solution.py:312
  37.4 1.5 %collective-permute-done.15.d = bf16[24,768]{1,0:T(8,128)(2,1)S(1)} collective-permute-done((bf16[24,768]{1,0:T(8,128)(2,1)S(1)}, bf16[24,768]{1,0:T(8,128)(2,1)S(1)}, u32[]{:S(2)}, u32[]{:S(2)}) %collective-permute-start.15) | collective-permute-done | bytes 36896 | tf_op jit(solution)/shard_map/ppermute | solution.py:312
  38.8 0.3 collective-permute-done.13.c
  39.4 0.3 collective-permute-start.12
  40.0 0.3 collective-permute-done.14.c
  40.6 0.9 %shard_map.76 = (f32[3,8,4096]{2,1,0:T(8,128)}, f32[3,8,2048]{2,1,0:T(8,128)}) custom-call(bf16[24,768]{1,0:T(8,128)(2,1)S(1)} %collective-permute-done.10.a, bf16[24,768]{1,0:T(8,128)(2,1)S(1)} %collective-permute-done.12.b, bf16[24,768]{1,0:T(8,128)(2,1)S(1)} %collective-permute-done.14.c, bf16[24,768]{1,0:T(8,128)(2,1)S(1)} %collective-permute-done.16.d, ...), custom_call_target="tpu_custom_call" | custom-call | flops 1000000 | bytes 10000 | tf_op jit(solution)/shard_map/pallas_call | solution.py:301
  (29 shorter events, 1.2 us)
Async XLA Ops:
  0.6 4.1 %copy-start = (bf16[3,8,4096]{2,1,0:T(8,128)(2,1)S(1)}, bf16[3,8,4096]{2,1,0:T(8,128)(2,1)}, u32[]{:S(2)}) copy-start(bf16[3,8,4096]{2,1,0:T(8,128)(2,1)} %param.8) | copy-start | bytes 589828
  0.6 7.4 %copy-start.4 = (bf16[3,1,128,2048]{3,2,1,0:T(8,128)(2,1)S(1)}, bf16[3,1,128,2048]{3,2,1,0:T(8,128)(2,1)}, u32[]{:S(2)}) copy-start(bf16[3,1,128,2048]{3,2,1,0:T(8,128)(2,1)} %frozen.1) | copy-start | bytes 4718596
  0.7 7.4 %copy-start.3 = (bf16[3,8,2048]{2,1,0:T(8,128)(2,1)S(1)}, bf16[3,8,2048]{2,1,0:T(8,128)(2,1)}, u32[]{:S(2)}) copy-start(bf16[3,8,2048]{2,1,0:T(8,128)(2,1)} %up.11) | copy-start | bytes 294916
  1.8 12.4 %collective-permute-start.1 = (bf16[2,64,1024]{2,1,0:T(8,128)(2,1)S(1)}, bf16[2,64,1024]{2,1,0:T(8,128)(2,1)S(1)}, u32[]{:S(2)}, u32[]{:S(2)}) collective-permute-start(bf16[2,64,1024]{2,1,0:T(8,128)(2,1)S(1)} %slice_bitcast_fusion), channel_id=1, source_target_pairs={{0,4},{4,8},{8,12},{12,16},{16,20},{20,24},{24,28},{28,0},{1,5},{5... | collective-permute-start | bytes 786440 | tf_op jit(solution)/shard_map/ppermute | solution.py:344
  6.5 2.2 %copy-start.1 = (bf16[1,128,2048]{2,1,0:T(8,128)(2,1)S(1)}, bf16[1,128,2048]{2,1,0:T(8,128)(2,1)}, u32[]{:S(2)}) copy-start(bf16[1,128,2048]{2,1,0:T(8,128)(2,1)} %grad.5) | copy-start | bytes 1572868
  6.5 7.7 %collective-permute-start = (bf16[2,8,64]{2,1,0:T(8,128)(2,1)S(1)}, bf16[2,8,64]{2,1,0:T(8,128)(2,1)S(1)}, u32[]{:S(2)}, u32[]{:S(2)}) collective-permute-start(bf16[2,8,64]{2,1,0:T(8,128)(2,1)S(1)} %slice.27), channel_id=1, source_target_pairs={{0,4},{4,8},{8,12},{12,16},{16,20},{20,24},{24,28},{28,0},{1,5},{5... | collective-permute-start | bytes 6152 | tf_op jit(solution)/shard_map/ppermute | solution.py:346
  14.9 3.7 %copy-start.2 = (bf16[1,128,4096]{2,1,0:T(8,128)(2,1)S(1)}, bf16[1,128,4096]{2,1,0:T(8,128)(2,1)}, u32[]{:S(2)}) copy-start(bf16[1,128,4096]{2,1,0:T(8,128)(2,1)} %tokens.1) | copy-start | bytes 3145732
  14.9 3.7 %collective-permute-start.2 = (f32[16,128]{1,0:T(8,128)S(1)}, f32[16,128]{1,0:T(8,128)S(1)}, u32[]{:S(2)}, u32[]{:S(2)}) collective-permute-start(f32[16,128]{1,0:T(8,128)S(1)} %get-tuple-element.48), channel_id=1, source_target_pairs={{0,28},{4,0},{8,4},{12,8},{16,12},{20,16},{24,20},{28,24},{1,29},{... | collective-permute-start | bytes 24584 | tf_op jit(solution)/shard_map/ppermute | solution.py:369
  18.9 1.4 %collective-permute-start.3 = (bf16[4,24,768]{2,1,0:T(8,128)(2,1)S(1)}, bf16[4,24,768]{2,1,0:T(8,128)(2,1)S(1)}, u32[]{:S(2)}, u32[]{:S(2)}) collective-permute-start(bf16[4,24,768]{2,1,0:T(8,128)(2,1)S(1)} %convert_element_type.49), channel_id=1, source_target_pairs={{0,1},{1,0},{2,3},{3,2},{4,5},{5,4},{6,7},{7,6},{8,9},{9,8},{10,11... | collective-permute-start | bytes 442376 | tf_op jit(solution)/shard_map/ppermute | solution.py:312
  20.4 4.5 %collective-permute-start.4 = (bf16[24,768]{1,0:T(8,128)(2,1)S(1)}, bf16[24,768]{1,0:T(8,128)(2,1)S(1)}, u32[]{:S(2)}, u32[]{:S(2)}) collective-permute-start(bf16[24,768]{1,0:T(8,128)(2,1)S(1)} %get-tuple-element.58), channel_id=1, source_target_pairs={{0,7},{1,6},{2,5},{3,4},{4,3},{5,2},{6,1},{7,0},{8,15},{9,14},{10,... | collective-permute-start | bytes 110600 | tf_op jit(solution)/shard_map/ppermute | solution.py:312
  21.3 4.5 %collective-permute-start.6 = (bf16[24,768]{1,0:T(8,128)(2,1)S(1)}, bf16[24,768]{1,0:T(8,128)(2,1)S(1)}, u32[]{:S(2)}, u32[]{:S(2)}) collective-permute-start(bf16[24,768]{1,0:T(8,128)(2,1)S(1)} %get-tuple-element.59), channel_id=1, source_target_pairs={{0,2},{1,3},{2,0},{3,1},{4,6},{5,7},{6,4},{7,5},{8,10},{9,11},{10,... | collective-permute-start | bytes 110600 | tf_op jit(solution)/shard_map/ppermute | solution.py:312
  22.0 3.8 %collective-permute-start.5 = (bf16[24,768]{1,0:T(8,128)(2,1)S(1)}, bf16[24,768]{1,0:T(8,128)(2,1)S(1)}, u32[]{:S(2)}, u32[]{:S(2)}) collective-permute-start(bf16[24,768]{1,0:T(8,128)(2,1)S(1)} %get-tuple-element.60), channel_id=1, source_target_pairs={{0,5},{1,4},{2,7},{3,6},{4,1},{5,0},{6,3},{7,2},{8,13},{9,12},{10,... | collective-permute-start | bytes 110600 | tf_op jit(solution)/shard_map/ppermute | solution.py:312
  25.9 5.0 %collective-permute-start.9 = (bf16[24,768]{1,0:T(8,128)(2,1)S(1)}, bf16[24,768]{1,0:T(8,128)(2,1)S(1)}, u32[]{:S(2)}, u32[]{:S(2)}) collective-permute-start(bf16[24,768]{1,0:T(8,128)(2,1)S(1)} %fusion.4), channel_id=1, source_target_pairs={{0,16},{1,17},{2,18},{3,19},{4,20},{5,21},{6,22},{7,23},{8,24},{9,... | collective-permute-start | bytes 110600 | tf_op jit(solution)/shard_map/ppermute | solution.py:312
  28.1 5.8 %collective-permute-start.8 = (bf16[24,768]{1,0:T(8,128)(2,1)S(1)}, bf16[24,768]{1,0:T(8,128)(2,1)S(1)}, u32[]{:S(2)}, u32[]{:S(2)}) collective-permute-start(bf16[24,768]{1,0:T(8,128)(2,1)S(1)} %fusion.4), channel_id=1, source_target_pairs={{0,24},{1,25},{2,26},{3,27},{4,28},{5,29},{6,30},{7,31},{8,16},{9,... | collective-permute-start | bytes 110600 | tf_op jit(solution)/shard_map/ppermute | solution.py:312
  30.4 4.0 %collective-permute-start.7 = (bf16[24,768]{1,0:T(8,128)(2,1)S(1)}, bf16[24,768]{1,0:T(8,128)(2,1)S(1)}, u32[]{:S(2)}, u32[]{:S(2)}) collective-permute-start(bf16[24,768]{1,0:T(8,128)(2,1)S(1)} %fusion.4), channel_id=1, source_target_pairs={{0,8},{1,9},{2,10},{3,11},{4,12},{5,13},{6,14},{7,15},{8,0},{9,1},... | collective-permute-start | bytes 110600 | tf_op jit(solution)/shard_map/ppermute | solution.py:312
  34.4 4.5 %collective-permute-start.15 = (bf16[24,768]{1,0:T(8,128)(2,1)S(1)}, bf16[24,768]{1,0:T(8,128)(2,1)S(1)}, u32[]{:S(2)}, u32[]{:S(2)}) collective-permute-start(bf16[24,768]{1,0:T(8,128)(2,1)S(1)} %add_convert_fusion.a), channel_id=1, source_target_pairs={{0,7},{1,6},{2,5},{3,4},{4,3},{5,2},{6,1},{7,0},{8,15},{9,14},{10,... | collective-permute-start | bytes 110600 | tf_op jit(solution)/shard_map/ppermute | solution.py:312
  34.4 4.7 %collective-permute-start.13 = (bf16[24,768]{1,0:T(8,128)(2,1)S(1)}, bf16[24,768]{1,0:T(8,128)(2,1)S(1)}, u32[]{:S(2)}, u32[]{:S(2)}) collective-permute-start(bf16[24,768]{1,0:T(8,128)(2,1)S(1)} %add_convert_fusion.a), channel_id=1, source_target_pairs={{0,2},{1,3},{2,0},{3,1},{4,6},{5,7},{6,4},{7,5},{8,10},{9,11},{10,... | collective-permute-start | bytes 110600 | tf_op jit(solution)/shard_map/ppermute | solution.py:312
  36.0 3.4 %collective-permute-start.11 = (bf16[24,768]{1,0:T(8,128)(2,1)S(1)}, bf16[24,768]{1,0:T(8,128)(2,1)S(1)}, u32[]{:S(2)}, u32[]{:S(2)}) collective-permute-start(bf16[24,768]{1,0:T(8,128)(2,1)S(1)} %add_convert_fusion.a), channel_id=1, source_target_pairs={{0,5},{1,4},{2,7},{3,6},{4,1},{5,0},{6,3},{7,2},{8,13},{9,12},{10,... | collective-permute-start | bytes 110600 | tf_op jit(solution)/shard_map/ppermute | solution.py:312
  37.4 2.4 %collective-permute-start.10 = (bf16[24,768]{1,0:T(8,128)(2,1)S(1)}, bf16[24,768]{1,0:T(8,128)(2,1)S(1)}, u32[]{:S(2)}, u32[]{:S(2)}) collective-permute-start(bf16[24,768]{1,0:T(8,128)(2,1)S(1)} %add_convert_fusion.a), channel_id=1, source_target_pairs={{0,1},{1,0},{2,3},{3,2},{4,5},{5,4},{6,7},{7,6},{8,9},{9,8},{10,11... | collective-permute-start | bytes 110600 | tf_op jit(solution)/shard_map/ppermute | solution.py:312
  38.8 1.2 %collective-permute-start.16 = (bf16[24,768]{1,0:T(8,128)(2,1)S(1)}, bf16[24,768]{1,0:T(8,128)(2,1)S(1)}, u32[]{:S(2)}, u32[]{:S(2)}) collective-permute-start(bf16[24,768]{1,0:T(8,128)(2,1)S(1)} %collective-permute-done.15.d), channel_id=1, source_target_pairs={{0,1},{1,0},{2,3},{3,2},{4,5},{5,4},{6,7},{7,6},{8,9},{9,8},{10,11... | collective-permute-start | bytes 110600 | tf_op jit(solution)/shard_map/ppermute | solution.py:312
  39.1 1.2 %collective-permute-start.14 = (bf16[24,768]{1,0:T(8,128)(2,1)S(1)}, bf16[24,768]{1,0:T(8,128)(2,1)S(1)}, u32[]{:S(2)}, u32[]{:S(2)}) collective-permute-start(bf16[24,768]{1,0:T(8,128)(2,1)S(1)} %collective-permute-done.13.c), channel_id=1, source_target_pairs={{0,1},{1,0},{2,3},{3,2},{4,5},{5,4},{6,7},{7,6},{8,9},{9,8},{10,11... | collective-permute-start | bytes 110600 | tf_op jit(solution)/shard_map/ppermute | solution.py:312
  39.4 1.2 %collective-permute-start.12 = (bf16[24,768]{1,0:T(8,128)(2,1)S(1)}, bf16[24,768]{1,0:T(8,128)(2,1)S(1)}, u32[]{:S(2)}, u32[]{:S(2)}) collective-permute-start(bf16[24,768]{1,0:T(8,128)(2,1)S(1)} %collective-permute-done.11.b), channel_id=1, source_target_pairs={{0,1},{1,0},{2,3},{3,2},{4,5},{5,4},{6,7},{7,6},{8,9},{9,8},{10,11... | collective-permute-start | bytes 110600 | tf_op jit(solution)/shard_map/ppermute | solution.py:312

commit v14 on v13

--- a/solution.py
+++ b/solution.py
@@ -267,9 +267,9 @@
         u = ADAPTER_SCALE * u
         slot = quarter ^ c
         keep[slot, :, :up_step] = jnp.where(first, u[:, :up_step], u[:, up_step:])
-        send[slot, :, :up_step] = jnp.where(first, u[:, up_step:], u[:, :up_step])
+        send[slot, :, :up_step] = jnp.where(first, u[:, up_step:], u[:, :up_step]).astype(BF)
         keep[slot, :, up_step:] = jnp.where(first, d[:, :down_step], d[:, down_step:])
-        send[slot, :, up_step:] = jnp.where(first, d[:, down_step:], d[:, :down_step])
+        send[slot, :, up_step:] = jnp.where(first, d[:, down_step:], d[:, :down_step]).astype(BF)
 
 
 def spread(pieces, own, down_out, up_out):
@@ -315,7 +315,7 @@
 def total_sum(keep, send, seqs, dps):
     total = seqs * dps
     partner = {1: dps | 1, 2: 2, 3: dps | 3}
-    keep = keep + swap(send.astype(BF), 1, total).astype(F32)
+    keep = keep + swap(send, 1, total).astype(F32)
     got = [swap(keep[s].astype(BF), partner[s], total).astype(F32) for s in (1, 2, 3)]
     own = keep[0] + got[2] + got[0] + got[1]
     bit = 2
@@ -373,7 +373,7 @@
     )
     columns = (width + tokens.shape[2]) // 8
     piece = sds((4, 24, columns), F32)
-    keep, send = call(down_kernel, [piece, piece], tokens, rank_plain, rank_near, rank_far, cross, up_plain, up_near, up_far)
+    keep, send = call(down_kernel, [piece, sds(piece.shape, BF)], tokens, rank_plain, rank_near, rank_far, cross, up_plain, up_near, up_far)
     mine, other = total_sum(keep, send, seqs, dps)
     outs = [sds((3, RANK, tokens.shape[2]), F32), sds((3, RANK, width), F32)]
     return tuple(call(last_spread, outs, *other, *call(first_spread, outs, *mine)))

time: 41.7 us -> 41.6 us (level)
  no operation moved by 1% of the time
where the time goes in v14:
time: 41.6 us; the launch traced here: 41.5 us
  starting transfers between devices  17.9 us (43%)
  waiting for transfers between devices  13.2 us (32%)
  Pallas kernels  6.73 us (16%)
  matrix products  1.6 us (4%)
  local copies, waits for them, and re-layouts  1.22 us (3%)
  between operations  0.76 us (2%)
    ppermute x14, starting transfers between devices, swap(): return lax.ppermute(x, AXES, [(i, i ^ bits) for i in range(total)])  11.6 us
    ppermute x14, waiting for transfers between devices, swap(): return lax.ppermute(x, AXES, [(i, i ^ bits) for i in range(total)])  9.99 us
    pallas_call x9, Pallas kernels, call(): pl.pallas_call(kernel, out_shape=outs, in_specs=[VMEM] * len(args), out_s...  6.73 us
    ppermute x1, starting transfers between devices, on_device(): frozen_kv = lax.ppermute(frozen[1:, 0, half:, half_width:], 'seq', forward)  2.99 us
    ppermute x1, waiting for transfers between devices, on_device(): low_kv = lax.ppermute(low_t[1:, :, half:], 'seq', forward)  2.23 us
    ppermute x1, starting transfers between devices, on_device(): cross = lax.ppermute(cross, 'seq', backward)  1.78 us
    dot_general x1, matrix products, on_device(): jnp.einsum('psw,gw->psg', down_weight, tokens[0], preferred_element_type=...  1.6 us
    ppermute x1, starting transfers between devices, on_device(): low_kv = lax.ppermute(low_t[1:, :, half:], 'seq', forward)  1.56 us
  transfers between devices with their start and end apart: 17, of which 12 were waited for; matrix products, arithmetic and copies ran while one was open for 4% of the time, Pallas kernels for 12%

profile of v14, /device:TPU:0, one launch (start us, length us, event | category | flops | bytes accessed | tf_op | source)
XLA Modules:
  0.0 41.5 jit_solution(14271082929543576269)
XLA Ops:
  0.7 1.1 %slice_bitcast_fusion = bf16[2,64,1024]{2,1,0:T(8,128)(2,1)S(1)} fusion(bf16[3,1,128,2048]{3,2,0,1:T(8,128)(2,1)} %bitcast.24), kind=kLoop, calls=%fused_computation.3 | loop fusion | bytes 524288 | tf_op jit(solution)/shard_map/squeeze | solution.py:344
  1.8 3.0 %collective-permute-start.1 = (bf16[2,64,1024]{2,1,0:T(8,128)(2,1)S(1)}, bf16[2,64,1024]{2,1,0:T(8,128)(2,1)S(1)}, u32[]{:S(2)}, u32[]{:S(2)}) collective-permute-start(bf16[2,64,1024]{2,1,0:T(8,128)(2,1)S(1)} %slice_bitcast_fusion), channel_id=1, source_target_pairs={{0,4},{4,8},{8,12},{12,16},{16,20},{20,24},{24,28},{28,0},{1,5},{5... | collective-permute-start | bytes 786440 | tf_op jit(solution)/shard_map/ppermute | solution.py:344
  4.8 1.6 %convolution_convert_fusion.low_t = bf16[3,8,128]{2,1,0:T(8,128)(2,1)S(1)} fusion(bf16[3,8,4096]{2,1,0:T(8,128)(2,1)S(1)} %copy-done, bf16[1,128,4096]{2,1,0:T(8,128)(2,1)} %tokens.1), kind=kOutput, calls=%fused_computation | convolution fusion | flops 25168896 | bytes 1251328 | tf_op jit(solution)/shard_map/psw,gw->psg/dot_general | solution.py:345
  6.5 1.6 %collective-permute-start = (bf16[2,8,64]{2,1,0:T(8,128)(2,1)S(1)}, bf16[2,8,64]{2,1,0:T(8,128)(2,1)S(1)}, u32[]{:S(2)}, u32[]{:S(2)}) collective-permute-start(bf16[2,8,64]{2,1,0:T(8,128)(2,1)S(1)} %slice.27), channel_id=1, source_target_pairs={{0,4},{4,8},{8,12},{12,16},{16,20},{20,24},{24,28},{28,0},{1,5},{5... | collective-permute-start | bytes 6152 | tf_op jit(solution)/shard_map/ppermute | solution.py:346
  8.0 0.6 %shard_map.68.projected = bf16[3,128,2048]{2,1,0:T(8,128)(2,1)S(1)} custom-call(bf16[3,1,128,2048]{3,2,1,0:T(8,128)(2,1)S(1)} %copy-done.4, bf16[3,8,128]{2,1,0:T(8,128)(2,1)S(1)} %convolution_convert_fusion.low_t, bf16[3,8,2048]{2,1,0:T(8,128)(2,1)S(1)} %copy-done.3), custom_call_target="tpu_custom_call" | custom-call | flops 1000000 | bytes 10000 | tf_op jit(solution)/shard_map/pallas_call | solution.py:301
  8.6 1.2 %shard_map.71 = (f32[24,1024]{1,0:T(8,128)S(1)}, f32[24,128]{1,0:T(8,128)S(1)}) custom-call(bf16[3,128,2048]{2,1,0:T(8,128)(2,1)S(1)} %shard_map.68.projected, bf16[1,128,2048]{2,1,0:T(8,128)(2,1)S(1)} %copy-done.1, bf16[3,8,128]{2,1,0:T(8,128)(2,1)S(1)} %convolution_convert_fusion.low_t, bf16[3,8,2048]{2,1,0:T(8,128)(2,1)S(1)} %copy-done.3), custom_call_target="tpu_custom_call" | custom-call | flops 1000000 | bytes 10000 | tf_op jit(solution)/shard_map/pallas_call | solution.py:301
  9.9 1.6 %shard_map.70 = (f32[24,1024]{1,0:T(8,128)S(1)}, f32[24,128]{1,0:T(8,128)S(1)}) custom-call(bf16[3,128,2048]{2,1,0:T(8,128)(2,1)S(1)} %shard_map.68.projected, bf16[1,128,2048]{2,1,0:T(8,128)(2,1)S(1)} %copy-done.1, bf16[3,8,128]{2,1,0:T(8,128)(2,1)S(1)} %convolution_convert_fusion.low_t, bf16[3,8,2048]{2,1,0:T(8,128)(2,1)S(1)} %copy-done.3), custom_call_target="tpu_custom_call" | custom-call | flops 1000000 | bytes 10000 | tf_op jit(solution)/shard_map/pallas_call | solution.py:301
  11.5 0.5 %shard_map.69 = (bf16[4,128,256]{2,1,0:T(8,128)(2,1)S(1)}, bf16[4,128,256]{2,1,0:T(8,128)(2,1)S(1)}, f32[4,64,128]{2,1,0:T(8,128)S(1)}, f32[4,64,128]{2,1,0:T(8,...) custom-call(bf16[3,128,2048]{2,1,0:T(8,128)(2,1)S(1)} %shard_map.68., ...), custom_call_target="tpu_custom_call" | custom-call | flops 1000000 | bytes 10000 | tf_op jit(solution)/shard_map/pallas_call | solution.py:301
  12.0 2.2 %collective-permute-done.low_kv = bf16[2,8,64]{2,1,0:T(8,128)(2,1)S(1)} collective-permute-done((bf16[2,8,64]{2,1,0:T(8,128)(2,1)S(1)}, bf16[2,8,64]{2,1,0:T(8,128)(2,1)S(1)}, u32[]{:S(2)}, u32[]{:S(2)}) %collective-permute-start) | collective-permute-done | bytes 2080 | tf_op jit(solution)/shard_map/ppermute | solution.py:346
  14.2 0.7 %shard_map.72 = (f32[16,128]{1,0:T(8,128)S(1)}, bf16[64,1024]{1,0:T(8,128)(2,1)S(1)}, bf16[4,64,128]{2,1,0:T(8,128)(2,1)S(1)}, bf16[4,64,128]{2,1,0:T(8,128)(2,1...) custom-call(bf16[2,64,1024]{2,1,0:T(8,128)(2,1)S(1)} %collective-permute-done.1.frozen_kv, ...), custom_call_target="tpu_custom_call" | custom-call | flops 1000000 | bytes 10000 | tf_op jit(solution)/shard_map/pallas_call | solution.py:301
  14.9 1.8 %collective-permute-start.2 = (f32[16,128]{1,0:T(8,128)S(1)}, f32[16,128]{1,0:T(8,128)S(1)}, u32[]{:S(2)}, u32[]{:S(2)}) collective-permute-start(f32[16,128]{1,0:T(8,128)S(1)} %get-tuple-element.48), channel_id=1, source_target_pairs={{0,28},{4,0},{8,4},{12,8},{16,12},{20,16},{24,20},{28,24},{1,29},{... | collective-permute-start | bytes 24584 | tf_op jit(solution)/shard_map/ppermute | solution.py:369
  16.7 0.9 %shard_map.73 = (f32[24,1024]{1,0:T(8,128)S(1)}, f32[24,128]{1,0:T(8,128)S(1)}) custom-call(bf16[3,128,2048]{2,1,0:T(8,128)(2,1)S(1)} %shard_map.68.projected, bf16[2,8,64]{2,1,0:T(8,128)(2,1)S(1)} %collective-permute-done.low_kv, bf16[3,8,128]{2,1,0:T(8,128)(2,1)S(1)} %convolution_convert_fusion.low_t, bf16[3,8,2048]{2,1,0:T(8,128)(2,1)S(1)} %copy-done.3, ...), custom_call_target="tpu_custom_call" | custom-call | flops 1000000 | bytes 10000 | tf_op jit(solution)/shard_map/pallas_call | solution.py:301
  17.6 1.0 %collective-permute-done.2.cross = f32[16,128]{1,0:T(8,128)S(1)} collective-permute-done((f32[16,128]{1,0:T(8,128)S(1)}, f32[16,128]{1,0:T(8,128)S(1)}, u32[]{:S(2)}, u32[]{:S(2)}) %collective-permute-start.2) | collective-permute-done | bytes 8224 | tf_op jit(solution)/shard_map/ppermute | solution.py:369
  18.6 0.3 shard_map.74
  18.9 1.4 %collective-permute-done.3 = bf16[4,24,768]{2,1,0:T(8,128)(2,1)S(1)} collective-permute-done((bf16[4,24,768]{2,1,0:T(8,128)(2,1)S(1)}, bf16[4,24,768]{2,1,0:T(8,128)(2,1)S(1)}, u32[]{:S(2)}, u32[]{:S(2)}) %collective-permute-start.3) | collective-permute-done | bytes 147488 | tf_op jit(solution)/shard_map/ppermute | solution.py:312
  20.4 0.9 %collective-permute-start.4 = (bf16[24,768]{1,0:T(8,128)(2,1)S(1)}, bf16[24,768]{1,0:T(8,128)(2,1)S(1)}, u32[]{:S(2)}, u32[]{:S(2)}) collective-permute-start(bf16[24,768]{1,0:T(8,128)(2,1)S(1)} %get-tuple-element.58), channel_id=1, source_target_pairs={{0,7},{1,6},{2,5},{3,4},{4,3},{5,2},{6,1},{7,0},{8,15},{9,14},{10,... | collective-permute-start | bytes 110600 | tf_op jit(solution)/shard_map/ppermute | solution.py:312
  21.3 0.7 %collective-permute-start.6 = (bf16[24,768]{1,0:T(8,128)(2,1)S(1)}, bf16[24,768]{1,0:T(8,128)(2,1)S(1)}, u32[]{:S(2)}, u32[]{:S(2)}) collective-permute-start(bf16[24,768]{1,0:T(8,128)(2,1)S(1)} %get-tuple-element.59), channel_id=1, source_target_pairs={{0,2},{1,3},{2,0},{3,1},{4,6},{5,7},{6,4},{7,5},{8,10},{9,11},{10,... | collective-permute-start | bytes 110600 | tf_op jit(solution)/shard_map/ppermute | solution.py:312
  22.0 1.3 %collective-permute-start.5 = (bf16[24,768]{1,0:T(8,128)(2,1)S(1)}, bf16[24,768]{1,0:T(8,128)(2,1)S(1)}, u32[]{:S(2)}, u32[]{:S(2)}) collective-permute-start(bf16[24,768]{1,0:T(8,128)(2,1)S(1)} %get-tuple-element.60), channel_id=1, source_target_pairs={{0,5},{1,4},{2,7},{3,6},{4,1},{5,0},{6,3},{7,2},{8,13},{9,12},{10,... | collective-permute-start | bytes 110600 | tf_op jit(solution)/shard_map/ppermute | solution.py:312
  23.4 1.5 %collective-permute-done.4 = bf16[24,768]{1,0:T(8,128)(2,1)S(1)} collective-permute-done((bf16[24,768]{1,0:T(8,128)(2,1)S(1)}, bf16[24,768]{1,0:T(8,128)(2,1)S(1)}, u32[]{:S(2)}, u32[]{:S(2)}) %collective-permute-start.4) | collective-permute-done | bytes 36896 | tf_op jit(solution)/shard_map/ppermute | solution.py:312
  24.9 1.0 %collective-permute-done.6 = bf16[24,768]{1,0:T(8,128)(2,1)S(1)} collective-permute-done((bf16[24,768]{1,0:T(8,128)(2,1)S(1)}, bf16[24,768]{1,0:T(8,128)(2,1)S(1)}, u32[]{:S(2)}, u32[]{:S(2)}) %collective-permute-start.6) | collective-permute-done | bytes 36896 | tf_op jit(solution)/shard_map/ppermute | solution.py:312
  25.9 2.2 %collective-permute-start.9 = (bf16[24,768]{1,0:T(8,128)(2,1)S(1)}, bf16[24,768]{1,0:T(8,128)(2,1)S(1)}, u32[]{:S(2)}, u32[]{:S(2)}) collective-permute-start(bf16[24,768]{1,0:T(8,128)(2,1)S(1)} %fusion.4), channel_id=1, source_target_pairs={{0,16},{1,17},{2,18},{3,19},{4,20},{5,21},{6,22},{7,23},{8,24},{9,... | collective-permute-start | bytes 110600 | tf_op jit(solution)/shard_map/ppermute | solution.py:312
  28.0 2.3 %collective-permute-start.8 = (bf16[24,768]{1,0:T(8,128)(2,1)S(1)}, bf16[24,768]{1,0:T(8,128)(2,1)S(1)}, u32[]{:S(2)}, u32[]{:S(2)}) collective-permute-start(bf16[24,768]{1,0:T(8,128)(2,1)S(1)} %fusion.4), channel_id=1, source_target_pairs={{0,24},{1,25},{2,26},{3,27},{4,28},{5,29},{6,30},{7,31},{8,16},{9,... | collective-permute-start | bytes 110600 | tf_op jit(solution)/shard_map/ppermute | solution.py:312
  30.4 0.5 %collective-permute-start.7 = (bf16[24,768]{1,0:T(8,128)(2,1)S(1)}, bf16[24,768]{1,0:T(8,128)(2,1)S(1)}, u32[]{:S(2)}, u32[]{:S(2)}) collective-permute-start(bf16[24,768]{1,0:T(8,128)(2,1)S(1)} %fusion.4), channel_id=1, source_target_pairs={{0,8},{1,9},{2,10},{3,11},{4,12},{5,13},{6,14},{7,15},{8,0},{9,1},... | collective-permute-start | bytes 110600 | tf_op jit(solution)/shard_map/ppermute | solution.py:312
  30.8 3.0 %collective-permute-done.8 = bf16[24,768]{1,0:T(8,128)(2,1)S(1)} collective-permute-done((bf16[24,768]{1,0:T(8,128)(2,1)S(1)}, bf16[24,768]{1,0:T(8,128)(2,1)S(1)}, u32[]{:S(2)}, u32[]{:S(2)}) %collective-permute-start.8) | collective-permute-done | bytes 36896 | tf_op jit(solution)/shard_map/ppermute | solution.py:312
  33.8 0.5 %collective-permute-done.7 = bf16[24,768]{1,0:T(8,128)(2,1)S(1)} collective-permute-done((bf16[24,768]{1,0:T(8,128)(2,1)S(1)}, bf16[24,768]{1,0:T(8,128)(2,1)S(1)}, u32[]{:S(2)}, u32[]{:S(2)}) %collective-permute-start.7) | collective-permute-done | bytes 36896 | tf_op jit(solution)/shard_map/ppermute | solution.py:312
  34.4 1.6 %collective-permute-start.13 = (bf16[24,768]{1,0:T(8,128)(2,1)S(1)}, bf16[24,768]{1,0:T(8,128)(2,1)S(1)}, u32[]{:S(2)}, u32[]{:S(2)}) collective-permute-start(bf16[24,768]{1,0:T(8,128)(2,1)S(1)} %add_convert_fusion.a), channel_id=1, source_target_pairs={{0,2},{1,3},{2,0},{3,1},{4,6},{5,7},{6,4},{7,5},{8,10},{9,11},{10,... | collective-permute-start | bytes 110600 | tf_op jit(solution)/shard_map/ppermute | solution.py:312
  36.0 1.3 %collective-permute-start.11 = (bf16[24,768]{1,0:T(8,128)(2,1)S(1)}, bf16[24,768]{1,0:T(8,128)(2,1)S(1)}, u32[]{:S(2)}, u32[]{:S(2)}) collective-permute-start(bf16[24,768]{1,0:T(8,128)(2,1)S(1)} %add_convert_fusion.a), channel_id=1, source_target_pairs={{0,5},{1,4},{2,7},{3,6},{4,1},{5,0},{6,3},{7,2},{8,13},{9,12},{10,... | collective-permute-start | bytes 110600 | tf_op jit(solution)/shard_map/ppermute | solution.py:312
  37.3 1.5 %collective-permute-done.15.d = bf16[24,768]{1,0:T(8,128)(2,1)S(1)} collective-permute-done((bf16[24,768]{1,0:T(8,128)(2,1)S(1)}, bf16[24,768]{1,0:T(8,128)(2,1)S(1)}, u32[]{:S(2)}, u32[]{:S(2)}) %collective-permute-start.15) | collective-permute-done | bytes 36896 | tf_op jit(solution)/shard_map/ppermute | solution.py:312
  38.8 0.3 collective-permute-done.13.c
  39.4 0.3 collective-permute-start.12
  40.0 0.3 collective-permute-done.14.c
  40.6 0.9 %shard_map.76 = (f32[3,8,4096]{2,1,0:T(8,128)}, f32[3,8,2048]{2,1,0:T(8,128)}) custom-call(bf16[24,768]{1,0:T(8,128)(2,1)S(1)} %collective-permute-done.10.a, bf16[24,768]{1,0:T(8,128)(2,1)S(1)} %collective-permute-done.12.b, bf16[24,768]{1,0:T(8,128)(2,1)S(1)} %collective-permute-done.14.c, bf16[24,768]{1,0:T(8,128)(2,1)S(1)} %collective-permute-done.16.d, ...), custom_call_target="tpu_custom_call" | custom-call | flops 1000000 | bytes 10000 | tf_op jit(solution)/shard_map/pallas_call | solution.py:301
  (28 shorter events, 1.2 us)
Async XLA Ops:
  0.6 4.1 %copy-start = (bf16[3,8,4096]{2,1,0:T(8,128)(2,1)S(1)}, bf16[3,8,4096]{2,1,0:T(8,128)(2,1)}, u32[]{:S(2)}) copy-start(bf16[3,8,4096]{2,1,0:T(8,128)(2,1)} %param.8) | copy-start | bytes 589828
  0.6 7.4 %copy-start.4 = (bf16[3,1,128,2048]{3,2,1,0:T(8,128)(2,1)S(1)}, bf16[3,1,128,2048]{3,2,1,0:T(8,128)(2,1)}, u32[]{:S(2)}) copy-start(bf16[3,1,128,2048]{3,2,1,0:T(8,128)(2,1)} %frozen.1) | copy-start | bytes 4718596
  0.7 7.4 %copy-start.3 = (bf16[3,8,2048]{2,1,0:T(8,128)(2,1)S(1)}, bf16[3,8,2048]{2,1,0:T(8,128)(2,1)}, u32[]{:S(2)}) copy-start(bf16[3,8,2048]{2,1,0:T(8,128)(2,1)} %up.11) | copy-start | bytes 294916
  1.8 12.4 %collective-permute-start.1 = (bf16[2,64,1024]{2,1,0:T(8,128)(2,1)S(1)}, bf16[2,64,1024]{2,1,0:T(8,128)(2,1)S(1)}, u32[]{:S(2)}, u32[]{:S(2)}) collective-permute-start(bf16[2,64,1024]{2,1,0:T(8,128)(2,1)S(1)} %slice_bitcast_fusion), channel_id=1, source_target_pairs={{0,4},{4,8},{8,12},{12,16},{16,20},{20,24},{24,28},{28,0},{1,5},{5... | collective-permute-start | bytes 786440 | tf_op jit(solution)/shard_map/ppermute | solution.py:344
  6.5 2.2 %copy-start.1 = (bf16[1,128,2048]{2,1,0:T(8,128)(2,1)S(1)}, bf16[1,128,2048]{2,1,0:T(8,128)(2,1)}, u32[]{:S(2)}) copy-start(bf16[1,128,2048]{2,1,0:T(8,128)(2,1)} %grad.5) | copy-start | bytes 1572868
  6.5 7.7 %collective-permute-start = (bf16[2,8,64]{2,1,0:T(8,128)(2,1)S(1)}, bf16[2,8,64]{2,1,0:T(8,128)(2,1)S(1)}, u32[]{:S(2)}, u32[]{:S(2)}) collective-permute-start(bf16[2,8,64]{2,1,0:T(8,128)(2,1)S(1)} %slice.27), channel_id=1, source_target_pairs={{0,4},{4,8},{8,12},{12,16},{16,20},{20,24},{24,28},{28,0},{1,5},{5... | collective-permute-start | bytes 6152 | tf_op jit(solution)/shard_map/ppermute | solution.py:346
  14.9 3.7 %copy-start.2 = (bf16[1,128,4096]{2,1,0:T(8,128)(2,1)S(1)}, bf16[1,128,4096]{2,1,0:T(8,128)(2,1)}, u32[]{:S(2)}) copy-start(bf16[1,128,4096]{2,1,0:T(8,128)(2,1)} %tokens.1) | copy-start | bytes 3145732
  14.9 3.7 %collective-permute-start.2 = (f32[16,128]{1,0:T(8,128)S(1)}, f32[16,128]{1,0:T(8,128)S(1)}, u32[]{:S(2)}, u32[]{:S(2)}) collective-permute-start(f32[16,128]{1,0:T(8,128)S(1)} %get-tuple-element.48), channel_id=1, source_target_pairs={{0,28},{4,0},{8,4},{12,8},{16,12},{20,16},{24,20},{28,24},{1,29},{... | collective-permute-start | bytes 24584 | tf_op jit(solution)/shard_map/ppermute | solution.py:369
  18.9 1.4 %collective-permute-start.3 = (bf16[4,24,768]{2,1,0:T(8,128)(2,1)S(1)}, bf16[4,24,768]{2,1,0:T(8,128)(2,1)S(1)}, u32[]{:S(2)}, u32[]{:S(2)}) collective-permute-start(bf16[4,24,768]{2,1,0:T(8,128)(2,1)S(1)} %get-tuple-element.53), channel_id=1, source_target_pairs={{0,1},{1,0},{2,3},{3,2},{4,5},{5,4},{6,7},{7,6},{8,9},{9,8},{10,11... | collective-permute-start | bytes 442376 | tf_op jit(solution)/shard_map/ppermute | solution.py:312
  20.4 4.5 %collective-permute-start.4 = (bf16[24,768]{1,0:T(8,128)(2,1)S(1)}, bf16[24,768]{1,0:T(8,128)(2,1)S(1)}, u32[]{:S(2)}, u32[]{:S(2)}) collective-permute-start(bf16[24,768]{1,0:T(8,128)(2,1)S(1)} %get-tuple-element.58), channel_id=1, source_target_pairs={{0,7},{1,6},{2,5},{3,4},{4,3},{5,2},{6,1},{7,0},{8,15},{9,14},{10,... | collective-permute-start | bytes 110600 | tf_op jit(solution)/shard_map/ppermute | solution.py:312
  21.3 4.5 %collective-permute-start.6 = (bf16[24,768]{1,0:T(8,128)(2,1)S(1)}, bf16[24,768]{1,0:T(8,128)(2,1)S(1)}, u32[]{:S(2)}, u32[]{:S(2)}) collective-permute-start(bf16[24,768]{1,0:T(8,128)(2,1)S(1)} %get-tuple-element.59), channel_id=1, source_target_pairs={{0,2},{1,3},{2,0},{3,1},{4,6},{5,7},{6,4},{7,5},{8,10},{9,11},{10,... | collective-permute-start | bytes 110600 | tf_op jit(solution)/shard_map/ppermute | solution.py:312
  22.0 3.8 %collective-permute-start.5 = (bf16[24,768]{1,0:T(8,128)(2,1)S(1)}, bf16[24,768]{1,0:T(8,128)(2,1)S(1)}, u32[]{:S(2)}, u32[]{:S(2)}) collective-permute-start(bf16[24,768]{1,0:T(8,128)(2,1)S(1)} %get-tuple-element.60), channel_id=1, source_target_pairs={{0,5},{1,4},{2,7},{3,6},{4,1},{5,0},{6,3},{7,2},{8,13},{9,12},{10,... | collective-permute-start | bytes 110600 | tf_op jit(solution)/shard_map/ppermute | solution.py:312
  25.9 5.0 %collective-permute-start.9 = (bf16[24,768]{1,0:T(8,128)(2,1)S(1)}, bf16[24,768]{1,0:T(8,128)(2,1)S(1)}, u32[]{:S(2)}, u32[]{:S(2)}) collective-permute-start(bf16[24,768]{1,0:T(8,128)(2,1)S(1)} %fusion.4), channel_id=1, source_target_pairs={{0,16},{1,17},{2,18},{3,19},{4,20},{5,21},{6,22},{7,23},{8,24},{9,... | collective-permute-start | bytes 110600 | tf_op jit(solution)/shard_map/ppermute | solution.py:312
  28.0 5.8 %collective-permute-start.8 = (bf16[24,768]{1,0:T(8,128)(2,1)S(1)}, bf16[24,768]{1,0:T(8,128)(2,1)S(1)}, u32[]{:S(2)}, u32[]{:S(2)}) collective-permute-start(bf16[24,768]{1,0:T(8,128)(2,1)S(1)} %fusion.4), channel_id=1, source_target_pairs={{0,24},{1,25},{2,26},{3,27},{4,28},{5,29},{6,30},{7,31},{8,16},{9,... | collective-permute-start | bytes 110600 | tf_op jit(solution)/shard_map/ppermute | solution.py:312
  30.4 4.0 %collective-permute-start.7 = (bf16[24,768]{1,0:T(8,128)(2,1)S(1)}, bf16[24,768]{1,0:T(8,128)(2,1)S(1)}, u32[]{:S(2)}, u32[]{:S(2)}) collective-permute-start(bf16[24,768]{1,0:T(8,128)(2,1)S(1)} %fusion.4), channel_id=1, source_target_pairs={{0,8},{1,9},{2,10},{3,11},{4,12},{5,13},{6,14},{7,15},{8,0},{9,1},... | collective-permute-start | bytes 110600 | tf_op jit(solution)/shard_map/ppermute | solution.py:312
  34.3 4.5 %collective-permute-start.15 = (bf16[24,768]{1,0:T(8,128)(2,1)S(1)}, bf16[24,768]{1,0:T(8,128)(2,1)S(1)}, u32[]{:S(2)}, u32[]{:S(2)}) collective-permute-start(bf16[24,768]{1,0:T(8,128)(2,1)S(1)} %add_convert_fusion.a), channel_id=1, source_target_pairs={{0,7},{1,6},{2,5},{3,4},{4,3},{5,2},{6,1},{7,0},{8,15},{9,14},{10,... | collective-permute-start | bytes 110600 | tf_op jit(solution)/shard_map/ppermute | solution.py:312
  34.4 4.7 %collective-permute-start.13 = (bf16[24,768]{1,0:T(8,128)(2,1)S(1)}, bf16[24,768]{1,0:T(8,128)(2,1)S(1)}, u32[]{:S(2)}, u32[]{:S(2)}) collective-permute-start(bf16[24,768]{1,0:T(8,128)(2,1)S(1)} %add_convert_fusion.a), channel_id=1, source_target_pairs={{0,2},{1,3},{2,0},{3,1},{4,6},{5,7},{6,4},{7,5},{8,10},{9,11},{10,... | collective-permute-start | bytes 110600 | tf_op jit(solution)/shard_map/ppermute | solution.py:312
  36.0 3.4 %collective-permute-start.11 = (bf16[24,768]{1,0:T(8,128)(2,1)S(1)}, bf16[24,768]{1,0:T(8,128)(2,1)S(1)}, u32[]{:S(2)}, u32[]{:S(2)}) collective-permute-start(bf16[24,768]{1,0:T(8,128)(2,1)S(1)} %add_convert_fusion.a), channel_id=1, source_target_pairs={{0,5},{1,4},{2,7},{3,6},{4,1},{5,0},{6,3},{7,2},{8,13},{9,12},{10,... | collective-permute-start | bytes 110600 | tf_op jit(solution)/shard_map/ppermute | solution.py:312
  37.3 2.4 %collective-permute-start.10 = (bf16[24,768]{1,0:T(8,128)(2,1)S(1)}, bf16[24,768]{1,0:T(8,128)(2,1)S(1)}, u32[]{:S(2)}, u32[]{:S(2)}) collective-permute-start(bf16[24,768]{1,0:T(8,128)(2,1)S(1)} %add_convert_fusion.a), channel_id=1, source_target_pairs={{0,1},{1,0},{2,3},{3,2},{4,5},{5,4},{6,7},{7,6},{8,9},{9,8},{10,11... | collective-permute-start | bytes 110600 | tf_op jit(solution)/shard_map/ppermute | solution.py:312
  38.8 1.2 %collective-permute-start.16 = (bf16[24,768]{1,0:T(8,128)(2,1)S(1)}, bf16[24,768]{1,0:T(8,128)(2,1)S(1)}, u32[]{:S(2)}, u32[]{:S(2)}) collective-permute-start(bf16[24,768]{1,0:T(8,128)(2,1)S(1)} %collective-permute-done.15.d), channel_id=1, source_target_pairs={{0,1},{1,0},{2,3},{3,2},{4,5},{5,4},{6,7},{7,6},{8,9},{9,8},{10,11... | collective-permute-start | bytes 110600 | tf_op jit(solution)/shard_map/ppermute | solution.py:312
  39.1 1.2 %collective-permute-start.14 = (bf16[24,768]{1,0:T(8,128)(2,1)S(1)}, bf16[24,768]{1,0:T(8,128)(2,1)S(1)}, u32[]{:S(2)}, u32[]{:S(2)}) collective-permute-start(bf16[24,768]{1,0:T(8,128)(2,1)S(1)} %collective-permute-done.13.c), channel_id=1, source_target_pairs={{0,1},{1,0},{2,3},{3,2},{4,5},{5,4},{6,7},{7,6},{8,9},{9,8},{10,11... | collective-permute-start | bytes 110600 | tf_op jit(solution)/shard_map/ppermute | solution.py:312
  39.4 1.2 %collective-permute-start.12 = (bf16[24,768]{1,0:T(8,128)(2,1)S(1)}, bf16[24,768]{1,0:T(8,128)(2,1)S(1)}, u32[]{:S(2)}, u32[]{:S(2)}) collective-permute-start(bf16[24,768]{1,0:T(8,128)(2,1)S(1)} %collective-permute-done.11.b), channel_id=1, source_target_pairs={{0,1},{1,0},{2,3},{3,2},{4,5},{5,4},{6,7},{7,6},{8,9},{9,8},{10,11... | collective-permute-start | bytes 110600 | tf_op jit(solution)/shard_map/ppermute | solution.py:312
